TPU v7x, 32 devices: a whole 2x2x4 slice. The times are simulated.
32 devices in a mesh: parts: 2 (over y), row: 4 (over z), col: 2 (over x), mode: 2 (over core).
Axes of the slice: x: 2, y: 2, z: 4, core: 2. Of those that a mesh axis runs over, the one named last changes fastest.
Arguments:
- obj: float32 [2, 1024, 512], P(None, ('parts', 'row'), 'col'), parts along dimension 1, may hold values from -5 to 5
- probe: float32 [2, 2, 256, 128], P('mode', None, 'parts'), parts along dimension 2, may hold values from -5 to 5
- positions: int32 [4, 2, 32, 2], P('row', 'col', 'parts'), parts along dimension 2, may hold values from -64 to 447, as said below
- counts: int32 [8, 2], P(('parts', 'row'), 'col'), parts along dimension 0, may hold values from 4 to 16, as said below
- measured: float32 [4, 2, 32, 128, 128], P('row', 'col', 'parts'), parts along dimension 2, may hold values from 0.1 to 6
Outputs:
- object_out: float32 [2, 1024, 512], P(None, ('parts', 'row'), 'col'), parts along dimension 1
- probe_out: float32 [2, 2, 256, 128], P('mode', None, 'parts'), parts along dimension 2
There are 2 independent parts, one for each index of `parts`. A program takes and returns all parts, laid end to end along the dimension named above; each array names one. Nothing has to cross between parts.
Inputs may be any that keep to these rules, and one draw needn't show every extreme that they name: `positions`: position s of tile (r, c) has row in [r * 128 - 128//2, (r+1) * 128 - 128//2) and column in [c * 256 - 128//2, (c+1) * 256 - 128//2). `counts`: some tile has all 16 slots live.
All inputs are finite; a program needn't handle non-finite values.
Results may differ from a plain program's by a relative error of at most 0.0001.
Values sent between devices are 32-bit elements; how exact they have to be, the bound alone decides.
No kernel may reach another device: no remote copies, remote signals or barrier semaphores. Data moves between devices by JAX's collectives and lax.ppermute only.
A program may use at most 64 MiB of HBM per device.

v0:
```python
import jax
import jax.numpy as jnp
from jax import lax
from jax.sharding import PartitionSpec as P

ITERS = 2


momentum = 0.5
object_rate = 0.1
probe_rate = 0.25


def passed_along(block, axis, distance):
    devices = range(lax.axis_size(axis))
    route = [(i - distance, i) for i in devices if i - distance in devices]
    return lax.ppermute(block, axis, route)


def padded(block, sides, width):
    for axis, dim in sides:
        count = lax.axis_size(axis)
        forward = [(i, i + 1) for i in range(count - 1)]
        backward = [(target, source) for source, target in forward]
        low = lax.ppermute(
            lax.slice_in_dim(block, block.shape[dim] - width, None, axis=dim), axis, forward
        )
        high = lax.ppermute(lax.slice_in_dim(block, 0, width, axis=dim), axis, backward)
        block = jnp.concatenate([low, block, high], axis=dim)
    return block


def tables(probe_size):
    steps_axis = jnp.arange(probe_size, dtype=jnp.int32)
    phase = steps_axis[:, None] * steps_axis[None, :] % probe_size
    angle = phase.astype(jnp.float32) * (2.0 * jnp.pi / probe_size)
    factor = 1.0 / jnp.sqrt(jnp.float32(probe_size))
    return (jnp.cos(angle) * factor, -jnp.sin(angle) * factor)


def transform(real_part, imag_part, table_real, table_imag):
    highest = lax.Precision.HIGHEST

    def from_left(matrix, values):
        return jnp.einsum("jk,pkl->pjl", matrix, values, precision=highest)

    def from_right(values, matrix):
        return jnp.einsum("pjl,ml->pjm", values, matrix, precision=highest)

    first_real = from_left(table_real, real_part) - from_left(table_imag, imag_part)
    first_imag = from_left(table_real, imag_part) + from_left(table_imag, real_part)
    second_real = from_right(first_real, table_real) - from_right(first_imag, table_imag)
    second_imag = from_right(first_real, table_imag) + from_right(first_imag, table_real)
    return (second_real, second_imag)


def block_terms(
    patches, probe_modes, measured_block, live_mask, table_real, table_imag, combine_modes
):
    count_pos = patches.shape[0]
    count_modes = probe_modes.shape[0]
    probe_size = patches.shape[-1]
    probe_real = probe_modes[:, 0][None]
    probe_imag = probe_modes[:, 1][None]
    patch_real = patches[:, 0][:, None]
    patch_imag = patches[:, 1][:, None]
    wave_real = (probe_real * patch_real - probe_imag * patch_imag).reshape(
        count_pos * count_modes, probe_size, probe_size
    )
    wave_imag = (probe_real * patch_imag + probe_imag * patch_real).reshape(
        count_pos * count_modes, probe_size, probe_size
    )
    far_real, far_imag = transform(wave_real, wave_imag, table_real, table_imag)
    far_real = far_real.reshape(count_pos, count_modes, probe_size, probe_size)
    far_imag = far_imag.reshape(count_pos, count_modes, probe_size, probe_size)
    intensity = combine_modes(jnp.sum(far_real * far_real + far_imag * far_imag, axis=1))
    weights = (1.0 - jnp.sqrt(measured_block) / jnp.sqrt(intensity + 1.0)) * live_mask[
        :, None, None
    ]
    scaled_real = (weights[:, None] * far_real).reshape(
        count_pos * count_modes, probe_size, probe_size
    )
    scaled_imag = (weights[:, None] * far_imag).reshape(
        count_pos * count_modes, probe_size, probe_size
    )
    back_real, back_imag = transform(scaled_real, scaled_imag, table_real, -table_imag)
    back_real = back_real.reshape(count_pos, count_modes, probe_size, probe_size)
    back_imag = back_imag.reshape(count_pos, count_modes, probe_size, probe_size)
    object_real = jnp.sum(probe_real * back_real + probe_imag * back_imag, axis=1)
    object_imag = jnp.sum(probe_real * back_imag - probe_imag * back_real, axis=1)
    grad_real = jnp.sum(patch_real * back_real + patch_imag * back_imag, axis=0)
    grad_imag = jnp.sum(patch_real * back_imag - patch_imag * back_real, axis=0)
    return (
        jnp.stack([object_real, object_imag], axis=1),
        jnp.stack([grad_real, grad_imag], axis=1),
    )


def extract(extended, offsets, probe_size):

    def cut(offset):
        return lax.dynamic_slice(
            extended, (jnp.int32(0), offset[0], offset[1]), (2, probe_size, probe_size)
        )

    return jax.vmap(cut)(offsets)


def place_all(grad, pieces, offsets):
    probe_size = pieces.shape[-1]

    def place(index, current_grad):
        offset = offsets[index]
        corner = (jnp.int32(0), offset[0], offset[1])
        current = lax.dynamic_slice(current_grad, corner, (2, probe_size, probe_size))
        return lax.dynamic_update_slice(current_grad, current + pieces[index], corner)

    return lax.fori_loop(0, pieces.shape[0], place, grad)


def sum_modes(intensity):
    return lax.psum(intensity, "mode")


def sum_object(grad):
    return lax.psum(grad, "mode")


def return_rims(grad, half_probe):
    inner_cols = grad.shape[2] - 2 * half_probe
    from_left = passed_along(grad[:, :, inner_cols + half_probe :], "col", 1)
    from_right = passed_along(grad[:, :, :half_probe], "col", -1)
    grad = grad.at[:, :, half_probe : 2 * half_probe].add(from_left)
    grad = grad.at[:, :, inner_cols : inner_cols + half_probe].add(from_right)
    grad = grad[:, :, half_probe : inner_cols + half_probe]
    inner_rows = grad.shape[1] - 2 * half_probe
    from_above = passed_along(grad[:, inner_rows + half_probe :, :], "row", 1)
    from_below = passed_along(grad[:, :half_probe, :], "row", -1)
    grad = grad.at[:, half_probe : 2 * half_probe, :].add(from_above)
    grad = grad.at[:, inner_rows : inner_rows + half_probe, :].add(from_below)
    return grad[:, half_probe : inner_rows + half_probe, :]


def on_device(obj, probe, positions, counts, measured):
    probe_size = probe.shape[-1]
    half_probe = probe_size // 2
    tile_rows = obj.shape[1]
    tile_cols = obj.shape[2]
    slot_count = positions.shape[2]
    table_real, table_imag = tables(probe_size)
    corner = jnp.stack(
        [
            lax.axis_index("row") * tile_rows - half_probe,
            lax.axis_index("col") * tile_cols - half_probe,
        ]
    )
    offsets = positions[0, 0] - corner[None, :]
    measured_block = measured[0, 0]
    live_mask = (jnp.arange(slot_count, dtype=jnp.int32) < counts[0, 0]).astype(jnp.float32)
    probe_step = probe_rate / (slot_count * lax.axis_size("row") * lax.axis_size("col"))
    prev_object, prev_probe = (obj, probe)
    cur_object, cur_probe = (obj, probe)
    for iteration in range(ITERS):
        ahead_object = cur_object + momentum * (cur_object - prev_object)
        ahead_probe = cur_probe + momentum * (cur_probe - prev_probe)
        extended = padded(ahead_object, (("row", 1), ("col", 2)), half_probe)
        patches = extract(extended, offsets, probe_size)
        pieces, probe_grad = block_terms(
            patches, ahead_probe, measured_block, live_mask, table_real, table_imag, sum_modes
        )
        probe_grad = lax.psum(probe_grad, ("row", "col"))
        object_grad = place_all(jnp.zeros_like(extended), pieces, offsets)
        object_grad = return_rims(sum_object(object_grad), half_probe)
        prev_object, prev_probe = (cur_object, cur_probe)
        cur_object = ahead_object - object_rate * object_grad
        cur_probe = ahead_probe - probe_step * probe_grad
    return (cur_object, cur_probe)


def solution(mesh):
    in_specs = (
        P(None, ("parts", "row"), "col"),
        P("mode", None, "parts", None),
        P("row", "col", "parts", None),
        P(("parts", "row"), "col"),
        P("row", "col", "parts", None, None),
    )
    out_specs = (P(None, ("parts", "row"), "col"), P("mode", None, "parts", None))
    return jax.shard_map(
        on_device, mesh=mesh, in_specs=in_specs, out_specs=out_specs, check_vma=False
    )
```

profile of v0, /device:TPU:0, one launch (start us, length us, event | category | flops | bytes accessed | tf_op | source)
XLA Modules:
  0.0 659.4 jit_solution(14160299892981163315)
XLA Ops:
  8.2 4.9 collective-permute-start
  16.2 3.8 collective-permute-done.1
  20.2 3.4 collective-permute-start.2
  25.0 2.8 collective-permute-done.2
  27.7 4.2 collective-permute-done.3
  32.5 30.9 %while.38 = (s32[]{:T(128)}, f32[2,256,384]{2,1,0:T(8,128)S(1)}, s32[16,3]{0,1:T(4,128)S(1)}, f32[16,2,128,128]{3,2,0,1:T(8,128)S(1)}, s32[]{:T(128)}) while((s32[]{:T(128)}, f32[2,256,384]{2,1,0:T(8,128)S(1)}, s32[16,3]{0,1:T(4,128)S(1)}, f32[16,2,128,128]{3,2,0,1:T(8,128)S(1)}, s32[]{:T(128)}) %tuple.142), condition=%wide.while_cond.8, body=%wide.while_body.8.sunk | while | flops 2 | bytes 262261 | solution.py:102
  75.4 2.3 convolution_subtract_fusion.6
  77.7 3.3 multiply_add_fusion.2
  81.8 18.4 %all-reduce.7.cloned.1.call-done = f32[16,128,128]{2,1,0:T(8,128)} async-done(((f32[16,128,128]{2,1,0:T(8,128)}), f32[16,128,128]{2,1,0:T(8,128)}) %all-reduce.7.cloned.1.call-update) | async-done | bytes 1048592 | tf_op jit(solution)/shard_map/psum | solution.py:122
  112.0 2.2 fusion.4
  118.9 107.4 %while.36 = (s32[]{:T(128)}, f32[2,256,384]{2,1,0:T(8,128)S(1)}, s32[16,2]{0,1:T(2,128)S(1)}, f32[16,2,128,128]{3,2,0,1:T(8,128)S(1)}, s32[]{:T(128)}, /*index=5*/s32[]{:T(128)}, s32[]{:T(128)}, s32[]{:T(128)}) while((s32[]{:T(128)}, f32[2,256,384]{2,1,0:T(8,128)S(1)}, s32[16,2]{0,1:T(2,128)S(1)}, f32[16,2,128,128]{3,2,0,1:T(8,128)S(1)}, ...), condition=%wide.region_2.3_spmd, body=%wide.region_1.2_spmd.sunk | while | flops 32776 | bytes 655565 | solution.py:118
  129.4 2.5 dynamic_update_slice.16
  136.2 2.2 dynamic_update_slice.16
  142.8 2.5 dynamic_update_slice.16
  149.7 2.4 dynamic_update_slice.16
  156.4 2.2 dynamic_update_slice.16
  163.0 2.3 dynamic_update_slice.16
  169.8 2.3 dynamic_update_slice.16
  176.5 2.4 dynamic_update_slice.16
  183.3 2.2 dynamic_update_slice.16
  189.9 2.4 dynamic_update_slice.16
  196.7 2.4 dynamic_update_slice.16
  203.5 2.5 dynamic_update_slice.16
  210.4 2.4 dynamic_update_slice.16
  217.1 2.5 dynamic_update_slice.16
  224.0 2.3 dynamic_update_slice.16
  227.3 20.2 %all-reduce.9.cloned.1.call-done = f32[2,256,384]{2,1,0:T(8,128)} async-done(((f32[2,256,384]{2,1,0:T(8,128)}), f32[2,256,384]{2,1,0:T(8,128)}) %all-reduce.9.cloned.1.call-update) | async-done | bytes 786448 | tf_op jit(solution)/shard_map/psum | solution.py:126
  248.7 3.7 collective-permute-start.4
  253.6 4.7 collective-permute-done.4
  259.4 2.3 scatter-add.26
  266.4 3.4 collective-permute-start.6
  274.2 4.7 collective-permute-done.7
  279.0 3.4 collective-permute-start.8
  283.7 57.1 %all-reduce.11.cloned.1.call-done = f32[1,2,128,128]{3,2,1,0:T(8,128)} async-done(((f32[1,2,128,128]{3,2,1,0:T(8,128)}), f32[1,2,128,128]{3,2,1,0:T(8,128)}) %all-reduce.11.cloned.1.call-update) | async-done | bytes 131088 | tf_op jit(solution)/shard_map/psum | solution.py:171
  342.0 2.7 collective-permute-start.10
  346.0 2.5 collective-permute-done.10
  348.5 4.4 collective-permute-done.11
  353.5 31.1 %while.39 = (s32[]{:T(128)}, f32[2,256,384]{2,1,0:T(8,128)S(1)}, s32[16,3]{0,1:T(4,128)S(1)}, f32[16,2,128,128]{3,2,0,1:T(8,128)S(1)}, s32[]{:T(128)}) while((s32[]{:T(128)}, f32[2,256,384]{2,1,0:T(8,128)S(1)}, s32[16,3]{0,1:T(4,128)S(1)}, f32[16,2,128,128]{3,2,0,1:T(8,128)S(1)}, s32[]{:T(128)}) %tuple.166), condition=%wide.while_cond.9, body=%wide.while_body.9.sunk | while | flops 2 | bytes 262261 | solution.py:102
  398.8 3.3 multiply_add_fusion
  402.2 18.8 %all-reduce.13.cloned.1.call-done = f32[16,128,128]{2,1,0:T(8,128)} async-done(((f32[16,128,128]{2,1,0:T(8,128)}), f32[16,128,128]{2,1,0:T(8,128)}) %all-reduce.13.cloned.1.call-update) | async-done | bytes 1048592 | tf_op jit(solution)/shard_map/psum | solution.py:122
  432.8 2.2 fusion
  439.8 106.3 %while.37 = (s32[]{:T(128)}, f32[2,256,384]{2,1,0:T(8,128)S(1)}, s32[16,2]{0,1:T(2,128)S(1)}, f32[16,2,128,128]{3,2,0,1:T(8,128)S(1)}, s32[]{:T(128)}, /*index=5*/s32[]{:T(128)}, s32[]{:T(128)}, s32[]{:T(128)}) while((s32[]{:T(128)}, f32[2,256,384]{2,1,0:T(8,128)S(1)}, s32[16,2]{0,1:T(2,128)S(1)}, f32[16,2,128,128]{3,2,0,1:T(8,128)S(1)}, ...), condition=%wide.region_9.10_spmd, body=%wide.region_8.9_spmd.sunk | while | flops 32776 | bytes 655565 | solution.py:118
  450.1 2.5 dynamic_update_slice.17
  456.9 2.2 dynamic_update_slice.17
  463.4 2.5 dynamic_update_slice.17
  470.2 2.4 dynamic_update_slice.17
  476.9 2.2 dynamic_update_slice.17
  483.4 2.3 dynamic_update_slice.17
  490.1 2.3 dynamic_update_slice.17
  496.7 2.4 dynamic_update_slice.17
  503.4 2.2 dynamic_update_slice.17
  510.0 2.4 dynamic_update_slice.17
  516.7 2.4 dynamic_update_slice.17
  523.4 2.5 dynamic_update_slice.17
  530.2 2.4 dynamic_update_slice.17
  537.0 2.5 dynamic_update_slice.17
  543.8 2.3 dynamic_update_slice.17
  547.1 20.1 %all-reduce.15.cloned.1.call-done = f32[2,256,384]{2,1,0:T(8,128)} async-done(((f32[2,256,384]{2,1,0:T(8,128)}), f32[2,256,384]{2,1,0:T(8,128)}) %all-reduce.15.cloned.1.call-update) | async-done | bytes 786448 | tf_op jit(solution)/shard_map/psum | solution.py:126
  568.5 3.7 collective-permute-start.12
  574.1 4.0 collective-permute-done.12
  580.8 2.6 collective-permute-done.13
  584.3 3.4 collective-permute-start.14
  587.7 55.1 %all-reduce.17.cloned.1.call-done = f32[1,2,128,128]{3,2,1,0:T(8,128)} async-done(((f32[1,2,128,128]{3,2,1,0:T(8,128)}), f32[1,2,128,128]{3,2,1,0:T(8,128)}) %all-reduce.17.cloned.1.call-update) | async-done | bytes 131088 | tf_op jit(solution)/shard_map/psum | solution.py:171
  646.0 5.4 collective-permute-done.15
  (316 shorter events, 182.0 us)
Async XLA Ops:
  7.2 92.9 %all-reduce.7.cloned.1.call-start = ((), (), s32[]{:S(2)}) async-start(), calls=%async_computation | async-start | bytes 2097152 | tf_op jit(solution)/shard_map/psum | solution.py:122
  8.2 8.0 %collective-permute-start = (f32[2,64,256]{2,1,0:T(8,128)S(1)}, f32[2,64,256]{2,1,0:T(8,128)S(1)}, u32[]{:S(2)}, u32[]{:S(2)}) collective-permute-start(f32[2,64,256]{2,1,0:T(8,128)S(1)} %get-tuple-element.344), channel_id=1, source_target_pairs={{0,4},{4,8},{8,12},{1,5},{5,9},{9,13},{2,6},{6,10},{10,14},{3,7},{... | collective-permute-start | bytes 393224 | tf_op jit(solution)/shard_map/ppermute | solution.py:25
  13.2 6.9 %collective-permute-start.1 = (f32[2,64,256]{2,1,0:T(8,128)S(1)}, f32[2,64,256]{2,1,0:T(8,128)S(1)}, u32[]{:S(2)}, u32[]{:S(2)}) collective-permute-start(f32[2,64,256]{2,1,0:T(8,128)S(1)} %get-tuple-element.345), channel_id=1, source_target_pairs={{4,0},{8,4},{12,8},{5,1},{9,5},{13,9},{6,2},{10,6},{14,10},{7,3},{... | collective-permute-start | bytes 393224 | tf_op jit(solution)/shard_map/ppermute | solution.py:28
  20.2 7.5 %collective-permute-start.2 = (f32[2,256,64]{2,1,0:T(8,128)S(1)}, f32[2,256,64]{2,1,0:T(8,128)S(1)}, u32[]{:S(2)}, u32[]{:S(2)}) collective-permute-start(f32[2,256,64]{2,1,0:T(8,128)S(1)} %get-tuple-element.340), channel_id=1, source_target_pairs={{0,2},{1,3},{4,6},{5,7},{8,10},{9,11},{12,14},{13,15},{16,18},{17,... | collective-permute-start | bytes 393224 | tf_op jit(solution)/shard_map/ppermute | solution.py:25
  23.6 8.3 %collective-permute-start.3 = (f32[2,256,64]{2,1,0:T(8,128)S(1)}, f32[2,256,64]{2,1,0:T(8,128)S(1)}, u32[]{:S(2)}, u32[]{:S(2)}) collective-permute-start(f32[2,256,64]{2,1,0:T(8,128)S(1)} %get-tuple-element.341), channel_id=1, source_target_pairs={{2,0},{3,1},{6,4},{7,5},{10,8},{11,9},{14,12},{15,13},{18,16},{19,... | collective-permute-start | bytes 393224 | tf_op jit(solution)/shard_map/ppermute | solution.py:28
  81.0 166.4 %all-reduce.9.cloned.1.call-start = ((), (), s32[]{:S(2)}) async-start(), calls=%async_computation.1 | async-start | bytes 1572864 | tf_op jit(solution)/shard_map/psum | solution.py:126
  102.1 2.0 copy-start
  226.3 0.9 copy-start.3
  227.3 113.6 %all-reduce.11.cloned.1.call-start = ((), (), s32[]{:S(2)}) async-start(), calls=%async_computation.2 | async-start | bytes 262144 | tf_op jit(solution)/shard_map/psum | solution.py:171
  248.7 9.7 %collective-permute-start.4 = (f32[2,256,64]{2,1,0:T(8,128)S(1)}, f32[2,256,64]{2,1,0:T(8,128)S(1)}, u32[]{:S(2)}, u32[]{:S(2)}) collective-permute-start(f32[2,256,64]{2,1,0:T(8,128)S(1)} %get-tuple-element.337), channel_id=1, source_target_pairs={{0,2},{1,3},{4,6},{5,7},{8,10},{9,11},{12,14},{13,15},{16,18},{17,... | collective-permute-start | bytes 393224 | tf_op jit(solution)/shard_map/ppermute | solution.py:17
  252.3 10.1 %collective-permute-start.5 = (f32[2,256,64]{2,1,0:T(8,128)S(1)}, f32[2,256,64]{2,1,0:T(8,128)S(1)}, u32[]{:S(2)}, u32[]{:S(2)}) collective-permute-start(f32[2,256,64]{2,1,0:T(8,128)S(1)} %get-tuple-element.336), channel_id=1, source_target_pairs={{2,0},{3,1},{6,4},{7,5},{10,8},{11,9},{14,12},{15,13},{18,16},{19,... | collective-permute-start | bytes 393224 | tf_op jit(solution)/shard_map/ppermute | solution.py:17
  261.7 17.2 %copy-start.7 = (f32[2,128,256]{2,1,0:T(8,128)S(1)}, f32[2,128,256]{2,1,0:T(8,128)}, u32[]{:S(2)}) copy-start(f32[2,128,256]{2,1,0:T(8,128)} %param.25) | copy-start | bytes 786436
  265.2 75.7 %copy-start.8 = (f32[1,2,128,128]{3,2,1,0:T(8,128)S(1)}, f32[1,2,128,128]{3,2,1,0:T(8,128)}, u32[]{:S(2)}) copy-start(f32[1,2,128,128]{3,2,1,0:T(8,128)} %param.26) | copy-start | bytes 393220
  266.4 6.8 %collective-permute-start.6 = (f32[2,64,256]{2,1,0:T(8,128)S(1)}, f32[2,64,256]{2,1,0:T(8,128)S(1)}, u32[]{:S(2)}, u32[]{:S(2)}) collective-permute-start(f32[2,64,256]{2,1,0:T(8,128)S(1)} %get-tuple-element.335), channel_id=1, source_target_pairs={{0,4},{4,8},{8,12},{1,5},{5,9},{9,13},{2,6},{6,10},{10,14},{3,7},{... | collective-permute-start | bytes 393224 | tf_op jit(solution)/shard_map/ppermute | solution.py:17
  270.5 150.5 %all-reduce.13.cloned.1.call-start = ((), (), s32[]{:S(2)}) async-start(), calls=%async_computation.3 | async-start | bytes 2097152 | tf_op jit(solution)/shard_map/psum | solution.py:122
  271.9 7.0 %collective-permute-start.7 = (f32[2,64,256]{2,1,0:T(8,128)S(1)}, f32[2,64,256]{2,1,0:T(8,128)S(1)}, u32[]{:S(2)}, u32[]{:S(2)}) collective-permute-start(f32[2,64,256]{2,1,0:T(8,128)S(1)} %get-tuple-element.334), channel_id=1, source_target_pairs={{4,0},{8,4},{12,8},{5,1},{9,5},{13,9},{6,2},{10,6},{14,10},{7,3},{... | collective-permute-start | bytes 393224 | tf_op jit(solution)/shard_map/ppermute | solution.py:17
  279.0 62.8 %collective-permute-start.8 = (f32[2,64,256]{2,1,0:T(8,128)S(1)}, f32[2,64,256]{2,1,0:T(8,128)S(1)}, u32[]{:S(2)}, u32[]{:S(2)}) collective-permute-start(f32[2,64,256]{2,1,0:T(8,128)S(1)} %get-tuple-element.342), channel_id=1, source_target_pairs={{0,4},{4,8},{8,12},{1,5},{5,9},{9,13},{2,6},{6,10},{10,14},{3,7},{... | collective-permute-start | bytes 393224 | tf_op jit(solution)/shard_map/ppermute | solution.py:25
  282.4 59.4 %collective-permute-start.9 = (f32[2,64,256]{2,1,0:T(8,128)S(1)}, f32[2,64,256]{2,1,0:T(8,128)S(1)}, u32[]{:S(2)}, u32[]{:S(2)}) collective-permute-start(f32[2,64,256]{2,1,0:T(8,128)S(1)} %get-tuple-element.343), channel_id=1, source_target_pairs={{4,0},{8,4},{12,8},{5,1},{9,5},{13,9},{6,2},{10,6},{14,10},{7,3},{... | collective-permute-start | bytes 393224 | tf_op jit(solution)/shard_map/ppermute | solution.py:28
  341.8 11.2 %copy-start.5 = (f32[1,2,128,128]{3,2,1,0:T(8,128)}, f32[1,2,128,128]{3,2,1,0:T(8,128)S(1)}, u32[]{:S(2)}) copy-start(f32[1,2,128,128]{3,2,1,0:T(8,128)S(1)} %multiply_add_fusion.10) | copy-start | bytes 393220
  342.0 6.6 collective-permute-start.10
  344.7 8.3 %collective-permute-start.11 = (f32[2,256,64]{2,1,0:T(8,128)S(1)}, f32[2,256,64]{2,1,0:T(8,128)S(1)}, u32[]{:S(2)}, u32[]{:S(2)}) collective-permute-start(f32[2,256,64]{2,1,0:T(8,128)S(1)} %get-tuple-element.339), channel_id=1, source_target_pairs={{2,0},{3,1},{6,4},{7,5},{10,8},{11,9},{14,12},{15,13},{18,16},{19,... | collective-permute-start | bytes 393224 | tf_op jit(solution)/shard_map/ppermute | solution.py:28
  402.1 165.1 %all-reduce.15.cloned.1.call-start = ((), (), s32[]{:S(2)}) async-start(), calls=%async_computation.4 | async-start | bytes 1572864 | tf_op jit(solution)/shard_map/psum | solution.py:126
  422.9 2.0 copy-start.1
  546.1 0.9 copy-start.2
  547.0 95.8 %copy-start.6 = (f32[1,2,128,128]{3,2,1,0:T(8,128)S(1)}, f32[1,2,128,128]{3,2,1,0:T(8,128)}, u32[]{:S(2)}) copy-start(f32[1,2,128,128]{3,2,1,0:T(8,128)} %copy-done.5) | copy-start | bytes 393220
  547.0 95.8 %all-reduce.17.cloned.1.call-start = ((), (), s32[]{:S(2)}) async-start(), calls=%async_computation.5 | async-start | bytes 262144 | tf_op jit(solution)/shard_map/psum | solution.py:171
  567.2 12.0 %copy-start.4 = (f32[2,256,384]{2,1,0:T(8,128)S(1)}, f32[2,256,384]{2,1,0:T(8,128)}, u32[]{:S(2)}) copy-start(f32[2,256,384]{2,1,0:T(8,128)} %all-reduce.15.cloned.1.call-done) | copy-start | bytes 2359300
  568.5 9.7 %collective-permute-start.12 = (f32[2,256,64]{2,1,0:T(8,128)S(1)}, f32[2,256,64]{2,1,0:T(8,128)S(1)}, u32[]{:S(2)}, u32[]{:S(2)}) collective-permute-start(f32[2,256,64]{2,1,0:T(8,128)S(1)} %get-tuple-element.333), channel_id=1, source_target_pairs={{0,2},{1,3},{4,6},{5,7},{8,10},{9,11},{12,14},{13,15},{16,18},{17,... | collective-permute-start | bytes 393224 | tf_op jit(solution)/shard_map/ppermute | solution.py:17
  572.8 10.6 %collective-permute-start.13 = (f32[2,256,64]{2,1,0:T(8,128)S(1)}, f32[2,256,64]{2,1,0:T(8,128)S(1)}, u32[]{:S(2)}, u32[]{:S(2)}) collective-permute-start(f32[2,256,64]{2,1,0:T(8,128)S(1)} %get-tuple-element.332), channel_id=1, source_target_pairs={{2,0},{3,1},{6,4},{7,5},{10,8},{11,9},{14,12},{15,13},{18,16},{19,... | collective-permute-start | bytes 393224 | tf_op jit(solution)/shard_map/ppermute | solution.py:17
  584.3 61.6 %collective-permute-start.14 = (f32[2,64,256]{2,1,0:T(8,128)S(1)}, f32[2,64,256]{2,1,0:T(8,128)S(1)}, u32[]{:S(2)}, u32[]{:S(2)}) collective-permute-start(f32[2,64,256]{2,1,0:T(8,128)S(1)} %get-tuple-element.331), channel_id=1, source_target_pairs={{0,4},{4,8},{8,12},{1,5},{5,9},{9,13},{2,6},{6,10},{10,14},{3,7},{... | collective-permute-start | bytes 393224 | tf_op jit(solution)/shard_map/ppermute | solution.py:17
  644.6 6.9 %collective-permute-start.15 = (f32[2,64,256]{2,1,0:T(8,128)S(1)}, f32[2,64,256]{2,1,0:T(8,128)S(1)}, u32[]{:S(2)}, u32[]{:S(2)}) collective-permute-start(f32[2,64,256]{2,1,0:T(8,128)S(1)} %get-tuple-element.330), channel_id=1, source_target_pairs={{4,0},{8,4},{12,8},{5,1},{9,5},{13,9},{6,2},{10,6},{14,10},{7,3},{... | collective-permute-start | bytes 393224 | tf_op jit(solution)/shard_map/ppermute | solution.py:17
Sparse Core Ops, SparseCore 0:
  81.2 18.8 all-reduce.6
  227.4 20.0 all-reduce.8
  270.6 70.1 all-reduce.10
  402.2 18.6 all-reduce.12
  547.1 20.0 all-reduce.14
  572.9 69.8 all-reduce.16
where the time goes:
time: 672 us; the launch traced here: 659 us
  waiting for transfers between devices  229 us (34%)
  local copies, waits for them, and re-layouts  169 us (25%)
  loops' own time  117 us (17%)
  matrix products  67.3 us (10%)
  starting transfers between devices  39.1 us (6%)
  other arithmetic  21.1 us (3%)
  between operations  15.9 us (2%)
    another operation x2, loops' own time, place_all(): return lax.fori_loop(0, pieces.shape[0], place, grad)  116 us
    psum x2, waiting for transfers between devices, on_device(): probe_grad = lax.psum(probe_grad, ('row', 'col'))  112 us
    dynamic_update_slice x32, local copies, waits for them, and re-layouts, place(): lax.dynamic_update_slice(current_grad, current + pieces[index], corner)  74.5 us
    gather x96, local copies, waits for them, and re-layouts  60.9 us
    psum x2, waiting for transfers between devices, sum_object(): return lax.psum(grad, 'mode')  40.3 us
    psum x2, waiting for transfers between devices, sum_modes(): return lax.psum(intensity, 'mode')  37.1 us
    dot_general x16, matrix products, from_right(): return jnp.einsum('pjl,ml->pjm', values, matrix, precision=highest)  34.8 us
    dot_general x16, matrix products, from_left(): return jnp.einsum('jk,pkl->pjl', matrix, values, precision=highest)  32.5 us
  transfers between devices with their start and end apart: 22, of which 17 were waited for; matrix products, arithmetic and copies ran while one was open for 2% of the time, Pallas kernels for 0%

commit v1 on v0

v1 whole, which is shorter than its diff:
```python
import jax
import jax.numpy as jnp
import ml_dtypes
import numpy as np
from jax import lax
from jax.experimental import pallas as pl
from jax.experimental.pallas import tpu as pltpu
from jax.sharding import PartitionSpec as P

ITERS = 2


momentum = 0.5
object_rate = 0.1
probe_rate = 0.25


def dft_tables(size):
    steps = np.arange(size)
    angle = (steps[:, None] * steps[None, :] % size) * (2.0 * np.pi / size)
    cosine, sine = np.cos(angle) / np.sqrt(size), np.sin(angle) / np.sqrt(size)
    ahead = np.block([[cosine, -sine], [sine, cosine]]).astype(np.float32)
    halves = []
    for table in (ahead, ahead.T):
        high = table.astype(ml_dtypes.bfloat16)
        low = (table - high.astype(np.float32)).astype(ml_dtypes.bfloat16)
        halves += [high, low]
    return halves


def split(values):
    high = values.astype(jnp.bfloat16)
    return high, (values - high.astype(jnp.float32)).astype(jnp.bfloat16)


def matmul(left, right):
    return jnp.dot(left, right, preferred_element_type=jnp.float32)


def from_right(values, high, low):
    values_high, values_low = split(values)
    return matmul(values_high, high) + (matmul(values_low, high) + matmul(values_high, low))


def from_left(high, low, values):
    values_high, values_low = split(values)
    return matmul(high, values_high) + (matmul(low, values_high) + matmul(high, values_low))


def gradient_kernel(
    scalars, mine, theirs, measured, ahead_high, ahead_low, behind_high, behind_low, keep, send,
    state, grad, *, group
):
    size = measured.shape[-1]
    slots = measured.shape[0]
    tiles = mine.shape[0] // size - 2
    me = scalars[0]
    live_slots = scalars[1]
    state[me] = mine[...]
    state[1 - me] = theirs[...]
    grad[...] = jnp.zeros_like(grad)
    lane = lax.broadcasted_iota(jnp.int32, (size, size), 1)
    base = tiles * size

    def plane(mode, part):
        return state[mode, base + part * size : base + (part + 1) * size, :]

    def rows_of(row, tile):
        return pl.ds(tile * (2 * size) + row, size)

    def one_group(first):
        places, patches, waves = [], [], []
        for index in range(group):
            slot = 2 * (first + index) + me
            row = scalars[2 + 2 * slot]
            col = scalars[3 + 2 * slot]
            tile = col // size
            shift = col % size
            places.append((slot, row, tile, shift))
            patch = []
            for part in range(2):
                near = state[part, rows_of(row, tile), :]
                far = state[part, rows_of(row, tile + 1), :]
                patch.append(
                    pltpu.roll(jnp.where(lane >= shift, near, far), (size - shift) % size, 1)
                )
            patches.append(patch)
            for mode in range(2):
                real, imag = plane(mode, 0), plane(mode, 1)
                waves.append(
                    jnp.concatenate(
                        [real * patch[0] - imag * patch[1], real * patch[1] + imag * patch[0]],
                        axis=1,
                    )
                )
        half = from_right(jnp.concatenate(waves, axis=0), ahead_high[...], ahead_low[...])
        scaled = []
        for index in range(group):
            first_mode = half[2 * index * size : (2 * index + 1) * size]
            second_mode = half[(2 * index + 1) * size : (2 * index + 2) * size]
            turned = jnp.concatenate(
                [
                    jnp.concatenate([first_mode[:, :size], second_mode[:, :size]], axis=1),
                    jnp.concatenate([first_mode[:, size:], second_mode[:, size:]], axis=1),
                ],
                axis=0,
            )
            far_field = from_left(behind_high[...], behind_low[...], turned)
            power = far_field * far_field
            power = power[:size] + power[size:]
            power = power[:, :size] + power[:, size:]
            slot = places[index][0]
            live = jnp.where(slot < live_slots, 1.0, 0.0).astype(jnp.float32)
            weight = (
                1.0 - jnp.sqrt(measured[first + index, 0]) * lax.rsqrt(power + 1.0)
            ) * live
            weight = jnp.concatenate([weight, weight], axis=1)
            weight = jnp.concatenate([weight, weight], axis=0)
            back = from_left(ahead_high[...], ahead_low[...], weight * far_field)
            for mode in range(2):
                lanes = slice(mode * size, (mode + 1) * size)
                scaled.append(jnp.concatenate([back[:size, lanes], back[size:, lanes]], axis=1))
        chi = from_right(jnp.concatenate(scaled, axis=0), behind_high[...], behind_low[...])
        for index in range(group):
            _, row, tile, shift = places[index]
            pieces = [0.0, 0.0]
            for mode in range(2):
                start = (2 * index + mode) * size
                chi_real = chi[start : start + size, :size]
                chi_imag = chi[start : start + size, size:]
                real, imag = plane(mode, 0), plane(mode, 1)
                pieces[0] = pieces[0] + (real * chi_real + imag * chi_imag)
                pieces[1] = pieces[1] + (real * chi_imag - imag * chi_real)
                patch_real, patch_imag = patches[index]
                grad[mode, base : base + size, :] += (
                    patch_real * chi_real + patch_imag * chi_imag
                )
                grad[mode, base + size : base + 2 * size, :] += (
                    patch_real * chi_imag - patch_imag * chi_real
                )
            for part in range(2):
                turned_back = pltpu.roll(pieces[part], shift, 1)
                inside = lane >= shift
                grad[part, rows_of(row, tile), :] += jnp.where(inside, turned_back, 0.0)
                grad[part, rows_of(row, tile + 1), :] += jnp.where(inside, 0.0, turned_back)

    @pl.loop(0, slots // group)
    def _(step):
        one_group(step * group)

    keep[...] = grad[me]
    send[...] = grad[1 - me]


def gradients(scalars, mine, theirs, measured):
    size = measured.shape[-1]
    slots = measured.shape[0] // 2
    shape = jax.ShapeDtypeStruct(mine.shape, jnp.float32)
    whole = pl.BlockSpec(mine.shape, lambda i, s: (0, 0))
    table = pl.BlockSpec((2 * size, 2 * size), lambda i, s: (0, 0))
    group = 4 if slots % 4 == 0 else 1

    def body(*refs):
        gradient_kernel(*refs, group=group)

    return pl.pallas_call(
        body,
        out_shape=(shape, shape),
        grid_spec=pltpu.PrefetchScalarGridSpec(
            num_scalar_prefetch=1,
            grid=(1,),
            in_specs=[
                whole,
                whole,
                pl.BlockSpec((slots, 1, size, size), lambda i, s: (0, s[0], 0, 0)),
                table,
                table,
                table,
                table,
            ],
            out_specs=[whole, whole],
            scratch_shapes=[
                pltpu.VMEM((2,) + mine.shape, jnp.float32),
                pltpu.VMEM((2,) + mine.shape, jnp.float32),
            ],
        ),
        compiler_params=pltpu.CompilerParams(vmem_limit_bytes=32 * 1024 * 1024),
        name="gradients",
    )(
        scalars,
        mine,
        theirs,
        measured.reshape(slots, 2, size, size),
        *[jnp.asarray(t) for t in dft_tables(size)],
    )


def neighbour_pairs(count, parity):
    pairs = [(i, i + 1) for i in range(parity, count - 1, 2)]
    return pairs + [(b, a) for a, b in pairs]


def sum_pairs(count, step):
    return [(i, i ^ (2 ** (step + 1) - 1)) for i in range(count)]


def swap_modes(block):
    return lax.ppermute(block, "mode", [(0, 1), (1, 0)])


def along_axis(block, axis, sides):
    count = lax.axis_size(axis)
    me = lax.axis_index(axis)
    low, high = sides
    steps = max(count - 1, 0).bit_length()
    done = 0
    for parity in (0, 1):
        pairs = neighbour_pairs(count, parity)
        if not pairs:
            continue
        is_low = me % 2 == parity
        shared = jnp.where(is_low, block[jnp.array(high)], block[jnp.array(low)])
        with_probe = parity == 0 or count == 4
        if with_probe:
            got = lax.ppermute(
                jnp.concatenate([shared, block[-2:]]), axis, sum_pairs(count, done)
            )
            done += 1
            probe = block[-2:] + got[-2:]
            got = got[:-2]
        else:
            got = lax.ppermute(shared, axis, pairs)
            probe = block[-2:]
        to_high = jnp.where(is_low & (me < count - 1), got, 0.0)
        to_low = jnp.where(jnp.logical_not(is_low) & (me > 0), got, 0.0)
        parts = [block[i] for i in range(block.shape[0] - 2)]
        for place, (a, b) in enumerate(zip(low, high, strict=True)):
            parts[a] = parts[a] + to_low[place]
            parts[b] = parts[b] + to_high[place]
        block = jnp.concatenate([jnp.stack(parts), probe])
    while done < steps:
        probe = block[-2:]
        probe = probe + lax.ppermute(probe, axis, sum_pairs(count, done))
        block = jnp.concatenate([block[:-2], probe])
        done += 1
    return block


def combine(keep, send, size):
    block = (keep + swap_modes(send)).reshape(-1, size, size)
    columns = (block.shape[0] - 2) // 2
    block = along_axis(block, "col", ((0, 1), (2 * columns - 2, 2 * columns - 1)))
    uppers = tuple(2 * i for i in range(columns))
    lowers = tuple(2 * i + 1 for i in range(columns))
    return along_axis(block, "row", (uppers, lowers))


def padded(block, sides, width):
    for axis, dim in sides:
        count = lax.axis_size(axis)
        me = lax.axis_index(axis)
        first = lax.slice_in_dim(block, 0, width, axis=dim)
        last = lax.slice_in_dim(block, block.shape[dim] - width, None, axis=dim)
        low = high = jnp.zeros_like(first)
        for parity in (0, 1):
            pairs = neighbour_pairs(count, parity)
            if not pairs:
                continue
            is_low = me % 2 == parity
            got = lax.ppermute(jnp.where(is_low, last, first), axis, pairs)
            low = jnp.where(is_low, low, got)
            high = jnp.where(is_low, got, high)
        block = jnp.concatenate([low, block, high], axis=dim)
    return block


def on_device(obj, probe, positions, counts, measured):
    size = probe.shape[-1]
    half = size // 2
    tile_rows, tile_cols = obj.shape[1:]
    slot_count = positions.shape[2]
    me = lax.axis_index("mode")
    row = lax.axis_index("row")
    col = lax.axis_index("col")
    corner = jnp.stack([row * tile_rows - half, col * tile_cols - half])
    offsets = positions[0, 0] - corner[None, :]
    scalars = jnp.concatenate([jnp.stack([me, counts[0, 0]]), offsets.reshape(-1)])
    probe_step = probe_rate / (slot_count * lax.axis_size("row") * lax.axis_size("col"))

    own = lax.dynamic_index_in_dim(obj, me, 0, keepdims=False)
    extended = padded(own, (("col", 1), ("row", 0)), half)
    ext_rows, ext_cols = extended.shape
    columns = ext_cols // size
    blocks = extended.reshape(2, size, columns, size).transpose(2, 0, 1, 3)
    start = jnp.concatenate([blocks.reshape(2 * columns, size, size), probe[0]])

    global_rows = (
        jnp.arange(ext_rows, dtype=jnp.int32).reshape(1, 2, size, 1) + row * tile_rows - half
    )
    global_cols = (
        jnp.arange(ext_cols, dtype=jnp.int32).reshape(columns, 1, 1, size) + col * tile_cols - half
    )
    inside = (
        (global_rows >= 0)
        & (global_rows < tile_rows * lax.axis_size("row"))
        & (global_cols >= 0)
        & (global_cols < tile_cols * lax.axis_size("col"))
    )
    rates = jnp.concatenate(
        [
            jnp.where(inside, object_rate, 0.0).reshape(2 * columns, size, size),
            jnp.full((2, size, size), probe_step, jnp.float32),
        ]
    ).astype(jnp.float32)

    previous, current = start, start
    for iteration in range(ITERS):
        ahead = current + momentum * (current - previous)
        flat = ahead.reshape(-1, size)
        keep, send = gradients(scalars, flat, swap_modes(flat), measured[0, 0])
        total = combine(keep, send, size)
        previous, current = current, ahead - rates * total

    tile = current[:-2].reshape(columns, 2, size, size).transpose(1, 2, 0, 3)
    tile = tile.reshape(ext_rows, ext_cols)[half : half + tile_rows, half : half + tile_cols]
    other = swap_modes(tile)
    whole = jnp.stack([jnp.where(me == 0, tile, other), jnp.where(me == 0, other, tile)])
    return (whole, current[None, -2:])


def solution(mesh):
    in_specs = (
        P(None, ("parts", "row"), "col"),
        P("mode", None, "parts", None),
        P("row", "col", "parts", None),
        P(("parts", "row"), "col"),
        P("row", "col", "parts", None, None),
    )
    out_specs = (P(None, ("parts", "row"), "col"), P("mode", None, "parts", None))
    return jax.shard_map(
        on_device, mesh=mesh, in_specs=in_specs, out_specs=out_specs, check_vma=False
    )
```

time: 672 us -> 139 us (0.21)
  the two profiles are of different devices: /device:TPU:0 before, /device:TPU:19 now
where the time goes in v1:
time: 139 us
  waiting for transfers between devices  69.4 us (50%)
  local copies, waits for them, and re-layouts  22.6 us (16%)
  other arithmetic  19 us (14%)
  Pallas kernels  14 us (10%)
  starting transfers between devices  11.5 us (8%)
  between operations  2.06 us (1%)
    ppermute x6, waiting for transfers between devices, along_axis(): lax.ppermute(jnp.concatenate([shared, block[-2:]]), axis, sum_pairs(count...  58.4 us
    pallas_call x2, Pallas kernels, gradients(): pl.pallas_call(body, out_shape=(shape, shape), grid_spec=pltpu.PrefetchSc...  14 us
    gather x12, local copies, waits for them, and re-layouts, along_axis(): shared = jnp.where(is_low, block[jnp.array(high)], block[jnp.array(low)])  11.7 us
    unnamed x45, local copies, waits for them, and re-layouts  7.41 us
    ppermute x5, starting transfers between devices, swap_modes(): return lax.ppermute(block, 'mode', [(0, 1), (1, 0)])  7.13 us
    unnamed x32, other arithmetic  6.71 us
    ppermute x3, waiting for transfers between devices, padded(): got = lax.ppermute(jnp.where(is_low, last, first), axis, pairs)  6.29 us
    ppermute x5, waiting for transfers between devices, swap_modes(): return lax.ppermute(block, 'mode', [(0, 1), (1, 0)])  4.73 us
  transfers between devices with their start and end apart: 14, of which 13 were waited for; matrix products, arithmetic and copies ran while one was open for 3% of the time, Pallas kernels for 0%

profile of v1, /device:TPU:19, one launch (start us, length us, event | category | flops | bytes accessed | tf_op | source)
XLA Modules:
  0.0 138.5 jit_solution(8521281981041057926)
XLA Ops:
  0.7 0.9 copy-done
  2.0 2.9 %collective-permute-done = f32[128,64]{1,0:T(8,128)S(1)} collective-permute-done((f32[128,64]{1,0:T(8,128)S(1)}, f32[128,64]{1,0:T(8,128)S(1)}, u32[]{:S(2)}, u32[]{:S(2)}) %collective-permute-start) | collective-permute-done | bytes 32800 | tf_op jit(solution)/shard_map/ppermute | solution.py:270
  5.1 1.4 collective-permute-start.1
  6.4 1.9 %collective-permute-start.2 = (f32[64,384]{1,0:T(8,128)S(1)}, f32[64,384]{1,0:T(8,128)S(1)}, u32[]{:S(2)}, u32[]{:S(2)}) collective-permute-start(f32[64,384]{1,0:T(8,128)S(1)} %get-tuple-element.39), channel_id=1, source_target_pairs={{4,8},{8,4},{5,9},{9,5},{6,10},{10,6},{7,11},{11,7},{20,24},{24,20... | collective-permute-start | bytes 294920 | tf_op jit(solution)/shard_map/ppermute | solution.py:270
  8.6 3.2 %collective-permute-done.2 = f32[64,384]{1,0:T(8,128)S(1)} collective-permute-done((f32[64,384]{1,0:T(8,128)S(1)}, f32[64,384]{1,0:T(8,128)S(1)}, u32[]{:S(2)}, u32[]{:S(2)}) %collective-permute-start.2) | collective-permute-done | bytes 98336 | tf_op jit(solution)/shard_map/ppermute | solution.py:270
  12.5 0.7 copy-done.12
  13.4 3.3 %collective-permute-start.3 = (f32[1024,128]{1,0:T(8,128)S(1)}, f32[1024,128]{1,0:T(8,128)S(1)}, u32[]{:S(2)}, u32[]{:S(2)}) collective-permute-start(f32[1024,128]{1,0:T(8,128)S(1)} %bitcast_add_fusion.refs_1_), channel_id=1, source_target_pairs={{0,1},{1,0},{2,3},{3,2},{4,5},{5,4},{6,7},{7,6},{8,9},{9,8},{10,11... | collective-permute-start | bytes 1572872 | tf_op jit(solution)/shard_map/ppermute | solution.py:208
  17.5 0.6 copy-done.15
  18.4 7.0 %gradients.2 = (f32[1024,128]{1,0:T(8,128)S(1)}, f32[1024,128]{1,0:T(8,128)S(1)}) custom-call(s32[34]{0:T(128)S(1)} %pad_add_fusion.1.refs_0_, f32[1024,128]{1,0:T(8,128)S(1)} %bitcast_add_fusion.refs_1_, f32[1024,128]{1,0:T(8,128)S(1)} %collective-permute-done.3.refs_2_, f32[8,2,128,128]{3,2,1,0:T(8,128)S(1)} %bitcast.164, bf16[256,256]{1,0:T(8,128)(2,1)S(1)} %copy-done.5, ...), custom_call_target="tpu_custom_call" | custom-call | tf_op jit(solution)/shard_map/gradients/pallas_call | solution.py:166
  26.1 1.3 collective-permute-done.4
  27.5 0.6 gather_fusion.1
  28.1 0.6 gather_fusion
  29.0 0.6 copy-done.16
  29.7 6.9 %collective-permute-done.5 = f32[4,128,128]{2,1,0:T(8,128)} collective-permute-done((f32[4,128,128]{2,1,0:T(8,128)S(1)}, f32[4,128,128]{2,1,0:T(8,128)}, u32[]{:S(2)}, u32[]{:S(2)}) %collective-permute-start.5) | collective-permute-done | bytes 262176 | tf_op jit(solution)/shard_map/ppermute | solution.py:225
  36.6 0.9 slice_select_fusion.10
  37.5 0.6 constant_dynamic-update-slice_fusion.6
  38.1 0.6 constant_dynamic-update-slice_fusion.5
  38.7 0.6 constant_dynamic-update-slice_fusion.4
  39.4 0.6 constant_dynamic-update-slice_fusion.3
  40.0 0.6 constant_dynamic-update-slice_fusion.2
  40.6 0.6 constant_dynamic-update-slice_fusion.1
  41.3 1.6 %constant_dynamic-update-slice_fusion = (f32[8,128,128]{2,1,0:T(8,128)}, f32[2,128,128]{2,1,0:T(8,128)S(1)}) fusion(f32[8,128,128]{2,1,0:T(8,128)} %constant_dynamic-update-slice_fusion.1, f32[2,128,128]{2,1,0:T(8,128)S(1)} %bitcast.176, f32[4,128,128]{2,1,0:T(8,128)} %collective-permute-done.5), kind=kLoop, calls=%fused_computation.64 | loop fusion | flops 32768 | bytes 524288 | tf_op jit(solution)/shard_map/concatenate | solution.py:240
  42.8 1.6 %gather_fusion.3 = f32[3,128,128]{2,1,0:T(8,128)S(1)} fusion(f32[8,128,128]{2,1,0:T(8,128)} %get-tuple-element.20, s32[1024]{0:T(1024)S(1)} %get-tuple-element.44), kind=kCustom, calls=%fused_computation.3 | custom fusion | bytes 393228 | tf_op jit(solution)/shard_map/gather | solution.py:222
  44.5 2.3 %gather_fusion.2 = f32[3,128,128]{2,1,0:T(8,128)} fusion(f32[8,128,128]{2,1,0:T(8,128)} %get-tuple-element.20, s32[1024]{0:T(1024)S(1)} %get-tuple-element.45), kind=kCustom, calls=%fused_computation.2 | custom fusion | bytes 393228 | tf_op jit(solution)/shard_map/gather | solution.py:222
  46.7 0.9 broadcast_select_fusion.3
  47.7 0.7 pad_maximum_fusion.2
  48.4 0.6 fusion.5
  49.0 0.6 and.97
  49.6 7.3 %collective-permute-done.6 = f32[5,128,128]{2,1,0:T(8,128)} collective-permute-done((f32[5,128,128]{2,1,0:T(8,128)}, f32[5,128,128]{2,1,0:T(8,128)}, u32[]{:S(2)}, u32[]{:S(2)}) %collective-permute-start.6) | collective-permute-done | bytes 327712 | tf_op jit(solution)/shard_map/ppermute | solution.py:225
  56.9 1.0 slice_select_fusion.6
  57.9 0.7 constant_dynamic-update-slice_fusion.13
  58.6 0.6 constant_dynamic-update-slice_fusion.12
  59.2 0.6 constant_dynamic-update-slice_fusion.11
  59.9 0.6 constant_dynamic-update-slice_fusion.10
  60.5 0.6 constant_dynamic-update-slice_fusion.9
  61.1 0.6 constant_dynamic-update-slice_fusion.8
  62.1 1.6 %constant_dynamic-update-slice_fusion.7 = (f32[8,128,128]{2,1,0:T(8,128)}, f32[2,128,128]{2,1,0:T(8,128)S(1)}) fusion(f32[8,128,128]{2,1,0:T(8,128)} %constant_dynamic-update-slice_fusion.8, f32[2,128,128]{2,1,0:T(8,128)S(1)} %copy-done.11, f32[5,128,128]{2,1,0:T(8,128)} %collective-permute-done.6), kind=kLoop, calls=%fused_computation.71 | loop fusion | flops 32768 | bytes 524288 | tf_op jit(solution)/shard_map/concatenate | solution.py:240
  63.6 1.6 %gather_fusion.5 = f32[3,128,128]{2,1,0:T(8,128)S(1)} fusion(f32[8,128,128]{2,1,0:T(8,128)} %get-tuple-element.18, s32[1024]{0:T(1024)S(1)} %get-tuple-element.44), kind=kCustom, calls=%fused_computation.5 | custom fusion | bytes 393228 | tf_op jit(solution)/shard_map/gather | solution.py:222
  65.2 1.6 %gather_fusion.4 = f32[3,128,128]{2,1,0:T(8,128)S(1)} fusion(f32[8,128,128]{2,1,0:T(8,128)} %get-tuple-element.18, s32[1024]{0:T(1024)S(1)} %get-tuple-element.45), kind=kCustom, calls=%fused_computation.4 | custom fusion | bytes 393228 | tf_op jit(solution)/shard_map/gather | solution.py:222
  66.9 0.8 pad_maximum_fusion.3
  67.7 0.6 and.90
  68.3 0.7 copy-done.18
  68.9 0.6 and.93
  69.5 0.9 and_select_fusion
  70.4 13.2 %collective-permute-done.7 = f32[5,128,128]{2,1,0:T(8,128)} collective-permute-done((f32[5,128,128]{2,1,0:T(8,128)}, f32[5,128,128]{2,1,0:T(8,128)}, u32[]{:S(2)}, u32[]{:S(2)}) %collective-permute-start.7) | collective-permute-done | bytes 327712 | tf_op jit(solution)/shard_map/ppermute | solution.py:225
  83.6 1.0 slice_select_fusion.4
  84.6 0.9 copy-done.7
  85.6 1.0 fusion.4
  86.7 1.6 %collective-permute-start.8 = (f32[1024,128]{1,0:T(8,128)S(1)}, f32[1024,128]{1,0:T(8,128)S(1)}, u32[]{:S(2)}, u32[]{:S(2)}) collective-permute-start(f32[1024,128]{1,0:T(8,128)S(1)} %bitcast.162), channel_id=1, source_target_pairs={{0,1},{1,0},{2,3},{3,2},{4,5},{5,4},{6,7},{7,6},{8,9},{9,8},{10,11... | collective-permute-start | bytes 1572872 | tf_op jit(solution)/shard_map/ppermute | solution.py:208
  88.3 1.5 %collective-permute-done.8.refs_2_ = f32[1024,128]{1,0:T(8,128)S(1)} collective-permute-done((f32[1024,128]{1,0:T(8,128)S(1)}, f32[1024,128]{1,0:T(8,128)S(1)}, u32[]{:S(2)}, u32[]{:S(2)}) %collective-permute-start.8) | collective-permute-done | bytes 524320 | tf_op jit(solution)/shard_map/ppermute | solution.py:208
  89.8 7.0 %gradients.3 = (f32[1024,128]{1,0:T(8,128)S(1)}, f32[1024,128]{1,0:T(8,128)S(1)}) custom-call(s32[34]{0:T(128)S(1)} %pad_add_fusion.1.refs_0_, f32[1024,128]{1,0:T(8,128)S(1)} %bitcast.163, f32[1024,128]{1,0:T(8,128)S(1)} %collective-permute-done.8.refs_2_, f32[8,2,128,128]{3,2,1,0:T(8,128)S(1)} %bitcast.165, bf16[256,256]{1,0:T(8,128)(2,1)S(1)} %copy-done.5, ...), custom_call_target="tpu_custom_call" | custom-call | tf_op jit(solution)/shard_map/gradients/pallas_call | solution.py:166
  97.3 1.6 %collective-permute-done.9 = f32[1024,128]{1,0:T(8,128)S(1)} collective-permute-done((f32[1024,128]{1,0:T(8,128)S(1)}, f32[1024,128]{1,0:T(8,128)S(1)}, u32[]{:S(2)}, u32[]{:S(2)}) %collective-permute-start.9) | collective-permute-done | bytes 524320 | tf_op jit(solution)/shard_map/ppermute | solution.py:208
  98.9 0.7 gather_fusion.7
  99.6 0.6 gather_fusion.6
  100.5 7.3 %collective-permute-done.10 = f32[4,128,128]{2,1,0:T(8,128)S(1)} collective-permute-done((f32[4,128,128]{2,1,0:T(8,128)S(1)}, f32[4,128,128]{2,1,0:T(8,128)S(1)}, u32[]{:S(2)}, u32[]{:S(2)}) %collective-permute-start.10) | collective-permute-done | bytes 262176 | tf_op jit(solution)/shard_map/ppermute | solution.py:225
  108.0 0.6 gather_fusion.9
  108.5 0.6 gather_fusion.8
  109.2 8.0 %collective-permute-done.11 = f32[5,128,128]{2,1,0:T(8,128)S(1)} collective-permute-done((f32[5,128,128]{2,1,0:T(8,128)S(1)}, f32[5,128,128]{2,1,0:T(8,128)S(1)}, u32[]{:S(2)}, u32[]{:S(2)}) %collective-permute-start.11) | collective-permute-done | bytes 327712 | tf_op jit(solution)/shard_map/ppermute | solution.py:225
  117.4 0.6 gather_fusion.11
  118.0 0.6 gather_fusion.10
  118.7 15.6 %collective-permute-done.12 = f32[5,128,128]{2,1,0:T(8,128)S(1)} collective-permute-done((f32[5,128,128]{2,1,0:T(8,128)S(1)}, f32[5,128,128]{2,1,0:T(8,128)S(1)}, u32[]{:S(2)}, u32[]{:S(2)}) %collective-permute-start.12) | collective-permute-done | bytes 327712 | tf_op jit(solution)/shard_map/ppermute | solution.py:225
  135.0 1.5 %collective-permute-start.13 = (f32[128,256]{0,1:T(8,128)S(1)}, f32[128,256]{0,1:T(8,128)S(1)}, u32[]{:S(2)}, u32[]{:S(2)}) collective-permute-start(f32[128,256]{0,1:T(8,128)S(1)} %slice.381), channel_id=1, source_target_pairs={{0,1},{1,0},{2,3},{3,2},{4,5},{5,4},{6,7},{7,6},{8,9},{9,8},{10,11... | collective-permute-start | bytes 393224 | tf_op jit(solution)/shard_map/ppermute | solution.py:208
  136.6 0.7 slice_bitcast_fusion
  137.7 0.8 copy.37
  (122 shorter events, 6.1 us)
Async XLA Ops:
  0.6 1.0 copy-start
  1.7 3.2 %collective-permute-start = (f32[128,64]{1,0:T(8,128)S(1)}, f32[128,64]{1,0:T(8,128)S(1)}, u32[]{:S(2)}, u32[]{:S(2)}) collective-permute-start(f32[128,64]{1,0:T(8,128)S(1)} %slice_select_fusion.14), channel_id=1, source_target_pairs={{0,2},{2,0},{1,3},{3,1},{4,6},{6,4},{5,7},{7,5},{8,10},{10,8},{9,1... | collective-permute-start | bytes 98312 | tf_op jit(solution)/shard_map/ppermute | solution.py:270
  5.1 3.5 %collective-permute-start.1 = (f32[64,384]{1,0:T(8,128)S(1)}, f32[64,384]{1,0:T(8,128)S(1)}, u32[]{:S(2)}, u32[]{:S(2)}) collective-permute-start(f32[64,384]{1,0:T(8,128)S(1)} %get-tuple-element.38), channel_id=1, source_target_pairs={{0,4},{8,12},{4,0},{12,8},{1,5},{9,13},{5,1},{13,9},{2,6},{10,14},... | collective-permute-start | bytes 294920 | tf_op jit(solution)/shard_map/ppermute | solution.py:270
  6.4 5.3 %collective-permute-start.2 = (f32[64,384]{1,0:T(8,128)S(1)}, f32[64,384]{1,0:T(8,128)S(1)}, u32[]{:S(2)}, u32[]{:S(2)}) collective-permute-start(f32[64,384]{1,0:T(8,128)S(1)} %get-tuple-element.39), channel_id=1, source_target_pairs={{4,8},{8,4},{5,9},{9,5},{6,10},{10,6},{7,11},{11,7},{20,24},{24,20... | collective-permute-start | bytes 294920 | tf_op jit(solution)/shard_map/ppermute | solution.py:270
  12.3 0.9 copy-start.12
  13.2 5.2 %copy-start.1 = (f32[1,1,16,128,128]{4,3,2,1,0:T(8,128)S(1)}, f32[1,1,16,128,128]{4,3,2,1,0:T(8,128)}, u32[]{:S(2)}) copy-start(f32[1,1,16,128,128]{4,3,2,1,0:T(8,128)} %param.29) | copy-start | bytes 3145732
  13.3 5.1 %copy-start.2 = (bf16[256,256]{1,0:T(8,128)(2,1)S(1)}, bf16[256,256]{1,0:T(8,128)(2,1)}, u32[]{:S(2)}) copy-start(bf16[256,256]{1,0:T(8,128)(2,1)} %constant.108.clone.refs_7_) | copy-start | bytes 393220
  13.3 5.1 %copy-start.3 = (bf16[256,256]{1,0:T(8,128)(2,1)S(1)}, bf16[256,256]{1,0:T(8,128)(2,1)}, u32[]{:S(2)}) copy-start(bf16[256,256]{1,0:T(8,128)(2,1)} %constant.107.clone.refs_6_) | copy-start | bytes 393220
  13.3 5.1 %copy-start.4 = (bf16[256,256]{1,0:T(8,128)(2,1)S(1)}, bf16[256,256]{1,0:T(8,128)(2,1)}, u32[]{:S(2)}) copy-start(bf16[256,256]{1,0:T(8,128)(2,1)} %constant.106.clone.refs_5_) | copy-start | bytes 393220
  13.3 5.1 %copy-start.5 = (bf16[256,256]{1,0:T(8,128)(2,1)S(1)}, bf16[256,256]{1,0:T(8,128)(2,1)}, u32[]{:S(2)}) copy-start(bf16[256,256]{1,0:T(8,128)(2,1)} %constant.105.clone.refs_4_) | copy-start | bytes 393220
  13.4 5.0 %collective-permute-start.3 = (f32[1024,128]{1,0:T(8,128)S(1)}, f32[1024,128]{1,0:T(8,128)S(1)}, u32[]{:S(2)}, u32[]{:S(2)}) collective-permute-start(f32[1024,128]{1,0:T(8,128)S(1)} %bitcast_add_fusion.refs_1_), channel_id=1, source_target_pairs={{0,1},{1,0},{2,3},{3,2},{4,5},{5,4},{6,7},{7,6},{8,9},{9,8},{10,11... | collective-permute-start | bytes 1572872 | tf_op jit(solution)/shard_map/ppermute | solution.py:208
  17.4 0.7 copy-start.15
  25.4 0.7 copy-start.17
  25.4 2.0 %collective-permute-start.4 = (f32[1024,128]{1,0:T(8,128)S(1)}, f32[1024,128]{1,0:T(8,128)S(1)}, u32[]{:S(2)}, u32[]{:S(2)}) collective-permute-start(f32[1024,128]{1,0:T(8,128)S(1)} %get-tuple-element.7), channel_id=1, source_target_pairs={{0,1},{1,0},{2,3},{3,2},{4,5},{5,4},{6,7},{7,6},{8,9},{9,8},{10,11... | collective-permute-start | bytes 1572872 | tf_op jit(solution)/shard_map/ppermute | solution.py:208
  26.1 1.4 %copy-start.14 = (s32[1024]{0:T(1024)}, s32[1024]{0:T(1024)S(1)}, u32[]{:S(2)}) copy-start(s32[1024]{0:T(1024)S(1)} %get-tuple-element.46) | copy-start | bytes 12292
  28.7 7.9 %collective-permute-start.5 = (f32[4,128,128]{2,1,0:T(8,128)S(1)}, f32[4,128,128]{2,1,0:T(8,128)}, u32[]{:S(2)}, u32[]{:S(2)}) collective-permute-start(f32[4,128,128]{2,1,0:T(8,128)S(1)} %pad_maximum_fusion.6), channel_id=1, source_target_pairs={{0,2},{2,0},{1,3},{3,1},{4,6},{6,4},{5,7},{7,5},{8,10},{10,8},{9,1... | collective-permute-start | bytes 786440 | tf_op jit(solution)/shard_map/ppermute | solution.py:225
  29.0 0.7 copy-start.16
  42.8 4.9 %copy-start.10 = (f32[2,128,128]{2,1,0:T(8,128)}, f32[2,128,128]{2,1,0:T(8,128)S(1)}, u32[]{:S(2)}) copy-start(f32[2,128,128]{2,1,0:T(8,128)S(1)} %get-tuple-element.21) | copy-start | bytes 393220
  48.4 8.5 %collective-permute-start.6 = (f32[5,128,128]{2,1,0:T(8,128)}, f32[5,128,128]{2,1,0:T(8,128)}, u32[]{:S(2)}, u32[]{:S(2)}) collective-permute-start(f32[5,128,128]{2,1,0:T(8,128)} %pad_maximum_fusion.2), channel_id=1, source_target_pairs={{0,4},{4,0},{8,12},{12,8},{1,5},{5,1},{9,13},{13,9},{2,6},{6,2},{1... | collective-permute-start | bytes 983048 | tf_op jit(solution)/shard_map/ppermute | solution.py:225
  57.9 2.6 %copy-start.8 = (f32[3,128,128]{2,1,0:T(8,128)}, f32[3,128,128]{2,1,0:T(8,128)S(1)}, u32[]{:S(2)}) copy-start(f32[3,128,128]{2,1,0:T(8,128)S(1)} %get-tuple-element.31) | copy-start | bytes 589828
  57.9 3.2 %copy-start.6 = (f32[3,128,128]{2,1,0:T(8,128)}, f32[3,128,128]{2,1,0:T(8,128)S(1)}, u32[]{:S(2)}) copy-start(f32[3,128,128]{2,1,0:T(8,128)S(1)} %get-tuple-element.30) | copy-start | bytes 589828
  61.1 0.9 copy-start.11
  67.6 16.0 %collective-permute-start.7 = (f32[5,128,128]{2,1,0:T(8,128)}, f32[5,128,128]{2,1,0:T(8,128)}, u32[]{:S(2)}, u32[]{:S(2)}) collective-permute-start(f32[5,128,128]{2,1,0:T(8,128)} %pad_maximum_fusion.3), channel_id=1, source_target_pairs={{0,12},{4,8},{8,4},{12,0},{1,13},{5,9},{9,5},{13,1},{2,14},{6,10},... | collective-permute-start | bytes 983048 | tf_op jit(solution)/shard_map/ppermute | solution.py:225
  68.3 0.7 copy-start.18
  70.4 14.2 %copy-start.9 = (f32[3,128,128]{2,1,0:T(8,128)S(1)}, f32[3,128,128]{2,1,0:T(8,128)}, u32[]{:S(2)}) copy-start(f32[3,128,128]{2,1,0:T(8,128)} %copy-done.8) | copy-start | bytes 589828
  84.6 0.9 copy-start.7
  85.6 1.0 copy-start.13
  86.7 3.1 %collective-permute-start.8 = (f32[1024,128]{1,0:T(8,128)S(1)}, f32[1024,128]{1,0:T(8,128)S(1)}, u32[]{:S(2)}, u32[]{:S(2)}) collective-permute-start(f32[1024,128]{1,0:T(8,128)S(1)} %bitcast.162), channel_id=1, source_target_pairs={{0,1},{1,0},{2,3},{3,2},{4,5},{5,4},{6,7},{7,6},{8,9},{9,8},{10,11... | collective-permute-start | bytes 1572872 | tf_op jit(solution)/shard_map/ppermute | solution.py:208
  96.8 2.0 %collective-permute-start.9 = (f32[1024,128]{1,0:T(8,128)S(1)}, f32[1024,128]{1,0:T(8,128)S(1)}, u32[]{:S(2)}, u32[]{:S(2)}) collective-permute-start(f32[1024,128]{1,0:T(8,128)S(1)} %get-tuple-element.9), channel_id=1, source_target_pairs={{0,1},{1,0},{2,3},{3,2},{4,5},{5,4},{6,7},{7,6},{8,9},{9,8},{10,11... | collective-permute-start | bytes 1572872 | tf_op jit(solution)/shard_map/ppermute | solution.py:208
  100.2 7.6 %collective-permute-start.10 = (f32[4,128,128]{2,1,0:T(8,128)S(1)}, f32[4,128,128]{2,1,0:T(8,128)S(1)}, u32[]{:S(2)}, u32[]{:S(2)}) collective-permute-start(f32[4,128,128]{2,1,0:T(8,128)S(1)} %pad_maximum_fusion.7), channel_id=1, source_target_pairs={{0,2},{2,0},{1,3},{3,1},{4,6},{6,4},{5,7},{7,5},{8,10},{10,8},{9,1... | collective-permute-start | bytes 786440 | tf_op jit(solution)/shard_map/ppermute | solution.py:225
  109.2 8.1 %collective-permute-start.11 = (f32[5,128,128]{2,1,0:T(8,128)S(1)}, f32[5,128,128]{2,1,0:T(8,128)S(1)}, u32[]{:S(2)}, u32[]{:S(2)}) collective-permute-start(f32[5,128,128]{2,1,0:T(8,128)S(1)} %pad_maximum_fusion.4), channel_id=1, source_target_pairs={{0,4},{4,0},{8,12},{12,8},{1,5},{5,1},{9,13},{13,9},{2,6},{6,2},{1... | collective-permute-start | bytes 983048 | tf_op jit(solution)/shard_map/ppermute | solution.py:225
  118.6 15.7 %collective-permute-start.12 = (f32[5,128,128]{2,1,0:T(8,128)S(1)}, f32[5,128,128]{2,1,0:T(8,128)S(1)}, u32[]{:S(2)}, u32[]{:S(2)}) collective-permute-start(f32[5,128,128]{2,1,0:T(8,128)S(1)} %pad_maximum_fusion.5), channel_id=1, source_target_pairs={{0,12},{4,8},{8,4},{12,0},{1,13},{5,9},{9,5},{13,1},{2,14},{6,10},... | collective-permute-start | bytes 983048 | tf_op jit(solution)/shard_map/ppermute | solution.py:225
  135.0 2.5 %collective-permute-start.13 = (f32[128,256]{0,1:T(8,128)S(1)}, f32[128,256]{0,1:T(8,128)S(1)}, u32[]{:S(2)}, u32[]{:S(2)}) collective-permute-start(f32[128,256]{0,1:T(8,128)S(1)} %slice.381), channel_id=1, source_target_pairs={{0,1},{1,0},{2,3},{3,2},{4,5},{5,4},{6,7},{7,6},{8,9},{9,8},{10,11... | collective-permute-start | bytes 393224 | tf_op jit(solution)/shard_map/ppermute | solution.py:208

commit v2 on v1

v2 whole, which is shorter than its diff:
```python
import jax
import jax.numpy as jnp
import ml_dtypes
import numpy as np
from jax import lax
from jax.experimental import pallas as pl
from jax.experimental.pallas import tpu as pltpu
from jax.sharding import PartitionSpec as P

ITERS = 2


momentum = 0.5
object_rate = 0.1
probe_rate = 0.25


def dft_tables(size):
    steps = np.arange(size)
    angle = (steps[:, None] * steps[None, :] % size) * (2.0 * np.pi / size)
    cosine, sine = np.cos(angle) / np.sqrt(size), np.sin(angle) / np.sqrt(size)
    ahead = np.block([[cosine, -sine], [sine, cosine]]).astype(np.float32)
    halves = []
    for table in (ahead, ahead.T):
        high = table.astype(ml_dtypes.bfloat16)
        low = (table - high.astype(np.float32)).astype(ml_dtypes.bfloat16)
        halves += [high, low]
    return halves


def split(values):
    high = values.astype(jnp.bfloat16)
    return high, (values - high.astype(jnp.float32)).astype(jnp.bfloat16)


def matmul(left, right):
    return jnp.dot(left, right, preferred_element_type=jnp.float32)


def from_right(values, high, low):
    values_high, values_low = split(values)
    return matmul(values_high, high) + (matmul(values_low, high) + matmul(values_high, low))


def from_left(high, low, values):
    values_high, values_low = split(values)
    return matmul(high, values_high) + (matmul(low, values_high) + matmul(high, values_low))


def gradient_kernel(scalars, *refs, columns, group):
    mine, theirs = refs[: columns + 1], refs[columns + 1 : 2 * columns + 2]
    measured, ahead_high, ahead_low, behind_high, behind_low = refs[2 * columns + 2 :][:5]
    keep, send, state, grad = refs[2 * columns + 7 :]
    size = measured.shape[-1]
    slots = measured.shape[0]
    me = scalars[0]
    live_slots = scalars[1]
    half_mine = scalars[2]
    lane = lax.broadcasted_iota(jnp.int32, (size, size), 1)
    base = columns * 2 * size

    def region(tile, half):
        return pl.ds(pl.multiple_of(tile * 2 * size + half * size, size), size)

    for blocks, half, mode in ((mine, half_mine, me), (theirs, 1 - half_mine, 1 - me)):
        for part in range(2):
            rows = slice(part * size, (part + 1) * size)
            for tile in range(columns):
                state[part, region(tile, half), :] = blocks[tile][rows, :]
            state[mode, base + part * size : base + (part + 1) * size, :] = blocks[-1][rows, :]
    grad[...] = jnp.zeros_like(grad)

    def plane(mode, part):
        return state[mode, base + part * size : base + (part + 1) * size, :]

    def rows_of(row, tile):
        return pl.ds(tile * (2 * size) + row, size)

    def one_group(first):
        places, patches, waves = [], [], []
        for index in range(group):
            slot = 2 * (first + index) + me
            row = scalars[3 + 2 * slot]
            col = scalars[4 + 2 * slot]
            tile = col // size
            shift = col % size
            places.append((slot, row, tile, shift))
            patch = []
            for part in range(2):
                near = state[part, rows_of(row, tile), :]
                far = state[part, rows_of(row, tile + 1), :]
                patch.append(
                    pltpu.roll(jnp.where(lane >= shift, near, far), (size - shift) % size, 1)
                )
            patches.append(patch)
            for mode in range(2):
                real, imag = plane(mode, 0), plane(mode, 1)
                waves.append(
                    jnp.concatenate(
                        [real * patch[0] - imag * patch[1], real * patch[1] + imag * patch[0]],
                        axis=1,
                    )
                )
        half = from_right(jnp.concatenate(waves, axis=0), ahead_high[...], ahead_low[...])
        scaled = []
        for index in range(group):
            first_mode = half[2 * index * size : (2 * index + 1) * size]
            second_mode = half[(2 * index + 1) * size : (2 * index + 2) * size]
            turned = jnp.concatenate(
                [
                    jnp.concatenate([first_mode[:, :size], second_mode[:, :size]], axis=1),
                    jnp.concatenate([first_mode[:, size:], second_mode[:, size:]], axis=1),
                ],
                axis=0,
            )
            far_field = from_left(behind_high[...], behind_low[...], turned)
            power = far_field * far_field
            power = power[:size] + power[size:]
            power = power[:, :size] + power[:, size:]
            slot = places[index][0]
            live = jnp.where(slot < live_slots, 1.0, 0.0).astype(jnp.float32)
            weight = (
                1.0 - jnp.sqrt(measured[first + index, 0]) * lax.rsqrt(power + 1.0)
            ) * live
            weight = jnp.concatenate([weight, weight], axis=1)
            weight = jnp.concatenate([weight, weight], axis=0)
            back = from_left(ahead_high[...], ahead_low[...], weight * far_field)
            for mode in range(2):
                lanes = slice(mode * size, (mode + 1) * size)
                scaled.append(jnp.concatenate([back[:size, lanes], back[size:, lanes]], axis=1))
        chi = from_right(jnp.concatenate(scaled, axis=0), behind_high[...], behind_low[...])
        for index in range(group):
            _, row, tile, shift = places[index]
            pieces = [0.0, 0.0]
            for mode in range(2):
                start = (2 * index + mode) * size
                chi_real = chi[start : start + size, :size]
                chi_imag = chi[start : start + size, size:]
                real, imag = plane(mode, 0), plane(mode, 1)
                pieces[0] = pieces[0] + (real * chi_real + imag * chi_imag)
                pieces[1] = pieces[1] + (real * chi_imag - imag * chi_real)
                patch_real, patch_imag = patches[index]
                grad[mode, base : base + size, :] += (
                    patch_real * chi_real + patch_imag * chi_imag
                )
                grad[mode, base + size : base + 2 * size, :] += (
                    patch_real * chi_imag - patch_imag * chi_real
                )
            for part in range(2):
                turned_back = pltpu.roll(pieces[part], shift, 1)
                inside = lane >= shift
                grad[part, rows_of(row, tile), :] += jnp.where(inside, turned_back, 0.0)
                grad[part, rows_of(row, tile + 1), :] += jnp.where(inside, 0.0, turned_back)

    @pl.loop(0, slots // group)
    def _(step):
        one_group(step * group)

    for target, half, mode in ((keep, half_mine, me), (send, 1 - half_mine, 1 - me)):
        for part in range(2):
            for tile in range(columns):
                start = (2 * tile + part) * size
                target[start : start + size, :] = grad[part, region(tile, half), :]
            start = base + part * size
            target[start : start + size, :] = grad[mode, start : start + size, :]


def gradients(scalars, mine, theirs, measured):
    size = measured.shape[-1]
    slots = measured.shape[0] // 2
    columns = len(mine) - 1
    height = (columns + 1) * 2 * size
    shape = jax.ShapeDtypeStruct((height, size), jnp.float32)
    whole = pl.BlockSpec((height, size), lambda i, s: (0, 0))
    block = pl.BlockSpec((2 * size, size), lambda i, s: (0, 0))
    table = pl.BlockSpec((2 * size, 2 * size), lambda i, s: (0, 0))
    group = 4 if slots % 4 == 0 else 1

    def body(*refs):
        gradient_kernel(*refs, columns=columns, group=group)

    return pl.pallas_call(
        body,
        out_shape=(shape, shape),
        grid_spec=pltpu.PrefetchScalarGridSpec(
            num_scalar_prefetch=1,
            grid=(1,),
            in_specs=[block] * (2 * columns + 2)
            + [pl.BlockSpec((slots, 1, size, size), lambda i, s: (0, s[0], 0, 0))]
            + [table] * 4,
            out_specs=[whole, whole],
            scratch_shapes=[
                pltpu.VMEM((2, height, size), jnp.float32),
                pltpu.VMEM((2, height, size), jnp.float32),
            ],
        ),
        compiler_params=pltpu.CompilerParams(vmem_limit_bytes=24 * 1024 * 1024),
        name="gradients",
    )(
        scalars,
        *mine,
        *theirs,
        measured.reshape(slots, 2, size, size),
        *[jnp.asarray(t) for t in dft_tables(size)],
    )


def swap_modes(block):
    return lax.ppermute(block, "mode", [(0, 1), (1, 0)])


def swap_rows(block):
    count = lax.axis_size("row")
    route = []
    for row in range(count):
        for mode in range(2):
            other = row + 1 if row % 2 == mode else row - 1
            other = other if 0 <= other < count else row
            route.append((2 * row + mode, 2 * other + mode))
    return lax.ppermute(block, ("row", "mode"), route)


def swap_cols(to_low, to_high):
    count = lax.axis_size("col")
    col = lax.axis_index("col")
    from_low = from_high = jnp.zeros_like(to_low)
    for parity in range(min(2, count - 1)):
        route = []
        for i in range(count):
            other = i + 1 if i % 2 == parity else i - 1
            route.append((i, other if 0 <= other < count else i))
        is_low = col % 2 == parity
        got = lax.ppermute(jnp.where(is_low, to_high, to_low), "col", route)
        from_high = jnp.where(is_low & (col < count - 1), got, from_high)
        from_low = jnp.where(jnp.logical_not(is_low) & (col > 0), got, from_low)
    return from_low, from_high


def sum_tiles(block):
    for axis in ("col", "row"):
        count = lax.axis_size(axis)
        reach = 1
        while reach < count:
            block = block + lax.ppermute(block, axis, [(i, i ^ (2 * reach - 1)) for i in range(count)])
            reach *= 2
    return block


def on_device(obj, probe, positions, counts, measured):
    size = probe.shape[-1]
    half = size // 2
    tile_rows, tile_cols = obj.shape[1:]
    columns = tile_cols // size + 1
    slot_count = positions.shape[2]
    rows_count, cols_count = lax.axis_size("row"), lax.axis_size("col")
    me = lax.axis_index("mode")
    row = lax.axis_index("row")
    col = lax.axis_index("col")
    lower = row % 2 == me
    paired = jnp.where(lower, row < rows_count - 1, row > 0)
    half_mine = lower.astype(jnp.int32)
    corner = jnp.stack([row * tile_rows - half, col * tile_cols - half])
    offsets = positions[0, 0] - corner[None, :]
    scalars = jnp.concatenate([jnp.stack([me, counts[0, 0], half_mine]), offsets.reshape(-1)])
    probe_step = probe_rate / (slot_count * rows_count * cols_count)

    strip = jnp.where(lower, obj[:, half:], obj[:, :half])
    beside = jnp.where(paired, swap_rows(strip), 0.0)
    region = jnp.concatenate(
        [jnp.where(lower, strip, beside), jnp.where(lower, beside, strip)], axis=1
    )
    from_low, from_high = swap_cols(region[:, :, :half], region[:, :, tile_cols - half :])
    wide = jnp.concatenate([from_low, region, from_high], axis=2)
    start = [
        wide[:, :, tile * size : (tile + 1) * size].reshape(2 * size, size)
        for tile in range(columns)
    ] + [probe[0].reshape(2 * size, size)]

    ext_rows = jnp.arange(size, dtype=jnp.int32)[:, None] + half_mine * size - half
    ext_rows = jnp.concatenate([ext_rows, ext_rows]) + row * tile_rows
    rows_inside = (ext_rows >= 0) & (ext_rows < tile_rows * rows_count)
    rates = []
    for tile in range(columns):
        ext_cols = jnp.arange(size, dtype=jnp.int32)[None, :] + tile * size - half + col * tile_cols
        inside = rows_inside & (ext_cols >= 0) & (ext_cols < tile_cols * cols_count)
        rates.append(jnp.where(inside, jnp.float32(object_rate), 0.0))

    previous, current = start, start
    for iteration in range(ITERS):
        ahead = [x + momentum * (x - y) for x, y in zip(current, previous, strict=True)]
        keep, send = gradients(scalars, ahead, [swap_modes(x) for x in ahead], measured[0, 0])
        total = keep + swap_modes(send)
        previous = current
        probe_grad = sum_tiles(total[columns * 2 * size :])
        object_grad = total[: columns * 2 * size]
        new_probe = ahead[-1] - probe_step * probe_grad
        if iteration < ITERS - 1:
            object_grad = object_grad + jnp.where(paired, swap_rows(object_grad), 0.0)
            parts = [
                object_grad[tile * 2 * size : (tile + 1) * 2 * size] for tile in range(columns)
            ]
            from_low, from_high = swap_cols(parts[0], parts[-1])
            parts[0] = parts[0] + from_low
            parts[-1] = parts[-1] + from_high
            current = [
                x - rate * g for x, rate, g in zip(ahead, rates, parts, strict=False)
            ] + [new_probe]
        else:
            object_grad = object_grad.reshape(columns, 2, size, size)
            given = jnp.where(lower, object_grad[:, :, half:], object_grad[:, :, :half])
            owned = jnp.where(lower, object_grad[:, :, :half], object_grad[:, :, half:])
            owned = owned + jnp.where(paired, swap_rows(given), 0.0)
            from_low, from_high = swap_cols(owned[0, :, :, :half], owned[-1, :, :, half:])
            owned = jnp.concatenate(
                [owned[0, :, :, half:] + from_low]
                + [owned[tile] for tile in range(1, columns - 1)]
                + [owned[-1, :, :, :half] + from_high],
                axis=2,
            )
            held = jnp.concatenate([x.reshape(2, size, size) for x in ahead[:-1]], axis=2)
            held = jnp.where(lower, held[:, :half], held[:, half:])
            strip = held[:, :, half : half + tile_cols] - object_rate * owned

    other = swap_modes(strip)
    whole = jnp.concatenate(
        [jnp.where(lower, other, strip), jnp.where(lower, strip, other)], axis=1
    )
    return (whole, new_probe.reshape(1, 2, size, size))


def solution(mesh):
    in_specs = (
        P(None, ("parts", "row"), "col"),
        P("mode", None, "parts", None),
        P("row", "col", "parts", None),
        P(("parts", "row"), "col"),
        P("row", "col", "parts", None, None),
    )
    out_specs = (P(None, ("parts", "row"), "col"), P("mode", None, "parts", None))
    return jax.shard_map(
        on_device, mesh=mesh, in_specs=in_specs, out_specs=out_specs, check_vma=False
    )
```

time: 139 us -> 84.9 us (0.61)
  the two profiles are of different devices: /device:TPU:19 before, /device:TPU:0 now
where the time goes in v2:
time: 84.9 us; the launch traced here: 84.7 us
  waiting for transfers between devices  35.4 us (42%)
  starting transfers between devices  27.8 us (33%)
  Pallas kernels  14.8 us (17%)
  other arithmetic  4 us (5%)
  between operations  1.73 us (2%)
  local copies, waits for them, and re-layouts  1 us (1%)
    ppermute x6, waiting for transfers between devices, sum_tiles(): lax.ppermute(block, axis, [(i, i ^ 2 * reach - 1) for i in range(count)])  18.1 us
    pallas_call x2, Pallas kernels, gradients(): pl.pallas_call(body, out_shape=(shape, shape), grid_spec=pltpu.PrefetchSc...  14.8 us
    ppermute x3, starting transfers between devices, swap_rows(): return lax.ppermute(block, ('row', 'mode'), route)  10.3 us
    ppermute x6, starting transfers between devices, sum_tiles(): lax.ppermute(block, axis, [(i, i ^ 2 * reach - 1) for i in range(count)])  10.1 us
    ppermute x3, waiting for transfers between devices, swap_cols(): got = lax.ppermute(jnp.where(is_low, to_high, to_low), 'col', route)  6.89 us
    ppermute x3, waiting for transfers between devices, swap_rows(): return lax.ppermute(block, ('row', 'mode'), route)  5.73 us
    ppermute x3, starting transfers between devices, swap_cols(): got = lax.ppermute(jnp.where(is_low, to_high, to_low), 'col', route)  5.14 us
    ppermute x11, waiting for transfers between devices, swap_modes(): return lax.ppermute(block, 'mode', [(0, 1), (1, 0)])  4.68 us
  transfers between devices with their start and end apart: 23, of which 15 were waited for; matrix products, arithmetic and copies ran while one was open for 3% of the time, Pallas kernels for 0%

profile of v2, /device:TPU:0, one launch (start us, length us, event | category | flops | bytes accessed | tf_op | source)
XLA Modules:
  0.0 84.7 jit_solution(8344344486179049425)
XLA Ops:
  0.7 1.0 %slice_select_fusion.2 = f32[2,64,256]{2,1,0:T(8,128)S(1)} fusion(f32[2,128,256]{2,1,0:T(8,128)} %param.13, pred[]{:T(512)S(6)} %eq.13), kind=kLoop, calls=%fused_computation.47 | loop fusion | flops 32768 | bytes 393217 | tf_op jit(solution)/shard_map/jit(_where)/select_n | solution.py:267
  1.7 4.9 %collective-permute-start = (f32[2,64,256]{2,1,0:T(8,128)S(1)}, f32[2,64,256]{2,1,0:T(8,128)S(1)}, u32[]{:S(2)}, u32[]{:S(2)}) collective-permute-start(f32[2,64,256]{2,1,0:T(8,128)S(1)} %slice_select_fusion.2), channel_id=1, source_target_pairs={{0,4},{1,1},{4,0},{5,9},{8,12},{9,5},{12,8},{13,13},{2,6},{3,3},{6... | collective-permute-start | bytes 393224 | tf_op jit(solution)/shard_map/ppermute | solution.py:220
  6.7 2.9 %collective-permute-done = f32[2,64,256]{2,1,0:T(8,128)S(1)} collective-permute-done((f32[2,64,256]{2,1,0:T(8,128)S(1)}, f32[2,64,256]{2,1,0:T(8,128)S(1)}, u32[]{:S(2)}, u32[]{:S(2)}) %collective-permute-start) | collective-permute-done | bytes 131104 | tf_op jit(solution)/shard_map/ppermute | solution.py:220
  9.6 0.0 copy-start.6
  9.6 0.1 fusion.1
  9.7 2.0 %collective-permute-start.1 = (f32[2,128,64]{2,1,0:T(8,128)S(1)}, f32[2,128,64]{2,1,0:T(8,128)S(1)}, u32[]{:S(2)}, u32[]{:S(2)}) collective-permute-start(f32[2,128,64]{2,1,0:T(8,128)S(1)} %fusion.1), channel_id=1, source_target_pairs={{0,2},{2,0},{1,3},{3,1},{4,6},{6,4},{5,7},{7,5},{8,10},{10,8},{9,1... | collective-permute-start | bytes 196616 | tf_op jit(solution)/shard_map/ppermute | solution.py:233
  11.7 0.1 collective-permute-start.5
  11.8 0.0 copy-start
  11.8 2.9 %collective-permute-done.1 = f32[2,128,64]{2,1,0:T(8,128)S(1)} collective-permute-done((f32[2,128,64]{2,1,0:T(8,128)S(1)}, f32[2,128,64]{2,1,0:T(8,128)S(1)}, u32[]{:S(2)}, u32[]{:S(2)}) %collective-permute-start.1) | collective-permute-done | bytes 65568 | tf_op jit(solution)/shard_map/ppermute | solution.py:233
  14.8 0.2 pad_maximum_fusion.4
  15.0 0.1 collective-permute-start.2
  15.1 0.0 copy-start.3
  15.1 0.0 copy-start.4
  15.1 0.5 collective-permute-start.3
  15.7 0.1 collective-permute-start.4
  15.8 0.1 pad_add_fusion
  15.9 0.1 sub.82
  16.0 0.6 copy-done.8
  16.6 0.1 copy.16
  16.6 0.1 squeeze.14
  17.4 0.1 pad_add_fusion.1.refs_0_
  17.5 0.0 collective-permute-done.5.refs_8_
  17.5 7.8 %gradients.2 = (f32[1024,128]{1,0:T(8,128)S(1)}, f32[1024,128]{1,0:T(8,128)}) custom-call(s32[35]{0:T(128)S(1)} %pad_add_fusion.1.refs_0_, f32[256,128]{1,0:T(8,128)S(1)} %bitcast_add_fusion.3.refs_1_, f32[256,128]{1,0:T(8,128)S(1)} %bitcast_add_fusion.2.refs_2_, f32[256,128]{1,0:T(8,128)S(1)} %bitcast_add_fusion.1.refs_3_, ...), custom_call_target="tpu_custom_call" | custom-call | tf_op jit(solution)/shard_map/gradients/pallas_call | solution.py:182
  25.3 0.5 collective-permute-start.6
  25.8 1.7 %collective-permute-done.6 = f32[1024,128]{1,0:T(8,128)S(1)} collective-permute-done((f32[1024,128]{1,0:T(8,128)}, f32[1024,128]{1,0:T(8,128)S(1)}, u32[]{:S(2)}, u32[]{:S(2)}) %collective-permute-start.6) | collective-permute-done | bytes 524320 | tf_op jit(solution)/shard_map/ppermute | solution.py:209
  27.6 0.1 add.200
  27.6 2.0 %collective-permute-start.9 = (f32[256,128]{1,0:T(8,128)S(1)}, f32[256,128]{1,0:T(8,128)S(1)}, u32[]{:S(2)}, u32[]{:S(2)}) collective-permute-start(f32[256,128]{1,0:T(8,128)S(1)} %slice.112), channel_id=1, source_target_pairs={{0,2},{2,0},{1,3},{3,1},{4,6},{6,4},{5,7},{7,5},{8,10},{10,8},{9,1... | collective-permute-start | bytes 393224 | tf_op jit(solution)/shard_map/ppermute | solution.py:244
  29.7 3.5 %collective-permute-start.7 = (f32[768,128]{1,0:T(8,128)S(1)}, f32[768,128]{1,0:T(8,128)S(1)}, u32[]{:S(2)}, u32[]{:S(2)}) collective-permute-start(f32[768,128]{1,0:T(8,128)S(1)} %slice.104), channel_id=1, source_target_pairs={{0,4},{1,1},{4,0},{5,9},{8,12},{9,5},{12,8},{13,13},{2,6},{3,3},{6... | collective-permute-start | bytes 1179656 | tf_op jit(solution)/shard_map/ppermute | solution.py:220
  33.2 0.5 collective-permute-done.9
  33.7 1.9 %collective-permute-start.10 = (f32[256,128]{1,0:T(8,128)S(1)}, f32[256,128]{1,0:T(8,128)S(1)}, u32[]{:S(2)}, u32[]{:S(2)}) collective-permute-start(f32[256,128]{1,0:T(8,128)S(1)} %slice_add_fusion.1), channel_id=1, source_target_pairs={{0,4},{4,0},{8,12},{12,8},{1,5},{5,1},{9,13},{13,9},{2,6},{6,2},{1... | collective-permute-start | bytes 393224 | tf_op jit(solution)/shard_map/ppermute | solution.py:244
  35.6 6.6 %collective-permute-done.10 = f32[256,128]{1,0:T(8,128)S(1)} collective-permute-done((f32[256,128]{1,0:T(8,128)S(1)}, f32[256,128]{1,0:T(8,128)S(1)}, u32[]{:S(2)}, u32[]{:S(2)}) %collective-permute-start.10) | collective-permute-done | bytes 131104 | tf_op jit(solution)/shard_map/ppermute | solution.py:244
  42.2 3.7 %collective-permute-start.11 = (f32[256,128]{1,0:T(8,128)S(1)}, f32[256,128]{1,0:T(8,128)S(1)}, u32[]{:S(2)}, u32[]{:S(2)}) collective-permute-start(f32[256,128]{1,0:T(8,128)S(1)} %add.210), channel_id=1, source_target_pairs={{0,12},{4,8},{8,4},{12,0},{1,13},{5,9},{9,5},{13,1},{2,14},{6,10},... | collective-permute-start | bytes 393224 | tf_op jit(solution)/shard_map/ppermute | solution.py:244
  45.9 0.1 select_add_fusion
  45.9 0.0 copy-start.7
  46.0 0.6 collective-permute-start.8
  46.6 2.6 %collective-permute-done.11 = f32[256,128]{1,0:T(8,128)S(1)} collective-permute-done((f32[256,128]{1,0:T(8,128)S(1)}, f32[256,128]{1,0:T(8,128)S(1)}, u32[]{:S(2)}, u32[]{:S(2)}) %collective-permute-start.11) | collective-permute-done | bytes 131104 | tf_op jit(solution)/shard_map/ppermute | solution.py:244
  49.2 0.1 collective-permute-start.15
  49.3 1.7 %collective-permute-done.8 = f32[256,128]{1,0:T(8,128)S(1)} collective-permute-done((f32[256,128]{1,0:T(8,128)S(1)}, f32[256,128]{1,0:T(8,128)S(1)}, u32[]{:S(2)}, u32[]{:S(2)}) %collective-permute-start.8) | collective-permute-done | bytes 131104 | tf_op jit(solution)/shard_map/ppermute | solution.py:233
  51.0 0.2 fusion.16
  51.2 0.1 collective-permute-start.12
  51.3 0.5 collective-permute-start.13
  51.8 0.1 collective-permute-start.14
  51.9 0.8 collective-permute-done.12.refs_5_
  52.7 0.2 collective-permute-done.13.refs_6_
  52.8 0.3 collective-permute-done.14.refs_7_
  53.2 7.0 %gradients.3 = (f32[1024,128]{1,0:T(8,128)S(1)}, f32[1024,128]{1,0:T(8,128)S(1)}) custom-call(s32[35]{0:T(128)S(1)} %pad_add_fusion.1.refs_0_, f32[256,128]{1,0:T(8,128)S(1)} %get-tuple-element.10.refs_1_, f32[256,128]{1,0:T(8,128)S(1)} %get-tuple-element.12.refs_2_, f32[256,128]{1,0:T(8,128)S(1)} %get-tuple-element.11.refs_3_, ...), custom_call_target="tpu_custom_call" | custom-call | tf_op jit(solution)/shard_map/gradients/pallas_call | solution.py:182
  60.2 0.3 collective-permute-start.16
  60.5 1.7 %collective-permute-done.16 = f32[1024,128]{1,0:T(8,128)S(1)} collective-permute-done((f32[1024,128]{1,0:T(8,128)S(1)}, f32[1024,128]{1,0:T(8,128)S(1)}, u32[]{:S(2)}, u32[]{:S(2)}) %collective-permute-start.16) | collective-permute-done | bytes 524320 | tf_op jit(solution)/shard_map/ppermute | solution.py:209
  62.1 0.1 add.213
  62.2 0.6 collective-permute-start.20
  62.9 1.9 %collective-permute-start.17 = (f32[3,2,64,128]{3,2,1,0:T(8,128)S(1)}, f32[3,2,64,128]{3,2,1,0:T(8,128)S(1)}, u32[]{:S(2)}, u32[]{:S(2)}) collective-permute-start(f32[3,2,64,128]{3,2,1,0:T(8,128)S(1)} %slice_select_fusion), channel_id=1, source_target_pairs={{0,4},{1,1},{4,0},{5,9},{8,12},{9,5},{12,8},{13,13},{2,6},{3,3},{6... | collective-permute-start | bytes 589832 | tf_op jit(solution)/shard_map/ppermute | solution.py:220
  64.8 3.1 %collective-permute-done.20 = f32[256,128]{1,0:T(8,128)S(1)} collective-permute-done((f32[256,128]{1,0:T(8,128)S(1)}, f32[256,128]{1,0:T(8,128)S(1)}, u32[]{:S(2)}, u32[]{:S(2)}) %collective-permute-start.20) | collective-permute-done | bytes 131104 | tf_op jit(solution)/shard_map/ppermute | solution.py:244
  67.9 0.1 collective-permute-start.21
  68.0 2.8 %collective-permute-done.17 = f32[3,2,64,128]{3,2,1,0:T(8,128)S(1)} collective-permute-done((f32[3,2,64,128]{3,2,1,0:T(8,128)S(1)}, f32[3,2,64,128]{3,2,1,0:T(8,128)S(1)}, u32[]{:S(2)}, u32[]{:S(2)}) %collective-permute-start.17) | collective-permute-done | bytes 196640 | tf_op jit(solution)/shard_map/ppermute | solution.py:220
  70.9 0.1 fusion.18
  70.9 2.6 %collective-permute-start.18 = (f32[2,64,64]{2,1,0:T(8,128)S(1)}, f32[2,64,64]{2,1,0:T(8,128)S(1)}, u32[]{:S(2)}, u32[]{:S(2)}) collective-permute-start(f32[2,64,64]{2,1,0:T(8,128)S(1)} %fusion.18), channel_id=1, source_target_pairs={{0,2},{2,0},{1,3},{3,1},{4,6},{6,4},{5,7},{7,5},{8,10},{10,8},{9,1... | collective-permute-start | bytes 98312 | tf_op jit(solution)/shard_map/ppermute | solution.py:233
  73.5 2.2 %collective-permute-done.18 = f32[2,64,64]{2,1,0:T(8,128)S(1)} collective-permute-done((f32[2,64,64]{2,1,0:T(8,128)S(1)}, f32[2,64,64]{2,1,0:T(8,128)S(1)}, u32[]{:S(2)}, u32[]{:S(2)}) %collective-permute-start.18) | collective-permute-done | bytes 32800 | tf_op jit(solution)/shard_map/ppermute | solution.py:233
  75.8 0.1 fusion.19
  75.9 0.2 fusion.3
  76.0 0.1 collective-permute-start.19
  76.2 1.8 %collective-permute-start.22 = (f32[256,128]{1,0:T(8,128)S(1)}, f32[256,128]{1,0:T(8,128)S(1)}, u32[]{:S(2)}, u32[]{:S(2)}) collective-permute-start(f32[256,128]{1,0:T(8,128)S(1)} %add.218), channel_id=1, source_target_pairs={{0,12},{4,8},{8,4},{12,0},{1,13},{5,9},{9,5},{13,1},{2,14},{6,10},... | collective-permute-start | bytes 393224 | tf_op jit(solution)/shard_map/ppermute | solution.py:244
  78.0 0.7 pad_maximum_fusion.1
  78.7 5.3 %collective-permute-done.22 = f32[256,128]{1,0:T(8,128)S(1)} collective-permute-done((f32[256,128]{1,0:T(8,128)S(1)}, f32[256,128]{1,0:T(8,128)S(1)}, u32[]{:S(2)}, u32[]{:S(2)}) %collective-permute-start.22) | collective-permute-done | bytes 131104 | tf_op jit(solution)/shard_map/ppermute | solution.py:244
  84.0 0.7 multiply_subtract_fusion
  (48 shorter events, 0.5 us)
Async XLA Ops:
  0.6 8.9 %copy-start.5 = (f32[2,128,256]{2,1,0:T(8,128)S(1)}, f32[2,128,256]{2,1,0:T(8,128)}, u32[]{:S(2)}) copy-start(f32[2,128,256]{2,1,0:T(8,128)} %param.13) | copy-start | bytes 786436
  1.7 7.9 %collective-permute-start = (f32[2,64,256]{2,1,0:T(8,128)S(1)}, f32[2,64,256]{2,1,0:T(8,128)S(1)}, u32[]{:S(2)}, u32[]{:S(2)}) collective-permute-start(f32[2,64,256]{2,1,0:T(8,128)S(1)} %slice_select_fusion.2), channel_id=1, source_target_pairs={{0,4},{1,1},{4,0},{5,9},{8,12},{9,5},{12,8},{13,13},{2,6},{3,3},{6... | collective-permute-start | bytes 393224 | tf_op jit(solution)/shard_map/ppermute | solution.py:220
  9.6 2.1 %copy-start.6 = (f32[1,2,128,128]{3,2,1,0:T(8,128)S(1)}, f32[1,2,128,128]{3,2,1,0:T(8,128)}, u32[]{:S(2)}) copy-start(f32[1,2,128,128]{3,2,1,0:T(8,128)} %param.14) | copy-start | bytes 393220
  9.7 5.0 %collective-permute-start.1 = (f32[2,128,64]{2,1,0:T(8,128)S(1)}, f32[2,128,64]{2,1,0:T(8,128)S(1)}, u32[]{:S(2)}, u32[]{:S(2)}) collective-permute-start(f32[2,128,64]{2,1,0:T(8,128)S(1)} %fusion.1), channel_id=1, source_target_pairs={{0,2},{2,0},{1,3},{3,1},{4,6},{6,4},{5,7},{7,5},{8,10},{10,8},{9,1... | collective-permute-start | bytes 196616 | tf_op jit(solution)/shard_map/ppermute | solution.py:233
  11.7 5.8 %collective-permute-start.5 = (f32[256,128]{1,0:T(8,128)S(1)}, f32[256,128]{1,0:T(8,128)S(1)}, u32[]{:S(2)}, u32[]{:S(2)}) collective-permute-start(f32[256,128]{1,0:T(8,128)S(1)} %bitcast_add_fusion.refs_4_), channel_id=1, source_target_pairs={{0,1},{1,0},{2,3},{3,2},{4,5},{5,4},{6,7},{7,6},{8,9},{9,8},{10,11... | collective-permute-start | bytes 393224 | tf_op jit(solution)/shard_map/ppermute | solution.py:209
  11.8 5.7 %copy-start = (f32[1,1,16,128,128]{4,3,2,1,0:T(8,128)S(1)}, f32[1,1,16,128,128]{4,3,2,1,0:T(8,128)}, u32[]{:S(2)}) copy-start(f32[1,1,16,128,128]{4,3,2,1,0:T(8,128)} %param.17) | copy-start | bytes 3145732
  15.0 2.5 %collective-permute-start.2 = (f32[256,128]{1,0:T(8,128)S(1)}, f32[256,128]{1,0:T(8,128)S(1)}, u32[]{:S(2)}, u32[]{:S(2)}) collective-permute-start(f32[256,128]{1,0:T(8,128)S(1)} %bitcast_add_fusion.3.refs_1_), channel_id=1, source_target_pairs={{0,1},{1,0},{2,3},{3,2},{4,5},{5,4},{6,7},{7,6},{8,9},{9,8},{10,11... | collective-permute-start | bytes 393224 | tf_op jit(solution)/shard_map/ppermute | solution.py:209
  15.1 2.4 %copy-start.3 = (bf16[256,256]{1,0:T(8,128)(2,1)S(1)}, bf16[256,256]{1,0:T(8,128)(2,1)}, u32[]{:S(2)}) copy-start(bf16[256,256]{1,0:T(8,128)(2,1)} %constant.84.clone.refs_12_) | copy-start | bytes 393220
  15.1 2.4 %copy-start.4 = (bf16[256,256]{1,0:T(8,128)(2,1)S(1)}, bf16[256,256]{1,0:T(8,128)(2,1)}, u32[]{:S(2)}) copy-start(bf16[256,256]{1,0:T(8,128)(2,1)} %constant.85.clone.refs_13_) | copy-start | bytes 393220
  15.1 2.4 %collective-permute-start.3 = (f32[256,128]{1,0:T(8,128)S(1)}, f32[256,128]{1,0:T(8,128)S(1)}, u32[]{:S(2)}, u32[]{:S(2)}) collective-permute-start(f32[256,128]{1,0:T(8,128)S(1)} %bitcast_add_fusion.2.refs_2_), channel_id=1, source_target_pairs={{0,1},{1,0},{2,3},{3,2},{4,5},{5,4},{6,7},{7,6},{8,9},{9,8},{10,11... | collective-permute-start | bytes 393224 | tf_op jit(solution)/shard_map/ppermute | solution.py:209
  15.7 1.9 %copy-start.1 = (bf16[256,256]{1,0:T(8,128)(2,1)S(1)}, bf16[256,256]{1,0:T(8,128)(2,1)}, u32[]{:S(2)}) copy-start(bf16[256,256]{1,0:T(8,128)(2,1)} %constant.82.clone.refs_10_) | copy-start | bytes 393220
  15.7 1.9 %copy-start.2 = (bf16[256,256]{1,0:T(8,128)(2,1)S(1)}, bf16[256,256]{1,0:T(8,128)(2,1)}, u32[]{:S(2)}) copy-start(bf16[256,256]{1,0:T(8,128)(2,1)} %constant.83.clone.refs_11_) | copy-start | bytes 393220
  15.7 1.8 %collective-permute-start.4 = (f32[256,128]{1,0:T(8,128)S(1)}, f32[256,128]{1,0:T(8,128)S(1)}, u32[]{:S(2)}, u32[]{:S(2)}) collective-permute-start(f32[256,128]{1,0:T(8,128)S(1)} %bitcast_add_fusion.1.refs_3_), channel_id=1, source_target_pairs={{0,1},{1,0},{2,3},{3,2},{4,5},{5,4},{6,7},{7,6},{8,9},{9,8},{10,11... | collective-permute-start | bytes 393224 | tf_op jit(solution)/shard_map/ppermute | solution.py:209
  15.9 0.7 copy-start.8
  25.3 2.2 %collective-permute-start.6 = (f32[1024,128]{1,0:T(8,128)}, f32[1024,128]{1,0:T(8,128)S(1)}, u32[]{:S(2)}, u32[]{:S(2)}) collective-permute-start(f32[1024,128]{1,0:T(8,128)} %get-tuple-element.7), channel_id=1, source_target_pairs={{0,1},{1,0},{2,3},{3,2},{4,5},{5,4},{6,7},{7,6},{8,9},{9,8},{10,11... | collective-permute-start | bytes 1572872 | tf_op jit(solution)/shard_map/ppermute | solution.py:209
  27.6 6.1 %collective-permute-start.9 = (f32[256,128]{1,0:T(8,128)S(1)}, f32[256,128]{1,0:T(8,128)S(1)}, u32[]{:S(2)}, u32[]{:S(2)}) collective-permute-start(f32[256,128]{1,0:T(8,128)S(1)} %slice.112), channel_id=1, source_target_pairs={{0,2},{2,0},{1,3},{3,1},{4,6},{6,4},{5,7},{7,5},{8,10},{10,8},{9,1... | collective-permute-start | bytes 393224 | tf_op jit(solution)/shard_map/ppermute | solution.py:244
  29.7 16.2 %collective-permute-start.7 = (f32[768,128]{1,0:T(8,128)S(1)}, f32[768,128]{1,0:T(8,128)S(1)}, u32[]{:S(2)}, u32[]{:S(2)}) collective-permute-start(f32[768,128]{1,0:T(8,128)S(1)} %slice.104), channel_id=1, source_target_pairs={{0,4},{1,1},{4,0},{5,9},{8,12},{9,5},{12,8},{13,13},{2,6},{3,3},{6... | collective-permute-start | bytes 1179656 | tf_op jit(solution)/shard_map/ppermute | solution.py:220
  33.7 8.5 %collective-permute-start.10 = (f32[256,128]{1,0:T(8,128)S(1)}, f32[256,128]{1,0:T(8,128)S(1)}, u32[]{:S(2)}, u32[]{:S(2)}) collective-permute-start(f32[256,128]{1,0:T(8,128)S(1)} %slice_add_fusion.1), channel_id=1, source_target_pairs={{0,4},{4,0},{8,12},{12,8},{1,5},{5,1},{9,13},{13,9},{2,6},{6,2},{1... | collective-permute-start | bytes 393224 | tf_op jit(solution)/shard_map/ppermute | solution.py:244
  42.2 6.9 %collective-permute-start.11 = (f32[256,128]{1,0:T(8,128)S(1)}, f32[256,128]{1,0:T(8,128)S(1)}, u32[]{:S(2)}, u32[]{:S(2)}) collective-permute-start(f32[256,128]{1,0:T(8,128)S(1)} %add.210), channel_id=1, source_target_pairs={{0,12},{4,8},{8,4},{12,0},{1,13},{5,9},{9,5},{13,1},{2,14},{6,10},... | collective-permute-start | bytes 393224 | tf_op jit(solution)/shard_map/ppermute | solution.py:244
  45.9 3.2 %copy-start.7 = (f32[1,2,128,128]{3,2,1,0:T(8,128)S(1)}, f32[1,2,128,128]{3,2,1,0:T(8,128)}, u32[]{:S(2)}) copy-start(f32[1,2,128,128]{3,2,1,0:T(8,128)} %param.14) | copy-start | bytes 393220
  46.0 5.0 %collective-permute-start.8 = (f32[256,128]{1,0:T(8,128)S(1)}, f32[256,128]{1,0:T(8,128)S(1)}, u32[]{:S(2)}, u32[]{:S(2)}) collective-permute-start(f32[256,128]{1,0:T(8,128)S(1)} %slice_select_fusion.3), channel_id=1, source_target_pairs={{0,2},{2,0},{1,3},{3,1},{4,6},{6,4},{5,7},{7,5},{8,10},{10,8},{9,1... | collective-permute-start | bytes 393224 | tf_op jit(solution)/shard_map/ppermute | solution.py:233
  49.2 2.7 %collective-permute-start.15 = (f32[256,128]{1,0:T(8,128)S(1)}, f32[256,128]{1,0:T(8,128)S(1)}, u32[]{:S(2)}, u32[]{:S(2)}) collective-permute-start(f32[256,128]{1,0:T(8,128)S(1)} %fusion.7.refs_4_), channel_id=1, source_target_pairs={{0,1},{1,0},{2,3},{3,2},{4,5},{5,4},{6,7},{7,6},{8,9},{9,8},{10,11... | collective-permute-start | bytes 393224 | tf_op jit(solution)/shard_map/ppermute | solution.py:209
  51.2 1.4 %collective-permute-start.12 = (f32[256,128]{1,0:T(8,128)S(1)}, f32[256,128]{1,0:T(8,128)S(1)}, u32[]{:S(2)}, u32[]{:S(2)}) collective-permute-start(f32[256,128]{1,0:T(8,128)S(1)} %get-tuple-element.10.refs_1_), channel_id=1, source_target_pairs={{0,1},{1,0},{2,3},{3,2},{4,5},{5,4},{6,7},{7,6},{8,9},{9,8},{10,11... | collective-permute-start | bytes 393224 | tf_op jit(solution)/shard_map/ppermute | solution.py:209
  51.3 1.5 %collective-permute-start.13 = (f32[256,128]{1,0:T(8,128)S(1)}, f32[256,128]{1,0:T(8,128)S(1)}, u32[]{:S(2)}, u32[]{:S(2)}) collective-permute-start(f32[256,128]{1,0:T(8,128)S(1)} %get-tuple-element.12.refs_2_), channel_id=1, source_target_pairs={{0,1},{1,0},{2,3},{3,2},{4,5},{5,4},{6,7},{7,6},{8,9},{9,8},{10,11... | collective-permute-start | bytes 393224 | tf_op jit(solution)/shard_map/ppermute | solution.py:209
  51.8 1.3 %collective-permute-start.14 = (f32[256,128]{1,0:T(8,128)S(1)}, f32[256,128]{1,0:T(8,128)S(1)}, u32[]{:S(2)}, u32[]{:S(2)}) collective-permute-start(f32[256,128]{1,0:T(8,128)S(1)} %get-tuple-element.11.refs_3_), channel_id=1, source_target_pairs={{0,1},{1,0},{2,3},{3,2},{4,5},{5,4},{6,7},{7,6},{8,9},{9,8},{10,11... | collective-permute-start | bytes 393224 | tf_op jit(solution)/shard_map/ppermute | solution.py:209
  60.2 2.0 %collective-permute-start.16 = (f32[1024,128]{1,0:T(8,128)S(1)}, f32[1024,128]{1,0:T(8,128)S(1)}, u32[]{:S(2)}, u32[]{:S(2)}) collective-permute-start(f32[1024,128]{1,0:T(8,128)S(1)} %get-tuple-element.9), channel_id=1, source_target_pairs={{0,1},{1,0},{2,3},{3,2},{4,5},{5,4},{6,7},{7,6},{8,9},{9,8},{10,11... | collective-permute-start | bytes 1572872 | tf_op jit(solution)/shard_map/ppermute | solution.py:209
  62.2 5.7 %collective-permute-start.20 = (f32[256,128]{1,0:T(8,128)S(1)}, f32[256,128]{1,0:T(8,128)S(1)}, u32[]{:S(2)}, u32[]{:S(2)}) collective-permute-start(f32[256,128]{1,0:T(8,128)S(1)} %slice.121), channel_id=1, source_target_pairs={{0,2},{2,0},{1,3},{3,1},{4,6},{6,4},{5,7},{7,5},{8,10},{10,8},{9,1... | collective-permute-start | bytes 393224 | tf_op jit(solution)/shard_map/ppermute | solution.py:244
  62.9 8.0 %collective-permute-start.17 = (f32[3,2,64,128]{3,2,1,0:T(8,128)S(1)}, f32[3,2,64,128]{3,2,1,0:T(8,128)S(1)}, u32[]{:S(2)}, u32[]{:S(2)}) collective-permute-start(f32[3,2,64,128]{3,2,1,0:T(8,128)S(1)} %slice_select_fusion), channel_id=1, source_target_pairs={{0,4},{1,1},{4,0},{5,9},{8,12},{9,5},{12,8},{13,13},{2,6},{3,3},{6... | collective-permute-start | bytes 589832 | tf_op jit(solution)/shard_map/ppermute | solution.py:220
  67.9 8.2 %collective-permute-start.21 = (f32[256,128]{1,0:T(8,128)S(1)}, f32[256,128]{1,0:T(8,128)S(1)}, u32[]{:S(2)}, u32[]{:S(2)}) collective-permute-start(f32[256,128]{1,0:T(8,128)S(1)} %slice_add_fusion), channel_id=1, source_target_pairs={{0,4},{4,0},{8,12},{12,8},{1,5},{5,1},{9,13},{13,9},{2,6},{6,2},{1... | collective-permute-start | bytes 393224 | tf_op jit(solution)/shard_map/ppermute | solution.py:244
  70.9 4.8 %collective-permute-start.18 = (f32[2,64,64]{2,1,0:T(8,128)S(1)}, f32[2,64,64]{2,1,0:T(8,128)S(1)}, u32[]{:S(2)}, u32[]{:S(2)}) collective-permute-start(f32[2,64,64]{2,1,0:T(8,128)S(1)} %fusion.18), channel_id=1, source_target_pairs={{0,2},{2,0},{1,3},{3,1},{4,6},{6,4},{5,7},{7,5},{8,10},{10,8},{9,1... | collective-permute-start | bytes 98312 | tf_op jit(solution)/shard_map/ppermute | solution.py:233
  76.0 1.9 %collective-permute-start.19 = (f32[2,64,256]{2,1,0:T(8,128)S(1)}, f32[2,64,256]{2,1,0:T(8,128)S(1)}, u32[]{:S(2)}, u32[]{:S(2)}) collective-permute-start(f32[2,64,256]{2,1,0:T(8,128)S(1)} %fusion.3), channel_id=1, source_target_pairs={{0,1},{1,0},{2,3},{3,2},{4,5},{5,4},{6,7},{7,6},{8,9},{9,8},{10,11... | collective-permute-start | bytes 393224 | tf_op jit(solution)/shard_map/ppermute | solution.py:209
  76.2 7.9 %collective-permute-start.22 = (f32[256,128]{1,0:T(8,128)S(1)}, f32[256,128]{1,0:T(8,128)S(1)}, u32[]{:S(2)}, u32[]{:S(2)}) collective-permute-start(f32[256,128]{1,0:T(8,128)S(1)} %add.218), channel_id=1, source_target_pairs={{0,12},{4,8},{8,4},{12,0},{1,13},{5,9},{9,5},{13,1},{2,14},{6,10},... | collective-permute-start | bytes 393224 | tf_op jit(solution)/shard_map/ppermute | solution.py:244

commit v3 on v2

--- a/solution.py
+++ b/solution.py
@@ -209,40 +209,67 @@
     return lax.ppermute(block, "mode", [(0, 1), (1, 0)])
 
 
-def swap_rows(block):
-    count = lax.axis_size("row")
+def paired_with(index, parity, count):
+    other = index + 1 if index % 2 == parity else index - 1
+    return other if 0 <= other < count else None
+
+
+def swap_neighbours(block, col_parity=None):
+    rows, cols = lax.axis_size("row"), lax.axis_size("col")
     route = []
-    for row in range(count):
-        for mode in range(2):
-            other = row + 1 if row % 2 == mode else row - 1
-            other = other if 0 <= other < count else row
-            route.append((2 * row + mode, 2 * other + mode))
-    return lax.ppermute(block, ("row", "mode"), route)
-
-
-def swap_cols(to_low, to_high):
+    for row in range(rows):
+        for col in range(cols):
+            for mode in range(2):
+                to_row = paired_with(row, mode, rows)
+                to_col = col if col_parity is None else paired_with(col, col_parity, cols)
+                if to_col is None:
+                    to_row, to_col = row, col
+                elif to_row is None:
+                    to_row = row
+                    to_col = col ^ 1 if cols % 2 == 0 and col_parity is None else to_col
+                route.append(
+                    ((row * cols + col) * 2 + mode, (to_row * cols + to_col) * 2 + mode)
+                )
+    return lax.ppermute(block, ("row", "col", "mode"), route)
+
+
+def from_cols(blocks, send):
     count = lax.axis_size("col")
     col = lax.axis_index("col")
+    to_low, to_high = blocks
     from_low = from_high = jnp.zeros_like(to_low)
     for parity in range(min(2, count - 1)):
-        route = []
-        for i in range(count):
-            other = i + 1 if i % 2 == parity else i - 1
-            route.append((i, other if 0 <= other < count else i))
         is_low = col % 2 == parity
-        got = lax.ppermute(jnp.where(is_low, to_high, to_low), "col", route)
+        got = send(jnp.where(is_low, to_high, to_low), parity)
         from_high = jnp.where(is_low & (col < count - 1), got, from_high)
         from_low = jnp.where(jnp.logical_not(is_low) & (col > 0), got, from_low)
     return from_low, from_high
 
 
+def swap_cols(block, parity):
+    count = lax.axis_size("col")
+    others = [paired_with(i, parity, count) for i in range(count)]
+    return lax.ppermute(block, "col", [(i, i if o is None else o) for i, o in enumerate(others)])
+
+
 def sum_tiles(block):
-    for axis in ("col", "row"):
-        count = lax.axis_size(axis)
-        reach = 1
-        while reach < count:
-            block = block + lax.ppermute(block, axis, [(i, i ^ (2 * reach - 1)) for i in range(count)])
-            reach *= 2
+    rows, cols = lax.axis_size("row"), lax.axis_size("col")
+    along_cols = [(0, 1 << k) for k in range((cols - 1).bit_length())]
+    along_rows = [(1 << k, 0) for k in range((rows - 1).bit_length())]
+    if len(along_rows) > 1:
+        turned = [(3, 0)] + along_cols + along_rows[:1] + along_rows[2:]
+    else:
+        turned = along_rows + along_cols
+    for steps in zip(along_cols + along_rows, turned, strict=True):
+        route = []
+        for row in range(rows):
+            for col in range(cols):
+                for mode in range(2):
+                    to_row, to_col = row ^ steps[mode][0], col ^ steps[mode][1]
+                    route.append(
+                        ((row * cols + col) * 2 + mode, (to_row * cols + to_col) * 2 + mode)
+                    )
+        block = block + lax.ppermute(block, ("row", "col", "mode"), route)
     return block
 
 
@@ -265,12 +292,16 @@
     probe_step = probe_rate / (slot_count * rows_count * cols_count)
 
     strip = jnp.where(lower, obj[:, half:], obj[:, :half])
-    beside = jnp.where(paired, swap_rows(strip), 0.0)
-    region = jnp.concatenate(
+    edges = (strip[:, :, :half], strip[:, :, tile_cols - half :])
+    beside = swap_neighbours(strip)
+    strip_low, strip_high = from_cols(edges, swap_cols)
+    corner_low, corner_high = from_cols(edges, swap_neighbours)
+    strip = jnp.concatenate([strip_low, strip, strip_high], axis=2)
+    beside = jnp.concatenate([corner_low, beside, corner_high], axis=2)
+    beside = jnp.where(paired, beside, 0.0)
+    wide = jnp.concatenate(
         [jnp.where(lower, strip, beside), jnp.where(lower, beside, strip)], axis=1
     )
-    from_low, from_high = swap_cols(region[:, :, :half], region[:, :, tile_cols - half :])
-    wide = jnp.concatenate([from_low, region, from_high], axis=2)
     start = [
         wide[:, :, tile * size : (tile + 1) * size].reshape(2 * size, size)
         for tile in range(columns)
@@ -295,11 +326,11 @@
         object_grad = total[: columns * 2 * size]
         new_probe = ahead[-1] - probe_step * probe_grad
         if iteration < ITERS - 1:
-            object_grad = object_grad + jnp.where(paired, swap_rows(object_grad), 0.0)
+            object_grad = object_grad + jnp.where(paired, swap_neighbours(object_grad), 0.0)
             parts = [
                 object_grad[tile * 2 * size : (tile + 1) * 2 * size] for tile in range(columns)
             ]
-            from_low, from_high = swap_cols(parts[0], parts[-1])
+            from_low, from_high = from_cols((parts[0], parts[-1]), swap_cols)
             parts[0] = parts[0] + from_low
             parts[-1] = parts[-1] + from_high
             current = [
@@ -309,8 +340,9 @@
             object_grad = object_grad.reshape(columns, 2, size, size)
             given = jnp.where(lower, object_grad[:, :, half:], object_grad[:, :, :half])
             owned = jnp.where(lower, object_grad[:, :, :half], object_grad[:, :, half:])
-            owned = owned + jnp.where(paired, swap_rows(given), 0.0)
-            from_low, from_high = swap_cols(owned[0, :, :, :half], owned[-1, :, :, half:])
+            owned = owned + jnp.where(paired, swap_neighbours(given), 0.0)
+            edges = (owned[0, :, :, :half], owned[-1, :, :, half:])
+            from_low, from_high = from_cols(edges, swap_cols)
             owned = jnp.concatenate(
                 [owned[0, :, :, half:] + from_low]
                 + [owned[tile] for tile in range(1, columns - 1)]

time: 84.9 us -> 76.3 us (0.90)
  starting transfers between devices: 27.8 us -> 16.3 us
  waiting for transfers between devices: 35.4 us -> 38.3 us
    ppermute x12 -> x13, starting transfers between devices: 25.5 us -> 13.5 us  [the longest x4 5.57 us: swap_neighbours(): return lax.ppermute(block, ('row', 'col', 'mode'), route)]
    ppermute x12 -> x13, waiting for transfers between devices: 30.7 us -> 33.4 us  [the longest x6 23 us: sum_tiles(): block = block + lax.ppermute(block, ('row', 'col', 'mode'), route)]
  transfers between devices with their start and end apart: 23 -> 24, of which waited for: 15 -> 16; matrix products, arithmetic and copies ran while one was open for 3% -> 3% of each run, Pallas kernels for 0% -> 0%
where the time goes in v3:
time: 76.3 us; the launch traced here: 76.1 us
  waiting for transfers between devices  38.3 us (50%)
  starting transfers between devices  16.3 us (21%)
  Pallas kernels  14.8 us (19%)
  other arithmetic  3.95 us (5%)
  between operations  1.71 us (2%)
  local copies, waits for them, and re-layouts  1 us (1%)
    ppermute x6, waiting for transfers between devices, sum_tiles(): block = block + lax.ppermute(block, ('row', 'col', 'mode'), route)  23 us
    pallas_call x2, Pallas kernels, gradients(): pl.pallas_call(body, out_shape=(shape, shape), grid_spec=pltpu.PrefetchSc...  14.8 us
    ppermute x3, waiting for transfers between devices, swap_cols(): lax.ppermute(block, 'col', [(i, i if o is None else o) for i, o in enumer...  5.88 us
    ppermute x4, starting transfers between devices, swap_neighbours(): return lax.ppermute(block, ('row', 'col', 'mode'), route)  5.57 us
    ppermute x6, starting transfers between devices, sum_tiles(): block = block + lax.ppermute(block, ('row', 'col', 'mode'), route)  5.31 us
    ppermute x11, waiting for transfers between devices, swap_modes(): return lax.ppermute(block, 'mode', [(0, 1), (1, 0)])  4.93 us
    ppermute x4, waiting for transfers between devices, swap_neighbours(): return lax.ppermute(block, ('row', 'col', 'mode'), route)  4.54 us
    ppermute x11, starting transfers between devices, swap_modes(): return lax.ppermute(block, 'mode', [(0, 1), (1, 0)])  2.81 us
  transfers between devices with their start and end apart: 24, of which 16 were waited for; matrix products, arithmetic and copies ran while one was open for 3% of the time, Pallas kernels for 0%

profile of v3, /device:TPU:0, one launch (start us, length us, event | category | flops | bytes accessed | tf_op | source)
XLA Modules:
  0.0 76.1 jit_solution(16970447166362053353)
XLA Ops:
  0.7 1.0 %slice_select_fusion.2 = f32[2,64,256]{2,1,0:T(8,128)S(1)} fusion(f32[2,128,256]{2,1,0:T(8,128)} %param.13, pred[]{:T(512)S(6)} %eq.15), kind=kLoop, calls=%fused_computation.44 | loop fusion | flops 32768 | bytes 393217 | tf_op jit(solution)/shard_map/jit(_where)/select_n | solution.py:294
  1.7 0.1 slice_select_fusion.5
  1.8 4.0 %collective-permute-start.1 = (f32[2,64,64]{2,1,0:T(8,128)S(1)}, f32[2,64,64]{2,1,0:T(8,128)S(1)}, u32[]{:S(2)}, u32[]{:S(2)}) collective-permute-start(f32[2,64,64]{2,1,0:T(8,128)S(1)} %slice_select_fusion.5), channel_id=1, source_target_pairs={{0,6},{1,3},{2,4},{3,1},{4,2},{5,11},{6,0},{7,9},{8,14},{9,7},{10,... | collective-permute-start | bytes 98312 | tf_op jit(solution)/shard_map/ppermute | solution.py:233
  5.8 0.5 collective-permute-start
  6.3 0.1 collective-permute-start.2
  6.4 0.1 collective-permute-start.6
  6.6 1.6 %collective-permute-done.1 = f32[2,64,64]{2,1,0:T(8,128)S(1)} collective-permute-done((f32[2,64,64]{2,1,0:T(8,128)S(1)}, f32[2,64,64]{2,1,0:T(8,128)S(1)}, u32[]{:S(2)}, u32[]{:S(2)}) %collective-permute-start.1) | collective-permute-done | bytes 32800 | tf_op jit(solution)/shard_map/ppermute | solution.py:233
  8.1 2.3 %collective-permute-done = f32[2,64,64]{2,1,0:T(8,128)S(1)} collective-permute-done((f32[2,64,64]{2,1,0:T(8,128)S(1)}, f32[2,64,64]{2,1,0:T(8,128)S(1)}, u32[]{:S(2)}, u32[]{:S(2)}) %collective-permute-start) | collective-permute-done | bytes 32800 | tf_op jit(solution)/shard_map/ppermute | solution.py:252
  10.4 0.8 %collective-permute-done.2 = f32[2,64,256]{2,1,0:T(8,128)S(1)} collective-permute-done((f32[2,64,256]{2,1,0:T(8,128)S(1)}, f32[2,64,256]{2,1,0:T(8,128)S(1)}, u32[]{:S(2)}, u32[]{:S(2)}) %collective-permute-start.2) | collective-permute-done | bytes 131104 | tf_op jit(solution)/shard_map/ppermute | solution.py:233
  11.3 0.2 fusion.17
  11.6 0.1 collective-permute-start.3
  11.6 0.0 copy-start.3
  11.6 0.0 copy-start.4
  11.7 0.5 collective-permute-start.4
  12.2 0.1 collective-permute-start.5
  12.3 0.1 pad_add_fusion
  12.4 0.1 sub.82
  12.5 0.6 copy-done.7
  13.1 0.1 copy.16
  13.2 0.1 squeeze.14
  13.9 0.1 pad_add_fusion.1.refs_0_
  14.1 7.8 %gradients.2 = (f32[1024,128]{1,0:T(8,128)S(1)}, f32[1024,128]{1,0:T(8,128)}) custom-call(s32[35]{0:T(128)S(1)} %pad_add_fusion.1.refs_0_, f32[256,128]{1,0:T(8,128)S(1)} %bitcast_add_fusion.3.refs_1_, f32[256,128]{1,0:T(8,128)S(1)} %bitcast_add_fusion.2.refs_2_, f32[256,128]{1,0:T(8,128)S(1)} %bitcast_add_fusion.1.refs_3_, ...), custom_call_target="tpu_custom_call" | custom-call | tf_op jit(solution)/shard_map/gradients/pallas_call | solution.py:182
  21.9 0.5 collective-permute-start.7
  22.4 1.7 %collective-permute-done.7 = f32[1024,128]{1,0:T(8,128)S(1)} collective-permute-done((f32[1024,128]{1,0:T(8,128)}, f32[1024,128]{1,0:T(8,128)S(1)}, u32[]{:S(2)}, u32[]{:S(2)}) %collective-permute-start.7) | collective-permute-done | bytes 524320 | tf_op jit(solution)/shard_map/ppermute | solution.py:209
  24.1 0.1 add.201
  24.2 1.5 %collective-permute-start.10 = (f32[256,128]{1,0:T(8,128)S(1)}, f32[256,128]{1,0:T(8,128)S(1)}, u32[]{:S(2)}, u32[]{:S(2)}) collective-permute-start(f32[256,128]{1,0:T(8,128)S(1)} %slice.112), channel_id=1, source_target_pairs={{0,2},{1,13},{2,0},{3,15},{4,6},{5,9},{6,4},{7,11},{8,10},{9,5},{1... | collective-permute-start | bytes 393224 | tf_op jit(solution)/shard_map/ppermute | solution.py:272
  25.8 0.5 collective-permute-start.8
  26.3 2.9 %collective-permute-done.10 = f32[256,128]{1,0:T(8,128)S(1)} collective-permute-done((f32[256,128]{1,0:T(8,128)S(1)}, f32[256,128]{1,0:T(8,128)S(1)}, u32[]{:S(2)}, u32[]{:S(2)}) %collective-permute-start.10) | collective-permute-done | bytes 131104 | tf_op jit(solution)/shard_map/ppermute | solution.py:272
  29.3 0.2 collective-permute-start.11
  29.5 6.6 %collective-permute-done.11 = f32[256,128]{1,0:T(8,128)S(1)} collective-permute-done((f32[256,128]{1,0:T(8,128)S(1)}, f32[256,128]{1,0:T(8,128)S(1)}, u32[]{:S(2)}, u32[]{:S(2)}) %collective-permute-start.11) | collective-permute-done | bytes 131104 | tf_op jit(solution)/shard_map/ppermute | solution.py:272
  36.2 1.5 %collective-permute-start.12 = (f32[256,128]{1,0:T(8,128)S(1)}, f32[256,128]{1,0:T(8,128)S(1)}, u32[]{:S(2)}, u32[]{:S(2)}) collective-permute-start(f32[256,128]{1,0:T(8,128)S(1)} %add.211), channel_id=1, source_target_pairs={{0,8},{1,5},{2,10},{3,7},{4,12},{5,1},{6,14},{7,3},{8,0},{9,13},{1... | collective-permute-start | bytes 393224 | tf_op jit(solution)/shard_map/ppermute | solution.py:272
  37.7 0.1 select_add_fusion
  37.8 0.0 copy-start.6
  37.8 0.8 %collective-permute-start.9 = (f32[256,128]{1,0:T(8,128)S(1)}, f32[256,128]{1,0:T(8,128)S(1)}, u32[]{:S(2)}, u32[]{:S(2)}) collective-permute-start(f32[256,128]{1,0:T(8,128)S(1)} %slice_select_fusion.3), channel_id=1, source_target_pairs={{0,2},{2,0},{1,3},{3,1},{4,6},{6,4},{5,7},{7,5},{8,10},{10,8},{9,1... | collective-permute-start | bytes 393224 | tf_op jit(solution)/shard_map/ppermute | solution.py:252
  38.6 4.9 %collective-permute-done.12 = f32[256,128]{1,0:T(8,128)S(1)} collective-permute-done((f32[256,128]{1,0:T(8,128)S(1)}, f32[256,128]{1,0:T(8,128)S(1)}, u32[]{:S(2)}, u32[]{:S(2)}) %collective-permute-start.12) | collective-permute-done | bytes 131104 | tf_op jit(solution)/shard_map/ppermute | solution.py:272
  43.5 0.1 collective-permute-start.16
  43.6 0.2 fusion.15
  43.9 0.6 collective-permute-start.13
  44.4 0.1 collective-permute-start.14
  44.5 0.4 collective-permute-start.15
  44.9 0.0 collective-permute-done.16.refs_8_
  45.0 0.4 collective-permute-done.13.refs_5_
  45.4 0.4 collective-permute-done.14.refs_6_
  45.8 0.2 collective-permute-done.15.refs_7_
  45.9 7.0 %gradients.3 = (f32[1024,128]{1,0:T(8,128)S(1)}, f32[1024,128]{1,0:T(8,128)S(1)}) custom-call(s32[35]{0:T(128)S(1)} %pad_add_fusion.1.refs_0_, f32[256,128]{1,0:T(8,128)S(1)} %get-tuple-element.10.refs_1_, f32[256,128]{1,0:T(8,128)S(1)} %get-tuple-element.14.refs_2_, f32[256,128]{1,0:T(8,128)S(1)} %get-tuple-element.11.refs_3_, ...), custom_call_target="tpu_custom_call" | custom-call | tf_op jit(solution)/shard_map/gradients/pallas_call | solution.py:182
  53.0 0.4 collective-permute-start.17
  53.4 1.5 %collective-permute-done.17 = f32[1024,128]{1,0:T(8,128)S(1)} collective-permute-done((f32[1024,128]{1,0:T(8,128)S(1)}, f32[1024,128]{1,0:T(8,128)S(1)}, u32[]{:S(2)}, u32[]{:S(2)}) %collective-permute-start.17) | collective-permute-done | bytes 524320 | tf_op jit(solution)/shard_map/ppermute | solution.py:209
  54.9 0.1 add.214
  55.0 0.7 collective-permute-start.21
  55.7 0.9 %collective-permute-start.18 = (f32[3,2,64,128]{3,2,1,0:T(8,128)S(1)}, f32[3,2,64,128]{3,2,1,0:T(8,128)S(1)}, u32[]{:S(2)}, u32[]{:S(2)}) collective-permute-start(f32[3,2,64,128]{3,2,1,0:T(8,128)S(1)} %slice_select_fusion), channel_id=1, source_target_pairs={{0,4},{1,3},{2,6},{3,1},{4,0},{5,9},{6,2},{7,11},{8,12},{9,5},{10,... | collective-permute-start | bytes 589832 | tf_op jit(solution)/shard_map/ppermute | solution.py:233
  56.6 3.4 %collective-permute-done.21 = f32[256,128]{1,0:T(8,128)S(1)} collective-permute-done((f32[256,128]{1,0:T(8,128)S(1)}, f32[256,128]{1,0:T(8,128)S(1)}, u32[]{:S(2)}, u32[]{:S(2)}) %collective-permute-start.21) | collective-permute-done | bytes 131104 | tf_op jit(solution)/shard_map/ppermute | solution.py:272
  60.1 0.6 collective-permute-start.22
  60.7 2.1 %collective-permute-done.18 = f32[3,2,64,128]{3,2,1,0:T(8,128)S(1)} collective-permute-done((f32[3,2,64,128]{3,2,1,0:T(8,128)S(1)}, f32[3,2,64,128]{3,2,1,0:T(8,128)S(1)}, u32[]{:S(2)}, u32[]{:S(2)}) %collective-permute-start.18) | collective-permute-done | bytes 196640 | tf_op jit(solution)/shard_map/ppermute | solution.py:233
  62.9 0.1 fusion.19
  63.0 1.2 %collective-permute-start.19 = (f32[2,64,64]{2,1,0:T(8,128)S(1)}, f32[2,64,64]{2,1,0:T(8,128)S(1)}, u32[]{:S(2)}, u32[]{:S(2)}) collective-permute-start(f32[2,64,64]{2,1,0:T(8,128)S(1)} %fusion.19), channel_id=1, source_target_pairs={{0,2},{2,0},{1,3},{3,1},{4,6},{6,4},{5,7},{7,5},{8,10},{10,8},{9,1... | collective-permute-start | bytes 98312 | tf_op jit(solution)/shard_map/ppermute | solution.py:252
  64.2 3.6 %collective-permute-done.19 = f32[2,64,64]{2,1,0:T(8,128)S(1)} collective-permute-done((f32[2,64,64]{2,1,0:T(8,128)S(1)}, f32[2,64,64]{2,1,0:T(8,128)S(1)}, u32[]{:S(2)}, u32[]{:S(2)}) %collective-permute-start.19) | collective-permute-done | bytes 32800 | tf_op jit(solution)/shard_map/ppermute | solution.py:252
  67.8 0.1 fusion.20
  67.9 0.2 fusion.2
  68.1 0.1 collective-permute-start.20
  68.2 0.7 collective-permute-start.23
  68.9 0.6 collective-permute-done.20
  69.6 0.7 pad_maximum_fusion.1
  70.3 5.1 %collective-permute-done.23 = f32[256,128]{1,0:T(8,128)S(1)} collective-permute-done((f32[256,128]{1,0:T(8,128)S(1)}, f32[256,128]{1,0:T(8,128)S(1)}, u32[]{:S(2)}, u32[]{:S(2)}) %collective-permute-start.23) | collective-permute-done | bytes 131104 | tf_op jit(solution)/shard_map/ppermute | solution.py:272
  75.4 0.7 multiply_subtract_fusion
  (49 shorter events, 0.5 us)
Async XLA Ops:
  1.7 4.8 %copy-start.5 = (f32[1,2,128,128]{3,2,1,0:T(8,128)S(1)}, f32[1,2,128,128]{3,2,1,0:T(8,128)}, u32[]{:S(2)}) copy-start(f32[1,2,128,128]{3,2,1,0:T(8,128)} %param.14) | copy-start | bytes 393220
  1.8 6.4 %collective-permute-start.1 = (f32[2,64,64]{2,1,0:T(8,128)S(1)}, f32[2,64,64]{2,1,0:T(8,128)S(1)}, u32[]{:S(2)}, u32[]{:S(2)}) collective-permute-start(f32[2,64,64]{2,1,0:T(8,128)S(1)} %slice_select_fusion.5), channel_id=1, source_target_pairs={{0,6},{1,3},{2,4},{3,1},{4,2},{5,11},{6,0},{7,9},{8,14},{9,7},{10,... | collective-permute-start | bytes 98312 | tf_op jit(solution)/shard_map/ppermute | solution.py:233
  5.8 4.6 %collective-permute-start = (f32[2,64,64]{2,1,0:T(8,128)S(1)}, f32[2,64,64]{2,1,0:T(8,128)S(1)}, u32[]{:S(2)}, u32[]{:S(2)}) collective-permute-start(f32[2,64,64]{2,1,0:T(8,128)S(1)} %slice_select_fusion.5), channel_id=1, source_target_pairs={{0,2},{2,0},{1,3},{3,1},{4,6},{6,4},{5,7},{7,5},{8,10},{10,8},{9,1... | collective-permute-start | bytes 98312 | tf_op jit(solution)/shard_map/ppermute | solution.py:252
  6.3 5.0 %collective-permute-start.2 = (f32[2,64,256]{2,1,0:T(8,128)S(1)}, f32[2,64,256]{2,1,0:T(8,128)S(1)}, u32[]{:S(2)}, u32[]{:S(2)}) collective-permute-start(f32[2,64,256]{2,1,0:T(8,128)S(1)} %slice_select_fusion.2), channel_id=1, source_target_pairs={{0,4},{1,3},{2,6},{3,1},{4,0},{5,9},{6,2},{7,11},{8,12},{9,5},{10,... | collective-permute-start | bytes 393224 | tf_op jit(solution)/shard_map/ppermute | solution.py:233
  6.4 7.6 %collective-permute-start.6 = (f32[256,128]{1,0:T(8,128)S(1)}, f32[256,128]{1,0:T(8,128)S(1)}, u32[]{:S(2)}, u32[]{:S(2)}) collective-permute-start(f32[256,128]{1,0:T(8,128)S(1)} %bitcast_add_fusion.refs_4_), channel_id=1, source_target_pairs={{0,1},{1,0},{2,3},{3,2},{4,5},{5,4},{6,7},{7,6},{8,9},{9,8},{10,11... | collective-permute-start | bytes 393224 | tf_op jit(solution)/shard_map/ppermute | solution.py:209
  11.5 2.6 %copy-start = (f32[1,1,16,128,128]{4,3,2,1,0:T(8,128)S(1)}, f32[1,1,16,128,128]{4,3,2,1,0:T(8,128)}, u32[]{:S(2)}) copy-start(f32[1,1,16,128,128]{4,3,2,1,0:T(8,128)} %param.17) | copy-start | bytes 3145732
  11.6 2.5 %collective-permute-start.3 = (f32[256,128]{1,0:T(8,128)S(1)}, f32[256,128]{1,0:T(8,128)S(1)}, u32[]{:S(2)}, u32[]{:S(2)}) collective-permute-start(f32[256,128]{1,0:T(8,128)S(1)} %bitcast_add_fusion.3.refs_1_), channel_id=1, source_target_pairs={{0,1},{1,0},{2,3},{3,2},{4,5},{5,4},{6,7},{7,6},{8,9},{9,8},{10,11... | collective-permute-start | bytes 393224 | tf_op jit(solution)/shard_map/ppermute | solution.py:209
  11.6 2.4 %copy-start.3 = (bf16[256,256]{1,0:T(8,128)(2,1)S(1)}, bf16[256,256]{1,0:T(8,128)(2,1)}, u32[]{:S(2)}) copy-start(bf16[256,256]{1,0:T(8,128)(2,1)} %constant.85.clone.refs_12_) | copy-start | bytes 393220
  11.6 2.4 %copy-start.4 = (bf16[256,256]{1,0:T(8,128)(2,1)S(1)}, bf16[256,256]{1,0:T(8,128)(2,1)}, u32[]{:S(2)}) copy-start(bf16[256,256]{1,0:T(8,128)(2,1)} %constant.86.clone.refs_13_) | copy-start | bytes 393220
  11.7 2.4 %collective-permute-start.4 = (f32[256,128]{1,0:T(8,128)S(1)}, f32[256,128]{1,0:T(8,128)S(1)}, u32[]{:S(2)}, u32[]{:S(2)}) collective-permute-start(f32[256,128]{1,0:T(8,128)S(1)} %bitcast_add_fusion.2.refs_2_), channel_id=1, source_target_pairs={{0,1},{1,0},{2,3},{3,2},{4,5},{5,4},{6,7},{7,6},{8,9},{9,8},{10,11... | collective-permute-start | bytes 393224 | tf_op jit(solution)/shard_map/ppermute | solution.py:209
  12.2 1.9 %copy-start.1 = (bf16[256,256]{1,0:T(8,128)(2,1)S(1)}, bf16[256,256]{1,0:T(8,128)(2,1)}, u32[]{:S(2)}) copy-start(bf16[256,256]{1,0:T(8,128)(2,1)} %constant.83.clone.refs_10_) | copy-start | bytes 393220
  12.2 1.9 %copy-start.2 = (bf16[256,256]{1,0:T(8,128)(2,1)S(1)}, bf16[256,256]{1,0:T(8,128)(2,1)}, u32[]{:S(2)}) copy-start(bf16[256,256]{1,0:T(8,128)(2,1)} %constant.84.clone.refs_11_) | copy-start | bytes 393220
  12.2 1.8 %collective-permute-start.5 = (f32[256,128]{1,0:T(8,128)S(1)}, f32[256,128]{1,0:T(8,128)S(1)}, u32[]{:S(2)}, u32[]{:S(2)}) collective-permute-start(f32[256,128]{1,0:T(8,128)S(1)} %bitcast_add_fusion.1.refs_3_), channel_id=1, source_target_pairs={{0,1},{1,0},{2,3},{3,2},{4,5},{5,4},{6,7},{7,6},{8,9},{9,8},{10,11... | collective-permute-start | bytes 393224 | tf_op jit(solution)/shard_map/ppermute | solution.py:209
  12.4 0.7 copy-start.7
  21.9 2.2 %collective-permute-start.7 = (f32[1024,128]{1,0:T(8,128)}, f32[1024,128]{1,0:T(8,128)S(1)}, u32[]{:S(2)}, u32[]{:S(2)}) collective-permute-start(f32[1024,128]{1,0:T(8,128)} %get-tuple-element.7), channel_id=1, source_target_pairs={{0,1},{1,0},{2,3},{3,2},{4,5},{5,4},{6,7},{7,6},{8,9},{9,8},{10,11... | collective-permute-start | bytes 1572872 | tf_op jit(solution)/shard_map/ppermute | solution.py:209
  24.2 5.0 %collective-permute-start.10 = (f32[256,128]{1,0:T(8,128)S(1)}, f32[256,128]{1,0:T(8,128)S(1)}, u32[]{:S(2)}, u32[]{:S(2)}) collective-permute-start(f32[256,128]{1,0:T(8,128)S(1)} %slice.112), channel_id=1, source_target_pairs={{0,2},{1,13},{2,0},{3,15},{4,6},{5,9},{6,4},{7,11},{8,10},{9,5},{1... | collective-permute-start | bytes 393224 | tf_op jit(solution)/shard_map/ppermute | solution.py:272
  25.8 11.9 %collective-permute-start.8 = (f32[768,128]{1,0:T(8,128)S(1)}, f32[768,128]{1,0:T(8,128)S(1)}, u32[]{:S(2)}, u32[]{:S(2)}) collective-permute-start(f32[768,128]{1,0:T(8,128)S(1)} %slice.104), channel_id=1, source_target_pairs={{0,4},{1,3},{2,6},{3,1},{4,0},{5,9},{6,2},{7,11},{8,12},{9,5},{10,... | collective-permute-start | bytes 1179656 | tf_op jit(solution)/shard_map/ppermute | solution.py:233
  29.3 6.9 %collective-permute-start.11 = (f32[256,128]{1,0:T(8,128)S(1)}, f32[256,128]{1,0:T(8,128)S(1)}, u32[]{:S(2)}, u32[]{:S(2)}) collective-permute-start(f32[256,128]{1,0:T(8,128)S(1)} %slice_add_fusion.1), channel_id=1, source_target_pairs={{0,4},{1,3},{2,6},{3,1},{4,0},{5,7},{6,2},{7,5},{8,12},{9,11},{10,... | collective-permute-start | bytes 393224 | tf_op jit(solution)/shard_map/ppermute | solution.py:272
  36.2 7.3 %collective-permute-start.12 = (f32[256,128]{1,0:T(8,128)S(1)}, f32[256,128]{1,0:T(8,128)S(1)}, u32[]{:S(2)}, u32[]{:S(2)}) collective-permute-start(f32[256,128]{1,0:T(8,128)S(1)} %add.211), channel_id=1, source_target_pairs={{0,8},{1,5},{2,10},{3,7},{4,12},{5,1},{6,14},{7,3},{8,0},{9,13},{1... | collective-permute-start | bytes 393224 | tf_op jit(solution)/shard_map/ppermute | solution.py:272
  37.8 5.7 %copy-start.6 = (f32[1,2,128,128]{3,2,1,0:T(8,128)S(1)}, f32[1,2,128,128]{3,2,1,0:T(8,128)}, u32[]{:S(2)}) copy-start(f32[1,2,128,128]{3,2,1,0:T(8,128)} %param.14) | copy-start | bytes 393220
  37.8 5.8 %collective-permute-start.9 = (f32[256,128]{1,0:T(8,128)S(1)}, f32[256,128]{1,0:T(8,128)S(1)}, u32[]{:S(2)}, u32[]{:S(2)}) collective-permute-start(f32[256,128]{1,0:T(8,128)S(1)} %slice_select_fusion.3), channel_id=1, source_target_pairs={{0,2},{2,0},{1,3},{3,1},{4,6},{6,4},{5,7},{7,5},{8,10},{10,8},{9,1... | collective-permute-start | bytes 393224 | tf_op jit(solution)/shard_map/ppermute | solution.py:252
  43.5 1.4 %collective-permute-start.16 = (f32[256,128]{1,0:T(8,128)S(1)}, f32[256,128]{1,0:T(8,128)S(1)}, u32[]{:S(2)}, u32[]{:S(2)}) collective-permute-start(f32[256,128]{1,0:T(8,128)S(1)} %fusion.6.refs_4_), channel_id=1, source_target_pairs={{0,1},{1,0},{2,3},{3,2},{4,5},{5,4},{6,7},{7,6},{8,9},{9,8},{10,11... | collective-permute-start | bytes 393224 | tf_op jit(solution)/shard_map/ppermute | solution.py:209
  43.9 1.5 %collective-permute-start.13 = (f32[256,128]{1,0:T(8,128)S(1)}, f32[256,128]{1,0:T(8,128)S(1)}, u32[]{:S(2)}, u32[]{:S(2)}) collective-permute-start(f32[256,128]{1,0:T(8,128)S(1)} %get-tuple-element.10.refs_1_), channel_id=1, source_target_pairs={{0,1},{1,0},{2,3},{3,2},{4,5},{5,4},{6,7},{7,6},{8,9},{9,8},{10,11... | collective-permute-start | bytes 393224 | tf_op jit(solution)/shard_map/ppermute | solution.py:209
  44.4 1.3 %collective-permute-start.14 = (f32[256,128]{1,0:T(8,128)S(1)}, f32[256,128]{1,0:T(8,128)S(1)}, u32[]{:S(2)}, u32[]{:S(2)}) collective-permute-start(f32[256,128]{1,0:T(8,128)S(1)} %get-tuple-element.14.refs_2_), channel_id=1, source_target_pairs={{0,1},{1,0},{2,3},{3,2},{4,5},{5,4},{6,7},{7,6},{8,9},{9,8},{10,11... | collective-permute-start | bytes 393224 | tf_op jit(solution)/shard_map/ppermute | solution.py:209
  44.5 1.5 %collective-permute-start.15 = (f32[256,128]{1,0:T(8,128)S(1)}, f32[256,128]{1,0:T(8,128)S(1)}, u32[]{:S(2)}, u32[]{:S(2)}) collective-permute-start(f32[256,128]{1,0:T(8,128)S(1)} %get-tuple-element.11.refs_3_), channel_id=1, source_target_pairs={{0,1},{1,0},{2,3},{3,2},{4,5},{5,4},{6,7},{7,6},{8,9},{9,8},{10,11... | collective-permute-start | bytes 393224 | tf_op jit(solution)/shard_map/ppermute | solution.py:209
  53.0 2.0 %collective-permute-start.17 = (f32[1024,128]{1,0:T(8,128)S(1)}, f32[1024,128]{1,0:T(8,128)S(1)}, u32[]{:S(2)}, u32[]{:S(2)}) collective-permute-start(f32[1024,128]{1,0:T(8,128)S(1)} %get-tuple-element.9), channel_id=1, source_target_pairs={{0,1},{1,0},{2,3},{3,2},{4,5},{5,4},{6,7},{7,6},{8,9},{9,8},{10,11... | collective-permute-start | bytes 1572872 | tf_op jit(solution)/shard_map/ppermute | solution.py:209
  55.0 5.0 %collective-permute-start.21 = (f32[256,128]{1,0:T(8,128)S(1)}, f32[256,128]{1,0:T(8,128)S(1)}, u32[]{:S(2)}, u32[]{:S(2)}) collective-permute-start(f32[256,128]{1,0:T(8,128)S(1)} %slice.121), channel_id=1, source_target_pairs={{0,2},{1,13},{2,0},{3,15},{4,6},{5,9},{6,4},{7,11},{8,10},{9,5},{1... | collective-permute-start | bytes 393224 | tf_op jit(solution)/shard_map/ppermute | solution.py:272
  55.7 7.1 %collective-permute-start.18 = (f32[3,2,64,128]{3,2,1,0:T(8,128)S(1)}, f32[3,2,64,128]{3,2,1,0:T(8,128)S(1)}, u32[]{:S(2)}, u32[]{:S(2)}) collective-permute-start(f32[3,2,64,128]{3,2,1,0:T(8,128)S(1)} %slice_select_fusion), channel_id=1, source_target_pairs={{0,4},{1,3},{2,6},{3,1},{4,0},{5,9},{6,2},{7,11},{8,12},{9,5},{10,... | collective-permute-start | bytes 589832 | tf_op jit(solution)/shard_map/ppermute | solution.py:233
  60.1 8.1 %collective-permute-start.22 = (f32[256,128]{1,0:T(8,128)S(1)}, f32[256,128]{1,0:T(8,128)S(1)}, u32[]{:S(2)}, u32[]{:S(2)}) collective-permute-start(f32[256,128]{1,0:T(8,128)S(1)} %slice_add_fusion), channel_id=1, source_target_pairs={{0,4},{1,3},{2,6},{3,1},{4,0},{5,7},{6,2},{7,5},{8,12},{9,11},{10,... | collective-permute-start | bytes 393224 | tf_op jit(solution)/shard_map/ppermute | solution.py:272
  63.0 4.8 %collective-permute-start.19 = (f32[2,64,64]{2,1,0:T(8,128)S(1)}, f32[2,64,64]{2,1,0:T(8,128)S(1)}, u32[]{:S(2)}, u32[]{:S(2)}) collective-permute-start(f32[2,64,64]{2,1,0:T(8,128)S(1)} %fusion.19), channel_id=1, source_target_pairs={{0,2},{2,0},{1,3},{3,1},{4,6},{6,4},{5,7},{7,5},{8,10},{10,8},{9,1... | collective-permute-start | bytes 98312 | tf_op jit(solution)/shard_map/ppermute | solution.py:252
  68.1 1.4 %collective-permute-start.20 = (f32[2,64,256]{2,1,0:T(8,128)S(1)}, f32[2,64,256]{2,1,0:T(8,128)S(1)}, u32[]{:S(2)}, u32[]{:S(2)}) collective-permute-start(f32[2,64,256]{2,1,0:T(8,128)S(1)} %fusion.2), channel_id=1, source_target_pairs={{0,1},{1,0},{2,3},{3,2},{4,5},{5,4},{6,7},{7,6},{8,9},{9,8},{10,11... | collective-permute-start | bytes 393224 | tf_op jit(solution)/shard_map/ppermute | solution.py:209
  68.2 7.2 %collective-permute-start.23 = (f32[256,128]{1,0:T(8,128)S(1)}, f32[256,128]{1,0:T(8,128)S(1)}, u32[]{:S(2)}, u32[]{:S(2)}) collective-permute-start(f32[256,128]{1,0:T(8,128)S(1)} %add.219), channel_id=1, source_target_pairs={{0,8},{1,5},{2,10},{3,7},{4,12},{5,1},{6,14},{7,3},{8,0},{9,13},{1... | collective-permute-start | bytes 393224 | tf_op jit(solution)/shard_map/ppermute | solution.py:272

commit v4 on v3

--- a/solution.py
+++ b/solution.py
@@ -13,6 +13,8 @@
 momentum = 0.5
 object_rate = 0.1
 probe_rate = 0.25
+
+VMEM_LIMIT = 16 * 1024 * 1024
 
 
 def dft_tables(size):
@@ -47,48 +49,53 @@
     return matmul(high, values_high) + (matmul(low, values_high) + matmul(high, values_low))
 
 
-def gradient_kernel(scalars, *refs, columns, group):
+def window_of(scalars, index, size):
+    me, corner_row, corner_col = scalars[0][0], scalars[0][2], scalars[0][3]
+    slot = 2 * index + me
+    row = scalars[1][0, slot] - corner_row
+    col = scalars[1][1, slot] - corner_col
+    return slot, row, col // size, col % size
+
+
+def region(tile, half, size):
+    return pl.ds(pl.multiple_of(tile * 2 * size + half * size, size), size)
+
+
+def rows_of(row, tile, size):
+    return pl.ds(tile * 2 * size + row, size)
+
+
+def wave_kernel(place, positions, counts, *refs, columns, group):
+    scalars = (place, positions)
     mine, theirs = refs[: columns + 1], refs[columns + 1 : 2 * columns + 2]
     measured, ahead_high, ahead_low, behind_high, behind_low = refs[2 * columns + 2 :][:5]
-    keep, send, state, grad = refs[2 * columns + 7 :]
+    keep, send, pieces, state, modes, grad = refs[2 * columns + 7 :]
     size = measured.shape[-1]
     slots = measured.shape[0]
-    me = scalars[0]
-    live_slots = scalars[1]
-    half_mine = scalars[2]
+    me, half_mine = place[0], place[1]
+    live_slots = counts[0, 0]
     lane = lax.broadcasted_iota(jnp.int32, (size, size), 1)
-    base = columns * 2 * size
-
-    def region(tile, half):
-        return pl.ds(pl.multiple_of(tile * 2 * size + half * size, size), size)
 
     for blocks, half, mode in ((mine, half_mine, me), (theirs, 1 - half_mine, 1 - me)):
         for part in range(2):
             rows = slice(part * size, (part + 1) * size)
             for tile in range(columns):
-                state[part, region(tile, half), :] = blocks[tile][rows, :]
-            state[mode, base + part * size : base + (part + 1) * size, :] = blocks[-1][rows, :]
+                state[part, region(tile, half, size), :] = blocks[tile][rows, :]
+        modes[mode] = blocks[-1][...]
     grad[...] = jnp.zeros_like(grad)
 
     def plane(mode, part):
-        return state[mode, base + part * size : base + (part + 1) * size, :]
-
-    def rows_of(row, tile):
-        return pl.ds(tile * (2 * size) + row, size)
+        return modes[mode, part * size : (part + 1) * size, :]
 
     def one_group(first):
-        places, patches, waves = [], [], []
+        windows, patches, waves = [], [], []
         for index in range(group):
-            slot = 2 * (first + index) + me
-            row = scalars[3 + 2 * slot]
-            col = scalars[4 + 2 * slot]
-            tile = col // size
-            shift = col % size
-            places.append((slot, row, tile, shift))
+            slot, row, tile, shift = window_of(scalars, first + index, size)
+            windows.append(slot)
             patch = []
             for part in range(2):
-                near = state[part, rows_of(row, tile), :]
-                far = state[part, rows_of(row, tile + 1), :]
+                near = state[part, rows_of(row, tile, size), :]
+                far = state[part, rows_of(row, tile + 1, size), :]
                 patch.append(
                     pltpu.roll(jnp.where(lane >= shift, near, far), (size - shift) % size, 1)
                 )
@@ -117,8 +124,7 @@
             power = far_field * far_field
             power = power[:size] + power[size:]
             power = power[:, :size] + power[:, size:]
-            slot = places[index][0]
-            live = jnp.where(slot < live_slots, 1.0, 0.0).astype(jnp.float32)
+            live = jnp.where(windows[index] < live_slots, 1.0, 0.0).astype(jnp.float32)
             weight = (
                 1.0 - jnp.sqrt(measured[first + index, 0]) * lax.rsqrt(power + 1.0)
             ) * live
@@ -130,79 +136,109 @@
                 scaled.append(jnp.concatenate([back[:size, lanes], back[size:, lanes]], axis=1))
         chi = from_right(jnp.concatenate(scaled, axis=0), behind_high[...], behind_low[...])
         for index in range(group):
-            _, row, tile, shift = places[index]
-            pieces = [0.0, 0.0]
+            total = [0.0, 0.0]
             for mode in range(2):
                 start = (2 * index + mode) * size
                 chi_real = chi[start : start + size, :size]
                 chi_imag = chi[start : start + size, size:]
                 real, imag = plane(mode, 0), plane(mode, 1)
-                pieces[0] = pieces[0] + (real * chi_real + imag * chi_imag)
-                pieces[1] = pieces[1] + (real * chi_imag - imag * chi_real)
+                total[0] = total[0] + (real * chi_real + imag * chi_imag)
+                total[1] = total[1] + (real * chi_imag - imag * chi_real)
                 patch_real, patch_imag = patches[index]
-                grad[mode, base : base + size, :] += (
-                    patch_real * chi_real + patch_imag * chi_imag
-                )
-                grad[mode, base + size : base + 2 * size, :] += (
-                    patch_real * chi_imag - patch_imag * chi_real
-                )
+                grad[mode, :size, :] += patch_real * chi_real + patch_imag * chi_imag
+                grad[mode, size:, :] += patch_real * chi_imag - patch_imag * chi_real
             for part in range(2):
-                turned_back = pltpu.roll(pieces[part], shift, 1)
-                inside = lane >= shift
-                grad[part, rows_of(row, tile), :] += jnp.where(inside, turned_back, 0.0)
-                grad[part, rows_of(row, tile + 1), :] += jnp.where(inside, 0.0, turned_back)
+                pieces[first + index, part] = total[part]
 
     @pl.loop(0, slots // group)
     def _(step):
         one_group(step * group)
 
-    for target, half, mode in ((keep, half_mine, me), (send, 1 - half_mine, 1 - me)):
+    keep[...] = grad[me]
+    send[...] = grad[1 - me]
+
+
+def place_kernel(place, positions, pieces, keep, send, grad, *, columns):
+    size = pieces.shape[-1]
+    half_mine = place[1]
+    lane = lax.broadcasted_iota(jnp.int32, (size, size), 1)
+    grad[...] = jnp.zeros_like(grad)
+    for index in range(pieces.shape[0]):
+        _, row, tile, shift = window_of((place, positions), index, size)
+        inside = lane >= shift
         for part in range(2):
-            for tile in range(columns):
+            turned = pltpu.roll(pieces[index, part], shift, 1)
+            grad[part, rows_of(row, tile, size), :] += jnp.where(inside, turned, 0.0)
+            grad[part, rows_of(row, tile + 1, size), :] += jnp.where(inside, 0.0, turned)
+    for target, half in ((keep, half_mine), (send, 1 - half_mine)):
+        for tile in range(columns):
+            for part in range(2):
                 start = (2 * tile + part) * size
-                target[start : start + size, :] = grad[part, region(tile, half), :]
-            start = base + part * size
-            target[start : start + size, :] = grad[mode, start : start + size, :]
-
-
-def gradients(scalars, mine, theirs, measured):
+                target[start : start + size, :] = grad[part, region(tile, half, size), :]
+
+
+def whole_block(shape):
+    return pl.BlockSpec(shape, lambda i, *_: (0,) * len(shape))
+
+
+def waves(scalars, mine, theirs, measured):
     size = measured.shape[-1]
     slots = measured.shape[0] // 2
     columns = len(mine) - 1
-    height = (columns + 1) * 2 * size
-    shape = jax.ShapeDtypeStruct((height, size), jnp.float32)
-    whole = pl.BlockSpec((height, size), lambda i, s: (0, 0))
-    block = pl.BlockSpec((2 * size, size), lambda i, s: (0, 0))
-    table = pl.BlockSpec((2 * size, 2 * size), lambda i, s: (0, 0))
     group = 4 if slots % 4 == 0 else 1
+    pair = (2 * size, size)
+    pieces = (slots, 2, size, size)
 
     def body(*refs):
-        gradient_kernel(*refs, columns=columns, group=group)
+        wave_kernel(*refs, columns=columns, group=group)
 
     return pl.pallas_call(
         body,
-        out_shape=(shape, shape),
+        out_shape=[jax.ShapeDtypeStruct(s, jnp.float32) for s in (pair, pair, pieces)],
         grid_spec=pltpu.PrefetchScalarGridSpec(
-            num_scalar_prefetch=1,
+            num_scalar_prefetch=3,
             grid=(1,),
-            in_specs=[block] * (2 * columns + 2)
-            + [pl.BlockSpec((slots, 1, size, size), lambda i, s: (0, s[0], 0, 0))]
-            + [table] * 4,
-            out_specs=[whole, whole],
+            in_specs=[whole_block(pair)] * (2 * columns + 2)
+            + [pl.BlockSpec((slots, 1, size, size), lambda i, s, *_: (0, s[0], 0, 0))]
+            + [whole_block((2 * size, 2 * size))] * 4,
+            out_specs=[whole_block(s) for s in (pair, pair, pieces)],
             scratch_shapes=[
-                pltpu.VMEM((2, height, size), jnp.float32),
-                pltpu.VMEM((2, height, size), jnp.float32),
+                pltpu.VMEM((2, columns * 2 * size, size), jnp.float32),
+                pltpu.VMEM((2,) + pair, jnp.float32),
+                pltpu.VMEM((2,) + pair, jnp.float32),
             ],
         ),
-        compiler_params=pltpu.CompilerParams(vmem_limit_bytes=24 * 1024 * 1024),
-        name="gradients",
+        compiler_params=pltpu.CompilerParams(vmem_limit_bytes=VMEM_LIMIT),
+        name="waves",
     )(
-        scalars,
+        *scalars,
         *mine,
         *theirs,
         measured.reshape(slots, 2, size, size),
         *[jnp.asarray(t) for t in dft_tables(size)],
     )
+
+
+def placed(scalars, pieces, columns):
+    size = pieces.shape[-1]
+    shape = (columns * 2 * size, size)
+
+    def body(*refs):
+        place_kernel(*refs, columns=columns)
+
+    return pl.pallas_call(
+        body,
+        out_shape=[jax.ShapeDtypeStruct(shape, jnp.float32)] * 2,
+        grid_spec=pltpu.PrefetchScalarGridSpec(
+            num_scalar_prefetch=2,
+            grid=(1,),
+            in_specs=[whole_block(pieces.shape)],
+            out_specs=[whole_block(shape)] * 2,
+            scratch_shapes=[pltpu.VMEM((2,) + shape, jnp.float32)],
+        ),
+        compiler_params=pltpu.CompilerParams(vmem_limit_bytes=VMEM_LIMIT),
+        name="placed",
+    )(*scalars[:2], pieces)
 
 
 def swap_modes(block):
@@ -286,9 +322,10 @@
     lower = row % 2 == me
     paired = jnp.where(lower, row < rows_count - 1, row > 0)
     half_mine = lower.astype(jnp.int32)
-    corner = jnp.stack([row * tile_rows - half, col * tile_cols - half])
-    offsets = positions[0, 0] - corner[None, :]
-    scalars = jnp.concatenate([jnp.stack([me, counts[0, 0], half_mine]), offsets.reshape(-1)])
+    place = jnp.stack(
+        [me, half_mine, row * tile_rows - half, col * tile_cols - half]
+    ).astype(jnp.int32)
+    scalars = (place, positions[0, 0].T, counts)
     probe_step = probe_rate / (slot_count * rows_count * cols_count)
 
     strip = jnp.where(lower, obj[:, half:], obj[:, :half])
@@ -319,11 +356,13 @@
     previous, current = start, start
     for iteration in range(ITERS):
         ahead = [x + momentum * (x - y) for x, y in zip(current, previous, strict=True)]
-        keep, send = gradients(scalars, ahead, [swap_modes(x) for x in ahead], measured[0, 0])
-        total = keep + swap_modes(send)
+        keep, send, pieces = waves(scalars, ahead, [swap_modes(x) for x in ahead], measured[0, 0])
+        probe_grad = keep + swap_modes(send)
+        keep, send = placed(scalars, pieces, columns)
+        probe_grad, keep, send = lax.optimization_barrier((probe_grad, keep, send))
         previous = current
-        probe_grad = sum_tiles(total[columns * 2 * size :])
-        object_grad = total[: columns * 2 * size]
+        probe_grad = sum_tiles(probe_grad)
+        object_grad = keep + swap_modes(send)
         new_probe = ahead[-1] - probe_step * probe_grad
         if iteration < ITERS - 1:
             object_grad = object_grad + jnp.where(paired, swap_neighbours(object_grad), 0.0)

time: 76.3 us -> 71.8 us (0.941)
  waiting for transfers between devices: 38.3 us -> 30.8 us
  starting transfers between devices: 16.3 us -> 19.6 us
    ppermute x6, waiting for transfers between devices: 23 us -> 20.2 us  [sum_tiles(): block = block + lax.ppermute(block, ('row', 'col', 'mode'), route)]
    ppermute x11 -> x13, waiting for transfers between devices: 4.93 us -> 2.15 us  [swap_modes(): return lax.ppermute(block, 'mode', [(0, 1), (1, 0)])]
    ppermute x6, starting transfers between devices: 5.31 us -> 6.52 us  [sum_tiles(): block = block + lax.ppermute(block, ('row', 'col', 'mode'), route)]
    ppermute x4, waiting for transfers between devices: 4.54 us -> 3.4 us  [swap_neighbours(): return lax.ppermute(block, ('row', 'col', 'mode'), route)]
    ppermute x3, starting transfers between devices: 2.57 us -> 3.63 us  [swap_cols(): lax.ppermute(block, 'col', [(i, i if o is None else o) for i, o in enumer...]
    ppermute x3, waiting for transfers between devices: 5.88 us -> 5.06 us  [swap_cols(): lax.ppermute(block, 'col', [(i, i if o is None else o) for i, o in enumer...]
    ppermute x11 -> x13, starting transfers between devices: 2.81 us -> 3.23 us  [swap_modes(): return lax.ppermute(block, 'mode', [(0, 1), (1, 0)])]
    pallas_call x2 -> x4, Pallas kernels: 14.8 us -> 15 us  [the longest x2 13.1 us: waves(): pl.pallas_call(body, out_shape=[jax.ShapeDtypeStruct(s, jnp.float32) for...]
  transfers between devices with their start and end apart: 24 -> 26, of which waited for: 16 -> 19; matrix products, arithmetic and copies ran while one was open for 3% -> 3% of each run, Pallas kernels for 0% -> 3%
where the time goes in v4:
time: 71.8 us; the launch traced here: 71.6 us
  waiting for transfers between devices  30.8 us (43%)
  starting transfers between devices  19.6 us (27%)
  Pallas kernels  15 us (21%)
  other arithmetic  3.88 us (5%)
  between operations  1.63 us (2%)
    ppermute x6, waiting for transfers between devices, sum_tiles(): block = block + lax.ppermute(block, ('row', 'col', 'mode'), route)  20.2 us
    pallas_call x2, Pallas kernels, waves(): pl.pallas_call(body, out_shape=[jax.ShapeDtypeStruct(s, jnp.float32) for...  13.1 us
    ppermute x6, starting transfers between devices, sum_tiles(): block = block + lax.ppermute(block, ('row', 'col', 'mode'), route)  6.52 us
    ppermute x4, starting transfers between devices, swap_neighbours(): return lax.ppermute(block, ('row', 'col', 'mode'), route)  6.2 us
    ppermute x3, waiting for transfers between devices, swap_cols(): lax.ppermute(block, 'col', [(i, i if o is None else o) for i, o in enumer...  5.06 us
    ppermute x3, starting transfers between devices, swap_cols(): lax.ppermute(block, 'col', [(i, i if o is None else o) for i, o in enumer...  3.63 us
    ppermute x4, waiting for transfers between devices, swap_neighbours(): return lax.ppermute(block, ('row', 'col', 'mode'), route)  3.4 us
    ppermute x13, starting transfers between devices, swap_modes(): return lax.ppermute(block, 'mode', [(0, 1), (1, 0)])  3.23 us
  transfers between devices with their start and end apart: 26, of which 19 were waited for; matrix products, arithmetic and copies ran while one was open for 3% of the time, Pallas kernels for 3%

profile of v4, /device:TPU:0, one launch (start us, length us, event | category | flops | bytes accessed | tf_op | source)
XLA Modules:
  0.0 71.6 jit_solution(4206207768875549305)
XLA Ops:
  0.7 1.0 %slice_select_fusion.2 = f32[2,64,256]{2,1,0:T(8,128)S(1)} fusion(f32[2,128,256]{2,1,0:T(8,128)} %param.13, pred[]{:T(512)S(6)} %eq.15), kind=kLoop, calls=%fused_computation.44 | loop fusion | flops 32768 | bytes 393217 | tf_op jit(solution)/shard_map/jit(_where)/select_n | solution.py:331
  1.7 0.1 slice_select_fusion.5
  1.8 4.0 %collective-permute-start.1 = (f32[2,64,64]{2,1,0:T(8,128)S(1)}, f32[2,64,64]{2,1,0:T(8,128)S(1)}, u32[]{:S(2)}, u32[]{:S(2)}) collective-permute-start(f32[2,64,64]{2,1,0:T(8,128)S(1)} %slice_select_fusion.5), channel_id=1, source_target_pairs={{0,6},{1,3},{2,4},{3,1},{4,2},{5,11},{6,0},{7,9},{8,14},{9,7},{10,... | collective-permute-start | bytes 98312 | tf_op jit(solution)/shard_map/ppermute | solution.py:269
  5.8 0.5 collective-permute-start
  6.3 0.1 collective-permute-start.2
  6.4 0.1 collective-permute-start.6
  6.5 1.6 %collective-permute-done.1 = f32[2,64,64]{2,1,0:T(8,128)S(1)} collective-permute-done((f32[2,64,64]{2,1,0:T(8,128)S(1)}, f32[2,64,64]{2,1,0:T(8,128)S(1)}, u32[]{:S(2)}, u32[]{:S(2)}) %collective-permute-start.1) | collective-permute-done | bytes 32800 | tf_op jit(solution)/shard_map/ppermute | solution.py:269
  8.1 2.3 %collective-permute-done = f32[2,64,64]{2,1,0:T(8,128)S(1)} collective-permute-done((f32[2,64,64]{2,1,0:T(8,128)S(1)}, f32[2,64,64]{2,1,0:T(8,128)S(1)}, u32[]{:S(2)}, u32[]{:S(2)}) %collective-permute-start) | collective-permute-done | bytes 32800 | tf_op jit(solution)/shard_map/ppermute | solution.py:288
  10.4 0.8 %collective-permute-done.2 = f32[2,64,256]{2,1,0:T(8,128)S(1)} collective-permute-done((f32[2,64,256]{2,1,0:T(8,128)S(1)}, f32[2,64,256]{2,1,0:T(8,128)S(1)}, u32[]{:S(2)}, u32[]{:S(2)}) %collective-permute-start.2) | collective-permute-done | bytes 131104 | tf_op jit(solution)/shard_map/ppermute | solution.py:269
  11.3 0.2 fusion.17
  11.5 0.1 collective-permute-start.3
  11.6 0.0 copy-start.3
  11.7 0.5 collective-permute-start.4
  12.2 0.1 collective-permute-start.5
  13.0 0.1 pad_add_fusion.refs_0_
  13.1 0.1 collective-permute-done.4.refs_8_
  13.2 0.5 collective-permute-done.5.refs_9_
  13.7 0.6 copy-done.5
  14.3 6.5 %waves.2 = (f32[256,128]{1,0:T(8,128)S(1)}, f32[256,128]{1,0:T(8,128)S(1)}, f32[8,2,128,128]{3,2,1,0:T(8,128)S(1)}) custom-call(s32[4]{0:T(128)S(1)} %pad_add_fusion.refs_0_, s32[2,16]{1,0:T(2,128)S(1)} %bitcast.86, s32[1,1]{1,0:T(1,128)S(6)} %copy.15.refs_2_, f32[256,128]{1,0:T(8,128)S(1)} %bitcast_add_fusion.3.refs_3_, ...), custom_call_target="tpu_custom_call" | custom-call | tf_op jit(solution)/shard_map/waves/pallas_call | solution.py:195
  20.9 0.2 collective-permute-start.7
  21.1 1.0 %placed.2 = (f32[768,128]{1,0:T(8,128)S(1)}, f32[768,128]{1,0:T(8,128)S(1)}) custom-call(s32[4]{0:T(128)S(1)} %pad_add_fusion.refs_0_, s32[2,16]{1,0:T(2,128)S(1)} %bitcast.87, f32[8,2,128,128]{3,2,1,0:T(8,128)S(1)} %get-tuple-element.20.refs_2_), custom_call_target="tpu_custom_call" | custom-call | tf_op jit(solution)/shard_map/placed/pallas_call | solution.py:229
  22.1 0.2 collective-permute-done.7
  22.3 0.2 collective-permute-start.8
  22.5 1.5 %collective-permute-start.11 = (f32[256,128]{1,0:T(8,128)S(1)}, f32[256,128]{1,0:T(8,128)S(1)}, u32[]{:S(2)}, u32[]{:S(2)}) collective-permute-start(f32[256,128]{1,0:T(8,128)S(1)} %add.207), channel_id=1, source_target_pairs={{0,2},{1,13},{2,0},{3,15},{4,6},{5,9},{6,4},{7,11},{8,10},{9,5},{1... | collective-permute-start | bytes 393224 | tf_op jit(solution)/shard_map/ppermute | solution.py:308
  24.0 0.1 collective-permute-done.8
  24.1 0.1 add.208
  24.1 0.5 collective-permute-start.9
  24.6 2.9 %collective-permute-done.11 = f32[256,128]{1,0:T(8,128)S(1)} collective-permute-done((f32[256,128]{1,0:T(8,128)S(1)}, f32[256,128]{1,0:T(8,128)S(1)}, u32[]{:S(2)}, u32[]{:S(2)}) %collective-permute-start.11) | collective-permute-done | bytes 131104 | tf_op jit(solution)/shard_map/ppermute | solution.py:308
  27.5 0.2 collective-permute-start.12
  27.8 6.6 %collective-permute-done.12 = f32[256,128]{1,0:T(8,128)S(1)} collective-permute-done((f32[256,128]{1,0:T(8,128)S(1)}, f32[256,128]{1,0:T(8,128)S(1)}, u32[]{:S(2)}, u32[]{:S(2)}) %collective-permute-start.12) | collective-permute-done | bytes 131104 | tf_op jit(solution)/shard_map/ppermute | solution.py:308
  34.4 1.7 %collective-permute-start.13 = (f32[256,128]{1,0:T(8,128)S(1)}, f32[256,128]{1,0:T(8,128)S(1)}, u32[]{:S(2)}, u32[]{:S(2)}) collective-permute-start(f32[256,128]{1,0:T(8,128)S(1)} %add.218), channel_id=1, source_target_pairs={{0,8},{1,5},{2,10},{3,7},{4,12},{5,1},{6,14},{7,3},{8,0},{9,13},{1... | collective-permute-start | bytes 393224 | tf_op jit(solution)/shard_map/ppermute | solution.py:308
  36.1 1.5 %collective-permute-start.10 = (f32[256,128]{1,0:T(8,128)S(1)}, f32[256,128]{1,0:T(8,128)S(1)}, u32[]{:S(2)}, u32[]{:S(2)}) collective-permute-start(f32[256,128]{1,0:T(8,128)S(1)} %slice_select_fusion.3), channel_id=1, source_target_pairs={{0,2},{2,0},{1,3},{3,1},{4,6},{6,4},{5,7},{7,5},{8,10},{10,8},{9,1... | collective-permute-start | bytes 393224 | tf_op jit(solution)/shard_map/ppermute | solution.py:288
  37.7 4.1 %collective-permute-done.13 = f32[256,128]{1,0:T(8,128)S(1)} collective-permute-done((f32[256,128]{1,0:T(8,128)S(1)}, f32[256,128]{1,0:T(8,128)S(1)}, u32[]{:S(2)}, u32[]{:S(2)}) %collective-permute-start.13) | collective-permute-done | bytes 131104 | tf_op jit(solution)/shard_map/ppermute | solution.py:308
  41.8 0.1 collective-permute-start.17
  41.9 0.2 fusion.15
  42.1 0.6 collective-permute-start.14
  42.7 0.1 collective-permute-start.15
  42.7 0.4 collective-permute-start.16
  43.2 0.0 collective-permute-done.17.refs_10_
  43.2 0.4 collective-permute-done.14.refs_7_
  43.7 0.4 collective-permute-done.15.refs_8_
  44.0 0.2 collective-permute-done.16.refs_9_
  44.2 6.5 %waves.3 = (f32[256,128]{1,0:T(8,128)S(1)}, f32[256,128]{1,0:T(8,128)S(1)}, f32[8,2,128,128]{3,2,1,0:T(8,128)S(1)}) custom-call(s32[4]{0:T(128)S(1)} %pad_add_fusion.refs_0_, s32[2,16]{1,0:T(2,128)S(1)} %bitcast.88, s32[1,1]{1,0:T(1,128)S(6)} %copy.15.refs_2_, f32[256,128]{1,0:T(8,128)S(1)} %get-tuple-element.34.refs_3_, ...), custom_call_target="tpu_custom_call" | custom-call | tf_op jit(solution)/shard_map/waves/pallas_call | solution.py:195
  50.7 0.4 collective-permute-start.18
  51.1 1.0 %placed.3 = (f32[768,128]{1,0:T(8,128)S(1)}, f32[768,128]{1,0:T(8,128)S(1)}) custom-call(s32[4]{0:T(128)S(1)} %pad_add_fusion.refs_0_, s32[2,16]{1,0:T(2,128)S(1)} %bitcast.89, f32[8,2,128,128]{3,2,1,0:T(8,128)S(1)} %get-tuple-element.28.refs_2_), custom_call_target="tpu_custom_call" | custom-call | tf_op jit(solution)/shard_map/placed/pallas_call | solution.py:229
  52.1 0.0 collective-permute-done.18
  52.2 0.4 collective-permute-start.19
  52.6 1.5 %collective-permute-start.23 = (f32[256,128]{1,0:T(8,128)S(1)}, f32[256,128]{1,0:T(8,128)S(1)}, u32[]{:S(2)}, u32[]{:S(2)}) collective-permute-start(f32[256,128]{1,0:T(8,128)S(1)} %add.221), channel_id=1, source_target_pairs={{0,2},{1,13},{2,0},{3,15},{4,6},{5,9},{6,4},{7,11},{8,10},{9,5},{1... | collective-permute-start | bytes 393224 | tf_op jit(solution)/shard_map/ppermute | solution.py:308
  54.1 3.5 %collective-permute-done.23 = f32[256,128]{1,0:T(8,128)S(1)} collective-permute-done((f32[256,128]{1,0:T(8,128)S(1)}, f32[256,128]{1,0:T(8,128)S(1)}, u32[]{:S(2)}, u32[]{:S(2)}) %collective-permute-start.23) | collective-permute-done | bytes 131104 | tf_op jit(solution)/shard_map/ppermute | solution.py:308
  57.5 0.5 collective-permute-start.24
  58.2 1.6 %collective-permute-start.20 = (f32[3,2,64,128]{3,2,1,0:T(8,128)S(1)}, f32[3,2,64,128]{3,2,1,0:T(8,128)S(1)}, u32[]{:S(2)}, u32[]{:S(2)}) collective-permute-start(f32[3,2,64,128]{3,2,1,0:T(8,128)S(1)} %slice_select_fusion), channel_id=1, source_target_pairs={{0,4},{1,3},{2,6},{3,1},{4,0},{5,9},{6,2},{7,11},{8,12},{9,5},{10,... | collective-permute-start | bytes 589832 | tf_op jit(solution)/shard_map/ppermute | solution.py:269
  59.8 2.8 %collective-permute-done.24 = f32[256,128]{1,0:T(8,128)S(1)} collective-permute-done((f32[256,128]{1,0:T(8,128)S(1)}, f32[256,128]{1,0:T(8,128)S(1)}, u32[]{:S(2)}, u32[]{:S(2)}) %collective-permute-start.24) | collective-permute-done | bytes 131104 | tf_op jit(solution)/shard_map/ppermute | solution.py:308
  62.6 1.1 %collective-permute-start.25 = (f32[256,128]{1,0:T(8,128)S(1)}, f32[256,128]{1,0:T(8,128)S(1)}, u32[]{:S(2)}, u32[]{:S(2)}) collective-permute-start(f32[256,128]{1,0:T(8,128)S(1)} %add.227), channel_id=1, source_target_pairs={{0,8},{1,5},{2,10},{3,7},{4,12},{5,1},{6,14},{7,3},{8,0},{9,13},{1... | collective-permute-start | bytes 393224 | tf_op jit(solution)/shard_map/ppermute | solution.py:308
  63.7 1.0 %collective-permute-done.20 = f32[3,2,64,128]{3,2,1,0:T(8,128)S(1)} collective-permute-done((f32[3,2,64,128]{3,2,1,0:T(8,128)S(1)}, f32[3,2,64,128]{3,2,1,0:T(8,128)S(1)}, u32[]{:S(2)}, u32[]{:S(2)}) %collective-permute-start.20) | collective-permute-done | bytes 196640 | tf_op jit(solution)/shard_map/ppermute | solution.py:269
  64.7 0.1 fusion.19
  64.8 1.5 %collective-permute-start.21 = (f32[2,64,64]{2,1,0:T(8,128)S(1)}, f32[2,64,64]{2,1,0:T(8,128)S(1)}, u32[]{:S(2)}, u32[]{:S(2)}) collective-permute-start(f32[2,64,64]{2,1,0:T(8,128)S(1)} %fusion.19), channel_id=1, source_target_pairs={{0,2},{2,0},{1,3},{3,1},{4,6},{6,4},{5,7},{7,5},{8,10},{10,8},{9,1... | collective-permute-start | bytes 98312 | tf_op jit(solution)/shard_map/ppermute | solution.py:288
  66.4 2.8 %collective-permute-done.21 = f32[2,64,64]{2,1,0:T(8,128)S(1)} collective-permute-done((f32[2,64,64]{2,1,0:T(8,128)S(1)}, f32[2,64,64]{2,1,0:T(8,128)S(1)}, u32[]{:S(2)}, u32[]{:S(2)}) %collective-permute-start.21) | collective-permute-done | bytes 32800 | tf_op jit(solution)/shard_map/ppermute | solution.py:288
  69.1 0.1 fusion.20
  69.2 0.2 fusion.2
  69.4 0.1 collective-permute-start.22
  69.5 0.4 collective-permute-done.25
  69.9 0.7 multiply_subtract_fusion
  70.6 0.3 collective-permute-done.22
  70.9 0.7 %pad_maximum_fusion.1 = f32[2,128,256]{2,1,0:T(8,128)} fusion(f32[2,64,256]{2,1,0:T(8,128)S(1)} %get-tuple-element.45, f32[2,64,256]{2,1,0:T(8,128)S(1)} %get-tuple-element.44), kind=kLoop, calls=%fused_computation.6 | loop fusion | flops 65536 | bytes 524288 | tf_op jit(solution)/shard_map/concatenate | solution.py:396
  (45 shorter events, 0.6 us)
Async XLA Ops:
  1.7 4.8 %copy-start.6 = (f32[1,2,128,128]{3,2,1,0:T(8,128)S(1)}, f32[1,2,128,128]{3,2,1,0:T(8,128)}, u32[]{:S(2)}) copy-start(f32[1,2,128,128]{3,2,1,0:T(8,128)} %param.14) | copy-start | bytes 393220
  1.8 6.4 %collective-permute-start.1 = (f32[2,64,64]{2,1,0:T(8,128)S(1)}, f32[2,64,64]{2,1,0:T(8,128)S(1)}, u32[]{:S(2)}, u32[]{:S(2)}) collective-permute-start(f32[2,64,64]{2,1,0:T(8,128)S(1)} %slice_select_fusion.5), channel_id=1, source_target_pairs={{0,6},{1,3},{2,4},{3,1},{4,2},{5,11},{6,0},{7,9},{8,14},{9,7},{10,... | collective-permute-start | bytes 98312 | tf_op jit(solution)/shard_map/ppermute | solution.py:269
  5.8 4.6 %collective-permute-start = (f32[2,64,64]{2,1,0:T(8,128)S(1)}, f32[2,64,64]{2,1,0:T(8,128)S(1)}, u32[]{:S(2)}, u32[]{:S(2)}) collective-permute-start(f32[2,64,64]{2,1,0:T(8,128)S(1)} %slice_select_fusion.5), channel_id=1, source_target_pairs={{0,2},{2,0},{1,3},{3,1},{4,6},{6,4},{5,7},{7,5},{8,10},{10,8},{9,1... | collective-permute-start | bytes 98312 | tf_op jit(solution)/shard_map/ppermute | solution.py:288
  6.3 5.0 %collective-permute-start.2 = (f32[2,64,256]{2,1,0:T(8,128)S(1)}, f32[2,64,256]{2,1,0:T(8,128)S(1)}, u32[]{:S(2)}, u32[]{:S(2)}) collective-permute-start(f32[2,64,256]{2,1,0:T(8,128)S(1)} %slice_select_fusion.2), channel_id=1, source_target_pairs={{0,4},{1,3},{2,6},{3,1},{4,0},{5,9},{6,2},{7,11},{8,12},{9,5},{10,... | collective-permute-start | bytes 393224 | tf_op jit(solution)/shard_map/ppermute | solution.py:269
  6.4 6.6 %collective-permute-start.6 = (f32[256,128]{1,0:T(8,128)S(1)}, f32[256,128]{1,0:T(8,128)S(1)}, u32[]{:S(2)}, u32[]{:S(2)}) collective-permute-start(f32[256,128]{1,0:T(8,128)S(1)} %bitcast_add_fusion.refs_6_), channel_id=1, source_target_pairs={{0,1},{1,0},{2,3},{3,2},{4,5},{5,4},{6,7},{7,6},{8,9},{9,8},{10,11... | collective-permute-start | bytes 393224 | tf_op jit(solution)/shard_map/ppermute | solution.py:245
  11.3 2.4 %copy-start = (f32[1,1,16,128,128]{4,3,2,1,0:T(8,128)S(1)}, f32[1,1,16,128,128]{4,3,2,1,0:T(8,128)}, u32[]{:S(2)}) copy-start(f32[1,1,16,128,128]{4,3,2,1,0:T(8,128)} %param.17) | copy-start | bytes 3145732
  11.5 1.5 %collective-permute-start.3 = (f32[256,128]{1,0:T(8,128)S(1)}, f32[256,128]{1,0:T(8,128)S(1)}, u32[]{:S(2)}, u32[]{:S(2)}) collective-permute-start(f32[256,128]{1,0:T(8,128)S(1)} %bitcast_add_fusion.3.refs_3_), channel_id=1, source_target_pairs={{0,1},{1,0},{2,3},{3,2},{4,5},{5,4},{6,7},{7,6},{8,9},{9,8},{10,11... | collective-permute-start | bytes 393224 | tf_op jit(solution)/shard_map/ppermute | solution.py:245
  11.6 2.0 %copy-start.3 = (bf16[256,256]{1,0:T(8,128)(2,1)S(1)}, bf16[256,256]{1,0:T(8,128)(2,1)}, u32[]{:S(2)}) copy-start(bf16[256,256]{1,0:T(8,128)(2,1)} %constant.85.clone.refs_14_) | copy-start | bytes 393220
  11.6 2.0 %copy-start.4 = (bf16[256,256]{1,0:T(8,128)(2,1)S(1)}, bf16[256,256]{1,0:T(8,128)(2,1)}, u32[]{:S(2)}) copy-start(bf16[256,256]{1,0:T(8,128)(2,1)} %constant.86.clone.refs_15_) | copy-start | bytes 393220
  11.7 1.5 %collective-permute-start.4 = (f32[256,128]{1,0:T(8,128)S(1)}, f32[256,128]{1,0:T(8,128)S(1)}, u32[]{:S(2)}, u32[]{:S(2)}) collective-permute-start(f32[256,128]{1,0:T(8,128)S(1)} %bitcast_add_fusion.2.refs_4_), channel_id=1, source_target_pairs={{0,1},{1,0},{2,3},{3,2},{4,5},{5,4},{6,7},{7,6},{8,9},{9,8},{10,11... | collective-permute-start | bytes 393224 | tf_op jit(solution)/shard_map/ppermute | solution.py:245
  12.2 1.5 %copy-start.1 = (bf16[256,256]{1,0:T(8,128)(2,1)S(1)}, bf16[256,256]{1,0:T(8,128)(2,1)}, u32[]{:S(2)}) copy-start(bf16[256,256]{1,0:T(8,128)(2,1)} %constant.83.clone.refs_12_) | copy-start | bytes 393220
  12.2 1.5 %copy-start.2 = (bf16[256,256]{1,0:T(8,128)(2,1)S(1)}, bf16[256,256]{1,0:T(8,128)(2,1)}, u32[]{:S(2)}) copy-start(bf16[256,256]{1,0:T(8,128)(2,1)} %constant.84.clone.refs_13_) | copy-start | bytes 393220
  12.2 1.4 %collective-permute-start.5 = (f32[256,128]{1,0:T(8,128)S(1)}, f32[256,128]{1,0:T(8,128)S(1)}, u32[]{:S(2)}, u32[]{:S(2)}) collective-permute-start(f32[256,128]{1,0:T(8,128)S(1)} %bitcast_add_fusion.1.refs_5_), channel_id=1, source_target_pairs={{0,1},{1,0},{2,3},{3,2},{4,5},{5,4},{6,7},{7,6},{8,9},{9,8},{10,11... | collective-permute-start | bytes 393224 | tf_op jit(solution)/shard_map/ppermute | solution.py:245
  13.6 0.7 copy-start.5
  20.9 1.4 %collective-permute-start.7 = (f32[256,128]{1,0:T(8,128)S(1)}, f32[256,128]{1,0:T(8,128)S(1)}, u32[]{:S(2)}, u32[]{:S(2)}) collective-permute-start(f32[256,128]{1,0:T(8,128)S(1)} %get-tuple-element.19), channel_id=1, source_target_pairs={{0,1},{1,0},{2,3},{3,2},{4,5},{5,4},{6,7},{7,6},{8,9},{9,8},{10,11... | collective-permute-start | bytes 393224 | tf_op jit(solution)/shard_map/ppermute | solution.py:245
  22.3 1.8 %collective-permute-start.8 = (f32[768,128]{1,0:T(8,128)S(1)}, f32[768,128]{1,0:T(8,128)S(1)}, u32[]{:S(2)}, u32[]{:S(2)}) collective-permute-start(f32[768,128]{1,0:T(8,128)S(1)} %get-tuple-element.24), channel_id=1, source_target_pairs={{0,1},{1,0},{2,3},{3,2},{4,5},{5,4},{6,7},{7,6},{8,9},{9,8},{10,11... | collective-permute-start | bytes 1179656 | tf_op jit(solution)/shard_map/ppermute | solution.py:245
  22.5 5.0 %collective-permute-start.11 = (f32[256,128]{1,0:T(8,128)S(1)}, f32[256,128]{1,0:T(8,128)S(1)}, u32[]{:S(2)}, u32[]{:S(2)}) collective-permute-start(f32[256,128]{1,0:T(8,128)S(1)} %add.207), channel_id=1, source_target_pairs={{0,2},{1,13},{2,0},{3,15},{4,6},{5,9},{6,4},{7,11},{8,10},{9,5},{1... | collective-permute-start | bytes 393224 | tf_op jit(solution)/shard_map/ppermute | solution.py:308
  24.1 11.9 %collective-permute-start.9 = (f32[768,128]{1,0:T(8,128)S(1)}, f32[768,128]{1,0:T(8,128)S(1)}, u32[]{:S(2)}, u32[]{:S(2)}) collective-permute-start(f32[768,128]{1,0:T(8,128)S(1)} %add.208), channel_id=1, source_target_pairs={{0,4},{1,3},{2,6},{3,1},{4,0},{5,9},{6,2},{7,11},{8,12},{9,5},{10,... | collective-permute-start | bytes 1179656 | tf_op jit(solution)/shard_map/ppermute | solution.py:269
  27.5 6.9 %collective-permute-start.12 = (f32[256,128]{1,0:T(8,128)S(1)}, f32[256,128]{1,0:T(8,128)S(1)}, u32[]{:S(2)}, u32[]{:S(2)}) collective-permute-start(f32[256,128]{1,0:T(8,128)S(1)} %add.217), channel_id=1, source_target_pairs={{0,4},{1,3},{2,6},{3,1},{4,0},{5,7},{6,2},{7,5},{8,12},{9,11},{10,... | collective-permute-start | bytes 393224 | tf_op jit(solution)/shard_map/ppermute | solution.py:308
  34.4 7.3 %collective-permute-start.13 = (f32[256,128]{1,0:T(8,128)S(1)}, f32[256,128]{1,0:T(8,128)S(1)}, u32[]{:S(2)}, u32[]{:S(2)}) collective-permute-start(f32[256,128]{1,0:T(8,128)S(1)} %add.218), channel_id=1, source_target_pairs={{0,8},{1,5},{2,10},{3,7},{4,12},{5,1},{6,14},{7,3},{8,0},{9,13},{1... | collective-permute-start | bytes 393224 | tf_op jit(solution)/shard_map/ppermute | solution.py:308
  36.1 5.7 %collective-permute-start.10 = (f32[256,128]{1,0:T(8,128)S(1)}, f32[256,128]{1,0:T(8,128)S(1)}, u32[]{:S(2)}, u32[]{:S(2)}) collective-permute-start(f32[256,128]{1,0:T(8,128)S(1)} %slice_select_fusion.3), channel_id=1, source_target_pairs={{0,2},{2,0},{1,3},{3,1},{4,6},{6,4},{5,7},{7,5},{8,10},{10,8},{9,1... | collective-permute-start | bytes 393224 | tf_op jit(solution)/shard_map/ppermute | solution.py:288
  41.8 1.4 %collective-permute-start.17 = (f32[256,128]{1,0:T(8,128)S(1)}, f32[256,128]{1,0:T(8,128)S(1)}, u32[]{:S(2)}, u32[]{:S(2)}) collective-permute-start(f32[256,128]{1,0:T(8,128)S(1)} %fusion.6.refs_6_), channel_id=1, source_target_pairs={{0,1},{1,0},{2,3},{3,2},{4,5},{5,4},{6,7},{7,6},{8,9},{9,8},{10,11... | collective-permute-start | bytes 393224 | tf_op jit(solution)/shard_map/ppermute | solution.py:245
  42.1 1.5 %collective-permute-start.14 = (f32[256,128]{1,0:T(8,128)S(1)}, f32[256,128]{1,0:T(8,128)S(1)}, u32[]{:S(2)}, u32[]{:S(2)}) collective-permute-start(f32[256,128]{1,0:T(8,128)S(1)} %get-tuple-element.34.refs_3_), channel_id=1, source_target_pairs={{0,1},{1,0},{2,3},{3,2},{4,5},{5,4},{6,7},{7,6},{8,9},{9,8},{10,11... | collective-permute-start | bytes 393224 | tf_op jit(solution)/shard_map/ppermute | solution.py:245
  42.7 1.3 %collective-permute-start.15 = (f32[256,128]{1,0:T(8,128)S(1)}, f32[256,128]{1,0:T(8,128)S(1)}, u32[]{:S(2)}, u32[]{:S(2)}) collective-permute-start(f32[256,128]{1,0:T(8,128)S(1)} %get-tuple-element.38.refs_4_), channel_id=1, source_target_pairs={{0,1},{1,0},{2,3},{3,2},{4,5},{5,4},{6,7},{7,6},{8,9},{9,8},{10,11... | collective-permute-start | bytes 393224 | tf_op jit(solution)/shard_map/ppermute | solution.py:245
  42.7 1.5 %collective-permute-start.16 = (f32[256,128]{1,0:T(8,128)S(1)}, f32[256,128]{1,0:T(8,128)S(1)}, u32[]{:S(2)}, u32[]{:S(2)}) collective-permute-start(f32[256,128]{1,0:T(8,128)S(1)} %get-tuple-element.35.refs_5_), channel_id=1, source_target_pairs={{0,1},{1,0},{2,3},{3,2},{4,5},{5,4},{6,7},{7,6},{8,9},{9,8},{10,11... | collective-permute-start | bytes 393224 | tf_op jit(solution)/shard_map/ppermute | solution.py:245
  50.7 1.4 %collective-permute-start.18 = (f32[256,128]{1,0:T(8,128)S(1)}, f32[256,128]{1,0:T(8,128)S(1)}, u32[]{:S(2)}, u32[]{:S(2)}) collective-permute-start(f32[256,128]{1,0:T(8,128)S(1)} %get-tuple-element.27), channel_id=1, source_target_pairs={{0,1},{1,0},{2,3},{3,2},{4,5},{5,4},{6,7},{7,6},{8,9},{9,8},{10,11... | collective-permute-start | bytes 393224 | tf_op jit(solution)/shard_map/ppermute | solution.py:245
  52.2 5.9 %collective-permute-start.19 = (f32[768,128]{1,0:T(8,128)S(1)}, f32[768,128]{1,0:T(8,128)S(1)}, u32[]{:S(2)}, u32[]{:S(2)}) collective-permute-start(f32[768,128]{1,0:T(8,128)S(1)} %get-tuple-element.32), channel_id=1, source_target_pairs={{0,1},{1,0},{2,3},{3,2},{4,5},{5,4},{6,7},{7,6},{8,9},{9,8},{10,11... | collective-permute-start | bytes 1179656 | tf_op jit(solution)/shard_map/ppermute | solution.py:245
  52.6 5.0 %collective-permute-start.23 = (f32[256,128]{1,0:T(8,128)S(1)}, f32[256,128]{1,0:T(8,128)S(1)}, u32[]{:S(2)}, u32[]{:S(2)}) collective-permute-start(f32[256,128]{1,0:T(8,128)S(1)} %add.221), channel_id=1, source_target_pairs={{0,2},{1,13},{2,0},{3,15},{4,6},{5,9},{6,4},{7,11},{8,10},{9,5},{1... | collective-permute-start | bytes 393224 | tf_op jit(solution)/shard_map/ppermute | solution.py:308
  57.5 5.0 %collective-permute-start.24 = (f32[256,128]{1,0:T(8,128)S(1)}, f32[256,128]{1,0:T(8,128)S(1)}, u32[]{:S(2)}, u32[]{:S(2)}) collective-permute-start(f32[256,128]{1,0:T(8,128)S(1)} %add.226), channel_id=1, source_target_pairs={{0,4},{1,3},{2,6},{3,1},{4,0},{5,7},{6,2},{7,5},{8,12},{9,11},{10,... | collective-permute-start | bytes 393224 | tf_op jit(solution)/shard_map/ppermute | solution.py:308
  58.2 6.5 %collective-permute-start.20 = (f32[3,2,64,128]{3,2,1,0:T(8,128)S(1)}, f32[3,2,64,128]{3,2,1,0:T(8,128)S(1)}, u32[]{:S(2)}, u32[]{:S(2)}) collective-permute-start(f32[3,2,64,128]{3,2,1,0:T(8,128)S(1)} %slice_select_fusion), channel_id=1, source_target_pairs={{0,4},{1,3},{2,6},{3,1},{4,0},{5,9},{6,2},{7,11},{8,12},{9,5},{10,... | collective-permute-start | bytes 589832 | tf_op jit(solution)/shard_map/ppermute | solution.py:269
  62.6 7.3 %collective-permute-start.25 = (f32[256,128]{1,0:T(8,128)S(1)}, f32[256,128]{1,0:T(8,128)S(1)}, u32[]{:S(2)}, u32[]{:S(2)}) collective-permute-start(f32[256,128]{1,0:T(8,128)S(1)} %add.227), channel_id=1, source_target_pairs={{0,8},{1,5},{2,10},{3,7},{4,12},{5,1},{6,14},{7,3},{8,0},{9,13},{1... | collective-permute-start | bytes 393224 | tf_op jit(solution)/shard_map/ppermute | solution.py:308
  64.8 4.3 %collective-permute-start.21 = (f32[2,64,64]{2,1,0:T(8,128)S(1)}, f32[2,64,64]{2,1,0:T(8,128)S(1)}, u32[]{:S(2)}, u32[]{:S(2)}) collective-permute-start(f32[2,64,64]{2,1,0:T(8,128)S(1)} %fusion.19), channel_id=1, source_target_pairs={{0,2},{2,0},{1,3},{3,1},{4,6},{6,4},{5,7},{7,5},{8,10},{10,8},{9,1... | collective-permute-start | bytes 98312 | tf_op jit(solution)/shard_map/ppermute | solution.py:288
  69.4 1.4 %collective-permute-start.22 = (f32[2,64,256]{2,1,0:T(8,128)S(1)}, f32[2,64,256]{2,1,0:T(8,128)S(1)}, u32[]{:S(2)}, u32[]{:S(2)}) collective-permute-start(f32[2,64,256]{2,1,0:T(8,128)S(1)} %fusion.2), channel_id=1, source_target_pairs={{0,1},{1,0},{2,3},{3,2},{4,5},{5,4},{6,7},{7,6},{8,9},{9,8},{10,11... | collective-permute-start | bytes 393224 | tf_op jit(solution)/shard_map/ppermute | solution.py:245

commit v5 on v4

--- a/solution.py
+++ b/solution.py
@@ -17,17 +17,21 @@
 VMEM_LIMIT = 16 * 1024 * 1024
 
 
-def dft_tables(size):
-    steps = np.arange(size)
-    angle = (steps[:, None] * steps[None, :] % size) * (2.0 * np.pi / size)
-    cosine, sine = np.cos(angle) / np.sqrt(size), np.sin(angle) / np.sqrt(size)
-    ahead = np.block([[cosine, -sine], [sine, cosine]]).astype(np.float32)
-    halves = []
-    for table in (ahead, ahead.T):
+def transform_tables(size):
+    half = size // 2
+    point, freq = np.arange(half)[:, None], np.arange(half)[None, :]
+    right, left, right_back, left_back = [], [], [], []
+    for odd in range(2):
+        angle = (point * (2 * freq + odd) % size) * (2.0 * np.pi / size)
+        cosine, sine = np.cos(angle) / np.sqrt(size), np.sin(angle) / np.sqrt(size)
+        table = np.block([[cosine, -sine], [sine, cosine]]).astype(np.float32)
         high = table.astype(ml_dtypes.bfloat16)
         low = (table - high.astype(np.float32)).astype(ml_dtypes.bfloat16)
-        halves += [high, low]
-    return halves
+        right.append(np.concatenate([high, low], axis=1))
+        left.append(np.concatenate([high.T, low.T], axis=0))
+        right_back.append(np.concatenate([high.T, low.T], axis=1))
+        left_back.append(np.concatenate([high, low], axis=0))
+    return [np.stack(t) for t in (right, left, left_back, right_back)]
 
 
 def split(values):
@@ -39,22 +43,65 @@
     return jnp.dot(left, right, preferred_element_type=jnp.float32)
 
 
-def from_right(values, high, low):
-    values_high, values_low = split(values)
-    return matmul(values_high, high) + (matmul(values_low, high) + matmul(values_high, low))
-
-
-def from_left(high, low, values):
-    values_high, values_low = split(values)
-    return matmul(high, values_high) + (matmul(low, values_high) + matmul(high, values_low))
-
-
-def window_of(scalars, index, size):
-    me, corner_row, corner_col = scalars[0][0], scalars[0][2], scalars[0][3]
-    slot = 2 * index + me
-    row = scalars[1][0, slot] - corner_row
-    col = scalars[1][1, slot] - corner_col
-    return slot, row, col // size, col % size
+def from_right(values, table):
+    size = values.shape[1]
+    both = matmul(
+        jnp.concatenate(split(values), axis=1), jnp.concatenate([table, table], axis=0)
+    )
+    return both[:, :size] + both[:, size:]
+
+
+def from_left(table, values):
+    size = values.shape[0]
+    both = matmul(
+        jnp.concatenate([table, table], axis=1), jnp.concatenate(split(values), axis=0)
+    )
+    return both[:size] + both[size:]
+
+
+def meld(first, second):
+    half = first.shape[1] // 2
+    low = lax.broadcasted_iota(jnp.int32, first.shape, 1) < half
+    turned = pltpu.roll(jnp.where(low, second, first), half, 1)
+    return jnp.where(low, first, turned), jnp.where(low, turned, second)
+
+
+def stack_rows(*blocks):
+    return jnp.concatenate(blocks, axis=0)
+
+
+def stack_lanes(*blocks):
+    return jnp.concatenate(blocks, axis=1)
+
+
+def prepare_kernel(place, positions, counts, measured, order, root, windows, planes):
+    slots, _, size, _ = measured.shape
+    half = size // 2
+    me = place[0]
+    for index in range(slots):
+        slot = 2 * index + me
+        col = positions[1, slot] - place[3]
+        windows[4 * index] = positions[0, slot] - place[2]
+        windows[4 * index + 1] = col // size
+        windows[4 * index + 2] = col % size
+        windows[4 * index + 3] = (slot < counts[0, 0]).astype(jnp.int32)
+    windows[4 * slots] = me
+    windows[4 * slots + 1] = place[1]
+    values = jnp.sqrt(measured[...].reshape(slots * size, size))
+    high = values.astype(jnp.bfloat16)
+    middle, low = split(values - high.astype(jnp.float32))
+    planes[...] = matmul(high, order[...]) + (
+        matmul(middle, order[...]) + matmul(low, order[...])
+    )
+    for index in range(slots):
+        for odd in range(2):
+            root[index, odd * half : (odd + 1) * half, :] = planes[
+                pl.ds(index * size + odd, half, stride=2), :
+            ]
+
+
+def window_of(windows, index):
+    return windows[4 * index], windows[4 * index + 1], windows[4 * index + 2]
 
 
 def region(tile, half, size):
@@ -65,22 +112,20 @@
     return pl.ds(tile * 2 * size + row, size)
 
 
-def wave_kernel(place, positions, counts, *refs, columns, group):
-    scalars = (place, positions)
+def wave_kernel(windows, *refs, columns, group):
     mine, theirs = refs[: columns + 1], refs[columns + 1 : 2 * columns + 2]
-    measured, ahead_high, ahead_low, behind_high, behind_low = refs[2 * columns + 2 :][:5]
+    root, right, left, left_back, right_back = refs[2 * columns + 2 :][:5]
     keep, send, pieces, state, modes, grad = refs[2 * columns + 7 :]
-    size = measured.shape[-1]
-    slots = measured.shape[0]
-    me, half_mine = place[0], place[1]
-    live_slots = counts[0, 0]
+    slots, size, _ = root.shape
+    half = size // 2
+    me, half_mine = windows[4 * slots], windows[4 * slots + 1]
     lane = lax.broadcasted_iota(jnp.int32, (size, size), 1)
 
-    for blocks, half, mode in ((mine, half_mine, me), (theirs, 1 - half_mine, 1 - me)):
+    for blocks, side, mode in ((mine, half_mine, me), (theirs, 1 - half_mine, 1 - me)):
         for part in range(2):
             rows = slice(part * size, (part + 1) * size)
             for tile in range(columns):
-                state[part, region(tile, half, size), :] = blocks[tile][rows, :]
+                state[part, region(tile, side, size), :] = blocks[tile][rows, :]
         modes[mode] = blocks[-1][...]
     grad[...] = jnp.zeros_like(grad)
 
@@ -88,10 +133,9 @@
         return modes[mode, part * size : (part + 1) * size, :]
 
     def one_group(first):
-        windows, patches, waves = [], [], []
+        patches, reals, imags = [], [], []
         for index in range(group):
-            slot, row, tile, shift = window_of(scalars, first + index, size)
-            windows.append(slot)
+            row, tile, shift = window_of(windows, first + index)
             patch = []
             for part in range(2):
                 near = state[part, rows_of(row, tile, size), :]
@@ -102,48 +146,51 @@
             patches.append(patch)
             for mode in range(2):
                 real, imag = plane(mode, 0), plane(mode, 1)
-                waves.append(
-                    jnp.concatenate(
-                        [real * patch[0] - imag * patch[1], real * patch[1] + imag * patch[0]],
-                        axis=1,
-                    )
+                reals.append(real * patch[0] - imag * patch[1])
+                imags.append(real * patch[1] + imag * patch[0])
+        first_half, second_half = meld(stack_rows(*reals), stack_rows(*imags))
+        real, imag = meld(
+            from_right(first_half + second_half, right[0]),
+            from_right(first_half - second_half, right[1]),
+        )
+        reals, imags = [], []
+        for index in range(group):
+            start = 2 * index * size
+            both = [
+                stack_lanes(x[start : start + size], x[start + size : start + 2 * size])
+                for x in (real, imag)
+            ]
+            waves_back = []
+            for odd in range(2):
+                merged = [x[:half] - x[half:] if odd else x[:half] + x[half:] for x in both]
+                far_field = from_left(left[odd], stack_rows(*merged))
+                power = far_field * far_field
+                power = power[:half] + power[half:]
+                power = power[:, :size] + power[:, size:]
+                live = windows[4 * (first + index) + 3].astype(jnp.float32)
+                roots = root[first + index, odd * half : (odd + 1) * half, :]
+                weight = (1.0 - roots * lax.rsqrt(power + 1.0)) * live
+                weight = stack_lanes(weight, weight)
+                waves_back.append(
+                    from_left(left_back[odd], stack_rows(weight, weight) * far_field)
                 )
-        half = from_right(jnp.concatenate(waves, axis=0), ahead_high[...], ahead_low[...])
-        scaled = []
-        for index in range(group):
-            first_mode = half[2 * index * size : (2 * index + 1) * size]
-            second_mode = half[(2 * index + 1) * size : (2 * index + 2) * size]
-            turned = jnp.concatenate(
-                [
-                    jnp.concatenate([first_mode[:, :size], second_mode[:, :size]], axis=1),
-                    jnp.concatenate([first_mode[:, size:], second_mode[:, size:]], axis=1),
-                ],
-                axis=0,
-            )
-            far_field = from_left(behind_high[...], behind_low[...], turned)
-            power = far_field * far_field
-            power = power[:size] + power[size:]
-            power = power[:, :size] + power[:, size:]
-            live = jnp.where(windows[index] < live_slots, 1.0, 0.0).astype(jnp.float32)
-            weight = (
-                1.0 - jnp.sqrt(measured[first + index, 0]) * lax.rsqrt(power + 1.0)
-            ) * live
-            weight = jnp.concatenate([weight, weight], axis=1)
-            weight = jnp.concatenate([weight, weight], axis=0)
-            back = from_left(ahead_high[...], ahead_low[...], weight * far_field)
+            even, odd = waves_back
+            sums, differences = even + odd, even - odd
             for mode in range(2):
                 lanes = slice(mode * size, (mode + 1) * size)
-                scaled.append(jnp.concatenate([back[:size, lanes], back[size:, lanes]], axis=1))
-        chi = from_right(jnp.concatenate(scaled, axis=0), behind_high[...], behind_low[...])
+                reals.append(stack_rows(sums[:half, lanes], differences[:half, lanes]))
+                imags.append(stack_rows(sums[half:, lanes], differences[half:, lanes]))
+        even, odd = meld(stack_rows(*reals), stack_rows(*imags))
+        even, odd = from_right(even, right_back[0]), from_right(odd, right_back[1])
+        real, imag = meld(even + odd, even - odd)
         for index in range(group):
             total = [0.0, 0.0]
             for mode in range(2):
                 start = (2 * index + mode) * size
-                chi_real = chi[start : start + size, :size]
-                chi_imag = chi[start : start + size, size:]
-                real, imag = plane(mode, 0), plane(mode, 1)
-                total[0] = total[0] + (real * chi_real + imag * chi_imag)
-                total[1] = total[1] + (real * chi_imag - imag * chi_real)
+                chi_real, chi_imag = real[start : start + size], imag[start : start + size]
+                probe_real, probe_imag = plane(mode, 0), plane(mode, 1)
+                total[0] = total[0] + (probe_real * chi_real + probe_imag * chi_imag)
+                total[1] = total[1] + (probe_real * chi_imag - probe_imag * chi_real)
                 patch_real, patch_imag = patches[index]
                 grad[mode, :size, :] += patch_real * chi_real + patch_imag * chi_imag
                 grad[mode, size:, :] += patch_real * chi_imag - patch_imag * chi_real
@@ -158,36 +205,80 @@
     send[...] = grad[1 - me]
 
 
-def place_kernel(place, positions, pieces, keep, send, grad, *, columns):
-    size = pieces.shape[-1]
-    half_mine = place[1]
+def place_kernel(windows, pieces, keep, send, grad, *, columns, owned_only):
+    slots, _, size, _ = pieces.shape
+    half_mine = windows[4 * slots + 1]
     lane = lax.broadcasted_iota(jnp.int32, (size, size), 1)
     grad[...] = jnp.zeros_like(grad)
-    for index in range(pieces.shape[0]):
-        _, row, tile, shift = window_of((place, positions), index, size)
+    for index in range(slots):
+        row, tile, shift = window_of(windows, index)
         inside = lane >= shift
         for part in range(2):
             turned = pltpu.roll(pieces[index, part], shift, 1)
             grad[part, rows_of(row, tile, size), :] += jnp.where(inside, turned, 0.0)
             grad[part, rows_of(row, tile + 1, size), :] += jnp.where(inside, 0.0, turned)
-    for target, half in ((keep, half_mine), (send, 1 - half_mine)):
-        for tile in range(columns):
-            for part in range(2):
-                start = (2 * tile + part) * size
-                target[start : start + size, :] = grad[part, region(tile, half, size), :]
+    cuts = 2 if owned_only else 1
+    height = size // cuts
+    for target, side in ((keep, half_mine), (send, 1 - half_mine)):
+        for cut in range(cuts):
+            for tile in range(columns):
+                for part in range(2):
+                    start = ((cut * columns + tile) * 2 + part) * height
+                    skip = (side if cut == 0 else 1 - side) * height if owned_only else 0
+                    first = tile * 2 * size + side * size + skip
+                    rows = pl.ds(pl.multiple_of(first, height), height)
+                    target[start : start + height, :] = grad[part, rows, :]
 
 
 def whole_block(shape):
     return pl.BlockSpec(shape, lambda i, *_: (0,) * len(shape))
 
 
-def waves(scalars, mine, theirs, measured):
+def prepared(place, positions, counts, measured):
     size = measured.shape[-1]
     slots = measured.shape[0] // 2
+    order = np.zeros((size, size), ml_dtypes.bfloat16)
+    order[np.concatenate([np.arange(0, size, 2), np.arange(1, size, 2)]), np.arange(size)] = 1
+    return pl.pallas_call(
+        prepare_kernel,
+        out_shape=[
+            jax.ShapeDtypeStruct((slots, size, size), jnp.float32),
+            jax.ShapeDtypeStruct((4 * slots + 2,), jnp.int32),
+        ],
+        grid_spec=pltpu.PrefetchScalarGridSpec(
+            num_scalar_prefetch=3,
+            grid=(1,),
+            in_specs=[
+                pl.BlockSpec((slots, 1, size, size), lambda i, s, *_: (0, s[0], 0, 0)),
+                whole_block((size, size)),
+            ],
+            out_specs=[
+                whole_block((slots, size, size)),
+                pl.BlockSpec(memory_space=pltpu.SMEM),
+            ],
+            scratch_shapes=[pltpu.VMEM((slots * size, size), jnp.float32)],
+        ),
+        compiler_params=pltpu.CompilerParams(vmem_limit_bytes=VMEM_LIMIT),
+        cost_estimate=pl.CostEstimate(
+            flops=6 * slots * size**3, bytes_accessed=8 * slots * size**2, transcendentals=0
+        ),
+        name="prepared",
+    )(
+        place,
+        positions,
+        counts,
+        measured.reshape(slots, 2, size, size),
+        jnp.asarray(order),
+    )
+
+
+def waves(windows, mine, theirs, root):
+    slots, size, _ = root.shape
     columns = len(mine) - 1
     group = 4 if slots % 4 == 0 else 1
     pair = (2 * size, size)
     pieces = (slots, 2, size, size)
+    tables = [jnp.asarray(t) for t in transform_tables(size)]
 
     def body(*refs):
         wave_kernel(*refs, columns=columns, group=group)
@@ -196,11 +287,11 @@
         body,
         out_shape=[jax.ShapeDtypeStruct(s, jnp.float32) for s in (pair, pair, pieces)],
         grid_spec=pltpu.PrefetchScalarGridSpec(
-            num_scalar_prefetch=3,
+            num_scalar_prefetch=1,
             grid=(1,),
             in_specs=[whole_block(pair)] * (2 * columns + 2)
-            + [pl.BlockSpec((slots, 1, size, size), lambda i, s, *_: (0, s[0], 0, 0))]
-            + [whole_block((2 * size, 2 * size))] * 4,
+            + [whole_block(root.shape)]
+            + [whole_block(t.shape) for t in tables],
             out_specs=[whole_block(s) for s in (pair, pair, pieces)],
             scratch_shapes=[
                 pltpu.VMEM((2, columns * 2 * size, size), jnp.float32),
@@ -210,27 +301,21 @@
         ),
         compiler_params=pltpu.CompilerParams(vmem_limit_bytes=VMEM_LIMIT),
         name="waves",
-    )(
-        *scalars,
-        *mine,
-        *theirs,
-        measured.reshape(slots, 2, size, size),
-        *[jnp.asarray(t) for t in dft_tables(size)],
-    )
-
-
-def placed(scalars, pieces, columns):
+    )(windows, *mine, *theirs, root, *tables)
+
+
+def placed(windows, pieces, columns, owned_only):
     size = pieces.shape[-1]
     shape = (columns * 2 * size, size)
 
     def body(*refs):
-        place_kernel(*refs, columns=columns)
+        place_kernel(*refs, columns=columns, owned_only=owned_only)
 
     return pl.pallas_call(
         body,
         out_shape=[jax.ShapeDtypeStruct(shape, jnp.float32)] * 2,
         grid_spec=pltpu.PrefetchScalarGridSpec(
-            num_scalar_prefetch=2,
+            num_scalar_prefetch=1,
             grid=(1,),
             in_specs=[whole_block(pieces.shape)],
             out_specs=[whole_block(shape)] * 2,
@@ -238,7 +323,7 @@
         ),
         compiler_params=pltpu.CompilerParams(vmem_limit_bytes=VMEM_LIMIT),
         name="placed",
-    )(*scalars[:2], pieces)
+    )(windows, pieces)
 
 
 def swap_modes(block):
@@ -325,7 +410,7 @@
     place = jnp.stack(
         [me, half_mine, row * tile_rows - half, col * tile_cols - half]
     ).astype(jnp.int32)
-    scalars = (place, positions[0, 0].T, counts)
+    root, windows = prepared(place, positions[0, 0].T, counts, measured[0, 0])
     probe_step = probe_rate / (slot_count * rows_count * cols_count)
 
     strip = jnp.where(lower, obj[:, half:], obj[:, :half])
@@ -333,6 +418,7 @@
     beside = swap_neighbours(strip)
     strip_low, strip_high = from_cols(edges, swap_cols)
     corner_low, corner_high = from_cols(edges, swap_neighbours)
+    beside, root, windows = lax.optimization_barrier((beside, root, windows))
     strip = jnp.concatenate([strip_low, strip, strip_high], axis=2)
     beside = jnp.concatenate([corner_low, beside, corner_high], axis=2)
     beside = jnp.where(paired, beside, 0.0)
@@ -354,16 +440,15 @@
         rates.append(jnp.where(inside, jnp.float32(object_rate), 0.0))
 
     previous, current = start, start
+    ahead, others = start, [swap_modes(x) for x in start]
     for iteration in range(ITERS):
-        ahead = [x + momentum * (x - y) for x, y in zip(current, previous, strict=True)]
-        keep, send, pieces = waves(scalars, ahead, [swap_modes(x) for x in ahead], measured[0, 0])
+        keep, send, pieces = waves(windows, ahead, others, root)
         probe_grad = keep + swap_modes(send)
-        keep, send = placed(scalars, pieces, columns)
+        keep, send = placed(windows, pieces, columns, iteration == ITERS - 1)
         probe_grad, keep, send = lax.optimization_barrier((probe_grad, keep, send))
         previous = current
         probe_grad = sum_tiles(probe_grad)
         object_grad = keep + swap_modes(send)
-        new_probe = ahead[-1] - probe_step * probe_grad
         if iteration < ITERS - 1:
             object_grad = object_grad + jnp.where(paired, swap_neighbours(object_grad), 0.0)
             parts = [
@@ -372,13 +457,16 @@
             from_low, from_high = from_cols((parts[0], parts[-1]), swap_cols)
             parts[0] = parts[0] + from_low
             parts[-1] = parts[-1] + from_high
-            current = [
-                x - rate * g for x, rate, g in zip(ahead, rates, parts, strict=False)
-            ] + [new_probe]
+            current = [x - rate * g for x, rate, g in zip(ahead, rates, parts, strict=False)]
+            tiles = [x + momentum * (x - y) for x, y in zip(current, previous, strict=False)]
+            others = [swap_modes(x) for x in tiles]
+            new_probe = ahead[-1] - probe_step * probe_grad
+            current = current + [new_probe]
+            ahead = tiles + [new_probe + momentum * (new_probe - previous[-1])]
+            others = others + [swap_modes(ahead[-1])]
         else:
-            object_grad = object_grad.reshape(columns, 2, size, size)
-            given = jnp.where(lower, object_grad[:, :, half:], object_grad[:, :, :half])
-            owned = jnp.where(lower, object_grad[:, :, :half], object_grad[:, :, half:])
+            object_grad = object_grad.reshape(2, columns, 2, half, size)
+            given, owned = object_grad[0], object_grad[1]
             owned = owned + jnp.where(paired, swap_neighbours(given), 0.0)
             edges = (owned[0, :, :, :half], owned[-1, :, :, half:])
             from_low, from_high = from_cols(edges, swap_cols)
@@ -396,6 +484,7 @@
     whole = jnp.concatenate(
         [jnp.where(lower, other, strip), jnp.where(lower, strip, other)], axis=1
     )
+    new_probe = ahead[-1] - probe_step * probe_grad
     return (whole, new_probe.reshape(1, 2, size, size))
 
 

time: 71.8 us -> 68 us (0.947)
  waiting for transfers between devices: 30.8 us -> 24.6 us
  starting transfers between devices: 19.6 us -> 22.5 us
  Pallas kernels: 15 us -> 13.2 us
  local copies, waits for them, and re-layouts: 0.71 us -> 1.99 us
    pallas_call x2, Pallas kernels: 13.1 us -> 9.68 us  [waves(): pl.pallas_call(body, out_shape=[jax.ShapeDtypeStruct(s, jnp.float32) for...]
    ppermute x6, waiting for transfers between devices: 20.2 us -> 17.1 us  [sum_tiles(): block = block + lax.ppermute(block, ('row', 'col', 'mode'), route)]
    ppermute x6, starting transfers between devices: 6.52 us -> 9.48 us  [sum_tiles(): block = block + lax.ppermute(block, ('row', 'col', 'mode'), route)]
    ppermute x3, waiting for transfers between devices: 5.06 us -> 2.79 us  [swap_cols(): lax.ppermute(block, 'col', [(i, i if o is None else o) for i, o in enumer...]
    ppermute x4, waiting for transfers between devices: 3.4 us -> 1.73 us  [swap_neighbours(): return lax.ppermute(block, ('row', 'col', 'mode'), route)]
    pallas_call x0 -> x1, Pallas kernels: none -> 1.61 us  [prepared(): pl.pallas_call(prepare_kernel, out_shape=[jax.ShapeDtypeStruct((slots, si...]
    unnamed x14 -> x16, local copies, waits for them, and re-layouts: 0.68 us -> 1.93 us
    ppermute x13, waiting for transfers between devices: 2.15 us -> 3.04 us  [swap_modes(): return lax.ppermute(block, 'mode', [(0, 1), (1, 0)])]
  transfers between devices with their start and end apart: 26 -> 26, of which waited for: 19 -> 18; matrix products, arithmetic and copies ran while one was open for 3% -> 3% of each run, Pallas kernels for 3% -> 5%
where the time goes in v5:
time: 68 us; the launch traced here: 67.8 us
  waiting for transfers between devices  24.6 us (36%)
  starting transfers between devices  22.5 us (33%)
  Pallas kernels  13.2 us (19%)
  other arithmetic  3.77 us (6%)
  local copies, waits for them, and re-layouts  1.99 us (3%)
  between operations  1.64 us (2%)
    ppermute x6, waiting for transfers between devices, sum_tiles(): block = block + lax.ppermute(block, ('row', 'col', 'mode'), route)  17.1 us
    pallas_call x2, Pallas kernels, waves(): pl.pallas_call(body, out_shape=[jax.ShapeDtypeStruct(s, jnp.float32) for...  9.68 us
    ppermute x6, starting transfers between devices, sum_tiles(): block = block + lax.ppermute(block, ('row', 'col', 'mode'), route)  9.48 us
    ppermute x4, starting transfers between devices, swap_neighbours(): return lax.ppermute(block, ('row', 'col', 'mode'), route)  6.31 us
    ppermute x3, starting transfers between devices, swap_cols(): lax.ppermute(block, 'col', [(i, i if o is None else o) for i, o in enumer...  3.59 us
    ppermute x13, starting transfers between devices, swap_modes(): return lax.ppermute(block, 'mode', [(0, 1), (1, 0)])  3.15 us
    ppermute x13, waiting for transfers between devices, swap_modes(): return lax.ppermute(block, 'mode', [(0, 1), (1, 0)])  3.04 us
    ppermute x3, waiting for transfers between devices, swap_cols(): lax.ppermute(block, 'col', [(i, i if o is None else o) for i, o in enumer...  2.79 us
  transfers between devices with their start and end apart: 26, of which 18 were waited for; matrix products, arithmetic and copies ran while one was open for 3% of the time, Pallas kernels for 5%

profile of v5, /device:TPU:0, one launch (start us, length us, event | category | flops | bytes accessed | tf_op | source)
XLA Modules:
  0.0 67.8 jit_solution(2549942097653911971)
XLA Ops:
  0.7 1.0 %slice_select_fusion.1 = f32[2,64,256]{2,1,0:T(8,128)S(1)} fusion(f32[2,128,256]{2,1,0:T(8,128)} %param.14, pred[]{:T(512)S(6)} %eq.15), kind=kLoop, calls=%fused_computation.23 | loop fusion | flops 32768 | bytes 393217 | tf_op jit(solution)/shard_map/jit(_where)/select_n | solution.py:416
  1.7 0.1 slice_select_fusion.4
  1.8 0.0 copy-start.6
  1.8 4.0 %collective-permute-start.1 = (f32[2,64,64]{2,1,0:T(8,128)S(1)}, f32[2,64,64]{2,1,0:T(8,128)S(1)}, u32[]{:S(2)}, u32[]{:S(2)}) collective-permute-start(f32[2,64,64]{2,1,0:T(8,128)S(1)} %slice_select_fusion.4), channel_id=1, source_target_pairs={{0,6},{1,3},{2,4},{3,1},{4,2},{5,11},{6,0},{7,9},{8,14},{9,7},{10,... | collective-permute-start | bytes 98312 | tf_op jit(solution)/shard_map/ppermute | solution.py:354
  5.8 0.5 collective-permute-start
  6.3 0.1 collective-permute-start.2
  6.4 0.1 pad_add_fusion.place
  7.2 0.7 copy-done.7
  7.9 1.2 %copy-done = f32[1,1,16,128,128]{4,3,2,1,0:T(8,128)S(1)} copy-done((f32[1,1,16,128,128]{4,3,2,1,0:T(8,128)S(1)}, f32[1,1,16,128,128]{4,3,2,1,0:T(8,128)}, u32[]{:S(2)}) %copy-start) | copy-done | bytes 1048600
  9.1 1.6 %prepared.1 = (f32[8,128,128]{2,1,0:T(8,128)S(1)}, s32[34]{0:T(128)S(1)}) custom-call(s32[4]{0:T(128)S(1)} %pad_add_fusion.place, s32[2,16]{1,0:T(2,128)S(1)} %bitcast.46, s32[1,1]{1,0:T(1,128)S(6)} %copy.16.counts, f32[8,2,128,128]{3,2,1,0:T(8,128)S(1)} %bitcast.43, bf16[128,128]{1,0:T(8,128)(2,1)S(1)} %copy-done.6), custom_call_target="tpu_custom_call" | custom-call | flops 100663296 | bytes 1048576 | tf_op jit(solution)/shard_map/prepared/pallas_call | solution.py:242
  10.8 0.5 collective-permute-done.2
  11.3 0.2 fusion.4
  11.5 0.0 copy-start.1
  11.6 0.1 collective-permute-start.3
  11.7 0.5 collective-permute-start.5
  12.2 0.1 collective-permute-start.4
  12.2 0.8 %collective-permute-done.3.refs_5_ = f32[256,128]{1,0:T(8,128)S(1)} collective-permute-done((f32[256,128]{1,0:T(8,128)S(1)}, f32[256,128]{1,0:T(8,128)S(1)}, u32[]{:S(2)}, u32[]{:S(2)}) %collective-permute-start.3) | collective-permute-done | bytes 131104 | tf_op jit(solution)/shard_map/ppermute | solution.py:330
  13.0 0.2 collective-permute-done.5.refs_7_
  13.2 0.3 collective-permute-done.4.refs_6_
  13.5 4.9 %waves.2 = (f32[256,128]{1,0:T(8,128)S(1)}, f32[256,128]{1,0:T(8,128)S(1)}, f32[8,2,128,128]{3,2,1,0:T(8,128)S(1)}) custom-call(s32[34]{0:T(128)S(1)} %get-tuple-element.26.refs_0_, f32[256,128]{1,0:T(8,128)S(1)} %bitcast.37, f32[256,128]{1,0:T(8,128)S(1)} %bitcast.39, f32[256,128]{1,0:T(8,128)S(1)} %bitcast.35, f32[256,128]{1,0:T(8,128)S(1)} %bitcast.45, ...), custom_call_target="tpu_custom_call" | custom-call | tf_op jit(solution)/shard_map/waves/pallas_call | solution.py:286
  18.4 0.3 collective-permute-start.7
  18.6 1.0 %placed.2 = (f32[768,128]{1,0:T(8,128)S(1)}, f32[768,128]{1,0:T(8,128)S(1)}) custom-call(s32[34]{0:T(128)S(1)} %get-tuple-element.26.refs_0_, f32[8,2,128,128]{3,2,1,0:T(8,128)S(1)} %get-tuple-element.30.refs_1_), custom_call_target="tpu_custom_call" | custom-call | tf_op jit(solution)/shard_map/placed/pallas_call | solution.py:314
  19.6 0.2 collective-permute-done.7
  19.8 0.3 collective-permute-start.8
  20.1 1.6 %collective-permute-start.11 = (f32[256,128]{1,0:T(8,128)S(1)}, f32[256,128]{1,0:T(8,128)S(1)}, u32[]{:S(2)}, u32[]{:S(2)}) collective-permute-start(f32[256,128]{1,0:T(8,128)S(1)} %add.191), channel_id=1, source_target_pairs={{0,2},{1,13},{2,0},{3,15},{4,6},{5,9},{6,4},{7,11},{8,10},{9,5},{1... | collective-permute-start | bytes 393224 | tf_op jit(solution)/shard_map/ppermute | solution.py:393
  21.7 0.1 add.192
  21.8 1.6 %collective-permute-start.9 = (f32[768,128]{1,0:T(8,128)S(1)}, f32[768,128]{1,0:T(8,128)S(1)}, u32[]{:S(2)}, u32[]{:S(2)}) collective-permute-start(f32[768,128]{1,0:T(8,128)S(1)} %add.192), channel_id=1, source_target_pairs={{0,4},{1,3},{2,6},{3,1},{4,0},{5,9},{6,2},{7,11},{8,12},{9,5},{10,... | collective-permute-start | bytes 1179656 | tf_op jit(solution)/shard_map/ppermute | solution.py:354
  23.4 1.6 %collective-permute-done.11 = f32[256,128]{1,0:T(8,128)S(1)} collective-permute-done((f32[256,128]{1,0:T(8,128)S(1)}, f32[256,128]{1,0:T(8,128)S(1)}, u32[]{:S(2)}, u32[]{:S(2)}) %collective-permute-start.11) | collective-permute-done | bytes 131104 | tf_op jit(solution)/shard_map/ppermute | solution.py:393
  25.1 1.8 %collective-permute-start.12 = (f32[256,128]{1,0:T(8,128)S(1)}, f32[256,128]{1,0:T(8,128)S(1)}, u32[]{:S(2)}, u32[]{:S(2)}) collective-permute-start(f32[256,128]{1,0:T(8,128)S(1)} %add.201), channel_id=1, source_target_pairs={{0,4},{1,3},{2,6},{3,1},{4,0},{5,7},{6,2},{7,5},{8,12},{9,11},{10,... | collective-permute-start | bytes 393224 | tf_op jit(solution)/shard_map/ppermute | solution.py:393
  26.9 5.1 %collective-permute-done.12 = f32[256,128]{1,0:T(8,128)S(1)} collective-permute-done((f32[256,128]{1,0:T(8,128)S(1)}, f32[256,128]{1,0:T(8,128)S(1)}, u32[]{:S(2)}, u32[]{:S(2)}) %collective-permute-start.12) | collective-permute-done | bytes 131104 | tf_op jit(solution)/shard_map/ppermute | solution.py:393
  32.0 1.7 %collective-permute-start.13 = (f32[256,128]{1,0:T(8,128)S(1)}, f32[256,128]{1,0:T(8,128)S(1)}, u32[]{:S(2)}, u32[]{:S(2)}) collective-permute-start(f32[256,128]{1,0:T(8,128)S(1)} %add.202), channel_id=1, source_target_pairs={{0,8},{1,5},{2,10},{3,7},{4,12},{5,1},{6,14},{7,3},{8,0},{9,13},{1... | collective-permute-start | bytes 393224 | tf_op jit(solution)/shard_map/ppermute | solution.py:393
  33.8 1.5 %collective-permute-start.10 = (f32[256,128]{1,0:T(8,128)S(1)}, f32[256,128]{1,0:T(8,128)S(1)}, u32[]{:S(2)}, u32[]{:S(2)}) collective-permute-start(f32[256,128]{1,0:T(8,128)S(1)} %slice_select_fusion.2), channel_id=1, source_target_pairs={{0,2},{2,0},{1,3},{3,1},{4,6},{6,4},{5,7},{7,5},{8,10},{10,8},{9,1... | collective-permute-start | bytes 393224 | tf_op jit(solution)/shard_map/ppermute | solution.py:373
  35.4 4.0 %collective-permute-done.13 = f32[256,128]{1,0:T(8,128)S(1)} collective-permute-done((f32[256,128]{1,0:T(8,128)S(1)}, f32[256,128]{1,0:T(8,128)S(1)}, u32[]{:S(2)}, u32[]{:S(2)}) %collective-permute-start.13) | collective-permute-done | bytes 131104 | tf_op jit(solution)/shard_map/ppermute | solution.py:393
  39.4 0.1 collective-permute-start.17
  39.5 0.2 multiply_add_fusion.3
  39.7 0.6 collective-permute-start.14
  40.2 0.1 collective-permute-start.16
  40.3 0.4 collective-permute-start.15
  40.8 0.0 collective-permute-done.17.refs_8_
  40.8 0.4 collective-permute-done.14.refs_5_
  41.2 0.4 collective-permute-done.16.refs_7_
  41.6 0.2 collective-permute-done.15.refs_6_
  41.8 4.8 %waves.3 = (f32[256,128]{1,0:T(8,128)S(1)}, f32[256,128]{1,0:T(8,128)S(1)}, f32[8,2,128,128]{3,2,1,0:T(8,128)S(1)}) custom-call(s32[34]{0:T(128)S(1)} %get-tuple-element.26.refs_0_, f32[256,128]{1,0:T(8,128)S(1)} %get-tuple-element.44.refs_1_, f32[256,128]{1,0:T(8,128)S(1)} %get-tuple-element.48.refs_2_, f32[256,128]{1,0:T(8,128)S(1)} %get-tuple-element.45.refs_3_, ...), custom_call_target="tpu_custom_call" | custom-call | tf_op jit(solution)/shard_map/waves/pallas_call | solution.py:286
  46.6 0.4 collective-permute-start.18
  47.0 1.0 %placed.3 = (f32[768,128]{1,0:T(8,128)S(1)}, f32[768,128]{1,0:T(8,128)S(1)}) custom-call(s32[34]{0:T(128)S(1)} %get-tuple-element.26.refs_0_, f32[8,2,128,128]{3,2,1,0:T(8,128)S(1)} %get-tuple-element.38.refs_1_), custom_call_target="tpu_custom_call" | custom-call | tf_op jit(solution)/shard_map/placed/pallas_call | solution.py:314
  48.0 0.1 collective-permute-done.18
  48.1 0.4 collective-permute-start.19
  48.5 1.5 %collective-permute-start.23 = (f32[256,128]{1,0:T(8,128)S(1)}, f32[256,128]{1,0:T(8,128)S(1)}, u32[]{:S(2)}, u32[]{:S(2)}) collective-permute-start(f32[256,128]{1,0:T(8,128)S(1)} %add.205), channel_id=1, source_target_pairs={{0,2},{1,13},{2,0},{3,15},{4,6},{5,9},{6,4},{7,11},{8,10},{9,5},{1... | collective-permute-start | bytes 393224 | tf_op jit(solution)/shard_map/ppermute | solution.py:393
  50.0 3.4 %collective-permute-done.23 = f32[256,128]{1,0:T(8,128)S(1)} collective-permute-done((f32[256,128]{1,0:T(8,128)S(1)}, f32[256,128]{1,0:T(8,128)S(1)}, u32[]{:S(2)}, u32[]{:S(2)}) %collective-permute-start.23) | collective-permute-done | bytes 131104 | tf_op jit(solution)/shard_map/ppermute | solution.py:393
  53.4 1.6 %collective-permute-start.24 = (f32[256,128]{1,0:T(8,128)S(1)}, f32[256,128]{1,0:T(8,128)S(1)}, u32[]{:S(2)}, u32[]{:S(2)}) collective-permute-start(f32[256,128]{1,0:T(8,128)S(1)} %add.210), channel_id=1, source_target_pairs={{0,4},{1,3},{2,6},{3,1},{4,0},{5,7},{6,2},{7,5},{8,12},{9,11},{10,... | collective-permute-start | bytes 393224 | tf_op jit(solution)/shard_map/ppermute | solution.py:393
  55.1 0.5 collective-permute-start.20
  55.7 2.8 %collective-permute-done.24 = f32[256,128]{1,0:T(8,128)S(1)} collective-permute-done((f32[256,128]{1,0:T(8,128)S(1)}, f32[256,128]{1,0:T(8,128)S(1)}, u32[]{:S(2)}, u32[]{:S(2)}) %collective-permute-start.24) | collective-permute-done | bytes 131104 | tf_op jit(solution)/shard_map/ppermute | solution.py:393
  58.5 1.2 %collective-permute-start.25 = (f32[256,128]{1,0:T(8,128)S(1)}, f32[256,128]{1,0:T(8,128)S(1)}, u32[]{:S(2)}, u32[]{:S(2)}) collective-permute-start(f32[256,128]{1,0:T(8,128)S(1)} %add.211), channel_id=1, source_target_pairs={{0,8},{1,5},{2,10},{3,7},{4,12},{5,1},{6,14},{7,3},{8,0},{9,13},{1... | collective-permute-start | bytes 393224 | tf_op jit(solution)/shard_map/ppermute | solution.py:393
  59.7 1.2 %collective-permute-done.20 = f32[3,2,64,128]{3,2,1,0:T(8,128)S(1)} collective-permute-done((f32[3,2,64,128]{3,2,1,0:T(8,128)S(1)}, f32[3,2,64,128]{3,2,1,0:T(8,128)S(1)}, u32[]{:S(2)}, u32[]{:S(2)}) %collective-permute-start.20) | collective-permute-done | bytes 196640 | tf_op jit(solution)/shard_map/ppermute | solution.py:354
  60.9 0.1 fusion.7
  61.0 1.5 %collective-permute-start.21 = (f32[2,64,64]{2,1,0:T(8,128)S(1)}, f32[2,64,64]{2,1,0:T(8,128)S(1)}, u32[]{:S(2)}, u32[]{:S(2)}) collective-permute-start(f32[2,64,64]{2,1,0:T(8,128)S(1)} %fusion.7), channel_id=1, source_target_pairs={{0,2},{2,0},{1,3},{3,1},{4,6},{6,4},{5,7},{7,5},{8,10},{10,8},{9,1... | collective-permute-start | bytes 98312 | tf_op jit(solution)/shard_map/ppermute | solution.py:373
  62.5 2.8 %collective-permute-done.21 = f32[2,64,64]{2,1,0:T(8,128)S(1)} collective-permute-done((f32[2,64,64]{2,1,0:T(8,128)S(1)}, f32[2,64,64]{2,1,0:T(8,128)S(1)}, u32[]{:S(2)}, u32[]{:S(2)}) %collective-permute-start.21) | collective-permute-done | bytes 32800 | tf_op jit(solution)/shard_map/ppermute | solution.py:373
  65.3 0.1 fusion.8
  65.4 0.2 fusion.2
  65.6 0.1 collective-permute-start.22
  65.7 0.1 collective-permute-done.25
  65.8 0.7 %multiply_subtract_fusion = f32[256,128]{1,0:T(8,128)} fusion(f32[256,128]{1,0:T(8,128)S(1)} %multiply_add_fusion.refs_4_, f32[256,128]{1,0:T(8,128)S(1)} %add.211, f32[256,128]{1,0:T(8,128)S(1)} %collective-permute-done.25), kind=kLoop, calls=%fused_computation.18 | loop fusion | flops 98304 | bytes 524288 | tf_op jit(solution)/shard_map/sub | solution.py:487
  66.5 0.5 collective-permute-done.22
  67.0 0.7 %pad_maximum_fusion.1 = f32[2,128,256]{2,1,0:T(8,128)} fusion(f32[2,64,256]{2,1,0:T(8,128)S(1)} %get-tuple-element.57, f32[2,64,256]{2,1,0:T(8,128)S(1)} %get-tuple-element.56), kind=kLoop, calls=%fused_computation.6 | loop fusion | flops 65536 | bytes 524288 | tf_op jit(solution)/shard_map/concatenate | solution.py:484
  (44 shorter events, 0.5 us)
Async XLA Ops:
  1.7 4.8 %copy-start.5 = (f32[1,2,128,128]{3,2,1,0:T(8,128)S(1)}, f32[1,2,128,128]{3,2,1,0:T(8,128)}, u32[]{:S(2)}) copy-start(f32[1,2,128,128]{3,2,1,0:T(8,128)} %param.15) | copy-start | bytes 393220
  1.8 5.4 %copy-start.6 = (bf16[128,128]{1,0:T(8,128)(2,1)S(1)}, bf16[128,128]{1,0:T(8,128)(2,1)}, u32[]{:S(2)}) copy-start(bf16[128,128]{1,0:T(8,128)(2,1)} %constant.85.clone.order) | copy-start | bytes 98308
  1.8 8.9 %collective-permute-start.1 = (f32[2,64,64]{2,1,0:T(8,128)S(1)}, f32[2,64,64]{2,1,0:T(8,128)S(1)}, u32[]{:S(2)}, u32[]{:S(2)}) collective-permute-start(f32[2,64,64]{2,1,0:T(8,128)S(1)} %slice_select_fusion.4), channel_id=1, source_target_pairs={{0,6},{1,3},{2,4},{3,1},{4,2},{5,11},{6,0},{7,9},{8,14},{9,7},{10,... | collective-permute-start | bytes 98312 | tf_op jit(solution)/shard_map/ppermute | solution.py:354
  5.8 5.0 %collective-permute-start = (f32[2,64,64]{2,1,0:T(8,128)S(1)}, f32[2,64,64]{2,1,0:T(8,128)S(1)}, u32[]{:S(2)}, u32[]{:S(2)}) collective-permute-start(f32[2,64,64]{2,1,0:T(8,128)S(1)} %slice_select_fusion.4), channel_id=1, source_target_pairs={{0,2},{2,0},{1,3},{3,1},{4,6},{6,4},{5,7},{7,5},{8,10},{10,8},{9,1... | collective-permute-start | bytes 98312 | tf_op jit(solution)/shard_map/ppermute | solution.py:373
  6.3 5.0 %collective-permute-start.2 = (f32[2,64,256]{2,1,0:T(8,128)S(1)}, f32[2,64,256]{2,1,0:T(8,128)S(1)}, u32[]{:S(2)}, u32[]{:S(2)}) collective-permute-start(f32[2,64,256]{2,1,0:T(8,128)S(1)} %slice_select_fusion.1), channel_id=1, source_target_pairs={{0,4},{1,3},{2,6},{3,1},{4,0},{5,9},{6,2},{7,11},{8,12},{9,5},{10,... | collective-permute-start | bytes 393224 | tf_op jit(solution)/shard_map/ppermute | solution.py:354
  6.4 5.8 %collective-permute-start.6 = (f32[256,128]{1,0:T(8,128)S(1)}, f32[256,128]{1,0:T(8,128)S(1)}, u32[]{:S(2)}, u32[]{:S(2)}) collective-permute-start(f32[256,128]{1,0:T(8,128)S(1)} %bitcast.44), channel_id=1, source_target_pairs={{0,1},{1,0},{2,3},{3,2},{4,5},{5,4},{6,7},{7,6},{8,9},{9,8},{10,11... | collective-permute-start | bytes 393224 | tf_op jit(solution)/shard_map/ppermute | solution.py:330
  7.2 0.7 %copy-start.7 = (s32[1,1,16,2]{2,3,1,0:T(2,128)S(1)}, s32[1,1,16,2]{2,3,1,0:T(2,128)}, u32[]{:S(2)}) copy-start(s32[1,1,16,2]{2,3,1,0:T(2,128)} %param.16) | copy-start | bytes 388
  7.9 1.2 %copy-start = (f32[1,1,16,128,128]{4,3,2,1,0:T(8,128)S(1)}, f32[1,1,16,128,128]{4,3,2,1,0:T(8,128)}, u32[]{:S(2)}) copy-start(f32[1,1,16,128,128]{4,3,2,1,0:T(8,128)} %param.18) | copy-start | bytes 3145732
  11.5 2.0 %copy-start.1 = (bf16[2,128,256]{2,1,0:T(8,128)(2,1)S(1)}, bf16[2,128,256]{2,1,0:T(8,128)(2,1)}, u32[]{:S(2)}) copy-start(bf16[2,128,256]{2,1,0:T(8,128)(2,1)} %constant.89.clone.refs_13_) | copy-start | bytes 393220
  11.5 2.0 %copy-start.2 = (bf16[2,256,128]{2,1,0:T(8,128)(2,1)S(1)}, bf16[2,256,128]{2,1,0:T(8,128)(2,1)}, u32[]{:S(2)}) copy-start(bf16[2,256,128]{2,1,0:T(8,128)(2,1)} %constant.88.clone.refs_12_) | copy-start | bytes 393220
  11.5 2.0 %copy-start.3 = (bf16[2,256,128]{2,1,0:T(8,128)(2,1)S(1)}, bf16[2,256,128]{2,1,0:T(8,128)(2,1)}, u32[]{:S(2)}) copy-start(bf16[2,256,128]{2,1,0:T(8,128)(2,1)} %constant.87.clone.refs_11_) | copy-start | bytes 393220
  11.5 2.0 %copy-start.4 = (bf16[2,128,256]{2,1,0:T(8,128)(2,1)S(1)}, bf16[2,128,256]{2,1,0:T(8,128)(2,1)}, u32[]{:S(2)}) copy-start(bf16[2,128,256]{2,1,0:T(8,128)(2,1)} %constant.86.clone.refs_10_) | copy-start | bytes 393220
  11.6 1.4 %collective-permute-start.3 = (f32[256,128]{1,0:T(8,128)S(1)}, f32[256,128]{1,0:T(8,128)S(1)}, u32[]{:S(2)}, u32[]{:S(2)}) collective-permute-start(f32[256,128]{1,0:T(8,128)S(1)} %bitcast.36), channel_id=1, source_target_pairs={{0,1},{1,0},{2,3},{3,2},{4,5},{5,4},{6,7},{7,6},{8,9},{9,8},{10,11... | collective-permute-start | bytes 393224 | tf_op jit(solution)/shard_map/ppermute | solution.py:330
  11.7 1.5 %collective-permute-start.5 = (f32[256,128]{1,0:T(8,128)S(1)}, f32[256,128]{1,0:T(8,128)S(1)}, u32[]{:S(2)}, u32[]{:S(2)}) collective-permute-start(f32[256,128]{1,0:T(8,128)S(1)} %bitcast.34), channel_id=1, source_target_pairs={{0,1},{1,0},{2,3},{3,2},{4,5},{5,4},{6,7},{7,6},{8,9},{9,8},{10,11... | collective-permute-start | bytes 393224 | tf_op jit(solution)/shard_map/ppermute | solution.py:330
  12.2 1.3 %collective-permute-start.4 = (f32[256,128]{1,0:T(8,128)S(1)}, f32[256,128]{1,0:T(8,128)S(1)}, u32[]{:S(2)}, u32[]{:S(2)}) collective-permute-start(f32[256,128]{1,0:T(8,128)S(1)} %bitcast.38), channel_id=1, source_target_pairs={{0,1},{1,0},{2,3},{3,2},{4,5},{5,4},{6,7},{7,6},{8,9},{9,8},{10,11... | collective-permute-start | bytes 393224 | tf_op jit(solution)/shard_map/ppermute | solution.py:330
  18.4 1.4 %collective-permute-start.7 = (f32[256,128]{1,0:T(8,128)S(1)}, f32[256,128]{1,0:T(8,128)S(1)}, u32[]{:S(2)}, u32[]{:S(2)}) collective-permute-start(f32[256,128]{1,0:T(8,128)S(1)} %get-tuple-element.29), channel_id=1, source_target_pairs={{0,1},{1,0},{2,3},{3,2},{4,5},{5,4},{6,7},{7,6},{8,9},{9,8},{10,11... | collective-permute-start | bytes 393224 | tf_op jit(solution)/shard_map/ppermute | solution.py:330
  19.8 1.9 %collective-permute-start.8 = (f32[768,128]{1,0:T(8,128)S(1)}, f32[768,128]{1,0:T(8,128)S(1)}, u32[]{:S(2)}, u32[]{:S(2)}) collective-permute-start(f32[768,128]{1,0:T(8,128)S(1)} %get-tuple-element.34), channel_id=1, source_target_pairs={{0,1},{1,0},{2,3},{3,2},{4,5},{5,4},{6,7},{7,6},{8,9},{9,8},{10,11... | collective-permute-start | bytes 1179656 | tf_op jit(solution)/shard_map/ppermute | solution.py:330
  20.1 5.0 %collective-permute-start.11 = (f32[256,128]{1,0:T(8,128)S(1)}, f32[256,128]{1,0:T(8,128)S(1)}, u32[]{:S(2)}, u32[]{:S(2)}) collective-permute-start(f32[256,128]{1,0:T(8,128)S(1)} %add.191), channel_id=1, source_target_pairs={{0,2},{1,13},{2,0},{3,15},{4,6},{5,9},{6,4},{7,11},{8,10},{9,5},{1... | collective-permute-start | bytes 393224 | tf_op jit(solution)/shard_map/ppermute | solution.py:393
  21.8 12.0 %collective-permute-start.9 = (f32[768,128]{1,0:T(8,128)S(1)}, f32[768,128]{1,0:T(8,128)S(1)}, u32[]{:S(2)}, u32[]{:S(2)}) collective-permute-start(f32[768,128]{1,0:T(8,128)S(1)} %add.192), channel_id=1, source_target_pairs={{0,4},{1,3},{2,6},{3,1},{4,0},{5,9},{6,2},{7,11},{8,12},{9,5},{10,... | collective-permute-start | bytes 1179656 | tf_op jit(solution)/shard_map/ppermute | solution.py:354
  25.1 6.9 %collective-permute-start.12 = (f32[256,128]{1,0:T(8,128)S(1)}, f32[256,128]{1,0:T(8,128)S(1)}, u32[]{:S(2)}, u32[]{:S(2)}) collective-permute-start(f32[256,128]{1,0:T(8,128)S(1)} %add.201), channel_id=1, source_target_pairs={{0,4},{1,3},{2,6},{3,1},{4,0},{5,7},{6,2},{7,5},{8,12},{9,11},{10,... | collective-permute-start | bytes 393224 | tf_op jit(solution)/shard_map/ppermute | solution.py:393
  32.0 7.3 %collective-permute-start.13 = (f32[256,128]{1,0:T(8,128)S(1)}, f32[256,128]{1,0:T(8,128)S(1)}, u32[]{:S(2)}, u32[]{:S(2)}) collective-permute-start(f32[256,128]{1,0:T(8,128)S(1)} %add.202), channel_id=1, source_target_pairs={{0,8},{1,5},{2,10},{3,7},{4,12},{5,1},{6,14},{7,3},{8,0},{9,13},{1... | collective-permute-start | bytes 393224 | tf_op jit(solution)/shard_map/ppermute | solution.py:393
  33.8 5.6 %collective-permute-start.10 = (f32[256,128]{1,0:T(8,128)S(1)}, f32[256,128]{1,0:T(8,128)S(1)}, u32[]{:S(2)}, u32[]{:S(2)}) collective-permute-start(f32[256,128]{1,0:T(8,128)S(1)} %slice_select_fusion.2), channel_id=1, source_target_pairs={{0,2},{2,0},{1,3},{3,1},{4,6},{6,4},{5,7},{7,5},{8,10},{10,8},{9,1... | collective-permute-start | bytes 393224 | tf_op jit(solution)/shard_map/ppermute | solution.py:373
  39.4 1.4 %collective-permute-start.17 = (f32[256,128]{1,0:T(8,128)S(1)}, f32[256,128]{1,0:T(8,128)S(1)}, u32[]{:S(2)}, u32[]{:S(2)}) collective-permute-start(f32[256,128]{1,0:T(8,128)S(1)} %multiply_add_fusion.refs_4_), channel_id=1, source_target_pairs={{0,1},{1,0},{2,3},{3,2},{4,5},{5,4},{6,7},{7,6},{8,9},{9,8},{10,11... | collective-permute-start | bytes 393224 | tf_op jit(solution)/shard_map/ppermute | solution.py:330
  39.7 1.5 %collective-permute-start.14 = (f32[256,128]{1,0:T(8,128)S(1)}, f32[256,128]{1,0:T(8,128)S(1)}, u32[]{:S(2)}, u32[]{:S(2)}) collective-permute-start(f32[256,128]{1,0:T(8,128)S(1)} %get-tuple-element.44.refs_1_), channel_id=1, source_target_pairs={{0,1},{1,0},{2,3},{3,2},{4,5},{5,4},{6,7},{7,6},{8,9},{9,8},{10,11... | collective-permute-start | bytes 393224 | tf_op jit(solution)/shard_map/ppermute | solution.py:330
  40.2 1.3 %collective-permute-start.16 = (f32[256,128]{1,0:T(8,128)S(1)}, f32[256,128]{1,0:T(8,128)S(1)}, u32[]{:S(2)}, u32[]{:S(2)}) collective-permute-start(f32[256,128]{1,0:T(8,128)S(1)} %get-tuple-element.45.refs_3_), channel_id=1, source_target_pairs={{0,1},{1,0},{2,3},{3,2},{4,5},{5,4},{6,7},{7,6},{8,9},{9,8},{10,11... | collective-permute-start | bytes 393224 | tf_op jit(solution)/shard_map/ppermute | solution.py:330
  40.3 1.5 %collective-permute-start.15 = (f32[256,128]{1,0:T(8,128)S(1)}, f32[256,128]{1,0:T(8,128)S(1)}, u32[]{:S(2)}, u32[]{:S(2)}) collective-permute-start(f32[256,128]{1,0:T(8,128)S(1)} %get-tuple-element.48.refs_2_), channel_id=1, source_target_pairs={{0,1},{1,0},{2,3},{3,2},{4,5},{5,4},{6,7},{7,6},{8,9},{9,8},{10,11... | collective-permute-start | bytes 393224 | tf_op jit(solution)/shard_map/ppermute | solution.py:330
  46.6 1.4 %collective-permute-start.18 = (f32[256,128]{1,0:T(8,128)S(1)}, f32[256,128]{1,0:T(8,128)S(1)}, u32[]{:S(2)}, u32[]{:S(2)}) collective-permute-start(f32[256,128]{1,0:T(8,128)S(1)} %get-tuple-element.37), channel_id=1, source_target_pairs={{0,1},{1,0},{2,3},{3,2},{4,5},{5,4},{6,7},{7,6},{8,9},{9,8},{10,11... | collective-permute-start | bytes 393224 | tf_op jit(solution)/shard_map/ppermute | solution.py:330
  48.1 7.0 %collective-permute-start.19 = (f32[768,128]{1,0:T(8,128)S(1)}, f32[768,128]{1,0:T(8,128)S(1)}, u32[]{:S(2)}, u32[]{:S(2)}) collective-permute-start(f32[768,128]{1,0:T(8,128)S(1)} %get-tuple-element.42), channel_id=1, source_target_pairs={{0,1},{1,0},{2,3},{3,2},{4,5},{5,4},{6,7},{7,6},{8,9},{9,8},{10,11... | collective-permute-start | bytes 1179656 | tf_op jit(solution)/shard_map/ppermute | solution.py:330
  48.5 5.0 %collective-permute-start.23 = (f32[256,128]{1,0:T(8,128)S(1)}, f32[256,128]{1,0:T(8,128)S(1)}, u32[]{:S(2)}, u32[]{:S(2)}) collective-permute-start(f32[256,128]{1,0:T(8,128)S(1)} %add.205), channel_id=1, source_target_pairs={{0,2},{1,13},{2,0},{3,15},{4,6},{5,9},{6,4},{7,11},{8,10},{9,5},{1... | collective-permute-start | bytes 393224 | tf_op jit(solution)/shard_map/ppermute | solution.py:393
  53.4 5.0 %collective-permute-start.24 = (f32[256,128]{1,0:T(8,128)S(1)}, f32[256,128]{1,0:T(8,128)S(1)}, u32[]{:S(2)}, u32[]{:S(2)}) collective-permute-start(f32[256,128]{1,0:T(8,128)S(1)} %add.210), channel_id=1, source_target_pairs={{0,4},{1,3},{2,6},{3,1},{4,0},{5,7},{6,2},{7,5},{8,12},{9,11},{10,... | collective-permute-start | bytes 393224 | tf_op jit(solution)/shard_map/ppermute | solution.py:393
  55.1 5.7 %collective-permute-start.20 = (f32[3,2,64,128]{3,2,1,0:T(8,128)S(1)}, f32[3,2,64,128]{3,2,1,0:T(8,128)S(1)}, u32[]{:S(2)}, u32[]{:S(2)}) collective-permute-start(f32[3,2,64,128]{3,2,1,0:T(8,128)S(1)} %bitcast.48), channel_id=1, source_target_pairs={{0,4},{1,3},{2,6},{3,1},{4,0},{5,9},{6,2},{7,11},{8,12},{9,5},{10,... | collective-permute-start | bytes 589832 | tf_op jit(solution)/shard_map/ppermute | solution.py:354
  58.5 7.3 %collective-permute-start.25 = (f32[256,128]{1,0:T(8,128)S(1)}, f32[256,128]{1,0:T(8,128)S(1)}, u32[]{:S(2)}, u32[]{:S(2)}) collective-permute-start(f32[256,128]{1,0:T(8,128)S(1)} %add.211), channel_id=1, source_target_pairs={{0,8},{1,5},{2,10},{3,7},{4,12},{5,1},{6,14},{7,3},{8,0},{9,13},{1... | collective-permute-start | bytes 393224 | tf_op jit(solution)/shard_map/ppermute | solution.py:393
  61.0 4.3 %collective-permute-start.21 = (f32[2,64,64]{2,1,0:T(8,128)S(1)}, f32[2,64,64]{2,1,0:T(8,128)S(1)}, u32[]{:S(2)}, u32[]{:S(2)}) collective-permute-start(f32[2,64,64]{2,1,0:T(8,128)S(1)} %fusion.7), channel_id=1, source_target_pairs={{0,2},{2,0},{1,3},{3,1},{4,6},{6,4},{5,7},{7,5},{8,10},{10,8},{9,1... | collective-permute-start | bytes 98312 | tf_op jit(solution)/shard_map/ppermute | solution.py:373
  65.6 1.4 %collective-permute-start.22 = (f32[2,64,256]{2,1,0:T(8,128)S(1)}, f32[2,64,256]{2,1,0:T(8,128)S(1)}, u32[]{:S(2)}, u32[]{:S(2)}) collective-permute-start(f32[2,64,256]{2,1,0:T(8,128)S(1)} %fusion.2), channel_id=1, source_target_pairs={{0,1},{1,0},{2,3},{3,2},{4,5},{5,4},{6,7},{7,6},{8,9},{9,8},{10,11... | collective-permute-start | bytes 393224 | tf_op jit(solution)/shard_map/ppermute | solution.py:330

commit v6 on v5

--- a/solution.py
+++ b/solution.py
@@ -1,3 +1,5 @@
+import math
+
 import jax
 import jax.numpy as jnp
 import ml_dtypes
@@ -113,9 +115,9 @@
 
 
 def wave_kernel(windows, *refs, columns, group):
-    mine, theirs = refs[: columns + 1], refs[columns + 1 : 2 * columns + 2]
-    root, right, left, left_back, right_back = refs[2 * columns + 2 :][:5]
-    keep, send, pieces, state, modes, grad = refs[2 * columns + 7 :]
+    mine, theirs = refs[:2], refs[2:4]
+    root, right, left, left_back, right_back = refs[4:9]
+    keep, send, pieces, state, modes, grad = refs[9:]
     slots, size, _ = root.shape
     half = size // 2
     me, half_mine = windows[4 * slots], windows[4 * slots + 1]
@@ -123,10 +125,10 @@
 
     for blocks, side, mode in ((mine, half_mine, me), (theirs, 1 - half_mine, 1 - me)):
         for part in range(2):
-            rows = slice(part * size, (part + 1) * size)
             for tile in range(columns):
-                state[part, region(tile, side, size), :] = blocks[tile][rows, :]
-        modes[mode] = blocks[-1][...]
+                start = (2 * tile + part) * size
+                state[part, region(tile, side, size), :] = blocks[0][start : start + size, :]
+        modes[mode] = blocks[1][...]
     grad[...] = jnp.zeros_like(grad)
 
     def plane(mode, part):
@@ -274,8 +276,8 @@
 
 def waves(windows, mine, theirs, root):
     slots, size, _ = root.shape
-    columns = len(mine) - 1
-    group = 4 if slots % 4 == 0 else 1
+    columns = mine[0].shape[0] // (2 * size)
+    group = slots if slots <= 8 else math.gcd(slots, 4)
     pair = (2 * size, size)
     pieces = (slots, 2, size, size)
     tables = [jnp.asarray(t) for t in transform_tables(size)]
@@ -289,7 +291,7 @@
         grid_spec=pltpu.PrefetchScalarGridSpec(
             num_scalar_prefetch=1,
             grid=(1,),
-            in_specs=[whole_block(pair)] * (2 * columns + 2)
+            in_specs=[whole_block(mine[0].shape), whole_block(pair)] * 2
             + [whole_block(root.shape)]
             + [whole_block(t.shape) for t in tables],
             out_specs=[whole_block(s) for s in (pair, pair, pieces)],
@@ -373,25 +375,39 @@
     return lax.ppermute(block, "col", [(i, i if o is None else o) for i, o in enumerate(others)])
 
 
-def sum_tiles(block):
+def tile_sum_stages(beside_little):
     rows, cols = lax.axis_size("row"), lax.axis_size("col")
-    along_cols = [(0, 1 << k) for k in range((cols - 1).bit_length())]
-    along_rows = [(1 << k, 0) for k in range((rows - 1).bit_length())]
-    if len(along_rows) > 1:
-        turned = [(3, 0)] + along_cols + along_rows[:1] + along_rows[2:]
+    if beside_little and (rows, cols) == (4, 2):
+        first = [[(0, 1)], [(2, 0), (1, 0), (3, 0)]]
+        second = [[(3, 0)], [(0, 1), (1, 0), (1, 1)]]
     else:
-        turned = along_rows + along_cols
-    for steps in zip(along_cols + along_rows, turned, strict=True):
-        route = []
-        for row in range(rows):
-            for col in range(cols):
-                for mode in range(2):
-                    to_row, to_col = row ^ steps[mode][0], col ^ steps[mode][1]
-                    route.append(
-                        ((row * cols + col) * 2 + mode, (to_row * cols + to_col) * 2 + mode)
-                    )
-        block = block + lax.ppermute(block, ("row", "col", "mode"), route)
-    return block
+        along_cols = [[(0, 1 << k)] for k in range((cols - 1).bit_length())]
+        along_rows = [[(1 << k, 0)] for k in range((rows - 1).bit_length())]
+        first = along_cols + along_rows
+        second = along_rows + along_cols
+        if len(along_rows) > 1:
+            second = [[(3, 0)]] + along_cols + along_rows[:1] + along_rows[2:]
+    return [list(zip(*stage, strict=True)) for stage in zip(first, second, strict=True)]
+
+
+def sum_tiles(block, stages):
+    sums = []
+    rows, cols = lax.axis_size("row"), lax.axis_size("col")
+    for stage in stages:
+        arrived = []
+        for flips in stage:
+            route = []
+            for row in range(rows):
+                for col in range(cols):
+                    for mode in range(2):
+                        to_row, to_col = row ^ flips[mode][0], col ^ flips[mode][1]
+                        route.append(
+                            ((row * cols + col) * 2 + mode, (to_row * cols + to_col) * 2 + mode)
+                        )
+            arrived.append(lax.ppermute(block, ("row", "col", "mode"), route))
+        block = sum(arrived, start=block)
+        sums.append(block)
+    return sums
 
 
 def on_device(obj, probe, positions, counts, measured):
@@ -425,10 +441,11 @@
     wide = jnp.concatenate(
         [jnp.where(lower, strip, beside), jnp.where(lower, beside, strip)], axis=1
     )
+    tiles = [wide[:, :, tile * size : (tile + 1) * size] for tile in range(columns)]
     start = [
-        wide[:, :, tile * size : (tile + 1) * size].reshape(2 * size, size)
-        for tile in range(columns)
-    ] + [probe[0].reshape(2 * size, size)]
+        jnp.concatenate(tiles).reshape(columns * 2 * size, size),
+        probe[0].reshape(2 * size, size),
+    ]
 
     ext_rows = jnp.arange(size, dtype=jnp.int32)[:, None] + half_mine * size - half
     ext_rows = jnp.concatenate([ext_rows, ext_rows]) + row * tile_rows
@@ -439,6 +456,7 @@
         inside = rows_inside & (ext_cols >= 0) & (ext_cols < tile_cols * cols_count)
         rates.append(jnp.where(inside, jnp.float32(object_rate), 0.0))
 
+    rates = jnp.concatenate(rates)
     previous, current = start, start
     ahead, others = start, [swap_modes(x) for x in start]
     for iteration in range(ITERS):
@@ -447,23 +465,24 @@
         keep, send = placed(windows, pieces, columns, iteration == ITERS - 1)
         probe_grad, keep, send = lax.optimization_barrier((probe_grad, keep, send))
         previous = current
-        probe_grad = sum_tiles(probe_grad)
+        sums = sum_tiles(probe_grad, tile_sum_stages(iteration == ITERS - 1))
+        probe_grad = sums[-1]
         object_grad = keep + swap_modes(send)
         if iteration < ITERS - 1:
             object_grad = object_grad + jnp.where(paired, swap_neighbours(object_grad), 0.0)
+            object_grad, _ = lax.optimization_barrier((object_grad, sums[1]))
             parts = [
                 object_grad[tile * 2 * size : (tile + 1) * 2 * size] for tile in range(columns)
             ]
             from_low, from_high = from_cols((parts[0], parts[-1]), swap_cols)
             parts[0] = parts[0] + from_low
             parts[-1] = parts[-1] + from_high
-            current = [x - rate * g for x, rate, g in zip(ahead, rates, parts, strict=False)]
-            tiles = [x + momentum * (x - y) for x, y in zip(current, previous, strict=False)]
-            others = [swap_modes(x) for x in tiles]
-            new_probe = ahead[-1] - probe_step * probe_grad
-            current = current + [new_probe]
-            ahead = tiles + [new_probe + momentum * (new_probe - previous[-1])]
-            others = others + [swap_modes(ahead[-1])]
+            new_object = ahead[0] - rates * jnp.concatenate(parts)
+            probe_grad, new_object = lax.optimization_barrier((probe_grad, new_object))
+            new_probe = ahead[1] - probe_step * probe_grad
+            current = [new_object, new_probe]
+            ahead = [x + momentum * (x - y) for x, y in zip(current, previous, strict=True)]
+            others = [swap_modes(x) for x in ahead]
         else:
             object_grad = object_grad.reshape(2, columns, 2, half, size)
             given, owned = object_grad[0], object_grad[1]
@@ -476,7 +495,8 @@
                 + [owned[-1, :, :, :half] + from_high],
                 axis=2,
             )
-            held = jnp.concatenate([x.reshape(2, size, size) for x in ahead[:-1]], axis=2)
+            held = ahead[0].reshape(columns, 2, size, size)
+            held = jnp.concatenate([held[tile] for tile in range(columns)], axis=2)
             held = jnp.where(lower, held[:, :half], held[:, half:])
             strip = held[:, :, half : half + tile_cols] - object_rate * owned
 

time: 68 us -> 66.9 us (0.984)
  waiting for transfers between devices: 24.6 us -> 21.4 us
  starting transfers between devices: 22.5 us -> 24.6 us
  Pallas kernels: 13.2 us -> 12.3 us
  local copies, waits for them, and re-layouts: 1.99 us -> 2.74 us
    ppermute x6 -> x7, starting transfers between devices: 9.48 us -> 11.5 us  [sum_tiles(): arrived.append(lax.ppermute(block, ('row', 'col', 'mode'), route))]
    ppermute x4, starting transfers between devices: 6.31 us -> 8.22 us  [swap_neighbours(): return lax.ppermute(block, ('row', 'col', 'mode'), route)]
    ppermute x6 -> x7, waiting for transfers between devices: 17.1 us -> 15.3 us  [sum_tiles(): arrived.append(lax.ppermute(block, ('row', 'col', 'mode'), route))]
    ppermute x4, waiting for transfers between devices: 1.73 us -> 0.01 us  [swap_neighbours(): return lax.ppermute(block, ('row', 'col', 'mode'), route)]
    ppermute x13 -> x9, starting transfers between devices: 3.15 us -> 1.58 us  [swap_modes(): return lax.ppermute(block, 'mode', [(0, 1), (1, 0)])]
    pallas_call x2, Pallas kernels: 9.68 us -> 8.78 us  [waves(): pl.pallas_call(body, out_shape=[jax.ShapeDtypeStruct(s, jnp.float32) for...]
    unnamed x16, local copies, waits for them, and re-layouts: 1.93 us -> 2.66 us
    ppermute x13 -> x9, waiting for transfers between devices: 3.04 us -> 3.17 us  [swap_modes(): return lax.ppermute(block, 'mode', [(0, 1), (1, 0)])]
  transfers between devices with their start and end apart: 26 -> 23, of which waited for: 18 -> 10; matrix products, arithmetic and copies ran while one was open for 3% -> 3% of each run, Pallas kernels for 5% -> 5%
where the time goes in v6:
time: 66.9 us; the launch traced here: 66.7 us
  starting transfers between devices  24.6 us (37%)
  waiting for transfers between devices  21.4 us (32%)
  Pallas kernels  12.3 us (18%)
  other arithmetic  3.86 us (6%)
  local copies, waits for them, and re-layouts  2.74 us (4%)
  between operations  1.69 us (3%)
    ppermute x7, waiting for transfers between devices, sum_tiles(): arrived.append(lax.ppermute(block, ('row', 'col', 'mode'), route))  15.3 us
    ppermute x7, starting transfers between devices, sum_tiles(): arrived.append(lax.ppermute(block, ('row', 'col', 'mode'), route))  11.5 us
    pallas_call x2, Pallas kernels, waves(): pl.pallas_call(body, out_shape=[jax.ShapeDtypeStruct(s, jnp.float32) for...  8.78 us
    ppermute x4, starting transfers between devices, swap_neighbours(): return lax.ppermute(block, ('row', 'col', 'mode'), route)  8.22 us
    ppermute x3, starting transfers between devices, swap_cols(): lax.ppermute(block, 'col', [(i, i if o is None else o) for i, o in enumer...  3.31 us
    ppermute x9, waiting for transfers between devices, swap_modes(): return lax.ppermute(block, 'mode', [(0, 1), (1, 0)])  3.17 us
    ppermute x3, waiting for transfers between devices, swap_cols(): lax.ppermute(block, 'col', [(i, i if o is None else o) for i, o in enumer...  2.92 us
    unnamed x16, local copies, waits for them, and re-layouts  2.66 us
  transfers between devices with their start and end apart: 23, of which 10 were waited for; matrix products, arithmetic and copies ran while one was open for 3% of the time, Pallas kernels for 5%

profile of v6, /device:TPU:0, one launch (start us, length us, event | category | flops | bytes accessed | tf_op | source)
XLA Modules:
  0.0 66.7 jit_solution(175282219139980431)
XLA Ops:
  0.6 1.0 %slice_select_fusion.1 = f32[2,64,256]{2,1,0:T(8,128)S(1)} fusion(f32[2,128,256]{2,1,0:T(8,128)} %param.14, pred[]{:T(512)S(6)} %eq.15), kind=kLoop, calls=%fused_computation.24 | loop fusion | flops 32768 | bytes 393217 | tf_op jit(solution)/shard_map/jit(_where)/select_n | solution.py:432
  1.6 3.1 %collective-permute-start = (f32[2,64,256]{2,1,0:T(8,128)S(1)}, f32[2,64,256]{2,1,0:T(8,128)S(1)}, u32[]{:S(2)}, u32[]{:S(2)}) collective-permute-start(f32[2,64,256]{2,1,0:T(8,128)S(1)} %slice_select_fusion.1), channel_id=1, source_target_pairs={{0,4},{1,3},{2,6},{3,1},{4,0},{5,9},{6,2},{7,11},{8,12},{9,5},{10,... | collective-permute-start | bytes 393224 | tf_op jit(solution)/shard_map/ppermute | solution.py:356
  4.7 0.1 slice_select_fusion.4
  4.8 0.0 copy-start.6
  4.8 1.4 %collective-permute-start.2 = (f32[2,64,64]{2,1,0:T(8,128)S(1)}, f32[2,64,64]{2,1,0:T(8,128)S(1)}, u32[]{:S(2)}, u32[]{:S(2)}) collective-permute-start(f32[2,64,64]{2,1,0:T(8,128)S(1)} %slice_select_fusion.4), channel_id=1, source_target_pairs={{0,6},{1,3},{2,4},{3,1},{4,2},{5,11},{6,0},{7,9},{8,14},{9,7},{10,... | collective-permute-start | bytes 98312 | tf_op jit(solution)/shard_map/ppermute | solution.py:356
  6.3 0.2 collective-permute-start.1
  6.5 0.1 pad_add_fusion.place
  7.2 0.0 copy-start.7
  7.2 0.7 copy-done.7
  7.9 1.2 %copy-done = f32[1,1,16,128,128]{4,3,2,1,0:T(8,128)S(1)} copy-done((f32[1,1,16,128,128]{4,3,2,1,0:T(8,128)S(1)}, f32[1,1,16,128,128]{4,3,2,1,0:T(8,128)}, u32[]{:S(2)}) %copy-start) | copy-done | bytes 1048600
  9.1 1.6 %prepared.1 = (f32[8,128,128]{2,1,0:T(8,128)S(1)}, s32[34]{0:T(128)S(1)}) custom-call(s32[4]{0:T(128)S(1)} %pad_add_fusion.place, s32[2,16]{1,0:T(2,128)S(1)} %bitcast.36, s32[1,1]{1,0:T(1,128)S(6)} %copy.16.counts, f32[8,2,128,128]{3,2,1,0:T(8,128)S(1)} %bitcast.33, bf16[128,128]{1,0:T(8,128)(2,1)S(1)} %copy-done.6), custom_call_target="tpu_custom_call" | custom-call | flops 100663296 | bytes 1048576 | tf_op jit(solution)/shard_map/prepared/pallas_call | solution.py:244
  10.7 0.0 collective-permute-done.2
  10.8 0.0 collective-permute-done.1
  10.8 0.2 fusion.6
  11.1 0.0 copy-start.1
  11.1 0.0 copy-start.2
  11.1 0.0 copy-start.3
  11.1 0.0 copy-start.4
  11.1 0.0 copy-start.5
  11.2 0.1 collective-permute-start.3
  11.2 0.7 %copy-done.1 = f32[1,2,128,128]{3,2,1,0:T(8,128)S(1)} copy-done((f32[1,2,128,128]{3,2,1,0:T(8,128)S(1)}, f32[1,2,128,128]{3,2,1,0:T(8,128)}, u32[]{:S(2)}) %copy-start.1) | copy-done | bytes 131096
  12.0 1.3 %collective-permute-done.4.refs_4_ = f32[256,128]{1,0:T(8,128)S(1)} collective-permute-done((f32[256,128]{1,0:T(8,128)S(1)}, f32[256,128]{1,0:T(8,128)S(1)}, u32[]{:S(2)}, u32[]{:S(2)}) %collective-permute-start.4) | collective-permute-done | bytes 131104 | tf_op jit(solution)/shard_map/ppermute | solution.py:332
  13.3 0.0 collective-permute-done.3.refs_3_
  13.3 4.4 %waves.2 = (f32[256,128]{1,0:T(8,128)S(1)}, f32[256,128]{1,0:T(8,128)S(1)}, f32[8,2,128,128]{3,2,1,0:T(8,128)S(1)}) custom-call(s32[34]{0:T(128)S(1)} %get-tuple-element.28.refs_0_, f32[768,128]{1,0:T(8,128)S(1)} %bitcast.32, f32[256,128]{1,0:T(8,128)S(1)} %bitcast.35, f32[768,128]{1,0:T(8,128)S(1)} %collective-permute-done.3.refs_3_, ...), custom_call_target="tpu_custom_call" | custom-call | tf_op jit(solution)/shard_map/waves/pallas_call | solution.py:288
  17.7 0.2 collective-permute-start.5
  17.9 1.0 %placed.2 = (f32[768,128]{1,0:T(8,128)S(1)}, f32[768,128]{1,0:T(8,128)S(1)}) custom-call(s32[34]{0:T(128)S(1)} %get-tuple-element.28.refs_0_, f32[8,2,128,128]{3,2,1,0:T(8,128)S(1)} %get-tuple-element.33.refs_1_), custom_call_target="tpu_custom_call" | custom-call | tf_op jit(solution)/shard_map/placed/pallas_call | solution.py:316
  18.9 0.2 collective-permute-done.5
  19.2 0.2 collective-permute-start.9
  19.4 1.8 %collective-permute-start.6 = (f32[256,128]{1,0:T(8,128)S(1)}, f32[256,128]{1,0:T(8,128)S(1)}, u32[]{:S(2)}, u32[]{:S(2)}) collective-permute-start(f32[256,128]{1,0:T(8,128)S(1)} %add.182), channel_id=1, source_target_pairs={{0,2},{1,13},{2,0},{3,15},{4,6},{5,9},{6,4},{7,11},{8,10},{9,5},{1... | collective-permute-start | bytes 393224 | tf_op jit(solution)/shard_map/ppermute | solution.py:407
  21.2 0.0 collective-permute-done.9
  21.2 0.1 add.194
  21.3 1.7 %collective-permute-start.10 = (f32[768,128]{1,0:T(8,128)S(1)}, f32[768,128]{1,0:T(8,128)S(1)}, u32[]{:S(2)}, u32[]{:S(2)}) collective-permute-start(f32[768,128]{1,0:T(8,128)S(1)} %add.194), channel_id=1, source_target_pairs={{0,4},{1,3},{2,6},{3,1},{4,0},{5,9},{6,2},{7,11},{8,12},{9,5},{10,... | collective-permute-start | bytes 1179656 | tf_op jit(solution)/shard_map/ppermute | solution.py:356
  23.0 1.4 %collective-permute-done.6 = f32[256,128]{1,0:T(8,128)S(1)} collective-permute-done((f32[256,128]{1,0:T(8,128)S(1)}, f32[256,128]{1,0:T(8,128)S(1)}, u32[]{:S(2)}, u32[]{:S(2)}) %collective-permute-start.6) | collective-permute-done | bytes 131104 | tf_op jit(solution)/shard_map/ppermute | solution.py:407
  24.4 2.0 %collective-permute-start.7 = (f32[256,128]{1,0:T(8,128)S(1)}, f32[256,128]{1,0:T(8,128)S(1)}, u32[]{:S(2)}, u32[]{:S(2)}) collective-permute-start(f32[256,128]{1,0:T(8,128)S(1)} %add.183), channel_id=1, source_target_pairs={{0,4},{1,3},{2,6},{3,1},{4,0},{5,7},{6,2},{7,5},{8,12},{9,11},{10,... | collective-permute-start | bytes 393224 | tf_op jit(solution)/shard_map/ppermute | solution.py:407
  26.4 5.3 %collective-permute-done.7 = f32[256,128]{1,0:T(8,128)S(1)} collective-permute-done((f32[256,128]{1,0:T(8,128)S(1)}, f32[256,128]{1,0:T(8,128)S(1)}, u32[]{:S(2)}, u32[]{:S(2)}) %collective-permute-start.7) | collective-permute-done | bytes 131104 | tf_op jit(solution)/shard_map/ppermute | solution.py:407
  31.7 1.7 %collective-permute-start.8 = (f32[256,128]{1,0:T(8,128)S(1)}, f32[256,128]{1,0:T(8,128)S(1)}, u32[]{:S(2)}, u32[]{:S(2)}) collective-permute-start(f32[256,128]{1,0:T(8,128)S(1)} %add.184), channel_id=1, source_target_pairs={{0,8},{1,5},{2,10},{3,7},{4,12},{5,1},{6,14},{7,3},{8,0},{9,13},{1... | collective-permute-start | bytes 393224 | tf_op jit(solution)/shard_map/ppermute | solution.py:407
  33.5 1.6 %collective-permute-start.11 = (f32[256,128]{1,0:T(8,128)S(1)}, f32[256,128]{1,0:T(8,128)S(1)}, u32[]{:S(2)}, u32[]{:S(2)}) collective-permute-start(f32[256,128]{1,0:T(8,128)S(1)} %slice_select_fusion.2), channel_id=1, source_target_pairs={{0,2},{2,0},{1,3},{3,1},{4,6},{6,4},{5,7},{7,5},{8,10},{10,8},{9,1... | collective-permute-start | bytes 393224 | tf_op jit(solution)/shard_map/ppermute | solution.py:375
  35.0 0.1 and_select_fusion.2
  35.1 3.9 %collective-permute-done.8 = f32[256,128]{1,0:T(8,128)S(1)} collective-permute-done((f32[256,128]{1,0:T(8,128)S(1)}, f32[256,128]{1,0:T(8,128)S(1)}, u32[]{:S(2)}, u32[]{:S(2)}) %collective-permute-start.8) | collective-permute-done | bytes 131104 | tf_op jit(solution)/shard_map/ppermute | solution.py:407
  39.0 0.0 collective-permute-done.11
  39.1 0.1 fusion.1
  39.2 0.1 collective-permute-start.12
  39.3 0.6 collective-permute-start.13
  39.9 1.3 %collective-permute-done.13.refs_4_ = f32[256,128]{1,0:T(8,128)S(1)} collective-permute-done((f32[256,128]{1,0:T(8,128)S(1)}, f32[256,128]{1,0:T(8,128)S(1)}, u32[]{:S(2)}, u32[]{:S(2)}) %collective-permute-start.13) | collective-permute-done | bytes 131104 | tf_op jit(solution)/shard_map/ppermute | solution.py:332
  41.2 4.4 %waves.3 = (f32[256,128]{1,0:T(8,128)S(1)}, f32[256,128]{1,0:T(8,128)S(1)}, f32[8,2,128,128]{3,2,1,0:T(8,128)S(1)}) custom-call(s32[34]{0:T(128)S(1)} %get-tuple-element.28.refs_0_, f32[768,128]{1,0:T(8,128)S(1)} %multiply_add_fusion.refs_1_, f32[256,128]{1,0:T(8,128)S(1)} %multiply_add_fusion.1.refs_2_, f32[768,128]{1,0:T(8,128)S(1)} %collective-permute-done.12.refs_3_, ...), custom_call_target="tpu_custom_call" | custom-call | tf_op jit(solution)/shard_map/waves/pallas_call | solution.py:288
  45.6 0.2 collective-permute-start.14
  45.8 1.0 %placed.3 = (f32[768,128]{1,0:T(8,128)S(1)}, f32[768,128]{1,0:T(8,128)S(1)}) custom-call(s32[34]{0:T(128)S(1)} %get-tuple-element.28.refs_0_, f32[8,2,128,128]{3,2,1,0:T(8,128)S(1)} %get-tuple-element.44.refs_1_), custom_call_target="tpu_custom_call" | custom-call | tf_op jit(solution)/shard_map/placed/pallas_call | solution.py:316
  46.7 0.3 collective-permute-done.14
  47.0 0.2 collective-permute-start.15
  47.3 1.6 %collective-permute-start.19 = (f32[256,128]{1,0:T(8,128)S(1)}, f32[256,128]{1,0:T(8,128)S(1)}, u32[]{:S(2)}, u32[]{:S(2)}) collective-permute-start(f32[256,128]{1,0:T(8,128)S(1)} %add.200), channel_id=1, source_target_pairs={{0,2},{1,13},{2,0},{3,15},{4,6},{5,9},{6,4},{7,11},{8,10},{9,5},{1... | collective-permute-start | bytes 393224 | tf_op jit(solution)/shard_map/ppermute | solution.py:407
  48.9 2.0 %collective-permute-start.16 = (f32[3,2,64,128]{3,2,1,0:T(8,128)S(1)}, f32[3,2,64,128]{3,2,1,0:T(8,128)S(1)}, u32[]{:S(2)}, u32[]{:S(2)}) collective-permute-start(f32[3,2,64,128]{3,2,1,0:T(8,128)S(1)} %bitcast.41), channel_id=1, source_target_pairs={{0,4},{1,3},{2,6},{3,1},{4,0},{5,9},{6,2},{7,11},{8,12},{9,5},{10,... | collective-permute-start | bytes 589832 | tf_op jit(solution)/shard_map/ppermute | solution.py:356
  50.9 1.4 %collective-permute-done.19 = f32[256,128]{1,0:T(8,128)S(1)} collective-permute-done((f32[256,128]{1,0:T(8,128)S(1)}, f32[256,128]{1,0:T(8,128)S(1)}, u32[]{:S(2)}, u32[]{:S(2)}) %collective-permute-start.19) | collective-permute-done | bytes 131104 | tf_op jit(solution)/shard_map/ppermute | solution.py:407
  52.3 1.6 %collective-permute-start.20 = (f32[256,128]{1,0:T(8,128)S(1)}, f32[256,128]{1,0:T(8,128)S(1)}, u32[]{:S(2)}, u32[]{:S(2)}) collective-permute-start(f32[256,128]{1,0:T(8,128)S(1)} %add.205), channel_id=1, source_target_pairs={{0,8},{1,3},{2,10},{3,1},{4,12},{5,7},{6,14},{7,5},{8,0},{9,11},{1... | collective-permute-start | bytes 393224 | tf_op jit(solution)/shard_map/ppermute | solution.py:407
  53.9 2.3 %collective-permute-start.21 = (f32[256,128]{1,0:T(8,128)S(1)}, f32[256,128]{1,0:T(8,128)S(1)}, u32[]{:S(2)}, u32[]{:S(2)}) collective-permute-start(f32[256,128]{1,0:T(8,128)S(1)} %add.205), channel_id=1, source_target_pairs={{0,4},{1,5},{2,6},{3,7},{4,0},{5,1},{6,2},{7,3},{8,12},{9,13},{10,... | collective-permute-start | bytes 393224 | tf_op jit(solution)/shard_map/ppermute | solution.py:407
  56.2 0.6 collective-permute-start.22
  56.8 0.1 fusion.8
  56.9 1.6 %collective-permute-start.17 = (f32[2,64,64]{2,1,0:T(8,128)S(1)}, f32[2,64,64]{2,1,0:T(8,128)S(1)}, u32[]{:S(2)}, u32[]{:S(2)}) collective-permute-start(f32[2,64,64]{2,1,0:T(8,128)S(1)} %fusion.8), channel_id=1, source_target_pairs={{0,2},{2,0},{1,3},{3,1},{4,6},{6,4},{5,7},{7,5},{8,10},{10,8},{9,1... | collective-permute-start | bytes 98312 | tf_op jit(solution)/shard_map/ppermute | solution.py:375
  58.5 2.9 %collective-permute-done.17 = f32[2,64,64]{2,1,0:T(8,128)S(1)} collective-permute-done((f32[2,64,64]{2,1,0:T(8,128)S(1)}, f32[2,64,64]{2,1,0:T(8,128)S(1)}, u32[]{:S(2)}, u32[]{:S(2)}) %collective-permute-start.17) | collective-permute-done | bytes 32800 | tf_op jit(solution)/shard_map/ppermute | solution.py:375
  61.4 0.1 fusion.9
  61.5 0.2 fusion.4
  61.7 0.1 collective-permute-start.18
  61.8 3.4 %collective-permute-done.22 = f32[256,128]{1,0:T(8,128)S(1)} collective-permute-done((f32[256,128]{1,0:T(8,128)S(1)}, f32[256,128]{1,0:T(8,128)S(1)}, u32[]{:S(2)}, u32[]{:S(2)}) %collective-permute-start.22) | collective-permute-done | bytes 131104 | tf_op jit(solution)/shard_map/ppermute | solution.py:407
  65.2 0.7 %multiply_subtract_fusion = f32[256,128]{1,0:T(8,128)} fusion(f32[256,128]{1,0:T(8,128)S(1)} %multiply_add_fusion.1.refs_2_, f32[256,128]{1,0:T(8,128)S(1)} %collective-permute-done.22, f32[256,128]{1,0:T(8,128)S(1)} %collective-permute-done.21, f32[256,128]{1,0:T(8,128)S(1)} %add.205, f32[256,128]{1,0:T(8,128)S(1)} %collective-permute-done.20), kind=kLoop, calls=%fused_computation.20 | loop fusion | flops 163840 | bytes 786432 | tf_op jit(solution)/shard_map/sub | solution.py:507
  65.9 0.7 %pad_maximum_fusion.2 = f32[2,128,256]{2,1,0:T(8,128)} fusion(f32[2,64,256]{2,1,0:T(8,128)S(1)} %get-tuple-element.65, f32[2,64,256]{2,1,0:T(8,128)S(1)} %get-tuple-element.64), kind=kLoop, calls=%fused_computation.11 | loop fusion | flops 65536 | bytes 524288 | tf_op jit(solution)/shard_map/concatenate | solution.py:504
  (43 shorter events, 0.6 us)
Async XLA Ops:
  1.6 9.2 %collective-permute-start = (f32[2,64,256]{2,1,0:T(8,128)S(1)}, f32[2,64,256]{2,1,0:T(8,128)S(1)}, u32[]{:S(2)}, u32[]{:S(2)}) collective-permute-start(f32[2,64,256]{2,1,0:T(8,128)S(1)} %slice_select_fusion.1), channel_id=1, source_target_pairs={{0,4},{1,3},{2,6},{3,1},{4,0},{5,9},{6,2},{7,11},{8,12},{9,5},{10,... | collective-permute-start | bytes 393224 | tf_op jit(solution)/shard_map/ppermute | solution.py:356
  4.8 2.4 %copy-start.6 = (bf16[128,128]{1,0:T(8,128)(2,1)S(1)}, bf16[128,128]{1,0:T(8,128)(2,1)}, u32[]{:S(2)}) copy-start(bf16[128,128]{1,0:T(8,128)(2,1)} %constant.86.clone.order) | copy-start | bytes 98308
  4.8 5.9 %collective-permute-start.2 = (f32[2,64,64]{2,1,0:T(8,128)S(1)}, f32[2,64,64]{2,1,0:T(8,128)S(1)}, u32[]{:S(2)}, u32[]{:S(2)}) collective-permute-start(f32[2,64,64]{2,1,0:T(8,128)S(1)} %slice_select_fusion.4), channel_id=1, source_target_pairs={{0,6},{1,3},{2,4},{3,1},{4,2},{5,11},{6,0},{7,9},{8,14},{9,7},{10,... | collective-permute-start | bytes 98312 | tf_op jit(solution)/shard_map/ppermute | solution.py:356
  6.3 4.5 %collective-permute-start.1 = (f32[2,64,64]{2,1,0:T(8,128)S(1)}, f32[2,64,64]{2,1,0:T(8,128)S(1)}, u32[]{:S(2)}, u32[]{:S(2)}) collective-permute-start(f32[2,64,64]{2,1,0:T(8,128)S(1)} %slice_select_fusion.4), channel_id=1, source_target_pairs={{0,2},{2,0},{1,3},{3,1},{4,6},{6,4},{5,7},{7,5},{8,10},{10,8},{9,1... | collective-permute-start | bytes 98312 | tf_op jit(solution)/shard_map/ppermute | solution.py:375
  7.2 0.7 %copy-start.7 = (s32[1,1,16,2]{2,3,1,0:T(2,128)S(1)}, s32[1,1,16,2]{2,3,1,0:T(2,128)}, u32[]{:S(2)}) copy-start(s32[1,1,16,2]{2,3,1,0:T(2,128)} %param.16) | copy-start | bytes 388
  7.9 1.2 %copy-start = (f32[1,1,16,128,128]{4,3,2,1,0:T(8,128)S(1)}, f32[1,1,16,128,128]{4,3,2,1,0:T(8,128)}, u32[]{:S(2)}) copy-start(f32[1,1,16,128,128]{4,3,2,1,0:T(8,128)} %param.18) | copy-start | bytes 3145732
  11.1 0.9 %copy-start.1 = (f32[1,2,128,128]{3,2,1,0:T(8,128)S(1)}, f32[1,2,128,128]{3,2,1,0:T(8,128)}, u32[]{:S(2)}) copy-start(f32[1,2,128,128]{3,2,1,0:T(8,128)} %param.15) | copy-start | bytes 393220
  11.1 2.2 %copy-start.2 = (bf16[2,128,256]{2,1,0:T(8,128)(2,1)S(1)}, bf16[2,128,256]{2,1,0:T(8,128)(2,1)}, u32[]{:S(2)}) copy-start(bf16[2,128,256]{2,1,0:T(8,128)(2,1)} %constant.87.clone.refs_6_) | copy-start | bytes 393220
  11.1 2.2 %copy-start.3 = (bf16[2,256,128]{2,1,0:T(8,128)(2,1)S(1)}, bf16[2,256,128]{2,1,0:T(8,128)(2,1)}, u32[]{:S(2)}) copy-start(bf16[2,256,128]{2,1,0:T(8,128)(2,1)} %constant.88.clone.refs_7_) | copy-start | bytes 393220
  11.1 2.2 %copy-start.4 = (bf16[2,256,128]{2,1,0:T(8,128)(2,1)S(1)}, bf16[2,256,128]{2,1,0:T(8,128)(2,1)}, u32[]{:S(2)}) copy-start(bf16[2,256,128]{2,1,0:T(8,128)(2,1)} %constant.89.clone.refs_8_) | copy-start | bytes 393220
  11.1 2.2 %copy-start.5 = (bf16[2,128,256]{2,1,0:T(8,128)(2,1)S(1)}, bf16[2,128,256]{2,1,0:T(8,128)(2,1)}, u32[]{:S(2)}) copy-start(bf16[2,128,256]{2,1,0:T(8,128)(2,1)} %constant.90.clone.refs_9_) | copy-start | bytes 393220
  11.2 2.2 %collective-permute-start.3 = (f32[768,128]{1,0:T(8,128)S(1)}, f32[768,128]{1,0:T(8,128)S(1)}, u32[]{:S(2)}, u32[]{:S(2)}) collective-permute-start(f32[768,128]{1,0:T(8,128)S(1)} %bitcast.31), channel_id=1, source_target_pairs={{0,1},{1,0},{2,3},{3,2},{4,5},{5,4},{6,7},{7,6},{8,9},{9,8},{10,11... | collective-permute-start | bytes 1179656 | tf_op jit(solution)/shard_map/ppermute | solution.py:332
  12.0 1.3 %collective-permute-start.4 = (f32[256,128]{1,0:T(8,128)S(1)}, f32[256,128]{1,0:T(8,128)S(1)}, u32[]{:S(2)}, u32[]{:S(2)}) collective-permute-start(f32[256,128]{1,0:T(8,128)S(1)} %bitcast.34), channel_id=1, source_target_pairs={{0,1},{1,0},{2,3},{3,2},{4,5},{5,4},{6,7},{7,6},{8,9},{9,8},{10,11... | collective-permute-start | bytes 393224 | tf_op jit(solution)/shard_map/ppermute | solution.py:332
  17.7 1.4 %collective-permute-start.5 = (f32[256,128]{1,0:T(8,128)S(1)}, f32[256,128]{1,0:T(8,128)S(1)}, u32[]{:S(2)}, u32[]{:S(2)}) collective-permute-start(f32[256,128]{1,0:T(8,128)S(1)} %get-tuple-element.32), channel_id=1, source_target_pairs={{0,1},{1,0},{2,3},{3,2},{4,5},{5,4},{6,7},{7,6},{8,9},{9,8},{10,11... | collective-permute-start | bytes 393224 | tf_op jit(solution)/shard_map/ppermute | solution.py:332
  19.2 2.0 %collective-permute-start.9 = (f32[768,128]{1,0:T(8,128)S(1)}, f32[768,128]{1,0:T(8,128)S(1)}, u32[]{:S(2)}, u32[]{:S(2)}) collective-permute-start(f32[768,128]{1,0:T(8,128)S(1)} %get-tuple-element.38), channel_id=1, source_target_pairs={{0,1},{1,0},{2,3},{3,2},{4,5},{5,4},{6,7},{7,6},{8,9},{9,8},{10,11... | collective-permute-start | bytes 1179656 | tf_op jit(solution)/shard_map/ppermute | solution.py:332
  19.4 5.0 %collective-permute-start.6 = (f32[256,128]{1,0:T(8,128)S(1)}, f32[256,128]{1,0:T(8,128)S(1)}, u32[]{:S(2)}, u32[]{:S(2)}) collective-permute-start(f32[256,128]{1,0:T(8,128)S(1)} %add.182), channel_id=1, source_target_pairs={{0,2},{1,13},{2,0},{3,15},{4,6},{5,9},{6,4},{7,11},{8,10},{9,5},{1... | collective-permute-start | bytes 393224 | tf_op jit(solution)/shard_map/ppermute | solution.py:407
  21.3 12.1 %collective-permute-start.10 = (f32[768,128]{1,0:T(8,128)S(1)}, f32[768,128]{1,0:T(8,128)S(1)}, u32[]{:S(2)}, u32[]{:S(2)}) collective-permute-start(f32[768,128]{1,0:T(8,128)S(1)} %add.194), channel_id=1, source_target_pairs={{0,4},{1,3},{2,6},{3,1},{4,0},{5,9},{6,2},{7,11},{8,12},{9,5},{10,... | collective-permute-start | bytes 1179656 | tf_op jit(solution)/shard_map/ppermute | solution.py:356
  24.4 7.3 %collective-permute-start.7 = (f32[256,128]{1,0:T(8,128)S(1)}, f32[256,128]{1,0:T(8,128)S(1)}, u32[]{:S(2)}, u32[]{:S(2)}) collective-permute-start(f32[256,128]{1,0:T(8,128)S(1)} %add.183), channel_id=1, source_target_pairs={{0,4},{1,3},{2,6},{3,1},{4,0},{5,7},{6,2},{7,5},{8,12},{9,11},{10,... | collective-permute-start | bytes 393224 | tf_op jit(solution)/shard_map/ppermute | solution.py:407
  31.7 7.3 %collective-permute-start.8 = (f32[256,128]{1,0:T(8,128)S(1)}, f32[256,128]{1,0:T(8,128)S(1)}, u32[]{:S(2)}, u32[]{:S(2)}) collective-permute-start(f32[256,128]{1,0:T(8,128)S(1)} %add.184), channel_id=1, source_target_pairs={{0,8},{1,5},{2,10},{3,7},{4,12},{5,1},{6,14},{7,3},{8,0},{9,13},{1... | collective-permute-start | bytes 393224 | tf_op jit(solution)/shard_map/ppermute | solution.py:407
  33.5 5.6 %collective-permute-start.11 = (f32[256,128]{1,0:T(8,128)S(1)}, f32[256,128]{1,0:T(8,128)S(1)}, u32[]{:S(2)}, u32[]{:S(2)}) collective-permute-start(f32[256,128]{1,0:T(8,128)S(1)} %slice_select_fusion.2), channel_id=1, source_target_pairs={{0,2},{2,0},{1,3},{3,1},{4,6},{6,4},{5,7},{7,5},{8,10},{10,8},{9,1... | collective-permute-start | bytes 393224 | tf_op jit(solution)/shard_map/ppermute | solution.py:375
  39.2 2.0 %collective-permute-start.12 = (f32[768,128]{1,0:T(8,128)S(1)}, f32[768,128]{1,0:T(8,128)S(1)}, u32[]{:S(2)}, u32[]{:S(2)}) collective-permute-start(f32[768,128]{1,0:T(8,128)S(1)} %multiply_add_fusion.refs_1_), channel_id=1, source_target_pairs={{0,1},{1,0},{2,3},{3,2},{4,5},{5,4},{6,7},{7,6},{8,9},{9,8},{10,11... | collective-permute-start | bytes 1179656 | tf_op jit(solution)/shard_map/ppermute | solution.py:332
  39.3 1.9 %collective-permute-start.13 = (f32[256,128]{1,0:T(8,128)S(1)}, f32[256,128]{1,0:T(8,128)S(1)}, u32[]{:S(2)}, u32[]{:S(2)}) collective-permute-start(f32[256,128]{1,0:T(8,128)S(1)} %multiply_add_fusion.1.refs_2_), channel_id=1, source_target_pairs={{0,1},{1,0},{2,3},{3,2},{4,5},{5,4},{6,7},{7,6},{8,9},{9,8},{10,11... | collective-permute-start | bytes 393224 | tf_op jit(solution)/shard_map/ppermute | solution.py:332
  45.6 1.4 %collective-permute-start.14 = (f32[256,128]{1,0:T(8,128)S(1)}, f32[256,128]{1,0:T(8,128)S(1)}, u32[]{:S(2)}, u32[]{:S(2)}) collective-permute-start(f32[256,128]{1,0:T(8,128)S(1)} %get-tuple-element.43), channel_id=1, source_target_pairs={{0,1},{1,0},{2,3},{3,2},{4,5},{5,4},{6,7},{7,6},{8,9},{9,8},{10,11... | collective-permute-start | bytes 393224 | tf_op jit(solution)/shard_map/ppermute | solution.py:332
  47.0 1.8 %collective-permute-start.15 = (f32[768,128]{1,0:T(8,128)S(1)}, f32[768,128]{1,0:T(8,128)S(1)}, u32[]{:S(2)}, u32[]{:S(2)}) collective-permute-start(f32[768,128]{1,0:T(8,128)S(1)} %get-tuple-element.48), channel_id=1, source_target_pairs={{0,1},{1,0},{2,3},{3,2},{4,5},{5,4},{6,7},{7,6},{8,9},{9,8},{10,11... | collective-permute-start | bytes 1179656 | tf_op jit(solution)/shard_map/ppermute | solution.py:332
  47.3 5.0 %collective-permute-start.19 = (f32[256,128]{1,0:T(8,128)S(1)}, f32[256,128]{1,0:T(8,128)S(1)}, u32[]{:S(2)}, u32[]{:S(2)}) collective-permute-start(f32[256,128]{1,0:T(8,128)S(1)} %add.200), channel_id=1, source_target_pairs={{0,2},{1,13},{2,0},{3,15},{4,6},{5,9},{6,4},{7,11},{8,10},{9,5},{1... | collective-permute-start | bytes 393224 | tf_op jit(solution)/shard_map/ppermute | solution.py:407
  48.9 7.9 %collective-permute-start.16 = (f32[3,2,64,128]{3,2,1,0:T(8,128)S(1)}, f32[3,2,64,128]{3,2,1,0:T(8,128)S(1)}, u32[]{:S(2)}, u32[]{:S(2)}) collective-permute-start(f32[3,2,64,128]{3,2,1,0:T(8,128)S(1)} %bitcast.41), channel_id=1, source_target_pairs={{0,4},{1,3},{2,6},{3,1},{4,0},{5,9},{6,2},{7,11},{8,12},{9,5},{10,... | collective-permute-start | bytes 589832 | tf_op jit(solution)/shard_map/ppermute | solution.py:356
  52.3 9.4 %collective-permute-start.20 = (f32[256,128]{1,0:T(8,128)S(1)}, f32[256,128]{1,0:T(8,128)S(1)}, u32[]{:S(2)}, u32[]{:S(2)}) collective-permute-start(f32[256,128]{1,0:T(8,128)S(1)} %add.205), channel_id=1, source_target_pairs={{0,8},{1,3},{2,10},{3,1},{4,12},{5,7},{6,14},{7,5},{8,0},{9,11},{1... | collective-permute-start | bytes 393224 | tf_op jit(solution)/shard_map/ppermute | solution.py:407
  53.9 7.8 %collective-permute-start.21 = (f32[256,128]{1,0:T(8,128)S(1)}, f32[256,128]{1,0:T(8,128)S(1)}, u32[]{:S(2)}, u32[]{:S(2)}) collective-permute-start(f32[256,128]{1,0:T(8,128)S(1)} %add.205), channel_id=1, source_target_pairs={{0,4},{1,5},{2,6},{3,7},{4,0},{5,1},{6,2},{7,3},{8,12},{9,13},{10,... | collective-permute-start | bytes 393224 | tf_op jit(solution)/shard_map/ppermute | solution.py:407
  56.2 9.0 %collective-permute-start.22 = (f32[256,128]{1,0:T(8,128)S(1)}, f32[256,128]{1,0:T(8,128)S(1)}, u32[]{:S(2)}, u32[]{:S(2)}) collective-permute-start(f32[256,128]{1,0:T(8,128)S(1)} %add.205), channel_id=1, source_target_pairs={{0,12},{1,7},{2,14},{3,5},{4,8},{5,3},{6,10},{7,1},{8,4},{9,15},{1... | collective-permute-start | bytes 393224 | tf_op jit(solution)/shard_map/ppermute | solution.py:407
  56.9 4.5 %collective-permute-start.17 = (f32[2,64,64]{2,1,0:T(8,128)S(1)}, f32[2,64,64]{2,1,0:T(8,128)S(1)}, u32[]{:S(2)}, u32[]{:S(2)}) collective-permute-start(f32[2,64,64]{2,1,0:T(8,128)S(1)} %fusion.8), channel_id=1, source_target_pairs={{0,2},{2,0},{1,3},{3,1},{4,6},{6,4},{5,7},{7,5},{8,10},{10,8},{9,1... | collective-permute-start | bytes 98312 | tf_op jit(solution)/shard_map/ppermute | solution.py:375
  61.7 4.2 %collective-permute-start.18 = (f32[2,64,256]{2,1,0:T(8,128)S(1)}, f32[2,64,256]{2,1,0:T(8,128)S(1)}, u32[]{:S(2)}, u32[]{:S(2)}) collective-permute-start(f32[2,64,256]{2,1,0:T(8,128)S(1)} %fusion.4), channel_id=1, source_target_pairs={{0,1},{1,0},{2,3},{3,2},{4,5},{5,4},{6,7},{7,6},{8,9},{9,8},{10,11... | collective-permute-start | bytes 393224 | tf_op jit(solution)/shard_map/ppermute | solution.py:332

commit v7 on v6

--- a/solution.py
+++ b/solution.py
@@ -379,14 +379,14 @@
     rows, cols = lax.axis_size("row"), lax.axis_size("col")
     if beside_little and (rows, cols) == (4, 2):
         first = [[(0, 1)], [(2, 0), (1, 0), (3, 0)]]
-        second = [[(3, 0)], [(0, 1), (1, 0), (1, 1)]]
+        second = [[(2, 0)], [(0, 1), (1, 0), (1, 1)]]
     else:
         along_cols = [[(0, 1 << k)] for k in range((cols - 1).bit_length())]
         along_rows = [[(1 << k, 0)] for k in range((rows - 1).bit_length())]
         first = along_cols + along_rows
         second = along_rows + along_cols
         if len(along_rows) > 1:
-            second = [[(3, 0)]] + along_cols + along_rows[:1] + along_rows[2:]
+            second = along_rows[1:2] + along_cols + along_rows[:1] + along_rows[2:]
     return [list(zip(*stage, strict=True)) for stage in zip(first, second, strict=True)]
 
 
@@ -504,6 +504,7 @@
     whole = jnp.concatenate(
         [jnp.where(lower, other, strip), jnp.where(lower, strip, other)], axis=1
     )
+    probe_grad, _ = lax.optimization_barrier((probe_grad, whole))
     new_probe = ahead[-1] - probe_step * probe_grad
     return (whole, new_probe.reshape(1, 2, size, size))
 

time: 66.9 us -> 66.5 us (level)
  waiting for transfers between devices: 21.4 us -> 19.3 us
  starting transfers between devices: 24.6 us -> 26.4 us
    ppermute x7, waiting for transfers between devices: 15.3 us -> 11.1 us  [sum_tiles(): arrived.append(lax.ppermute(block, ('row', 'col', 'mode'), route))]
    ppermute x3, waiting for transfers between devices: 2.92 us -> 5.07 us  [swap_cols(): lax.ppermute(block, 'col', [(i, i if o is None else o) for i, o in enumer...]
    ppermute x7, starting transfers between devices: 11.5 us -> 12.7 us  [sum_tiles(): arrived.append(lax.ppermute(block, ('row', 'col', 'mode'), route))]
  transfers between devices with their start and end apart: 23 -> 23, of which waited for: 10 -> 11; matrix products, arithmetic and copies ran while one was open for 3% -> 2% of each run, Pallas kernels for 5% -> 5%
where the time goes in v7:
time: 66.5 us; the launch traced here: 66.3 us
  starting transfers between devices  26.4 us (40%)
  waiting for transfers between devices  19.3 us (29%)
  Pallas kernels  12.3 us (18%)
  other arithmetic  3.87 us (6%)
  local copies, waits for them, and re-layouts  2.74 us (4%)
  between operations  1.7 us (3%)
    ppermute x7, starting transfers between devices, sum_tiles(): arrived.append(lax.ppermute(block, ('row', 'col', 'mode'), route))  12.7 us
    ppermute x7, waiting for transfers between devices, sum_tiles(): arrived.append(lax.ppermute(block, ('row', 'col', 'mode'), route))  11.1 us
    ppermute x4, starting transfers between devices, swap_neighbours(): return lax.ppermute(block, ('row', 'col', 'mode'), route)  8.77 us
    pallas_call x2, Pallas kernels, waves(): pl.pallas_call(body, out_shape=[jax.ShapeDtypeStruct(s, jnp.float32) for...  8.73 us
    ppermute x3, waiting for transfers between devices, swap_cols(): lax.ppermute(block, 'col', [(i, i if o is None else o) for i, o in enumer...  5.07 us
    ppermute x3, starting transfers between devices, swap_cols(): lax.ppermute(block, 'col', [(i, i if o is None else o) for i, o in enumer...  3.31 us
    ppermute x9, waiting for transfers between devices, swap_modes(): return lax.ppermute(block, 'mode', [(0, 1), (1, 0)])  3.14 us
    unnamed x16, local copies, waits for them, and re-layouts  2.66 us
  transfers between devices with their start and end apart: 23, of which 11 were waited for; matrix products, arithmetic and copies ran while one was open for 2% of the time, Pallas kernels for 5%

profile of v7, /device:TPU:0, one launch (start us, length us, event | category | flops | bytes accessed | tf_op | source)
XLA Modules:
  0.0 66.3 jit_solution(16291603318308408640)
XLA Ops:
  0.6 1.0 %slice_select_fusion.1 = f32[2,64,256]{2,1,0:T(8,128)S(1)} fusion(f32[2,128,256]{2,1,0:T(8,128)} %param.14, pred[]{:T(512)S(6)} %eq.15), kind=kLoop, calls=%fused_computation.25 | loop fusion | flops 32768 | bytes 393217 | tf_op jit(solution)/shard_map/jit(_where)/select_n | solution.py:432
  1.6 3.1 %collective-permute-start = (f32[2,64,256]{2,1,0:T(8,128)S(1)}, f32[2,64,256]{2,1,0:T(8,128)S(1)}, u32[]{:S(2)}, u32[]{:S(2)}) collective-permute-start(f32[2,64,256]{2,1,0:T(8,128)S(1)} %slice_select_fusion.1), channel_id=1, source_target_pairs={{0,4},{1,3},{2,6},{3,1},{4,0},{5,9},{6,2},{7,11},{8,12},{9,5},{10,... | collective-permute-start | bytes 393224 | tf_op jit(solution)/shard_map/ppermute | solution.py:356
  4.7 0.1 slice_select_fusion.4
  4.8 0.0 copy-start.6
  4.8 1.4 %collective-permute-start.2 = (f32[2,64,64]{2,1,0:T(8,128)S(1)}, f32[2,64,64]{2,1,0:T(8,128)S(1)}, u32[]{:S(2)}, u32[]{:S(2)}) collective-permute-start(f32[2,64,64]{2,1,0:T(8,128)S(1)} %slice_select_fusion.4), channel_id=1, source_target_pairs={{0,6},{1,3},{2,4},{3,1},{4,2},{5,11},{6,0},{7,9},{8,14},{9,7},{10,... | collective-permute-start | bytes 98312 | tf_op jit(solution)/shard_map/ppermute | solution.py:356
  6.3 0.2 collective-permute-start.1
  6.5 0.1 pad_add_fusion.place
  7.2 0.0 copy-start.7
  7.2 0.7 copy-done.7
  7.9 1.2 %copy-done = f32[1,1,16,128,128]{4,3,2,1,0:T(8,128)S(1)} copy-done((f32[1,1,16,128,128]{4,3,2,1,0:T(8,128)S(1)}, f32[1,1,16,128,128]{4,3,2,1,0:T(8,128)}, u32[]{:S(2)}) %copy-start) | copy-done | bytes 1048600
  9.1 1.6 %prepared.1 = (f32[8,128,128]{2,1,0:T(8,128)S(1)}, s32[34]{0:T(128)S(1)}) custom-call(s32[4]{0:T(128)S(1)} %pad_add_fusion.place, s32[2,16]{1,0:T(2,128)S(1)} %bitcast.36, s32[1,1]{1,0:T(1,128)S(6)} %copy.16.counts, f32[8,2,128,128]{3,2,1,0:T(8,128)S(1)} %bitcast.33, bf16[128,128]{1,0:T(8,128)(2,1)S(1)} %copy-done.6), custom_call_target="tpu_custom_call" | custom-call | flops 100663296 | bytes 1048576 | tf_op jit(solution)/shard_map/prepared/pallas_call | solution.py:244
  10.7 0.0 collective-permute-done.2
  10.8 0.0 collective-permute-done
  10.8 0.2 fusion.6
  11.1 0.0 copy-start.1
  11.1 0.0 copy-start.2
  11.1 0.0 copy-start.3
  11.1 0.0 copy-start.4
  11.1 0.0 copy-start.5
  11.2 0.1 collective-permute-start.3
  11.2 0.7 %copy-done.1 = f32[1,2,128,128]{3,2,1,0:T(8,128)S(1)} copy-done((f32[1,2,128,128]{3,2,1,0:T(8,128)S(1)}, f32[1,2,128,128]{3,2,1,0:T(8,128)}, u32[]{:S(2)}) %copy-start.1) | copy-done | bytes 131096
  12.0 1.3 %collective-permute-done.4.refs_4_ = f32[256,128]{1,0:T(8,128)S(1)} collective-permute-done((f32[256,128]{1,0:T(8,128)S(1)}, f32[256,128]{1,0:T(8,128)S(1)}, u32[]{:S(2)}, u32[]{:S(2)}) %collective-permute-start.4) | collective-permute-done | bytes 131104 | tf_op jit(solution)/shard_map/ppermute | solution.py:332
  13.3 0.0 collective-permute-done.3.refs_3_
  13.3 4.4 %waves.2 = (f32[256,128]{1,0:T(8,128)S(1)}, f32[256,128]{1,0:T(8,128)S(1)}, f32[8,2,128,128]{3,2,1,0:T(8,128)S(1)}) custom-call(s32[34]{0:T(128)S(1)} %get-tuple-element.29.refs_0_, f32[768,128]{1,0:T(8,128)S(1)} %bitcast.32, f32[256,128]{1,0:T(8,128)S(1)} %bitcast.35, f32[768,128]{1,0:T(8,128)S(1)} %collective-permute-done.3.refs_3_, ...), custom_call_target="tpu_custom_call" | custom-call | tf_op jit(solution)/shard_map/waves/pallas_call | solution.py:288
  17.7 0.2 collective-permute-start.5
  17.9 1.0 %placed.2 = (f32[768,128]{1,0:T(8,128)S(1)}, f32[768,128]{1,0:T(8,128)S(1)}) custom-call(s32[34]{0:T(128)S(1)} %get-tuple-element.29.refs_0_, f32[8,2,128,128]{3,2,1,0:T(8,128)S(1)} %get-tuple-element.34.refs_1_), custom_call_target="tpu_custom_call" | custom-call | tf_op jit(solution)/shard_map/placed/pallas_call | solution.py:316
  18.9 0.2 collective-permute-done.5
  19.2 0.2 collective-permute-start.9
  19.4 1.8 %collective-permute-start.6 = (f32[256,128]{1,0:T(8,128)S(1)}, f32[256,128]{1,0:T(8,128)S(1)}, u32[]{:S(2)}, u32[]{:S(2)}) collective-permute-start(f32[256,128]{1,0:T(8,128)S(1)} %add.182), channel_id=1, source_target_pairs={{0,2},{1,9},{2,0},{3,11},{4,6},{5,13},{6,4},{7,15},{8,10},{9,1},{1... | collective-permute-start | bytes 393224 | tf_op jit(solution)/shard_map/ppermute | solution.py:407
  21.2 0.1 add.194
  21.3 1.7 %collective-permute-start.10 = (f32[768,128]{1,0:T(8,128)S(1)}, f32[768,128]{1,0:T(8,128)S(1)}, u32[]{:S(2)}, u32[]{:S(2)}) collective-permute-start(f32[768,128]{1,0:T(8,128)S(1)} %add.194), channel_id=1, source_target_pairs={{0,4},{1,3},{2,6},{3,1},{4,0},{5,9},{6,2},{7,11},{8,12},{9,5},{10,... | collective-permute-start | bytes 1179656 | tf_op jit(solution)/shard_map/ppermute | solution.py:356
  23.0 1.3 %collective-permute-done.6 = f32[256,128]{1,0:T(8,128)S(1)} collective-permute-done((f32[256,128]{1,0:T(8,128)S(1)}, f32[256,128]{1,0:T(8,128)S(1)}, u32[]{:S(2)}, u32[]{:S(2)}) %collective-permute-start.6) | collective-permute-done | bytes 131104 | tf_op jit(solution)/shard_map/ppermute | solution.py:407
  24.4 2.0 %collective-permute-start.7 = (f32[256,128]{1,0:T(8,128)S(1)}, f32[256,128]{1,0:T(8,128)S(1)}, u32[]{:S(2)}, u32[]{:S(2)}) collective-permute-start(f32[256,128]{1,0:T(8,128)S(1)} %add.183), channel_id=1, source_target_pairs={{0,4},{1,3},{2,6},{3,1},{4,0},{5,7},{6,2},{7,5},{8,12},{9,11},{10,... | collective-permute-start | bytes 393224 | tf_op jit(solution)/shard_map/ppermute | solution.py:407
  26.4 4.4 %collective-permute-done.7 = f32[256,128]{1,0:T(8,128)S(1)} collective-permute-done((f32[256,128]{1,0:T(8,128)S(1)}, f32[256,128]{1,0:T(8,128)S(1)}, u32[]{:S(2)}, u32[]{:S(2)}) %collective-permute-start.7) | collective-permute-done | bytes 131104 | tf_op jit(solution)/shard_map/ppermute | solution.py:407
  30.8 2.9 %collective-permute-start.8 = (f32[256,128]{1,0:T(8,128)S(1)}, f32[256,128]{1,0:T(8,128)S(1)}, u32[]{:S(2)}, u32[]{:S(2)}) collective-permute-start(f32[256,128]{1,0:T(8,128)S(1)} %add.184), channel_id=1, source_target_pairs={{0,8},{1,5},{2,10},{3,7},{4,12},{5,1},{6,14},{7,3},{8,0},{9,13},{1... | collective-permute-start | bytes 393224 | tf_op jit(solution)/shard_map/ppermute | solution.py:407
  33.7 0.0 collective-permute-done.10
  33.7 1.6 %collective-permute-start.11 = (f32[256,128]{1,0:T(8,128)S(1)}, f32[256,128]{1,0:T(8,128)S(1)}, u32[]{:S(2)}, u32[]{:S(2)}) collective-permute-start(f32[256,128]{1,0:T(8,128)S(1)} %slice_select_fusion.2), channel_id=1, source_target_pairs={{0,2},{2,0},{1,3},{3,1},{4,6},{6,4},{5,7},{7,5},{8,10},{10,8},{9,1... | collective-permute-start | bytes 393224 | tf_op jit(solution)/shard_map/ppermute | solution.py:375
  35.3 0.1 and_select_fusion.2
  35.4 1.3 %collective-permute-done.8 = f32[256,128]{1,0:T(8,128)S(1)} collective-permute-done((f32[256,128]{1,0:T(8,128)S(1)}, f32[256,128]{1,0:T(8,128)S(1)}, u32[]{:S(2)}, u32[]{:S(2)}) %collective-permute-start.8) | collective-permute-done | bytes 131104 | tf_op jit(solution)/shard_map/ppermute | solution.py:407
  36.7 2.0 %collective-permute-done.11 = f32[256,128]{1,0:T(8,128)S(1)} collective-permute-done((f32[256,128]{1,0:T(8,128)S(1)}, f32[256,128]{1,0:T(8,128)S(1)}, u32[]{:S(2)}, u32[]{:S(2)}) %collective-permute-start.11) | collective-permute-done | bytes 131104 | tf_op jit(solution)/shard_map/ppermute | solution.py:375
  38.8 0.1 fusion.1
  38.9 0.1 collective-permute-start.12
  39.1 0.6 collective-permute-start.13
  39.6 1.3 %collective-permute-done.13.refs_4_ = f32[256,128]{1,0:T(8,128)S(1)} collective-permute-done((f32[256,128]{1,0:T(8,128)S(1)}, f32[256,128]{1,0:T(8,128)S(1)}, u32[]{:S(2)}, u32[]{:S(2)}) %collective-permute-start.13) | collective-permute-done | bytes 131104 | tf_op jit(solution)/shard_map/ppermute | solution.py:332
  40.9 4.4 %waves.3 = (f32[256,128]{1,0:T(8,128)S(1)}, f32[256,128]{1,0:T(8,128)S(1)}, f32[8,2,128,128]{3,2,1,0:T(8,128)S(1)}) custom-call(s32[34]{0:T(128)S(1)} %get-tuple-element.29.refs_0_, f32[768,128]{1,0:T(8,128)S(1)} %multiply_add_fusion.refs_1_, f32[256,128]{1,0:T(8,128)S(1)} %multiply_add_fusion.1.refs_2_, f32[768,128]{1,0:T(8,128)S(1)} %collective-permute-done.12.refs_3_, ...), custom_call_target="tpu_custom_call" | custom-call | tf_op jit(solution)/shard_map/waves/pallas_call | solution.py:288
  45.3 0.2 collective-permute-start.14
  45.5 1.0 %placed.3 = (f32[768,128]{1,0:T(8,128)S(1)}, f32[768,128]{1,0:T(8,128)S(1)}) custom-call(s32[34]{0:T(128)S(1)} %get-tuple-element.29.refs_0_, f32[8,2,128,128]{3,2,1,0:T(8,128)S(1)} %get-tuple-element.45.refs_1_), custom_call_target="tpu_custom_call" | custom-call | tf_op jit(solution)/shard_map/placed/pallas_call | solution.py:316
  46.5 0.2 collective-permute-done.14
  46.7 0.2 collective-permute-start.15
  47.0 1.6 %collective-permute-start.19 = (f32[256,128]{1,0:T(8,128)S(1)}, f32[256,128]{1,0:T(8,128)S(1)}, u32[]{:S(2)}, u32[]{:S(2)}) collective-permute-start(f32[256,128]{1,0:T(8,128)S(1)} %add.200), channel_id=1, source_target_pairs={{0,2},{1,9},{2,0},{3,11},{4,6},{5,13},{6,4},{7,15},{8,10},{9,1},{1... | collective-permute-start | bytes 393224 | tf_op jit(solution)/shard_map/ppermute | solution.py:407
  48.7 2.5 %collective-permute-start.16 = (f32[3,2,64,128]{3,2,1,0:T(8,128)S(1)}, f32[3,2,64,128]{3,2,1,0:T(8,128)S(1)}, u32[]{:S(2)}, u32[]{:S(2)}) collective-permute-start(f32[3,2,64,128]{3,2,1,0:T(8,128)S(1)} %bitcast.41), channel_id=1, source_target_pairs={{0,4},{1,3},{2,6},{3,1},{4,0},{5,9},{6,2},{7,11},{8,12},{9,5},{10,... | collective-permute-start | bytes 589832 | tf_op jit(solution)/shard_map/ppermute | solution.py:356
  51.2 1.5 %collective-permute-done.19 = f32[256,128]{1,0:T(8,128)S(1)} collective-permute-done((f32[256,128]{1,0:T(8,128)S(1)}, f32[256,128]{1,0:T(8,128)S(1)}, u32[]{:S(2)}, u32[]{:S(2)}) %collective-permute-start.19) | collective-permute-done | bytes 131104 | tf_op jit(solution)/shard_map/ppermute | solution.py:407
  52.7 0.6 collective-permute-start.20
  53.3 2.9 %collective-permute-start.21 = (f32[256,128]{1,0:T(8,128)S(1)}, f32[256,128]{1,0:T(8,128)S(1)}, u32[]{:S(2)}, u32[]{:S(2)}) collective-permute-start(f32[256,128]{1,0:T(8,128)S(1)} %add.205), channel_id=1, source_target_pairs={{0,4},{1,5},{2,6},{3,7},{4,0},{5,1},{6,2},{7,3},{8,12},{9,13},{10,... | collective-permute-start | bytes 393224 | tf_op jit(solution)/shard_map/ppermute | solution.py:407
  56.2 1.0 %collective-permute-start.22 = (f32[256,128]{1,0:T(8,128)S(1)}, f32[256,128]{1,0:T(8,128)S(1)}, u32[]{:S(2)}, u32[]{:S(2)}) collective-permute-start(f32[256,128]{1,0:T(8,128)S(1)} %add.205), channel_id=1, source_target_pairs={{0,12},{1,7},{2,14},{3,5},{4,8},{5,3},{6,10},{7,1},{8,4},{9,15},{1... | collective-permute-start | bytes 393224 | tf_op jit(solution)/shard_map/ppermute | solution.py:407
  57.2 0.1 fusion.8
  57.3 1.6 %collective-permute-start.17 = (f32[2,64,64]{2,1,0:T(8,128)S(1)}, f32[2,64,64]{2,1,0:T(8,128)S(1)}, u32[]{:S(2)}, u32[]{:S(2)}) collective-permute-start(f32[2,64,64]{2,1,0:T(8,128)S(1)} %fusion.8), channel_id=1, source_target_pairs={{0,2},{2,0},{1,3},{3,1},{4,6},{6,4},{5,7},{7,5},{8,10},{10,8},{9,1... | collective-permute-start | bytes 98312 | tf_op jit(solution)/shard_map/ppermute | solution.py:375
  58.9 3.0 %collective-permute-done.17 = f32[2,64,64]{2,1,0:T(8,128)S(1)} collective-permute-done((f32[2,64,64]{2,1,0:T(8,128)S(1)}, f32[2,64,64]{2,1,0:T(8,128)S(1)}, u32[]{:S(2)}, u32[]{:S(2)}) %collective-permute-start.17) | collective-permute-done | bytes 32800 | tf_op jit(solution)/shard_map/ppermute | solution.py:375
  61.9 0.1 fusion.9
  62.0 0.2 fusion.4
  62.2 0.1 collective-permute-start.18
  62.3 2.6 %collective-permute-done.22 = f32[256,128]{1,0:T(8,128)S(1)} collective-permute-done((f32[256,128]{1,0:T(8,128)S(1)}, f32[256,128]{1,0:T(8,128)S(1)}, u32[]{:S(2)}, u32[]{:S(2)}) %collective-permute-start.22) | collective-permute-done | bytes 131104 | tf_op jit(solution)/shard_map/ppermute | solution.py:407
  64.9 0.7 %pad_maximum_fusion.2 = f32[2,128,256]{2,1,0:T(8,128)} fusion(f32[2,64,256]{2,1,0:T(8,128)S(1)} %get-tuple-element.67, f32[2,64,256]{2,1,0:T(8,128)S(1)} %get-tuple-element.66), kind=kLoop, calls=%fused_computation.11 | loop fusion | flops 65536 | bytes 524288 | tf_op jit(solution)/shard_map/concatenate | solution.py:504
  65.7 0.7 %multiply_subtract_fusion = f32[256,128]{1,0:T(8,128)} fusion(f32[256,128]{1,0:T(8,128)S(1)} %multiply_add_fusion.1.refs_2_, f32[256,128]{1,0:T(8,128)S(1)} %add_add_fusion), kind=kLoop, calls=%fused_computation.20 | loop fusion | flops 65536 | bytes 393216 | tf_op jit(solution)/shard_map/sub | solution.py:508
  (44 shorter events, 0.7 us)
Async XLA Ops:
  1.6 9.2 %collective-permute-start = (f32[2,64,256]{2,1,0:T(8,128)S(1)}, f32[2,64,256]{2,1,0:T(8,128)S(1)}, u32[]{:S(2)}, u32[]{:S(2)}) collective-permute-start(f32[2,64,256]{2,1,0:T(8,128)S(1)} %slice_select_fusion.1), channel_id=1, source_target_pairs={{0,4},{1,3},{2,6},{3,1},{4,0},{5,9},{6,2},{7,11},{8,12},{9,5},{10,... | collective-permute-start | bytes 393224 | tf_op jit(solution)/shard_map/ppermute | solution.py:356
  4.8 2.4 %copy-start.6 = (bf16[128,128]{1,0:T(8,128)(2,1)S(1)}, bf16[128,128]{1,0:T(8,128)(2,1)}, u32[]{:S(2)}) copy-start(bf16[128,128]{1,0:T(8,128)(2,1)} %constant.86.clone.order) | copy-start | bytes 98308
  4.8 5.9 %collective-permute-start.2 = (f32[2,64,64]{2,1,0:T(8,128)S(1)}, f32[2,64,64]{2,1,0:T(8,128)S(1)}, u32[]{:S(2)}, u32[]{:S(2)}) collective-permute-start(f32[2,64,64]{2,1,0:T(8,128)S(1)} %slice_select_fusion.4), channel_id=1, source_target_pairs={{0,6},{1,3},{2,4},{3,1},{4,2},{5,11},{6,0},{7,9},{8,14},{9,7},{10,... | collective-permute-start | bytes 98312 | tf_op jit(solution)/shard_map/ppermute | solution.py:356
  6.3 4.5 %collective-permute-start.1 = (f32[2,64,64]{2,1,0:T(8,128)S(1)}, f32[2,64,64]{2,1,0:T(8,128)S(1)}, u32[]{:S(2)}, u32[]{:S(2)}) collective-permute-start(f32[2,64,64]{2,1,0:T(8,128)S(1)} %slice_select_fusion.4), channel_id=1, source_target_pairs={{0,2},{2,0},{1,3},{3,1},{4,6},{6,4},{5,7},{7,5},{8,10},{10,8},{9,1... | collective-permute-start | bytes 98312 | tf_op jit(solution)/shard_map/ppermute | solution.py:375
  7.2 0.7 %copy-start.7 = (s32[1,1,16,2]{2,3,1,0:T(2,128)S(1)}, s32[1,1,16,2]{2,3,1,0:T(2,128)}, u32[]{:S(2)}) copy-start(s32[1,1,16,2]{2,3,1,0:T(2,128)} %param.16) | copy-start | bytes 388
  7.9 1.2 %copy-start = (f32[1,1,16,128,128]{4,3,2,1,0:T(8,128)S(1)}, f32[1,1,16,128,128]{4,3,2,1,0:T(8,128)}, u32[]{:S(2)}) copy-start(f32[1,1,16,128,128]{4,3,2,1,0:T(8,128)} %param.18) | copy-start | bytes 3145732
  11.1 0.9 %copy-start.1 = (f32[1,2,128,128]{3,2,1,0:T(8,128)S(1)}, f32[1,2,128,128]{3,2,1,0:T(8,128)}, u32[]{:S(2)}) copy-start(f32[1,2,128,128]{3,2,1,0:T(8,128)} %param.15) | copy-start | bytes 393220
  11.1 2.2 %copy-start.2 = (bf16[2,128,256]{2,1,0:T(8,128)(2,1)S(1)}, bf16[2,128,256]{2,1,0:T(8,128)(2,1)}, u32[]{:S(2)}) copy-start(bf16[2,128,256]{2,1,0:T(8,128)(2,1)} %constant.87.clone.refs_6_) | copy-start | bytes 393220
  11.1 2.2 %copy-start.3 = (bf16[2,256,128]{2,1,0:T(8,128)(2,1)S(1)}, bf16[2,256,128]{2,1,0:T(8,128)(2,1)}, u32[]{:S(2)}) copy-start(bf16[2,256,128]{2,1,0:T(8,128)(2,1)} %constant.88.clone.refs_7_) | copy-start | bytes 393220
  11.1 2.2 %copy-start.4 = (bf16[2,256,128]{2,1,0:T(8,128)(2,1)S(1)}, bf16[2,256,128]{2,1,0:T(8,128)(2,1)}, u32[]{:S(2)}) copy-start(bf16[2,256,128]{2,1,0:T(8,128)(2,1)} %constant.89.clone.refs_8_) | copy-start | bytes 393220
  11.1 2.2 %copy-start.5 = (bf16[2,128,256]{2,1,0:T(8,128)(2,1)S(1)}, bf16[2,128,256]{2,1,0:T(8,128)(2,1)}, u32[]{:S(2)}) copy-start(bf16[2,128,256]{2,1,0:T(8,128)(2,1)} %constant.90.clone.refs_9_) | copy-start | bytes 393220
  11.2 2.2 %collective-permute-start.3 = (f32[768,128]{1,0:T(8,128)S(1)}, f32[768,128]{1,0:T(8,128)S(1)}, u32[]{:S(2)}, u32[]{:S(2)}) collective-permute-start(f32[768,128]{1,0:T(8,128)S(1)} %bitcast.31), channel_id=1, source_target_pairs={{0,1},{1,0},{2,3},{3,2},{4,5},{5,4},{6,7},{7,6},{8,9},{9,8},{10,11... | collective-permute-start | bytes 1179656 | tf_op jit(solution)/shard_map/ppermute | solution.py:332
  12.0 1.3 %collective-permute-start.4 = (f32[256,128]{1,0:T(8,128)S(1)}, f32[256,128]{1,0:T(8,128)S(1)}, u32[]{:S(2)}, u32[]{:S(2)}) collective-permute-start(f32[256,128]{1,0:T(8,128)S(1)} %bitcast.34), channel_id=1, source_target_pairs={{0,1},{1,0},{2,3},{3,2},{4,5},{5,4},{6,7},{7,6},{8,9},{9,8},{10,11... | collective-permute-start | bytes 393224 | tf_op jit(solution)/shard_map/ppermute | solution.py:332
  17.7 1.4 %collective-permute-start.5 = (f32[256,128]{1,0:T(8,128)S(1)}, f32[256,128]{1,0:T(8,128)S(1)}, u32[]{:S(2)}, u32[]{:S(2)}) collective-permute-start(f32[256,128]{1,0:T(8,128)S(1)} %get-tuple-element.33), channel_id=1, source_target_pairs={{0,1},{1,0},{2,3},{3,2},{4,5},{5,4},{6,7},{7,6},{8,9},{9,8},{10,11... | collective-permute-start | bytes 393224 | tf_op jit(solution)/shard_map/ppermute | solution.py:332
  19.2 2.1 %collective-permute-start.9 = (f32[768,128]{1,0:T(8,128)S(1)}, f32[768,128]{1,0:T(8,128)S(1)}, u32[]{:S(2)}, u32[]{:S(2)}) collective-permute-start(f32[768,128]{1,0:T(8,128)S(1)} %get-tuple-element.39), channel_id=1, source_target_pairs={{0,1},{1,0},{2,3},{3,2},{4,5},{5,4},{6,7},{7,6},{8,9},{9,8},{10,11... | collective-permute-start | bytes 1179656 | tf_op jit(solution)/shard_map/ppermute | solution.py:332
  19.4 5.0 %collective-permute-start.6 = (f32[256,128]{1,0:T(8,128)S(1)}, f32[256,128]{1,0:T(8,128)S(1)}, u32[]{:S(2)}, u32[]{:S(2)}) collective-permute-start(f32[256,128]{1,0:T(8,128)S(1)} %add.182), channel_id=1, source_target_pairs={{0,2},{1,9},{2,0},{3,11},{4,6},{5,13},{6,4},{7,15},{8,10},{9,1},{1... | collective-permute-start | bytes 393224 | tf_op jit(solution)/shard_map/ppermute | solution.py:407
  21.3 12.4 %collective-permute-start.10 = (f32[768,128]{1,0:T(8,128)S(1)}, f32[768,128]{1,0:T(8,128)S(1)}, u32[]{:S(2)}, u32[]{:S(2)}) collective-permute-start(f32[768,128]{1,0:T(8,128)S(1)} %add.194), channel_id=1, source_target_pairs={{0,4},{1,3},{2,6},{3,1},{4,0},{5,9},{6,2},{7,11},{8,12},{9,5},{10,... | collective-permute-start | bytes 1179656 | tf_op jit(solution)/shard_map/ppermute | solution.py:356
  24.4 6.4 %collective-permute-start.7 = (f32[256,128]{1,0:T(8,128)S(1)}, f32[256,128]{1,0:T(8,128)S(1)}, u32[]{:S(2)}, u32[]{:S(2)}) collective-permute-start(f32[256,128]{1,0:T(8,128)S(1)} %add.183), channel_id=1, source_target_pairs={{0,4},{1,3},{2,6},{3,1},{4,0},{5,7},{6,2},{7,5},{8,12},{9,11},{10,... | collective-permute-start | bytes 393224 | tf_op jit(solution)/shard_map/ppermute | solution.py:407
  30.8 5.9 %collective-permute-start.8 = (f32[256,128]{1,0:T(8,128)S(1)}, f32[256,128]{1,0:T(8,128)S(1)}, u32[]{:S(2)}, u32[]{:S(2)}) collective-permute-start(f32[256,128]{1,0:T(8,128)S(1)} %add.184), channel_id=1, source_target_pairs={{0,8},{1,5},{2,10},{3,7},{4,12},{5,1},{6,14},{7,3},{8,0},{9,13},{1... | collective-permute-start | bytes 393224 | tf_op jit(solution)/shard_map/ppermute | solution.py:407
  33.7 5.0 %collective-permute-start.11 = (f32[256,128]{1,0:T(8,128)S(1)}, f32[256,128]{1,0:T(8,128)S(1)}, u32[]{:S(2)}, u32[]{:S(2)}) collective-permute-start(f32[256,128]{1,0:T(8,128)S(1)} %slice_select_fusion.2), channel_id=1, source_target_pairs={{0,2},{2,0},{1,3},{3,1},{4,6},{6,4},{5,7},{7,5},{8,10},{10,8},{9,1... | collective-permute-start | bytes 393224 | tf_op jit(solution)/shard_map/ppermute | solution.py:375
  38.9 2.0 %collective-permute-start.12 = (f32[768,128]{1,0:T(8,128)S(1)}, f32[768,128]{1,0:T(8,128)S(1)}, u32[]{:S(2)}, u32[]{:S(2)}) collective-permute-start(f32[768,128]{1,0:T(8,128)S(1)} %multiply_add_fusion.refs_1_), channel_id=1, source_target_pairs={{0,1},{1,0},{2,3},{3,2},{4,5},{5,4},{6,7},{7,6},{8,9},{9,8},{10,11... | collective-permute-start | bytes 1179656 | tf_op jit(solution)/shard_map/ppermute | solution.py:332
  39.1 1.9 %collective-permute-start.13 = (f32[256,128]{1,0:T(8,128)S(1)}, f32[256,128]{1,0:T(8,128)S(1)}, u32[]{:S(2)}, u32[]{:S(2)}) collective-permute-start(f32[256,128]{1,0:T(8,128)S(1)} %multiply_add_fusion.1.refs_2_), channel_id=1, source_target_pairs={{0,1},{1,0},{2,3},{3,2},{4,5},{5,4},{6,7},{7,6},{8,9},{9,8},{10,11... | collective-permute-start | bytes 393224 | tf_op jit(solution)/shard_map/ppermute | solution.py:332
  45.3 1.4 %collective-permute-start.14 = (f32[256,128]{1,0:T(8,128)S(1)}, f32[256,128]{1,0:T(8,128)S(1)}, u32[]{:S(2)}, u32[]{:S(2)}) collective-permute-start(f32[256,128]{1,0:T(8,128)S(1)} %get-tuple-element.44), channel_id=1, source_target_pairs={{0,1},{1,0},{2,3},{3,2},{4,5},{5,4},{6,7},{7,6},{8,9},{9,8},{10,11... | collective-permute-start | bytes 393224 | tf_op jit(solution)/shard_map/ppermute | solution.py:332
  46.7 1.8 %collective-permute-start.15 = (f32[768,128]{1,0:T(8,128)S(1)}, f32[768,128]{1,0:T(8,128)S(1)}, u32[]{:S(2)}, u32[]{:S(2)}) collective-permute-start(f32[768,128]{1,0:T(8,128)S(1)} %get-tuple-element.49), channel_id=1, source_target_pairs={{0,1},{1,0},{2,3},{3,2},{4,5},{5,4},{6,7},{7,6},{8,9},{9,8},{10,11... | collective-permute-start | bytes 1179656 | tf_op jit(solution)/shard_map/ppermute | solution.py:332
  47.0 5.7 %collective-permute-start.19 = (f32[256,128]{1,0:T(8,128)S(1)}, f32[256,128]{1,0:T(8,128)S(1)}, u32[]{:S(2)}, u32[]{:S(2)}) collective-permute-start(f32[256,128]{1,0:T(8,128)S(1)} %add.200), channel_id=1, source_target_pairs={{0,2},{1,9},{2,0},{3,11},{4,6},{5,13},{6,4},{7,15},{8,10},{9,1},{1... | collective-permute-start | bytes 393224 | tf_op jit(solution)/shard_map/ppermute | solution.py:407
  48.7 8.5 %collective-permute-start.16 = (f32[3,2,64,128]{3,2,1,0:T(8,128)S(1)}, f32[3,2,64,128]{3,2,1,0:T(8,128)S(1)}, u32[]{:S(2)}, u32[]{:S(2)}) collective-permute-start(f32[3,2,64,128]{3,2,1,0:T(8,128)S(1)} %bitcast.41), channel_id=1, source_target_pairs={{0,4},{1,3},{2,6},{3,1},{4,0},{5,9},{6,2},{7,11},{8,12},{9,5},{10,... | collective-permute-start | bytes 589832 | tf_op jit(solution)/shard_map/ppermute | solution.py:356
  52.7 9.5 %collective-permute-start.20 = (f32[256,128]{1,0:T(8,128)S(1)}, f32[256,128]{1,0:T(8,128)S(1)}, u32[]{:S(2)}, u32[]{:S(2)}) collective-permute-start(f32[256,128]{1,0:T(8,128)S(1)} %add.205), channel_id=1, source_target_pairs={{0,8},{1,3},{2,10},{3,1},{4,12},{5,7},{6,14},{7,5},{8,0},{9,11},{1... | collective-permute-start | bytes 393224 | tf_op jit(solution)/shard_map/ppermute | solution.py:407
  53.3 9.0 %collective-permute-start.21 = (f32[256,128]{1,0:T(8,128)S(1)}, f32[256,128]{1,0:T(8,128)S(1)}, u32[]{:S(2)}, u32[]{:S(2)}) collective-permute-start(f32[256,128]{1,0:T(8,128)S(1)} %add.205), channel_id=1, source_target_pairs={{0,4},{1,5},{2,6},{3,7},{4,0},{5,1},{6,2},{7,3},{8,12},{9,13},{10,... | collective-permute-start | bytes 393224 | tf_op jit(solution)/shard_map/ppermute | solution.py:407
  56.2 8.7 %collective-permute-start.22 = (f32[256,128]{1,0:T(8,128)S(1)}, f32[256,128]{1,0:T(8,128)S(1)}, u32[]{:S(2)}, u32[]{:S(2)}) collective-permute-start(f32[256,128]{1,0:T(8,128)S(1)} %add.205), channel_id=1, source_target_pairs={{0,12},{1,7},{2,14},{3,5},{4,8},{5,3},{6,10},{7,1},{8,4},{9,15},{1... | collective-permute-start | bytes 393224 | tf_op jit(solution)/shard_map/ppermute | solution.py:407
  57.3 4.6 %collective-permute-start.17 = (f32[2,64,64]{2,1,0:T(8,128)S(1)}, f32[2,64,64]{2,1,0:T(8,128)S(1)}, u32[]{:S(2)}, u32[]{:S(2)}) collective-permute-start(f32[2,64,64]{2,1,0:T(8,128)S(1)} %fusion.8), channel_id=1, source_target_pairs={{0,2},{2,0},{1,3},{3,1},{4,6},{6,4},{5,7},{7,5},{8,10},{10,8},{9,1... | collective-permute-start | bytes 98312 | tf_op jit(solution)/shard_map/ppermute | solution.py:375
  62.2 2.7 %collective-permute-start.18 = (f32[2,64,256]{2,1,0:T(8,128)S(1)}, f32[2,64,256]{2,1,0:T(8,128)S(1)}, u32[]{:S(2)}, u32[]{:S(2)}) collective-permute-start(f32[2,64,256]{2,1,0:T(8,128)S(1)} %fusion.4), channel_id=1, source_target_pairs={{0,1},{1,0},{2,3},{3,2},{4,5},{5,4},{6,7},{7,6},{8,9},{9,8},{10,11... | collective-permute-start | bytes 393224 | tf_op jit(solution)/shard_map/ppermute | solution.py:332

commit v8 on v7

--- a/solution.py
+++ b/solution.py
@@ -378,8 +378,8 @@
 def tile_sum_stages(beside_little):
     rows, cols = lax.axis_size("row"), lax.axis_size("col")
     if beside_little and (rows, cols) == (4, 2):
-        first = [[(0, 1)], [(2, 0), (1, 0), (3, 0)]]
-        second = [[(2, 0)], [(0, 1), (1, 0), (1, 1)]]
+        first = [[(0, 1)], [(3, 0), (2, 0), (1, 0)]]
+        second = [[(2, 0)], [(1, 1), (1, 0), (0, 1)]]
     else:
         along_cols = [[(0, 1 << k)] for k in range((cols - 1).bit_length())]
         along_rows = [[(1 << k, 0)] for k in range((rows - 1).bit_length())]

time: 66.5 us -> 65.6 us (0.986)
  waiting for transfers between devices: 19.3 us -> 18.4 us
    ppermute x7, waiting for transfers between devices: 11.1 us -> 10.4 us  [sum_tiles(): arrived.append(lax.ppermute(block, ('row', 'col', 'mode'), route))]
  transfers between devices with their start and end apart: 23 -> 23, of which waited for: 11 -> 12; matrix products, arithmetic and copies ran while one was open for 2% -> 2% of each run, Pallas kernels for 5% -> 5%
where the time goes in v8:
time: 65.6 us; the launch traced here: 65.3 us
  starting transfers between devices  26.3 us (40%)
  waiting for transfers between devices  18.4 us (28%)
  Pallas kernels  12.3 us (19%)
  other arithmetic  3.87 us (6%)
  local copies, waits for them, and re-layouts  2.74 us (4%)
  between operations  1.69 us (3%)
    ppermute x7, starting transfers between devices, sum_tiles(): arrived.append(lax.ppermute(block, ('row', 'col', 'mode'), route))  12.7 us
    ppermute x7, waiting for transfers between devices, sum_tiles(): arrived.append(lax.ppermute(block, ('row', 'col', 'mode'), route))  10.4 us
    pallas_call x2, Pallas kernels, waves(): pl.pallas_call(body, out_shape=[jax.ShapeDtypeStruct(s, jnp.float32) for...  8.76 us
    ppermute x4, starting transfers between devices, swap_neighbours(): return lax.ppermute(block, ('row', 'col', 'mode'), route)  8.73 us
    ppermute x3, waiting for transfers between devices, swap_cols(): lax.ppermute(block, 'col', [(i, i if o is None else o) for i, o in enumer...  4.89 us
    ppermute x3, starting transfers between devices, swap_cols(): lax.ppermute(block, 'col', [(i, i if o is None else o) for i, o in enumer...  3.33 us
    ppermute x9, waiting for transfers between devices, swap_modes(): return lax.ppermute(block, 'mode', [(0, 1), (1, 0)])  3.18 us
    unnamed x16, local copies, waits for them, and re-layouts  2.66 us
  transfers between devices with their start and end apart: 23, of which 12 were waited for; matrix products, arithmetic and copies ran while one was open for 2% of the time, Pallas kernels for 5%

profile of v8, /device:TPU:0, one launch (start us, length us, event | category | flops | bytes accessed | tf_op | source)
XLA Modules:
  0.0 65.3 jit_solution(17666667118847360274)
XLA Ops:
  0.6 1.0 %slice_select_fusion.1 = f32[2,64,256]{2,1,0:T(8,128)S(1)} fusion(f32[2,128,256]{2,1,0:T(8,128)} %param.14, pred[]{:T(512)S(6)} %eq.15), kind=kLoop, calls=%fused_computation.25 | loop fusion | flops 32768 | bytes 393217 | tf_op jit(solution)/shard_map/jit(_where)/select_n | solution.py:432
  1.6 3.1 %collective-permute-start = (f32[2,64,256]{2,1,0:T(8,128)S(1)}, f32[2,64,256]{2,1,0:T(8,128)S(1)}, u32[]{:S(2)}, u32[]{:S(2)}) collective-permute-start(f32[2,64,256]{2,1,0:T(8,128)S(1)} %slice_select_fusion.1), channel_id=1, source_target_pairs={{0,4},{1,3},{2,6},{3,1},{4,0},{5,9},{6,2},{7,11},{8,12},{9,5},{10,... | collective-permute-start | bytes 393224 | tf_op jit(solution)/shard_map/ppermute | solution.py:356
  4.7 0.1 slice_select_fusion.4
  4.8 0.0 copy-start.6
  4.8 1.4 %collective-permute-start.2 = (f32[2,64,64]{2,1,0:T(8,128)S(1)}, f32[2,64,64]{2,1,0:T(8,128)S(1)}, u32[]{:S(2)}, u32[]{:S(2)}) collective-permute-start(f32[2,64,64]{2,1,0:T(8,128)S(1)} %slice_select_fusion.4), channel_id=1, source_target_pairs={{0,6},{1,3},{2,4},{3,1},{4,2},{5,11},{6,0},{7,9},{8,14},{9,7},{10,... | collective-permute-start | bytes 98312 | tf_op jit(solution)/shard_map/ppermute | solution.py:356
  6.3 0.2 collective-permute-start.1
  6.5 0.1 pad_add_fusion.place
  7.2 0.0 copy-start.7
  7.2 0.7 %copy-done.7 = s32[1,1,16,2]{2,3,1,0:T(2,128)S(1)} copy-done((s32[1,1,16,2]{2,3,1,0:T(2,128)S(1)}, s32[1,1,16,2]{2,3,1,0:T(2,128)}, u32[]{:S(2)}) %copy-start.7) | copy-done | bytes 152
  7.9 1.2 %copy-done = f32[1,1,16,128,128]{4,3,2,1,0:T(8,128)S(1)} copy-done((f32[1,1,16,128,128]{4,3,2,1,0:T(8,128)S(1)}, f32[1,1,16,128,128]{4,3,2,1,0:T(8,128)}, u32[]{:S(2)}) %copy-start) | copy-done | bytes 1048600
  9.1 1.6 %prepared.1 = (f32[8,128,128]{2,1,0:T(8,128)S(1)}, s32[34]{0:T(128)S(1)}) custom-call(s32[4]{0:T(128)S(1)} %pad_add_fusion.place, s32[2,16]{1,0:T(2,128)S(1)} %bitcast.36, s32[1,1]{1,0:T(1,128)S(6)} %copy.16.counts, f32[8,2,128,128]{3,2,1,0:T(8,128)S(1)} %bitcast.33, bf16[128,128]{1,0:T(8,128)(2,1)S(1)} %copy-done.6), custom_call_target="tpu_custom_call" | custom-call | flops 100663296 | bytes 1048576 | tf_op jit(solution)/shard_map/prepared/pallas_call | solution.py:244
  10.7 0.0 collective-permute-done.2
  10.8 0.0 collective-permute-done.1
  10.8 0.2 fusion.6
  11.1 0.0 copy-start.1
  11.1 0.0 copy-start.2
  11.1 0.0 copy-start.3
  11.1 0.0 copy-start.4
  11.1 0.0 copy-start.5
  11.2 0.1 collective-permute-start.3
  11.2 0.7 %copy-done.1 = f32[1,2,128,128]{3,2,1,0:T(8,128)S(1)} copy-done((f32[1,2,128,128]{3,2,1,0:T(8,128)S(1)}, f32[1,2,128,128]{3,2,1,0:T(8,128)}, u32[]{:S(2)}) %copy-start.1) | copy-done | bytes 131096
  12.0 1.3 %collective-permute-done.4.refs_4_ = f32[256,128]{1,0:T(8,128)S(1)} collective-permute-done((f32[256,128]{1,0:T(8,128)S(1)}, f32[256,128]{1,0:T(8,128)S(1)}, u32[]{:S(2)}, u32[]{:S(2)}) %collective-permute-start.4) | collective-permute-done | bytes 131104 | tf_op jit(solution)/shard_map/ppermute | solution.py:332
  13.3 4.4 %waves.2 = (f32[256,128]{1,0:T(8,128)S(1)}, f32[256,128]{1,0:T(8,128)S(1)}, f32[8,2,128,128]{3,2,1,0:T(8,128)S(1)}) custom-call(s32[34]{0:T(128)S(1)} %get-tuple-element.29.refs_0_, f32[768,128]{1,0:T(8,128)S(1)} %bitcast.32, f32[256,128]{1,0:T(8,128)S(1)} %bitcast.35, f32[768,128]{1,0:T(8,128)S(1)} %collective-permute-done.3.refs_3_, ...), custom_call_target="tpu_custom_call" | custom-call | tf_op jit(solution)/shard_map/waves/pallas_call | solution.py:288
  17.7 0.2 collective-permute-start.5
  17.9 1.0 %placed.2 = (f32[768,128]{1,0:T(8,128)S(1)}, f32[768,128]{1,0:T(8,128)S(1)}) custom-call(s32[34]{0:T(128)S(1)} %get-tuple-element.29.refs_0_, f32[8,2,128,128]{3,2,1,0:T(8,128)S(1)} %get-tuple-element.34.refs_1_), custom_call_target="tpu_custom_call" | custom-call | tf_op jit(solution)/shard_map/placed/pallas_call | solution.py:316
  18.9 0.3 collective-permute-done.5
  19.2 0.2 collective-permute-start.9
  19.4 1.8 %collective-permute-start.6 = (f32[256,128]{1,0:T(8,128)S(1)}, f32[256,128]{1,0:T(8,128)S(1)}, u32[]{:S(2)}, u32[]{:S(2)}) collective-permute-start(f32[256,128]{1,0:T(8,128)S(1)} %add.182), channel_id=1, source_target_pairs={{0,2},{1,9},{2,0},{3,11},{4,6},{5,13},{6,4},{7,15},{8,10},{9,1},{1... | collective-permute-start | bytes 393224 | tf_op jit(solution)/shard_map/ppermute | solution.py:407
  21.2 0.0 collective-permute-done.9
  21.2 0.1 add.194
  21.3 1.7 %collective-permute-start.10 = (f32[768,128]{1,0:T(8,128)S(1)}, f32[768,128]{1,0:T(8,128)S(1)}, u32[]{:S(2)}, u32[]{:S(2)}) collective-permute-start(f32[768,128]{1,0:T(8,128)S(1)} %add.194), channel_id=1, source_target_pairs={{0,4},{1,3},{2,6},{3,1},{4,0},{5,9},{6,2},{7,11},{8,12},{9,5},{10,... | collective-permute-start | bytes 1179656 | tf_op jit(solution)/shard_map/ppermute | solution.py:356
  23.0 1.4 %collective-permute-done.6 = f32[256,128]{1,0:T(8,128)S(1)} collective-permute-done((f32[256,128]{1,0:T(8,128)S(1)}, f32[256,128]{1,0:T(8,128)S(1)}, u32[]{:S(2)}, u32[]{:S(2)}) %collective-permute-start.6) | collective-permute-done | bytes 131104 | tf_op jit(solution)/shard_map/ppermute | solution.py:407
  24.4 2.0 %collective-permute-start.7 = (f32[256,128]{1,0:T(8,128)S(1)}, f32[256,128]{1,0:T(8,128)S(1)}, u32[]{:S(2)}, u32[]{:S(2)}) collective-permute-start(f32[256,128]{1,0:T(8,128)S(1)} %add.183), channel_id=1, source_target_pairs={{0,4},{1,3},{2,6},{3,1},{4,0},{5,7},{6,2},{7,5},{8,12},{9,11},{10,... | collective-permute-start | bytes 393224 | tf_op jit(solution)/shard_map/ppermute | solution.py:407
  26.4 4.4 %collective-permute-done.7 = f32[256,128]{1,0:T(8,128)S(1)} collective-permute-done((f32[256,128]{1,0:T(8,128)S(1)}, f32[256,128]{1,0:T(8,128)S(1)}, u32[]{:S(2)}, u32[]{:S(2)}) %collective-permute-start.7) | collective-permute-done | bytes 131104 | tf_op jit(solution)/shard_map/ppermute | solution.py:407
  30.8 2.8 %collective-permute-start.8 = (f32[256,128]{1,0:T(8,128)S(1)}, f32[256,128]{1,0:T(8,128)S(1)}, u32[]{:S(2)}, u32[]{:S(2)}) collective-permute-start(f32[256,128]{1,0:T(8,128)S(1)} %add.184), channel_id=1, source_target_pairs={{0,8},{1,5},{2,10},{3,7},{4,12},{5,1},{6,14},{7,3},{8,0},{9,13},{1... | collective-permute-start | bytes 393224 | tf_op jit(solution)/shard_map/ppermute | solution.py:407
  33.7 1.6 %collective-permute-start.11 = (f32[256,128]{1,0:T(8,128)S(1)}, f32[256,128]{1,0:T(8,128)S(1)}, u32[]{:S(2)}, u32[]{:S(2)}) collective-permute-start(f32[256,128]{1,0:T(8,128)S(1)} %slice_select_fusion.2), channel_id=1, source_target_pairs={{0,2},{2,0},{1,3},{3,1},{4,6},{6,4},{5,7},{7,5},{8,10},{10,8},{9,1... | collective-permute-start | bytes 393224 | tf_op jit(solution)/shard_map/ppermute | solution.py:375
  35.3 0.1 and_select_fusion.2
  35.4 1.3 %collective-permute-done.8 = f32[256,128]{1,0:T(8,128)S(1)} collective-permute-done((f32[256,128]{1,0:T(8,128)S(1)}, f32[256,128]{1,0:T(8,128)S(1)}, u32[]{:S(2)}, u32[]{:S(2)}) %collective-permute-start.8) | collective-permute-done | bytes 131104 | tf_op jit(solution)/shard_map/ppermute | solution.py:407
  36.8 2.0 %collective-permute-done.11 = f32[256,128]{1,0:T(8,128)S(1)} collective-permute-done((f32[256,128]{1,0:T(8,128)S(1)}, f32[256,128]{1,0:T(8,128)S(1)}, u32[]{:S(2)}, u32[]{:S(2)}) %collective-permute-start.11) | collective-permute-done | bytes 131104 | tf_op jit(solution)/shard_map/ppermute | solution.py:375
  38.8 0.1 fusion.1
  38.9 0.1 collective-permute-start.12
  39.0 0.6 collective-permute-start.13
  39.6 1.3 %collective-permute-done.13.refs_4_ = f32[256,128]{1,0:T(8,128)S(1)} collective-permute-done((f32[256,128]{1,0:T(8,128)S(1)}, f32[256,128]{1,0:T(8,128)S(1)}, u32[]{:S(2)}, u32[]{:S(2)}) %collective-permute-start.13) | collective-permute-done | bytes 131104 | tf_op jit(solution)/shard_map/ppermute | solution.py:332
  40.9 4.4 %waves.3 = (f32[256,128]{1,0:T(8,128)S(1)}, f32[256,128]{1,0:T(8,128)S(1)}, f32[8,2,128,128]{3,2,1,0:T(8,128)S(1)}) custom-call(s32[34]{0:T(128)S(1)} %get-tuple-element.29.refs_0_, f32[768,128]{1,0:T(8,128)S(1)} %multiply_add_fusion.refs_1_, f32[256,128]{1,0:T(8,128)S(1)} %multiply_add_fusion.1.refs_2_, f32[768,128]{1,0:T(8,128)S(1)} %collective-permute-done.12.refs_3_, ...), custom_call_target="tpu_custom_call" | custom-call | tf_op jit(solution)/shard_map/waves/pallas_call | solution.py:288
  45.3 0.2 collective-permute-start.14
  45.5 1.0 %placed.3 = (f32[768,128]{1,0:T(8,128)S(1)}, f32[768,128]{1,0:T(8,128)S(1)}) custom-call(s32[34]{0:T(128)S(1)} %get-tuple-element.29.refs_0_, f32[8,2,128,128]{3,2,1,0:T(8,128)S(1)} %get-tuple-element.45.refs_1_), custom_call_target="tpu_custom_call" | custom-call | tf_op jit(solution)/shard_map/placed/pallas_call | solution.py:316
  46.5 0.2 collective-permute-done.14
  46.7 0.2 collective-permute-start.15
  47.0 1.6 %collective-permute-start.19 = (f32[256,128]{1,0:T(8,128)S(1)}, f32[256,128]{1,0:T(8,128)S(1)}, u32[]{:S(2)}, u32[]{:S(2)}) collective-permute-start(f32[256,128]{1,0:T(8,128)S(1)} %add.200), channel_id=1, source_target_pairs={{0,2},{1,9},{2,0},{3,11},{4,6},{5,13},{6,4},{7,15},{8,10},{9,1},{1... | collective-permute-start | bytes 393224 | tf_op jit(solution)/shard_map/ppermute | solution.py:407
  48.7 2.5 %collective-permute-start.16 = (f32[3,2,64,128]{3,2,1,0:T(8,128)S(1)}, f32[3,2,64,128]{3,2,1,0:T(8,128)S(1)}, u32[]{:S(2)}, u32[]{:S(2)}) collective-permute-start(f32[3,2,64,128]{3,2,1,0:T(8,128)S(1)} %bitcast.41), channel_id=1, source_target_pairs={{0,4},{1,3},{2,6},{3,1},{4,0},{5,9},{6,2},{7,11},{8,12},{9,5},{10,... | collective-permute-start | bytes 589832 | tf_op jit(solution)/shard_map/ppermute | solution.py:356
  51.2 1.5 %collective-permute-done.19 = f32[256,128]{1,0:T(8,128)S(1)} collective-permute-done((f32[256,128]{1,0:T(8,128)S(1)}, f32[256,128]{1,0:T(8,128)S(1)}, u32[]{:S(2)}, u32[]{:S(2)}) %collective-permute-start.19) | collective-permute-done | bytes 131104 | tf_op jit(solution)/shard_map/ppermute | solution.py:407
  52.7 2.9 %collective-permute-start.20 = (f32[256,128]{1,0:T(8,128)S(1)}, f32[256,128]{1,0:T(8,128)S(1)}, u32[]{:S(2)}, u32[]{:S(2)}) collective-permute-start(f32[256,128]{1,0:T(8,128)S(1)} %add.205), channel_id=1, source_target_pairs={{0,12},{1,7},{2,14},{3,5},{4,8},{5,3},{6,10},{7,1},{8,4},{9,15},{1... | collective-permute-start | bytes 393224 | tf_op jit(solution)/shard_map/ppermute | solution.py:407
  55.7 0.4 collective-permute-start.21
  56.0 1.1 %collective-permute-start.22 = (f32[256,128]{1,0:T(8,128)S(1)}, f32[256,128]{1,0:T(8,128)S(1)}, u32[]{:S(2)}, u32[]{:S(2)}) collective-permute-start(f32[256,128]{1,0:T(8,128)S(1)} %add.205), channel_id=1, source_target_pairs={{0,4},{1,3},{2,6},{3,1},{4,0},{5,7},{6,2},{7,5},{8,12},{9,11},{10,... | collective-permute-start | bytes 393224 | tf_op jit(solution)/shard_map/ppermute | solution.py:407
  57.2 0.1 fusion.8
  57.3 1.6 %collective-permute-start.17 = (f32[2,64,64]{2,1,0:T(8,128)S(1)}, f32[2,64,64]{2,1,0:T(8,128)S(1)}, u32[]{:S(2)}, u32[]{:S(2)}) collective-permute-start(f32[2,64,64]{2,1,0:T(8,128)S(1)} %fusion.8), channel_id=1, source_target_pairs={{0,2},{2,0},{1,3},{3,1},{4,6},{6,4},{5,7},{7,5},{8,10},{10,8},{9,1... | collective-permute-start | bytes 98312 | tf_op jit(solution)/shard_map/ppermute | solution.py:375
  58.9 2.9 %collective-permute-done.17 = f32[2,64,64]{2,1,0:T(8,128)S(1)} collective-permute-done((f32[2,64,64]{2,1,0:T(8,128)S(1)}, f32[2,64,64]{2,1,0:T(8,128)S(1)}, u32[]{:S(2)}, u32[]{:S(2)}) %collective-permute-start.17) | collective-permute-done | bytes 32800 | tf_op jit(solution)/shard_map/ppermute | solution.py:375
  61.8 0.1 fusion.9
  61.9 0.2 fusion.4
  62.0 0.1 collective-permute-start.18
  62.1 1.2 %collective-permute-done.21 = f32[256,128]{1,0:T(8,128)S(1)} collective-permute-done((f32[256,128]{1,0:T(8,128)S(1)}, f32[256,128]{1,0:T(8,128)S(1)}, u32[]{:S(2)}, u32[]{:S(2)}) %collective-permute-start.21) | collective-permute-done | bytes 131104 | tf_op jit(solution)/shard_map/ppermute | solution.py:407
  63.3 0.6 collective-permute-done.22
  63.9 0.7 %pad_maximum_fusion.2 = f32[2,128,256]{2,1,0:T(8,128)} fusion(f32[2,64,256]{2,1,0:T(8,128)S(1)} %get-tuple-element.67, f32[2,64,256]{2,1,0:T(8,128)S(1)} %get-tuple-element.66), kind=kLoop, calls=%fused_computation.11 | loop fusion | flops 65536 | bytes 524288 | tf_op jit(solution)/shard_map/concatenate | solution.py:504
  64.7 0.7 %multiply_subtract_fusion = f32[256,128]{1,0:T(8,128)} fusion(f32[256,128]{1,0:T(8,128)S(1)} %multiply_add_fusion.1.refs_2_, f32[256,128]{1,0:T(8,128)S(1)} %add_add_fusion), kind=kLoop, calls=%fused_computation.20 | loop fusion | flops 65536 | bytes 393216 | tf_op jit(solution)/shard_map/sub | solution.py:508
  (44 shorter events, 0.7 us)
Async XLA Ops:
  1.6 9.2 %collective-permute-start = (f32[2,64,256]{2,1,0:T(8,128)S(1)}, f32[2,64,256]{2,1,0:T(8,128)S(1)}, u32[]{:S(2)}, u32[]{:S(2)}) collective-permute-start(f32[2,64,256]{2,1,0:T(8,128)S(1)} %slice_select_fusion.1), channel_id=1, source_target_pairs={{0,4},{1,3},{2,6},{3,1},{4,0},{5,9},{6,2},{7,11},{8,12},{9,5},{10,... | collective-permute-start | bytes 393224 | tf_op jit(solution)/shard_map/ppermute | solution.py:356
  4.8 2.4 %copy-start.6 = (bf16[128,128]{1,0:T(8,128)(2,1)S(1)}, bf16[128,128]{1,0:T(8,128)(2,1)}, u32[]{:S(2)}) copy-start(bf16[128,128]{1,0:T(8,128)(2,1)} %constant.86.clone.order) | copy-start | bytes 98308
  4.8 5.9 %collective-permute-start.2 = (f32[2,64,64]{2,1,0:T(8,128)S(1)}, f32[2,64,64]{2,1,0:T(8,128)S(1)}, u32[]{:S(2)}, u32[]{:S(2)}) collective-permute-start(f32[2,64,64]{2,1,0:T(8,128)S(1)} %slice_select_fusion.4), channel_id=1, source_target_pairs={{0,6},{1,3},{2,4},{3,1},{4,2},{5,11},{6,0},{7,9},{8,14},{9,7},{10,... | collective-permute-start | bytes 98312 | tf_op jit(solution)/shard_map/ppermute | solution.py:356
  6.3 4.5 %collective-permute-start.1 = (f32[2,64,64]{2,1,0:T(8,128)S(1)}, f32[2,64,64]{2,1,0:T(8,128)S(1)}, u32[]{:S(2)}, u32[]{:S(2)}) collective-permute-start(f32[2,64,64]{2,1,0:T(8,128)S(1)} %slice_select_fusion.4), channel_id=1, source_target_pairs={{0,2},{2,0},{1,3},{3,1},{4,6},{6,4},{5,7},{7,5},{8,10},{10,8},{9,1... | collective-permute-start | bytes 98312 | tf_op jit(solution)/shard_map/ppermute | solution.py:375
  7.2 0.7 %copy-start.7 = (s32[1,1,16,2]{2,3,1,0:T(2,128)S(1)}, s32[1,1,16,2]{2,3,1,0:T(2,128)}, u32[]{:S(2)}) copy-start(s32[1,1,16,2]{2,3,1,0:T(2,128)} %param.16) | copy-start | bytes 388
  7.9 1.2 %copy-start = (f32[1,1,16,128,128]{4,3,2,1,0:T(8,128)S(1)}, f32[1,1,16,128,128]{4,3,2,1,0:T(8,128)}, u32[]{:S(2)}) copy-start(f32[1,1,16,128,128]{4,3,2,1,0:T(8,128)} %param.18) | copy-start | bytes 3145732
  11.1 0.9 %copy-start.1 = (f32[1,2,128,128]{3,2,1,0:T(8,128)S(1)}, f32[1,2,128,128]{3,2,1,0:T(8,128)}, u32[]{:S(2)}) copy-start(f32[1,2,128,128]{3,2,1,0:T(8,128)} %param.15) | copy-start | bytes 393220
  11.1 2.2 %copy-start.2 = (bf16[2,128,256]{2,1,0:T(8,128)(2,1)S(1)}, bf16[2,128,256]{2,1,0:T(8,128)(2,1)}, u32[]{:S(2)}) copy-start(bf16[2,128,256]{2,1,0:T(8,128)(2,1)} %constant.87.clone.refs_6_) | copy-start | bytes 393220
  11.1 2.2 %copy-start.3 = (bf16[2,256,128]{2,1,0:T(8,128)(2,1)S(1)}, bf16[2,256,128]{2,1,0:T(8,128)(2,1)}, u32[]{:S(2)}) copy-start(bf16[2,256,128]{2,1,0:T(8,128)(2,1)} %constant.88.clone.refs_7_) | copy-start | bytes 393220
  11.1 2.2 %copy-start.4 = (bf16[2,256,128]{2,1,0:T(8,128)(2,1)S(1)}, bf16[2,256,128]{2,1,0:T(8,128)(2,1)}, u32[]{:S(2)}) copy-start(bf16[2,256,128]{2,1,0:T(8,128)(2,1)} %constant.89.clone.refs_8_) | copy-start | bytes 393220
  11.1 2.2 %copy-start.5 = (bf16[2,128,256]{2,1,0:T(8,128)(2,1)S(1)}, bf16[2,128,256]{2,1,0:T(8,128)(2,1)}, u32[]{:S(2)}) copy-start(bf16[2,128,256]{2,1,0:T(8,128)(2,1)} %constant.90.clone.refs_9_) | copy-start | bytes 393220
  11.2 2.2 %collective-permute-start.3 = (f32[768,128]{1,0:T(8,128)S(1)}, f32[768,128]{1,0:T(8,128)S(1)}, u32[]{:S(2)}, u32[]{:S(2)}) collective-permute-start(f32[768,128]{1,0:T(8,128)S(1)} %bitcast.31), channel_id=1, source_target_pairs={{0,1},{1,0},{2,3},{3,2},{4,5},{5,4},{6,7},{7,6},{8,9},{9,8},{10,11... | collective-permute-start | bytes 1179656 | tf_op jit(solution)/shard_map/ppermute | solution.py:332
  12.0 1.3 %collective-permute-start.4 = (f32[256,128]{1,0:T(8,128)S(1)}, f32[256,128]{1,0:T(8,128)S(1)}, u32[]{:S(2)}, u32[]{:S(2)}) collective-permute-start(f32[256,128]{1,0:T(8,128)S(1)} %bitcast.34), channel_id=1, source_target_pairs={{0,1},{1,0},{2,3},{3,2},{4,5},{5,4},{6,7},{7,6},{8,9},{9,8},{10,11... | collective-permute-start | bytes 393224 | tf_op jit(solution)/shard_map/ppermute | solution.py:332
  17.7 1.4 %collective-permute-start.5 = (f32[256,128]{1,0:T(8,128)S(1)}, f32[256,128]{1,0:T(8,128)S(1)}, u32[]{:S(2)}, u32[]{:S(2)}) collective-permute-start(f32[256,128]{1,0:T(8,128)S(1)} %get-tuple-element.33), channel_id=1, source_target_pairs={{0,1},{1,0},{2,3},{3,2},{4,5},{5,4},{6,7},{7,6},{8,9},{9,8},{10,11... | collective-permute-start | bytes 393224 | tf_op jit(solution)/shard_map/ppermute | solution.py:332
  19.2 2.1 %collective-permute-start.9 = (f32[768,128]{1,0:T(8,128)S(1)}, f32[768,128]{1,0:T(8,128)S(1)}, u32[]{:S(2)}, u32[]{:S(2)}) collective-permute-start(f32[768,128]{1,0:T(8,128)S(1)} %get-tuple-element.39), channel_id=1, source_target_pairs={{0,1},{1,0},{2,3},{3,2},{4,5},{5,4},{6,7},{7,6},{8,9},{9,8},{10,11... | collective-permute-start | bytes 1179656 | tf_op jit(solution)/shard_map/ppermute | solution.py:332
  19.4 5.0 %collective-permute-start.6 = (f32[256,128]{1,0:T(8,128)S(1)}, f32[256,128]{1,0:T(8,128)S(1)}, u32[]{:S(2)}, u32[]{:S(2)}) collective-permute-start(f32[256,128]{1,0:T(8,128)S(1)} %add.182), channel_id=1, source_target_pairs={{0,2},{1,9},{2,0},{3,11},{4,6},{5,13},{6,4},{7,15},{8,10},{9,1},{1... | collective-permute-start | bytes 393224 | tf_op jit(solution)/shard_map/ppermute | solution.py:407
  21.3 12.4 %collective-permute-start.10 = (f32[768,128]{1,0:T(8,128)S(1)}, f32[768,128]{1,0:T(8,128)S(1)}, u32[]{:S(2)}, u32[]{:S(2)}) collective-permute-start(f32[768,128]{1,0:T(8,128)S(1)} %add.194), channel_id=1, source_target_pairs={{0,4},{1,3},{2,6},{3,1},{4,0},{5,9},{6,2},{7,11},{8,12},{9,5},{10,... | collective-permute-start | bytes 1179656 | tf_op jit(solution)/shard_map/ppermute | solution.py:356
  24.4 6.4 %collective-permute-start.7 = (f32[256,128]{1,0:T(8,128)S(1)}, f32[256,128]{1,0:T(8,128)S(1)}, u32[]{:S(2)}, u32[]{:S(2)}) collective-permute-start(f32[256,128]{1,0:T(8,128)S(1)} %add.183), channel_id=1, source_target_pairs={{0,4},{1,3},{2,6},{3,1},{4,0},{5,7},{6,2},{7,5},{8,12},{9,11},{10,... | collective-permute-start | bytes 393224 | tf_op jit(solution)/shard_map/ppermute | solution.py:407
  30.8 5.9 %collective-permute-start.8 = (f32[256,128]{1,0:T(8,128)S(1)}, f32[256,128]{1,0:T(8,128)S(1)}, u32[]{:S(2)}, u32[]{:S(2)}) collective-permute-start(f32[256,128]{1,0:T(8,128)S(1)} %add.184), channel_id=1, source_target_pairs={{0,8},{1,5},{2,10},{3,7},{4,12},{5,1},{6,14},{7,3},{8,0},{9,13},{1... | collective-permute-start | bytes 393224 | tf_op jit(solution)/shard_map/ppermute | solution.py:407
  33.7 5.0 %collective-permute-start.11 = (f32[256,128]{1,0:T(8,128)S(1)}, f32[256,128]{1,0:T(8,128)S(1)}, u32[]{:S(2)}, u32[]{:S(2)}) collective-permute-start(f32[256,128]{1,0:T(8,128)S(1)} %slice_select_fusion.2), channel_id=1, source_target_pairs={{0,2},{2,0},{1,3},{3,1},{4,6},{6,4},{5,7},{7,5},{8,10},{10,8},{9,1... | collective-permute-start | bytes 393224 | tf_op jit(solution)/shard_map/ppermute | solution.py:375
  38.9 2.0 %collective-permute-start.12 = (f32[768,128]{1,0:T(8,128)S(1)}, f32[768,128]{1,0:T(8,128)S(1)}, u32[]{:S(2)}, u32[]{:S(2)}) collective-permute-start(f32[768,128]{1,0:T(8,128)S(1)} %multiply_add_fusion.refs_1_), channel_id=1, source_target_pairs={{0,1},{1,0},{2,3},{3,2},{4,5},{5,4},{6,7},{7,6},{8,9},{9,8},{10,11... | collective-permute-start | bytes 1179656 | tf_op jit(solution)/shard_map/ppermute | solution.py:332
  39.0 1.9 %collective-permute-start.13 = (f32[256,128]{1,0:T(8,128)S(1)}, f32[256,128]{1,0:T(8,128)S(1)}, u32[]{:S(2)}, u32[]{:S(2)}) collective-permute-start(f32[256,128]{1,0:T(8,128)S(1)} %multiply_add_fusion.1.refs_2_), channel_id=1, source_target_pairs={{0,1},{1,0},{2,3},{3,2},{4,5},{5,4},{6,7},{7,6},{8,9},{9,8},{10,11... | collective-permute-start | bytes 393224 | tf_op jit(solution)/shard_map/ppermute | solution.py:332
  45.3 1.4 %collective-permute-start.14 = (f32[256,128]{1,0:T(8,128)S(1)}, f32[256,128]{1,0:T(8,128)S(1)}, u32[]{:S(2)}, u32[]{:S(2)}) collective-permute-start(f32[256,128]{1,0:T(8,128)S(1)} %get-tuple-element.44), channel_id=1, source_target_pairs={{0,1},{1,0},{2,3},{3,2},{4,5},{5,4},{6,7},{7,6},{8,9},{9,8},{10,11... | collective-permute-start | bytes 393224 | tf_op jit(solution)/shard_map/ppermute | solution.py:332
  46.7 1.9 %collective-permute-start.15 = (f32[768,128]{1,0:T(8,128)S(1)}, f32[768,128]{1,0:T(8,128)S(1)}, u32[]{:S(2)}, u32[]{:S(2)}) collective-permute-start(f32[768,128]{1,0:T(8,128)S(1)} %get-tuple-element.49), channel_id=1, source_target_pairs={{0,1},{1,0},{2,3},{3,2},{4,5},{5,4},{6,7},{7,6},{8,9},{9,8},{10,11... | collective-permute-start | bytes 1179656 | tf_op jit(solution)/shard_map/ppermute | solution.py:332
  47.0 5.7 %collective-permute-start.19 = (f32[256,128]{1,0:T(8,128)S(1)}, f32[256,128]{1,0:T(8,128)S(1)}, u32[]{:S(2)}, u32[]{:S(2)}) collective-permute-start(f32[256,128]{1,0:T(8,128)S(1)} %add.200), channel_id=1, source_target_pairs={{0,2},{1,9},{2,0},{3,11},{4,6},{5,13},{6,4},{7,15},{8,10},{9,1},{1... | collective-permute-start | bytes 393224 | tf_op jit(solution)/shard_map/ppermute | solution.py:407
  48.7 8.5 %collective-permute-start.16 = (f32[3,2,64,128]{3,2,1,0:T(8,128)S(1)}, f32[3,2,64,128]{3,2,1,0:T(8,128)S(1)}, u32[]{:S(2)}, u32[]{:S(2)}) collective-permute-start(f32[3,2,64,128]{3,2,1,0:T(8,128)S(1)} %bitcast.41), channel_id=1, source_target_pairs={{0,4},{1,3},{2,6},{3,1},{4,0},{5,9},{6,2},{7,11},{8,12},{9,5},{10,... | collective-permute-start | bytes 589832 | tf_op jit(solution)/shard_map/ppermute | solution.py:356
  52.7 9.4 %collective-permute-start.20 = (f32[256,128]{1,0:T(8,128)S(1)}, f32[256,128]{1,0:T(8,128)S(1)}, u32[]{:S(2)}, u32[]{:S(2)}) collective-permute-start(f32[256,128]{1,0:T(8,128)S(1)} %add.205), channel_id=1, source_target_pairs={{0,12},{1,7},{2,14},{3,5},{4,8},{5,3},{6,10},{7,1},{8,4},{9,15},{1... | collective-permute-start | bytes 393224 | tf_op jit(solution)/shard_map/ppermute | solution.py:407
  55.7 7.6 %collective-permute-start.21 = (f32[256,128]{1,0:T(8,128)S(1)}, f32[256,128]{1,0:T(8,128)S(1)}, u32[]{:S(2)}, u32[]{:S(2)}) collective-permute-start(f32[256,128]{1,0:T(8,128)S(1)} %add.205), channel_id=1, source_target_pairs={{0,8},{1,5},{2,10},{3,7},{4,12},{5,1},{6,14},{7,3},{8,0},{9,13},{1... | collective-permute-start | bytes 393224 | tf_op jit(solution)/shard_map/ppermute | solution.py:407
  56.0 7.8 %collective-permute-start.22 = (f32[256,128]{1,0:T(8,128)S(1)}, f32[256,128]{1,0:T(8,128)S(1)}, u32[]{:S(2)}, u32[]{:S(2)}) collective-permute-start(f32[256,128]{1,0:T(8,128)S(1)} %add.205), channel_id=1, source_target_pairs={{0,4},{1,3},{2,6},{3,1},{4,0},{5,7},{6,2},{7,5},{8,12},{9,11},{10,... | collective-permute-start | bytes 393224 | tf_op jit(solution)/shard_map/ppermute | solution.py:407
  57.3 4.5 %collective-permute-start.17 = (f32[2,64,64]{2,1,0:T(8,128)S(1)}, f32[2,64,64]{2,1,0:T(8,128)S(1)}, u32[]{:S(2)}, u32[]{:S(2)}) collective-permute-start(f32[2,64,64]{2,1,0:T(8,128)S(1)} %fusion.8), channel_id=1, source_target_pairs={{0,2},{2,0},{1,3},{3,1},{4,6},{6,4},{5,7},{7,5},{8,10},{10,8},{9,1... | collective-permute-start | bytes 98312 | tf_op jit(solution)/shard_map/ppermute | solution.py:375
  62.0 1.9 %collective-permute-start.18 = (f32[2,64,256]{2,1,0:T(8,128)S(1)}, f32[2,64,256]{2,1,0:T(8,128)S(1)}, u32[]{:S(2)}, u32[]{:S(2)}) collective-permute-start(f32[2,64,256]{2,1,0:T(8,128)S(1)} %fusion.4), channel_id=1, source_target_pairs={{0,1},{1,0},{2,3},{3,2},{4,5},{5,4},{6,7},{7,6},{8,9},{9,8},{10,11... | collective-permute-start | bytes 393224 | tf_op jit(solution)/shard_map/ppermute | solution.py:332

commit v9 on v8

--- a/solution.py
+++ b/solution.py
@@ -431,6 +431,7 @@
 
     strip = jnp.where(lower, obj[:, half:], obj[:, :half])
     edges = (strip[:, :, :half], strip[:, :, tile_cols - half :])
+    strip, *edges = lax.optimization_barrier((strip, *edges))
     beside = swap_neighbours(strip)
     strip_low, strip_high = from_cols(edges, swap_cols)
     corner_low, corner_high = from_cols(edges, swap_neighbours)

time: 65.6 us -> 65.5 us (level)
  starting transfers between devices: 26.3 us -> 24.8 us
  waiting for transfers between devices: 18.4 us -> 19.9 us
    ppermute x7, waiting for transfers between devices: 10.4 us -> 13.2 us  [sum_tiles(): arrived.append(lax.ppermute(block, ('row', 'col', 'mode'), route))]
    ppermute x3, waiting for transfers between devices: 4.89 us -> 2.99 us  [swap_cols(): lax.ppermute(block, 'col', [(i, i if o is None else o) for i, o in enumer...]
    ppermute x7, starting transfers between devices: 12.7 us -> 11.3 us  [sum_tiles(): arrived.append(lax.ppermute(block, ('row', 'col', 'mode'), route))]
  transfers between devices with their start and end apart: 23 -> 23, of which waited for: 12 -> 14; matrix products, arithmetic and copies ran while one was open for 2% -> 2% of each run, Pallas kernels for 5% -> 5%
where the time goes in v9:
time: 65.5 us; the launch traced here: 65.3 us
  starting transfers between devices  24.8 us (38%)
  waiting for transfers between devices  19.9 us (30%)
  Pallas kernels  12.3 us (19%)
  other arithmetic  3.8 us (6%)
  local copies, waits for them, and re-layouts  2.82 us (4%)
  between operations  1.68 us (3%)
    ppermute x7, waiting for transfers between devices, sum_tiles(): arrived.append(lax.ppermute(block, ('row', 'col', 'mode'), route))  13.2 us
    ppermute x7, starting transfers between devices, sum_tiles(): arrived.append(lax.ppermute(block, ('row', 'col', 'mode'), route))  11.3 us
    pallas_call x2, Pallas kernels, waves(): pl.pallas_call(body, out_shape=[jax.ShapeDtypeStruct(s, jnp.float32) for...  8.73 us
    ppermute x4, starting transfers between devices, swap_neighbours(): return lax.ppermute(block, ('row', 'col', 'mode'), route)  8.13 us
    ppermute x3, starting transfers between devices, swap_cols(): lax.ppermute(block, 'col', [(i, i if o is None else o) for i, o in enumer...  3.67 us
    ppermute x9, waiting for transfers between devices, swap_modes(): return lax.ppermute(block, 'mode', [(0, 1), (1, 0)])  3.17 us
    ppermute x3, waiting for transfers between devices, swap_cols(): lax.ppermute(block, 'col', [(i, i if o is None else o) for i, o in enumer...  2.99 us
    unnamed x16, local copies, waits for them, and re-layouts  2.66 us
  transfers between devices with their start and end apart: 23, of which 14 were waited for; matrix products, arithmetic and copies ran while one was open for 2% of the time, Pallas kernels for 5%

profile of v9, /device:TPU:0, one launch (start us, length us, event | category | flops | bytes accessed | tf_op | source)
XLA Modules:
  0.0 65.3 jit_solution(4992988569681170200)
XLA Ops:
  0.6 1.0 %slice_select_fusion.1 = f32[2,64,256]{2,1,0:T(8,128)S(1)} fusion(f32[2,128,256]{2,1,0:T(8,128)} %param.14, pred[]{:T(512)S(6)} %eq.15), kind=kLoop, calls=%fused_computation.25 | loop fusion | flops 32768 | bytes 393217 | tf_op jit(solution)/shard_map/jit(_where)/select_n | solution.py:432
  1.6 0.1 fusion.19
  1.7 0.0 copy-start.6
  1.8 4.0 %collective-permute-start.2 = (f32[2,64,64]{2,1,0:T(8,128)S(1)}, f32[2,64,64]{2,1,0:T(8,128)S(1)}, u32[]{:S(2)}, u32[]{:S(2)}) collective-permute-start(f32[2,64,64]{2,1,0:T(8,128)S(1)} %broadcast_select_fusion.6), channel_id=1, source_target_pairs={{0,6},{1,3},{2,4},{3,1},{4,2},{5,11},{6,0},{7,9},{8,14},{9,7},{10,... | collective-permute-start | bytes 98312 | tf_op jit(solution)/shard_map/ppermute | solution.py:356
  5.8 0.5 collective-permute-start.1
  6.3 0.1 collective-permute-start
  6.4 0.1 pad_add_fusion.place
  7.2 0.0 copy-start.7
  7.2 0.7 %copy-done.7 = s32[1,1,16,2]{2,3,1,0:T(2,128)S(1)} copy-done((s32[1,1,16,2]{2,3,1,0:T(2,128)S(1)}, s32[1,1,16,2]{2,3,1,0:T(2,128)}, u32[]{:S(2)}) %copy-start.7) | copy-done | bytes 152
  7.8 1.2 %copy-done = f32[1,1,16,128,128]{4,3,2,1,0:T(8,128)S(1)} copy-done((f32[1,1,16,128,128]{4,3,2,1,0:T(8,128)S(1)}, f32[1,1,16,128,128]{4,3,2,1,0:T(8,128)}, u32[]{:S(2)}) %copy-start) | copy-done | bytes 1048600
  9.1 1.6 %prepared.1 = (f32[8,128,128]{2,1,0:T(8,128)S(1)}, s32[34]{0:T(128)S(1)}) custom-call(s32[4]{0:T(128)S(1)} %pad_add_fusion.place, s32[2,16]{1,0:T(2,128)S(1)} %bitcast.36, s32[1,1]{1,0:T(1,128)S(6)} %copy.16.counts, f32[8,2,128,128]{3,2,1,0:T(8,128)S(1)} %bitcast.33, bf16[128,128]{1,0:T(8,128)(2,1)S(1)} %copy-done.6), custom_call_target="tpu_custom_call" | custom-call | flops 100663296 | bytes 1048576 | tf_op jit(solution)/shard_map/prepared/pallas_call | solution.py:244
  10.7 0.0 collective-permute-done.1
  10.8 0.5 collective-permute-done
  11.3 0.2 fusion.6
  11.5 0.0 copy-start.1
  11.5 0.0 copy-start.2
  11.5 0.0 copy-start.3
  11.6 0.0 copy-start.4
  11.6 0.0 copy-start.5
  11.6 0.1 collective-permute-start.3
  11.7 0.7 %copy-done.1 = f32[1,2,128,128]{3,2,1,0:T(8,128)S(1)} copy-done((f32[1,2,128,128]{3,2,1,0:T(8,128)S(1)}, f32[1,2,128,128]{3,2,1,0:T(8,128)}, u32[]{:S(2)}) %copy-start.1) | copy-done | bytes 131096
  12.4 1.3 %collective-permute-done.4.refs_4_ = f32[256,128]{1,0:T(8,128)S(1)} collective-permute-done((f32[256,128]{1,0:T(8,128)S(1)}, f32[256,128]{1,0:T(8,128)S(1)}, u32[]{:S(2)}, u32[]{:S(2)}) %collective-permute-start.4) | collective-permute-done | bytes 131104 | tf_op jit(solution)/shard_map/ppermute | solution.py:332
  13.8 4.4 %waves.2 = (f32[256,128]{1,0:T(8,128)S(1)}, f32[256,128]{1,0:T(8,128)S(1)}, f32[8,2,128,128]{3,2,1,0:T(8,128)S(1)}) custom-call(s32[34]{0:T(128)S(1)} %get-tuple-element.33.refs_0_, f32[768,128]{1,0:T(8,128)S(1)} %bitcast.32, f32[256,128]{1,0:T(8,128)S(1)} %bitcast.35, f32[768,128]{1,0:T(8,128)S(1)} %collective-permute-done.3.refs_3_, ...), custom_call_target="tpu_custom_call" | custom-call | tf_op jit(solution)/shard_map/waves/pallas_call | solution.py:288
  18.2 0.2 collective-permute-start.5
  18.4 1.0 %placed.2 = (f32[768,128]{1,0:T(8,128)S(1)}, f32[768,128]{1,0:T(8,128)S(1)}) custom-call(s32[34]{0:T(128)S(1)} %get-tuple-element.33.refs_0_, f32[8,2,128,128]{3,2,1,0:T(8,128)S(1)} %get-tuple-element.40.refs_1_), custom_call_target="tpu_custom_call" | custom-call | tf_op jit(solution)/shard_map/placed/pallas_call | solution.py:316
  19.4 0.2 collective-permute-done.5
  19.6 0.2 collective-permute-start.9
  19.8 1.5 %collective-permute-start.6 = (f32[256,128]{1,0:T(8,128)S(1)}, f32[256,128]{1,0:T(8,128)S(1)}, u32[]{:S(2)}, u32[]{:S(2)}) collective-permute-start(f32[256,128]{1,0:T(8,128)S(1)} %add.182), channel_id=1, source_target_pairs={{0,2},{1,9},{2,0},{3,11},{4,6},{5,13},{6,4},{7,15},{8,10},{9,1},{1... | collective-permute-start | bytes 393224 | tf_op jit(solution)/shard_map/ppermute | solution.py:407
  21.3 0.1 collective-permute-done.9
  21.4 0.1 add.194
  21.5 1.5 %collective-permute-start.10 = (f32[768,128]{1,0:T(8,128)S(1)}, f32[768,128]{1,0:T(8,128)S(1)}, u32[]{:S(2)}, u32[]{:S(2)}) collective-permute-start(f32[768,128]{1,0:T(8,128)S(1)} %add.194), channel_id=1, source_target_pairs={{0,4},{1,3},{2,6},{3,1},{4,0},{5,9},{6,2},{7,11},{8,12},{9,5},{10,... | collective-permute-start | bytes 1179656 | tf_op jit(solution)/shard_map/ppermute | solution.py:356
  23.0 1.9 %collective-permute-done.6 = f32[256,128]{1,0:T(8,128)S(1)} collective-permute-done((f32[256,128]{1,0:T(8,128)S(1)}, f32[256,128]{1,0:T(8,128)S(1)}, u32[]{:S(2)}, u32[]{:S(2)}) %collective-permute-start.6) | collective-permute-done | bytes 131104 | tf_op jit(solution)/shard_map/ppermute | solution.py:407
  24.8 1.5 %collective-permute-start.7 = (f32[256,128]{1,0:T(8,128)S(1)}, f32[256,128]{1,0:T(8,128)S(1)}, u32[]{:S(2)}, u32[]{:S(2)}) collective-permute-start(f32[256,128]{1,0:T(8,128)S(1)} %add.183), channel_id=1, source_target_pairs={{0,4},{1,3},{2,6},{3,1},{4,0},{5,7},{6,2},{7,5},{8,12},{9,11},{10,... | collective-permute-start | bytes 393224 | tf_op jit(solution)/shard_map/ppermute | solution.py:407
  26.3 4.8 %collective-permute-done.7 = f32[256,128]{1,0:T(8,128)S(1)} collective-permute-done((f32[256,128]{1,0:T(8,128)S(1)}, f32[256,128]{1,0:T(8,128)S(1)}, u32[]{:S(2)}, u32[]{:S(2)}) %collective-permute-start.7) | collective-permute-done | bytes 131104 | tf_op jit(solution)/shard_map/ppermute | solution.py:407
  31.2 2.3 %collective-permute-start.8 = (f32[256,128]{1,0:T(8,128)S(1)}, f32[256,128]{1,0:T(8,128)S(1)}, u32[]{:S(2)}, u32[]{:S(2)}) collective-permute-start(f32[256,128]{1,0:T(8,128)S(1)} %add.184), channel_id=1, source_target_pairs={{0,8},{1,5},{2,10},{3,7},{4,12},{5,1},{6,14},{7,3},{8,0},{9,13},{1... | collective-permute-start | bytes 393224 | tf_op jit(solution)/shard_map/ppermute | solution.py:407
  33.6 1.6 %collective-permute-start.11 = (f32[256,128]{1,0:T(8,128)S(1)}, f32[256,128]{1,0:T(8,128)S(1)}, u32[]{:S(2)}, u32[]{:S(2)}) collective-permute-start(f32[256,128]{1,0:T(8,128)S(1)} %slice_select_fusion.2), channel_id=1, source_target_pairs={{0,2},{2,0},{1,3},{3,1},{4,6},{6,4},{5,7},{7,5},{8,10},{10,8},{9,1... | collective-permute-start | bytes 393224 | tf_op jit(solution)/shard_map/ppermute | solution.py:375
  35.1 0.1 and_select_fusion.2
  35.3 3.2 %collective-permute-done.8 = f32[256,128]{1,0:T(8,128)S(1)} collective-permute-done((f32[256,128]{1,0:T(8,128)S(1)}, f32[256,128]{1,0:T(8,128)S(1)}, u32[]{:S(2)}, u32[]{:S(2)}) %collective-permute-start.8) | collective-permute-done | bytes 131104 | tf_op jit(solution)/shard_map/ppermute | solution.py:407
  38.5 0.1 collective-permute-done.11
  38.7 0.1 fusion.1
  38.8 0.1 collective-permute-start.12
  38.9 0.6 collective-permute-start.13
  39.4 1.3 %collective-permute-done.13.refs_4_ = f32[256,128]{1,0:T(8,128)S(1)} collective-permute-done((f32[256,128]{1,0:T(8,128)S(1)}, f32[256,128]{1,0:T(8,128)S(1)}, u32[]{:S(2)}, u32[]{:S(2)}) %collective-permute-start.13) | collective-permute-done | bytes 131104 | tf_op jit(solution)/shard_map/ppermute | solution.py:332
  40.8 4.4 %waves.3 = (f32[256,128]{1,0:T(8,128)S(1)}, f32[256,128]{1,0:T(8,128)S(1)}, f32[8,2,128,128]{3,2,1,0:T(8,128)S(1)}) custom-call(s32[34]{0:T(128)S(1)} %get-tuple-element.33.refs_0_, f32[768,128]{1,0:T(8,128)S(1)} %multiply_add_fusion.refs_1_, f32[256,128]{1,0:T(8,128)S(1)} %multiply_add_fusion.1.refs_2_, f32[768,128]{1,0:T(8,128)S(1)} %collective-permute-done.12.refs_3_, ...), custom_call_target="tpu_custom_call" | custom-call | tf_op jit(solution)/shard_map/waves/pallas_call | solution.py:288
  45.1 0.2 collective-permute-start.14
  45.3 1.0 %placed.3 = (f32[768,128]{1,0:T(8,128)S(1)}, f32[768,128]{1,0:T(8,128)S(1)}) custom-call(s32[34]{0:T(128)S(1)} %get-tuple-element.33.refs_0_, f32[8,2,128,128]{3,2,1,0:T(8,128)S(1)} %get-tuple-element.51.refs_1_), custom_call_target="tpu_custom_call" | custom-call | tf_op jit(solution)/shard_map/placed/pallas_call | solution.py:316
  46.3 0.2 collective-permute-done.14
  46.6 0.2 collective-permute-start.15
  46.8 1.6 %collective-permute-start.19 = (f32[256,128]{1,0:T(8,128)S(1)}, f32[256,128]{1,0:T(8,128)S(1)}, u32[]{:S(2)}, u32[]{:S(2)}) collective-permute-start(f32[256,128]{1,0:T(8,128)S(1)} %add.200), channel_id=1, source_target_pairs={{0,2},{1,9},{2,0},{3,11},{4,6},{5,13},{6,4},{7,15},{8,10},{9,1},{1... | collective-permute-start | bytes 393224 | tf_op jit(solution)/shard_map/ppermute | solution.py:407
  48.5 2.5 %collective-permute-start.16 = (f32[3,2,64,128]{3,2,1,0:T(8,128)S(1)}, f32[3,2,64,128]{3,2,1,0:T(8,128)S(1)}, u32[]{:S(2)}, u32[]{:S(2)}) collective-permute-start(f32[3,2,64,128]{3,2,1,0:T(8,128)S(1)} %bitcast.41), channel_id=1, source_target_pairs={{0,4},{1,3},{2,6},{3,1},{4,0},{5,9},{6,2},{7,11},{8,12},{9,5},{10,... | collective-permute-start | bytes 589832 | tf_op jit(solution)/shard_map/ppermute | solution.py:356
  51.1 1.5 %collective-permute-done.19 = f32[256,128]{1,0:T(8,128)S(1)} collective-permute-done((f32[256,128]{1,0:T(8,128)S(1)}, f32[256,128]{1,0:T(8,128)S(1)}, u32[]{:S(2)}, u32[]{:S(2)}) %collective-permute-start.19) | collective-permute-done | bytes 131104 | tf_op jit(solution)/shard_map/ppermute | solution.py:407
  52.6 2.9 %collective-permute-start.20 = (f32[256,128]{1,0:T(8,128)S(1)}, f32[256,128]{1,0:T(8,128)S(1)}, u32[]{:S(2)}, u32[]{:S(2)}) collective-permute-start(f32[256,128]{1,0:T(8,128)S(1)} %add.205), channel_id=1, source_target_pairs={{0,12},{1,7},{2,14},{3,5},{4,8},{5,3},{6,10},{7,1},{8,4},{9,15},{1... | collective-permute-start | bytes 393224 | tf_op jit(solution)/shard_map/ppermute | solution.py:407
  55.5 0.5 collective-permute-start.21
  55.9 1.1 %collective-permute-start.22 = (f32[256,128]{1,0:T(8,128)S(1)}, f32[256,128]{1,0:T(8,128)S(1)}, u32[]{:S(2)}, u32[]{:S(2)}) collective-permute-start(f32[256,128]{1,0:T(8,128)S(1)} %add.205), channel_id=1, source_target_pairs={{0,4},{1,3},{2,6},{3,1},{4,0},{5,7},{6,2},{7,5},{8,12},{9,11},{10,... | collective-permute-start | bytes 393224 | tf_op jit(solution)/shard_map/ppermute | solution.py:407
  57.1 0.1 fusion.8
  57.1 1.6 %collective-permute-start.17 = (f32[2,64,64]{2,1,0:T(8,128)S(1)}, f32[2,64,64]{2,1,0:T(8,128)S(1)}, u32[]{:S(2)}, u32[]{:S(2)}) collective-permute-start(f32[2,64,64]{2,1,0:T(8,128)S(1)} %fusion.8), channel_id=1, source_target_pairs={{0,2},{2,0},{1,3},{3,1},{4,6},{6,4},{5,7},{7,5},{8,10},{10,8},{9,1... | collective-permute-start | bytes 98312 | tf_op jit(solution)/shard_map/ppermute | solution.py:375
  58.7 2.9 %collective-permute-done.17 = f32[2,64,64]{2,1,0:T(8,128)S(1)} collective-permute-done((f32[2,64,64]{2,1,0:T(8,128)S(1)}, f32[2,64,64]{2,1,0:T(8,128)S(1)}, u32[]{:S(2)}, u32[]{:S(2)}) %collective-permute-start.17) | collective-permute-done | bytes 32800 | tf_op jit(solution)/shard_map/ppermute | solution.py:375
  61.6 0.1 fusion.9
  61.7 0.2 fusion.4
  61.9 0.1 collective-permute-start.18
  62.0 1.2 %collective-permute-done.21 = f32[256,128]{1,0:T(8,128)S(1)} collective-permute-done((f32[256,128]{1,0:T(8,128)S(1)}, f32[256,128]{1,0:T(8,128)S(1)}, u32[]{:S(2)}, u32[]{:S(2)}) %collective-permute-start.21) | collective-permute-done | bytes 131104 | tf_op jit(solution)/shard_map/ppermute | solution.py:407
  63.2 0.6 collective-permute-done.22
  63.9 0.7 %pad_maximum_fusion.2 = f32[2,128,256]{2,1,0:T(8,128)} fusion(f32[2,64,256]{2,1,0:T(8,128)S(1)} %get-tuple-element.73, f32[2,64,256]{2,1,0:T(8,128)S(1)} %get-tuple-element.72), kind=kLoop, calls=%fused_computation.11 | loop fusion | flops 65536 | bytes 524288 | tf_op jit(solution)/shard_map/concatenate | solution.py:505
  64.6 0.7 %multiply_subtract_fusion = f32[256,128]{1,0:T(8,128)} fusion(f32[256,128]{1,0:T(8,128)S(1)} %multiply_add_fusion.1.refs_2_, f32[256,128]{1,0:T(8,128)S(1)} %add_add_fusion), kind=kLoop, calls=%fused_computation.20 | loop fusion | flops 65536 | bytes 393216 | tf_op jit(solution)/shard_map/sub | solution.py:509
  (45 shorter events, 0.7 us)
Async XLA Ops:
  1.7 5.4 %copy-start.6 = (bf16[128,128]{1,0:T(8,128)(2,1)S(1)}, bf16[128,128]{1,0:T(8,128)(2,1)}, u32[]{:S(2)}) copy-start(bf16[128,128]{1,0:T(8,128)(2,1)} %constant.86.clone.order) | copy-start | bytes 98308
  1.8 8.9 %collective-permute-start.2 = (f32[2,64,64]{2,1,0:T(8,128)S(1)}, f32[2,64,64]{2,1,0:T(8,128)S(1)}, u32[]{:S(2)}, u32[]{:S(2)}) collective-permute-start(f32[2,64,64]{2,1,0:T(8,128)S(1)} %broadcast_select_fusion.6), channel_id=1, source_target_pairs={{0,6},{1,3},{2,4},{3,1},{4,2},{5,11},{6,0},{7,9},{8,14},{9,7},{10,... | collective-permute-start | bytes 98312 | tf_op jit(solution)/shard_map/ppermute | solution.py:356
  5.8 5.0 %collective-permute-start.1 = (f32[2,64,64]{2,1,0:T(8,128)S(1)}, f32[2,64,64]{2,1,0:T(8,128)S(1)}, u32[]{:S(2)}, u32[]{:S(2)}) collective-permute-start(f32[2,64,64]{2,1,0:T(8,128)S(1)} %broadcast_select_fusion.6), channel_id=1, source_target_pairs={{0,2},{2,0},{1,3},{3,1},{4,6},{6,4},{5,7},{7,5},{8,10},{10,8},{9,1... | collective-permute-start | bytes 98312 | tf_op jit(solution)/shard_map/ppermute | solution.py:375
  6.3 5.0 %collective-permute-start = (f32[2,64,256]{2,1,0:T(8,128)S(1)}, f32[2,64,256]{2,1,0:T(8,128)S(1)}, u32[]{:S(2)}, u32[]{:S(2)}) collective-permute-start(f32[2,64,256]{2,1,0:T(8,128)S(1)} %slice_select_fusion.1), channel_id=1, source_target_pairs={{0,4},{1,3},{2,6},{3,1},{4,0},{5,9},{6,2},{7,11},{8,12},{9,5},{10,... | collective-permute-start | bytes 393224 | tf_op jit(solution)/shard_map/ppermute | solution.py:356
  7.2 0.7 %copy-start.7 = (s32[1,1,16,2]{2,3,1,0:T(2,128)S(1)}, s32[1,1,16,2]{2,3,1,0:T(2,128)}, u32[]{:S(2)}) copy-start(s32[1,1,16,2]{2,3,1,0:T(2,128)} %param.16) | copy-start | bytes 388
  7.8 1.2 %copy-start = (f32[1,1,16,128,128]{4,3,2,1,0:T(8,128)S(1)}, f32[1,1,16,128,128]{4,3,2,1,0:T(8,128)}, u32[]{:S(2)}) copy-start(f32[1,1,16,128,128]{4,3,2,1,0:T(8,128)} %param.18) | copy-start | bytes 3145732
  11.5 0.9 %copy-start.1 = (f32[1,2,128,128]{3,2,1,0:T(8,128)S(1)}, f32[1,2,128,128]{3,2,1,0:T(8,128)}, u32[]{:S(2)}) copy-start(f32[1,2,128,128]{3,2,1,0:T(8,128)} %param.15) | copy-start | bytes 393220
  11.5 2.2 %copy-start.2 = (bf16[2,128,256]{2,1,0:T(8,128)(2,1)S(1)}, bf16[2,128,256]{2,1,0:T(8,128)(2,1)}, u32[]{:S(2)}) copy-start(bf16[2,128,256]{2,1,0:T(8,128)(2,1)} %constant.87.clone.refs_6_) | copy-start | bytes 393220
  11.5 2.2 %copy-start.3 = (bf16[2,256,128]{2,1,0:T(8,128)(2,1)S(1)}, bf16[2,256,128]{2,1,0:T(8,128)(2,1)}, u32[]{:S(2)}) copy-start(bf16[2,256,128]{2,1,0:T(8,128)(2,1)} %constant.88.clone.refs_7_) | copy-start | bytes 393220
  11.6 2.2 %copy-start.4 = (bf16[2,256,128]{2,1,0:T(8,128)(2,1)S(1)}, bf16[2,256,128]{2,1,0:T(8,128)(2,1)}, u32[]{:S(2)}) copy-start(bf16[2,256,128]{2,1,0:T(8,128)(2,1)} %constant.89.clone.refs_8_) | copy-start | bytes 393220
  11.6 2.2 %copy-start.5 = (bf16[2,128,256]{2,1,0:T(8,128)(2,1)S(1)}, bf16[2,128,256]{2,1,0:T(8,128)(2,1)}, u32[]{:S(2)}) copy-start(bf16[2,128,256]{2,1,0:T(8,128)(2,1)} %constant.90.clone.refs_9_) | copy-start | bytes 393220
  11.6 2.2 %collective-permute-start.3 = (f32[768,128]{1,0:T(8,128)S(1)}, f32[768,128]{1,0:T(8,128)S(1)}, u32[]{:S(2)}, u32[]{:S(2)}) collective-permute-start(f32[768,128]{1,0:T(8,128)S(1)} %bitcast.31), channel_id=1, source_target_pairs={{0,1},{1,0},{2,3},{3,2},{4,5},{5,4},{6,7},{7,6},{8,9},{9,8},{10,11... | collective-permute-start | bytes 1179656 | tf_op jit(solution)/shard_map/ppermute | solution.py:332
  12.4 1.3 %collective-permute-start.4 = (f32[256,128]{1,0:T(8,128)S(1)}, f32[256,128]{1,0:T(8,128)S(1)}, u32[]{:S(2)}, u32[]{:S(2)}) collective-permute-start(f32[256,128]{1,0:T(8,128)S(1)} %bitcast.34), channel_id=1, source_target_pairs={{0,1},{1,0},{2,3},{3,2},{4,5},{5,4},{6,7},{7,6},{8,9},{9,8},{10,11... | collective-permute-start | bytes 393224 | tf_op jit(solution)/shard_map/ppermute | solution.py:332
  18.2 1.4 %collective-permute-start.5 = (f32[256,128]{1,0:T(8,128)S(1)}, f32[256,128]{1,0:T(8,128)S(1)}, u32[]{:S(2)}, u32[]{:S(2)}) collective-permute-start(f32[256,128]{1,0:T(8,128)S(1)} %get-tuple-element.39), channel_id=1, source_target_pairs={{0,1},{1,0},{2,3},{3,2},{4,5},{5,4},{6,7},{7,6},{8,9},{9,8},{10,11... | collective-permute-start | bytes 393224 | tf_op jit(solution)/shard_map/ppermute | solution.py:332
  19.6 1.8 %collective-permute-start.9 = (f32[768,128]{1,0:T(8,128)S(1)}, f32[768,128]{1,0:T(8,128)S(1)}, u32[]{:S(2)}, u32[]{:S(2)}) collective-permute-start(f32[768,128]{1,0:T(8,128)S(1)} %get-tuple-element.45), channel_id=1, source_target_pairs={{0,1},{1,0},{2,3},{3,2},{4,5},{5,4},{6,7},{7,6},{8,9},{9,8},{10,11... | collective-permute-start | bytes 1179656 | tf_op jit(solution)/shard_map/ppermute | solution.py:332
  19.8 5.0 %collective-permute-start.6 = (f32[256,128]{1,0:T(8,128)S(1)}, f32[256,128]{1,0:T(8,128)S(1)}, u32[]{:S(2)}, u32[]{:S(2)}) collective-permute-start(f32[256,128]{1,0:T(8,128)S(1)} %add.182), channel_id=1, source_target_pairs={{0,2},{1,9},{2,0},{3,11},{4,6},{5,13},{6,4},{7,15},{8,10},{9,1},{1... | collective-permute-start | bytes 393224 | tf_op jit(solution)/shard_map/ppermute | solution.py:407
  21.5 12.1 %collective-permute-start.10 = (f32[768,128]{1,0:T(8,128)S(1)}, f32[768,128]{1,0:T(8,128)S(1)}, u32[]{:S(2)}, u32[]{:S(2)}) collective-permute-start(f32[768,128]{1,0:T(8,128)S(1)} %add.194), channel_id=1, source_target_pairs={{0,4},{1,3},{2,6},{3,1},{4,0},{5,9},{6,2},{7,11},{8,12},{9,5},{10,... | collective-permute-start | bytes 1179656 | tf_op jit(solution)/shard_map/ppermute | solution.py:356
  24.8 6.3 %collective-permute-start.7 = (f32[256,128]{1,0:T(8,128)S(1)}, f32[256,128]{1,0:T(8,128)S(1)}, u32[]{:S(2)}, u32[]{:S(2)}) collective-permute-start(f32[256,128]{1,0:T(8,128)S(1)} %add.183), channel_id=1, source_target_pairs={{0,4},{1,3},{2,6},{3,1},{4,0},{5,7},{6,2},{7,5},{8,12},{9,11},{10,... | collective-permute-start | bytes 393224 | tf_op jit(solution)/shard_map/ppermute | solution.py:407
  31.2 7.3 %collective-permute-start.8 = (f32[256,128]{1,0:T(8,128)S(1)}, f32[256,128]{1,0:T(8,128)S(1)}, u32[]{:S(2)}, u32[]{:S(2)}) collective-permute-start(f32[256,128]{1,0:T(8,128)S(1)} %add.184), channel_id=1, source_target_pairs={{0,8},{1,5},{2,10},{3,7},{4,12},{5,1},{6,14},{7,3},{8,0},{9,13},{1... | collective-permute-start | bytes 393224 | tf_op jit(solution)/shard_map/ppermute | solution.py:407
  33.6 5.0 %collective-permute-start.11 = (f32[256,128]{1,0:T(8,128)S(1)}, f32[256,128]{1,0:T(8,128)S(1)}, u32[]{:S(2)}, u32[]{:S(2)}) collective-permute-start(f32[256,128]{1,0:T(8,128)S(1)} %slice_select_fusion.2), channel_id=1, source_target_pairs={{0,2},{2,0},{1,3},{3,1},{4,6},{6,4},{5,7},{7,5},{8,10},{10,8},{9,1... | collective-permute-start | bytes 393224 | tf_op jit(solution)/shard_map/ppermute | solution.py:375
  38.8 2.0 %collective-permute-start.12 = (f32[768,128]{1,0:T(8,128)S(1)}, f32[768,128]{1,0:T(8,128)S(1)}, u32[]{:S(2)}, u32[]{:S(2)}) collective-permute-start(f32[768,128]{1,0:T(8,128)S(1)} %multiply_add_fusion.refs_1_), channel_id=1, source_target_pairs={{0,1},{1,0},{2,3},{3,2},{4,5},{5,4},{6,7},{7,6},{8,9},{9,8},{10,11... | collective-permute-start | bytes 1179656 | tf_op jit(solution)/shard_map/ppermute | solution.py:332
  38.9 1.9 %collective-permute-start.13 = (f32[256,128]{1,0:T(8,128)S(1)}, f32[256,128]{1,0:T(8,128)S(1)}, u32[]{:S(2)}, u32[]{:S(2)}) collective-permute-start(f32[256,128]{1,0:T(8,128)S(1)} %multiply_add_fusion.1.refs_2_), channel_id=1, source_target_pairs={{0,1},{1,0},{2,3},{3,2},{4,5},{5,4},{6,7},{7,6},{8,9},{9,8},{10,11... | collective-permute-start | bytes 393224 | tf_op jit(solution)/shard_map/ppermute | solution.py:332
  45.1 1.4 %collective-permute-start.14 = (f32[256,128]{1,0:T(8,128)S(1)}, f32[256,128]{1,0:T(8,128)S(1)}, u32[]{:S(2)}, u32[]{:S(2)}) collective-permute-start(f32[256,128]{1,0:T(8,128)S(1)} %get-tuple-element.50), channel_id=1, source_target_pairs={{0,1},{1,0},{2,3},{3,2},{4,5},{5,4},{6,7},{7,6},{8,9},{9,8},{10,11... | collective-permute-start | bytes 393224 | tf_op jit(solution)/shard_map/ppermute | solution.py:332
  46.6 1.9 %collective-permute-start.15 = (f32[768,128]{1,0:T(8,128)S(1)}, f32[768,128]{1,0:T(8,128)S(1)}, u32[]{:S(2)}, u32[]{:S(2)}) collective-permute-start(f32[768,128]{1,0:T(8,128)S(1)} %get-tuple-element.55), channel_id=1, source_target_pairs={{0,1},{1,0},{2,3},{3,2},{4,5},{5,4},{6,7},{7,6},{8,9},{9,8},{10,11... | collective-permute-start | bytes 1179656 | tf_op jit(solution)/shard_map/ppermute | solution.py:332
  46.8 5.7 %collective-permute-start.19 = (f32[256,128]{1,0:T(8,128)S(1)}, f32[256,128]{1,0:T(8,128)S(1)}, u32[]{:S(2)}, u32[]{:S(2)}) collective-permute-start(f32[256,128]{1,0:T(8,128)S(1)} %add.200), channel_id=1, source_target_pairs={{0,2},{1,9},{2,0},{3,11},{4,6},{5,13},{6,4},{7,15},{8,10},{9,1},{1... | collective-permute-start | bytes 393224 | tf_op jit(solution)/shard_map/ppermute | solution.py:407
  48.5 8.5 %collective-permute-start.16 = (f32[3,2,64,128]{3,2,1,0:T(8,128)S(1)}, f32[3,2,64,128]{3,2,1,0:T(8,128)S(1)}, u32[]{:S(2)}, u32[]{:S(2)}) collective-permute-start(f32[3,2,64,128]{3,2,1,0:T(8,128)S(1)} %bitcast.41), channel_id=1, source_target_pairs={{0,4},{1,3},{2,6},{3,1},{4,0},{5,9},{6,2},{7,11},{8,12},{9,5},{10,... | collective-permute-start | bytes 589832 | tf_op jit(solution)/shard_map/ppermute | solution.py:356
  52.6 9.4 %collective-permute-start.20 = (f32[256,128]{1,0:T(8,128)S(1)}, f32[256,128]{1,0:T(8,128)S(1)}, u32[]{:S(2)}, u32[]{:S(2)}) collective-permute-start(f32[256,128]{1,0:T(8,128)S(1)} %add.205), channel_id=1, source_target_pairs={{0,12},{1,7},{2,14},{3,5},{4,8},{5,3},{6,10},{7,1},{8,4},{9,15},{1... | collective-permute-start | bytes 393224 | tf_op jit(solution)/shard_map/ppermute | solution.py:407
  55.5 7.7 %collective-permute-start.21 = (f32[256,128]{1,0:T(8,128)S(1)}, f32[256,128]{1,0:T(8,128)S(1)}, u32[]{:S(2)}, u32[]{:S(2)}) collective-permute-start(f32[256,128]{1,0:T(8,128)S(1)} %add.205), channel_id=1, source_target_pairs={{0,8},{1,5},{2,10},{3,7},{4,12},{5,1},{6,14},{7,3},{8,0},{9,13},{1... | collective-permute-start | bytes 393224 | tf_op jit(solution)/shard_map/ppermute | solution.py:407
  55.9 7.9 %collective-permute-start.22 = (f32[256,128]{1,0:T(8,128)S(1)}, f32[256,128]{1,0:T(8,128)S(1)}, u32[]{:S(2)}, u32[]{:S(2)}) collective-permute-start(f32[256,128]{1,0:T(8,128)S(1)} %add.205), channel_id=1, source_target_pairs={{0,4},{1,3},{2,6},{3,1},{4,0},{5,7},{6,2},{7,5},{8,12},{9,11},{10,... | collective-permute-start | bytes 393224 | tf_op jit(solution)/shard_map/ppermute | solution.py:407
  57.1 4.5 %collective-permute-start.17 = (f32[2,64,64]{2,1,0:T(8,128)S(1)}, f32[2,64,64]{2,1,0:T(8,128)S(1)}, u32[]{:S(2)}, u32[]{:S(2)}) collective-permute-start(f32[2,64,64]{2,1,0:T(8,128)S(1)} %fusion.8), channel_id=1, source_target_pairs={{0,2},{2,0},{1,3},{3,1},{4,6},{6,4},{5,7},{7,5},{8,10},{10,8},{9,1... | collective-permute-start | bytes 98312 | tf_op jit(solution)/shard_map/ppermute | solution.py:375
  61.9 1.9 %collective-permute-start.18 = (f32[2,64,256]{2,1,0:T(8,128)S(1)}, f32[2,64,256]{2,1,0:T(8,128)S(1)}, u32[]{:S(2)}, u32[]{:S(2)}) collective-permute-start(f32[2,64,256]{2,1,0:T(8,128)S(1)} %fusion.4), channel_id=1, source_target_pairs={{0,1},{1,0},{2,3},{3,2},{4,5},{5,4},{6,7},{7,6},{8,9},{9,8},{10,11... | collective-permute-start | bytes 393224 | tf_op jit(solution)/shard_map/ppermute | solution.py:332
